TPU v7x, 32 devices: a whole 2x2x4 slice. The times are simulated.
32 devices in a mesh: dp: 2 (over core), ctx: 4 (over z), tp: 4 (over y, x).
Axes of the slice: x: 2, y: 2, z: 4, core: 2. Of those that a mesh axis runs over, the one named last changes fastest.
Arguments:
- query: bfloat16 [2048, 32, 128], P(('dp', 'ctx'), 'tp'), parts along dimension 0, may hold values from -30 to 30
- keys: bfloat16 [2048, 4, 128], P(('dp', 'ctx'), 'tp'), parts along dimension 0, may hold values from -6 to 6
- values: bfloat16 [2048, 4, 128], P(('dp', 'ctx'), 'tp'), parts along dimension 0, may hold values from -6 to 6
- output_gradient: bfloat16 [2048, 32, 128], P(('dp', 'ctx'), 'tp'), parts along dimension 0, may hold values from -6 to 6
- doc_lengths: int32 [16], P('dp'), parts along dimension 0, may hold values from 1 to 512, 1024 in all
- block_owner: int32 [8, 4], P('dp'), parts along dimension 0, may hold values from 0 to 3, each once within a row
Outputs:
- attended: bfloat16 [2048, 32, 128], P(('dp', 'ctx'), 'tp'), parts along dimension 0
- query_grad: bfloat16 [2048, 32, 128], P(('dp', 'ctx'), 'tp'), parts along dimension 0
- key_grad: bfloat16 [2048, 4, 128], P(('dp', 'ctx'), 'tp'), parts along dimension 0
- value_grad: bfloat16 [2048, 4, 128], P(('dp', 'ctx'), 'tp'), parts along dimension 0
There are 2 independent parts, one for each index of `dp`. A program takes and returns all parts, laid end to end along the dimension named above; each array names one. Nothing has to cross between parts.
Inputs may be any that keep to these rules, and one draw needn't show every extreme that they name: `block_owner`: each row lists the owners of one loader shard's 4 blocks in order and names every owner once. `doc_lengths`: the lengths sum to 1024.
All inputs are finite; a program needn't handle non-finite values.
Results may differ from a plain program's by a relative error of at most 0.039.
Values may be sent and summed in bfloat16 or wider, within the bound.
No kernel may reach another device: no remote copies, remote signals or barrier semaphores. Data moves between devices by JAX's collectives and lax.ppermute only.
A program may use at most 64 MiB of HBM per device.

v0:
```python
import jax
import jax.numpy as jnp
from jax import lax
from jax.sharding import PartitionSpec as P

NEG_LARGE = -1e30


def passed_along(array, axis, by):
    size = lax.axis_size(axis)
    return lax.ppermute(array, axis, [(i, (i + by) % size) for i in range(size)])


def document_index(token_positions, doc_lengths):
    doc_ends = jnp.cumsum(doc_lengths)
    return jnp.sum((doc_ends[None, :] <= token_positions[:, None]).astype(jnp.int32), axis=1)


def owner_positions(block_owner, owner_id, local_rows):
    cycle_size = block_owner.shape[0]
    block_rows = local_rows // cycle_size
    slot_ids = jnp.arange(cycle_size, dtype=jnp.int32)
    matches = (block_owner == owner_id).astype(jnp.int32)
    slot_of = jnp.sum(matches * slot_ids[None, :], axis=1)
    starts = slot_ids * local_rows + slot_of * block_rows
    return (starts[:, None] + jnp.arange(block_rows, dtype=jnp.int32)[None, :]).reshape(-1)


def on_device(query, keys, values, output_gradient, doc_lengths, block_owner):
    cycle_size = lax.axis_size("ctx")
    own_index = lax.axis_index("ctx")
    local_rows, heads_here, head_width = query.shape
    groups_here = keys.shape[1]
    heads_per_group = heads_here // groups_here
    block_rows = local_rows // cycle_size
    softmax_scale = head_width ** (-0.5)
    own_targets = lax.dynamic_index_in_dim(block_owner, own_index, 0, keepdims=False)
    slot_ids = jnp.arange(cycle_size, dtype=jnp.int32)
    send_order = jnp.sum(
        (own_targets[:, None] == slot_ids[None, :]).astype(jnp.int32) * slot_ids[:, None], axis=0
    )

    def arrange(source):
        return jnp.take(source.reshape(cycle_size, block_rows, -1), send_order, axis=0)

    loaded_pairs = jnp.stack([keys, values], axis=1)
    received = (
        lax.all_to_all(arrange(query), "ctx", split_axis=0, concat_axis=0, tiled=True),
        lax.all_to_all(arrange(loaded_pairs), "ctx", split_axis=0, concat_axis=0, tiled=True),
        lax.all_to_all(arrange(output_gradient), "ctx", split_axis=0, concat_axis=0, tiled=True),
    )
    query_rows_all = received[0].reshape(local_rows, groups_here, heads_per_group, head_width)
    key_value = received[1].reshape(local_rows, 2, groups_here, head_width)
    output_gradients = received[2].reshape(local_rows, groups_here, heads_per_group, head_width)
    query_pos = owner_positions(block_owner, own_index, local_rows)
    query_doc = document_index(query_pos, doc_lengths)

    def visible(owner_id):
        key_pos = owner_positions(block_owner, owner_id, local_rows)
        key_doc = document_index(key_pos, doc_lengths)
        return (query_doc[:, None] == key_doc[None, :]) & (key_pos[None, :] <= query_pos[:, None])

    def forward_tile(softmax_state, pair_rows, allowed):
        row_max, row_sum, totals = softmax_state
        scores = (
            jnp.einsum(
                "tgrd,ugd->tgru",
                query_rows_all,
                pair_rows[:, 0],
                preferred_element_type=jnp.float32,
            )
            * softmax_scale
        )
        allowed = allowed[:, None, None, :]
        scores = jnp.where(allowed, scores, NEG_LARGE)
        new_max = jnp.maximum(row_max, jnp.max(scores, axis=-1))
        weights = jnp.where(allowed, jnp.exp(scores - new_max[..., None]), 0.0)
        rescale = jnp.exp(row_max - new_max)
        row_sum = row_sum * rescale + jnp.sum(weights, axis=-1)
        totals = totals * rescale[..., None] + jnp.einsum(
            "tgru,ugd->tgrd",
            weights.astype(jnp.bfloat16),
            pair_rows[:, 1],
            preferred_element_type=jnp.float32,
        )
        return (new_max, row_sum, totals)

    stat_shape = (local_rows, groups_here, heads_per_group)
    softmax_state = (
        jnp.full(stat_shape, NEG_LARGE, jnp.float32),
        jnp.zeros(stat_shape, jnp.float32),
        jnp.zeros(query_rows_all.shape, jnp.float32),
    )
    softmax_state = forward_tile(softmax_state, key_value, visible(own_index))

    def forward_turn(turn_index, loop_state):
        moving, partial_state = loop_state
        moving = passed_along(moving, "ctx", 1)
        owner_id = (own_index - turn_index) % cycle_size
        return (moving, forward_tile(partial_state, moving, visible(owner_id)))

    softmax_state = lax.fori_loop(1, cycle_size, forward_turn, (key_value, softmax_state))[1]
    row_max, row_sum, totals = softmax_state
    attended = (totals / row_sum[..., None]).astype(jnp.bfloat16)
    log_sums = row_max + jnp.log(row_sum)
    row_delta_sum = jnp.sum(
        output_gradients.astype(jnp.float32) * attended.astype(jnp.float32), axis=-1
    )

    def backward_tile(pair_rows, allowed):
        scores = (
            jnp.einsum(
                "tgrd,ugd->tgru",
                query_rows_all,
                pair_rows[:, 0],
                preferred_element_type=jnp.float32,
            )
            * softmax_scale
        )
        probs = jnp.where(allowed[:, None, None, :], jnp.exp(scores - log_sums[..., None]), 0.0)
        value_part = jnp.einsum(
            "tgru,tgrd->ugd",
            probs.astype(jnp.bfloat16),
            output_gradients,
            preferred_element_type=jnp.float32,
        )
        products = jnp.einsum(
            "tgrd,ugd->tgru", output_gradients, pair_rows[:, 1], preferred_element_type=jnp.float32
        )
        slopes = (probs * (products - row_delta_sum[..., None])).astype(jnp.bfloat16)
        query_part = (
            jnp.einsum(
                "tgru,ugd->tgrd", slopes, pair_rows[:, 0], preferred_element_type=jnp.float32
            )
            * softmax_scale
        )
        key_part = (
            jnp.einsum("tgru,tgrd->ugd", slopes, query_rows_all, preferred_element_type=jnp.float32)
            * softmax_scale
        )
        return (query_part, jnp.stack([key_part, value_part], axis=1))

    query_grad, pair_grad = backward_tile(key_value, visible(own_index))

    def backward_turn(turn_index, loop_state):
        moving, moving_grad, query_acc = loop_state
        moving = passed_along(moving, "ctx", 1)
        moving_grad = passed_along(moving_grad.astype(jnp.bfloat16), "ctx", 1).astype(
            moving_grad.dtype
        )
        owner_id = (own_index - turn_index) % cycle_size
        query_part, pair_part = backward_tile(moving, visible(owner_id))
        return (moving, moving_grad + pair_part, query_acc + query_part)

    loop_out = lax.fori_loop(1, cycle_size, backward_turn, (key_value, pair_grad, query_grad))
    pair_grad = passed_along(loop_out[1].astype(jnp.bfloat16), "ctx", 1).astype(jnp.float32)
    query_grad = loop_out[2]
    return (
        attended.reshape(local_rows, heads_here, head_width),
        query_grad.astype(jnp.bfloat16).reshape(local_rows, heads_here, head_width),
        pair_grad[:, 0].astype(jnp.bfloat16),
        pair_grad[:, 1].astype(jnp.bfloat16),
    )


def solution(mesh):
    placed = (
        P(("dp", "ctx"), "tp", None),
        P(("dp", "ctx"), "tp", None),
        P(("dp", "ctx"), "tp", None),
        P(("dp", "ctx"), "tp", None),
        P("dp"),
        P("dp", None),
    )
    return jax.shard_map(
        on_device,
        mesh=mesh,
        in_specs=placed,
        out_specs=(
            P(("dp", "ctx"), "tp", None),
            P(("dp", "ctx"), "tp", None),
            P(("dp", "ctx"), "tp", None),
            P(("dp", "ctx"), "tp", None),
        ),
        check_vma=False,
    )
```

profile of v0, /device:TPU:0, one launch (start us, length us, event | category | flops | bytes accessed | tf_op | source)
XLA Modules:
  0.0 133.4 jit_solution(1578177129235384709)
XLA Ops:
  3.9 6.3 %all-to-all-start = ((bf16[4,64,256]{2,1,0:T(8,128)(2,1)}), bf16[4,64,256]{2,1,0:T(8,128)(2,1)S(1)}, u32[]{:S(2)}, u32[]{:S(2)}) async-start(bf16[4,64,256]{2,1,0:T(8,128)(2,1)} %broadcast_select_fusion.2), calls=%async_computation | async-start | bytes 262144 | tf_op jit(solution)/shard_map/all_to_all | solution.py:49
  11.0 1.3 reshape.773
  13.7 1.1 broadcast_select_fusion.1
  14.9 1.4 %all-to-all-done = bf16[4,64,256]{2,1,0:T(8,128)(2,1)S(1)} async-done(((bf16[4,64,256]{2,1,0:T(8,128)(2,1)}), bf16[4,64,256]{2,1,0:T(8,128)(2,1)S(1)}, u32[]{:S(2)}, u32[]{:S(2)}) %all-to-all-start) | async-done | bytes 131104 | tf_op jit(solution)/shard_map/all_to_all | solution.py:49
  16.3 3.7 %all-to-all-start.1 = ((bf16[4,64,1024]{2,1,0:T(8,128)(2,1)}), bf16[4,64,1024]{2,1,0:T(8,128)(2,1)S(1)}, u32[]{:S(2)}, u32[]{:S(2)}) async-start(bf16[4,64,1024]{2,1,0:T(8,128)(2,1)} %get-tuple-element.800), calls=%async_computation.1 | async-start | bytes 1048576 | tf_op jit(solution)/shard_map/all_to_all | solution.py:48
  20.9 13.0 %all-to-all-done.1 = bf16[4,64,1024]{2,1,0:T(8,128)(2,1)S(1)} async-done(((bf16[4,64,1024]{2,1,0:T(8,128)(2,1)}), bf16[4,64,1024]{2,1,0:T(8,128)(2,1)S(1)}, u32[]{:S(2)}, u32[]{:S(2)}) %all-to-all-start.1) | async-done | bytes 524320 | tf_op jit(solution)/shard_map/all_to_all | solution.py:48
  33.9 4.1 %all-to-all-start.2 = ((bf16[4,64,1024]{2,1,0:T(8,128)(2,1)}), bf16[4,64,1024]{2,1,0:T(8,128)(2,1)}, u32[]{:S(2)}, u32[]{:S(2)}) async-start(bf16[4,64,1024]{2,1,0:T(8,128)(2,1)} %get-tuple-element.801), calls=%async_computation.2 | async-start | bytes 1048576 | tf_op jit(solution)/shard_map/all_to_all | solution.py:50
  39.2 1.7 %fusion.44 = f32[256,1,8,128]{0,3,2,1:T(8,128)} fusion(f32[256,256,8]{1,0,2:T(8,128)S(1)} %get-tuple-element.803, f32[256,8]{0,1:T(8,128)S(1)} %get-tuple-element.799, pred[256,256]{0,1:T(8,128)(4,1)S(1)} %compare_and_fusion.2, f32[256,8]{0,1:T(8,128)S(1)} %get-tuple-element.797, bf16[256,1,1,128]{0,3,2,1:T(8,128)(2,1)S(1)} %copy.113), kind=kOutput, calls=%fused_computation.81 | convolution fusion | flops 137101312 | bytes 3293184 | tf_op jit(solution)/shard_map/tgru,ugd->tgrd/dot_general | solution.py:80
  40.9 2.6 %copy.87 = f32[256,1,8,128]{3,0,2,1:T(8,128)} copy(f32[256,1,8,128]{0,3,2,1:T(8,128)} %fusion.44) | data formatting | bytes 2097152
  43.6 32.7 %while.42 = (s32[]{:T(128)}, bf16[256,2,1,128]{3,0,2,1:T(8,128)(2,1)S(1)}, f32[256,1,8]{0,2,1:T(8,128)S(1)}, f32[256,1,8]{0,2,1:T(8,128)S(1)}, f32[256,1,8,128]{...) while((s32[]{:T(128)}, ...), condition=%wide.region_11.13_spmd.clone, body=%wide.region_6.12_spmd.clone.sunk | while | flops 275984704 | bytes 18625048 | solution.py:102
  43.6 2.0 %collective-permute-start = (bf16[256,2,1,128]{3,0,2,1:T(8,128)(2,1)S(1)}, bf16[256,2,1,128]{3,0,2,1:T(8,128)(2,1)S(1)}, u32[]{:S(2)}, u32[]{:S(2)}) collective-permute-start(bf16[256,2,1,128]{3,0,2,1:T(8,128)(2,1)S(1)} %get-tuple-element.974), channel_id=1, source_target_pairs={{0,4},{4,8},{8,12},{12,0},{1,5},{5,9},{9,13},{13,1},{2,6},{6,10},{... | collective-permute-start | bytes 393224 | tf_op jit(solution)/shard_map/while/body/eval_jaxpr/ppermute | solution.py:11
  46.3 6.6 %collective-permute-done = bf16[256,2,1,128]{3,0,2,1:T(8,128)(2,1)S(1)} collective-permute-done((bf16[256,2,1,128]{3,0,2,1:T(8,128)(2,1)S(1)}, bf16[256,2,1,128]{3,0,2,1:T(8,128)(2,1)S(1)}, u32[]{:S(2)}, u32[]{:S(2)}) %collective-permute-start) | collective-permute-done | bytes 131104 | tf_op jit(solution)/shard_map/while/body/eval_jaxpr/ppermute | solution.py:11
  54.2 1.0 fusion.94
  57.4 5.6 %collective-permute-done = bf16[256,2,1,128]{3,0,2,1:T(8,128)(2,1)S(1)} collective-permute-done((bf16[256,2,1,128]{3,0,2,1:T(8,128)(2,1)S(1)}, bf16[256,2,1,128]{3,0,2,1:T(8,128)(2,1)S(1)}, u32[]{:S(2)}, u32[]{:S(2)}) %collective-permute-start) | collective-permute-done | bytes 131104 | tf_op jit(solution)/shard_map/while/body/eval_jaxpr/ppermute | solution.py:11
  66.9 6.1 %collective-permute-done = bf16[256,2,1,128]{3,0,2,1:T(8,128)(2,1)S(1)} collective-permute-done((bf16[256,2,1,128]{3,0,2,1:T(8,128)(2,1)S(1)}, bf16[256,2,1,128]{3,0,2,1:T(8,128)(2,1)S(1)}, u32[]{:S(2)}, u32[]{:S(2)}) %collective-permute-start) | collective-permute-done | bytes 131104 | tf_op jit(solution)/shard_map/while/body/eval_jaxpr/ppermute | solution.py:11
  74.3 1.0 fusion.94
  77.0 1.1 copy.116
  78.2 3.0 %multiply_reduce_fusion = (f32[256,8]{1,0:T(8,128)S(1)}, bf16[256,1,8,128]{3,2,0,1:T(8,128)(2,1)}) fusion(bf16[256,1,8,128]{3,2,0,1:T(8,128)(2,1)S(1)} %bitcast.350, f32[256,8]{1,0:T(8,128)S(1)} %copy.89, f32[256,1,8,128]{3,0,2,1:T(8,128)} %get-tuple-element.586), kind=kLoop, calls=%fused_computation.91 | loop fusion | flops 1570816 | bytes 2113536 | tf_op jit(solution)/shard_map/reduce_sum | solution.py:106
  81.9 1.5 %fusion.41 = bf16[256,8,256]{0,2,1:T(8,128)(2,1)S(1)} fusion(f32[256,256,8]{1,0,2:T(8,128)S(1)} %get-tuple-element.803, f32[256,8]{0,1:T(8,128)} %copy.93, f32[256,8]{0,1:T(8,128)} %bitcast.367, pred[256,256]{0,1:T(8,128)(4,1)S(1)} %compare_and_fusion.2, bf16[256,8,128]{2,1,0:T(8,128)(2,1)S(1)} %bitcast.351, bf16[256,1,1,128]{0,3,2,1:T(8,128)(2,1)S(1)} %copy.113), kind=kOutput, calls=%fused_computation.76 | convolution fusion | flops 137363456 | bytes 3817472 | tf_op jit(solution)/shard_map/tgrd,ugd->tgru/dot_general | solution.py:127
  84.4 1.3 fusion.42
  85.7 2.7 %copy.94 = bf16[256,8,256]{2,1,0:T(8,128)(2,1)} copy(bf16[256,8,256]{0,2,1:T(8,128)(2,1)} %copy-done.7) | data formatting | bytes 2097152 | tf_op jit(solution)/shard_map/reshape.50
  88.4 1.4 %fusion.49 = bf16[256,8,256]{0,2,1:T(8,128)(2,1)} fusion(f32[256,256,8]{1,0,2:T(8,128)S(1)} %get-tuple-element.803, f32[256,8]{0,1:T(8,128)S(1)} %bitcast.368, pred[256,256]{0,1:T(8,128)(4,1)S(1)} %compare_and_fusion.2), kind=kLoop, calls=%fused_computation.87 | loop fusion | flops 2097152 | bytes 3219456 | tf_op jit(solution)/shard_map/reshape.53
  89.9 1.6 %copy.100 = f32[256,1,8,128]{3,0,2,1:T(8,128)S(1)} copy(f32[256,1,8,128]{0,3,2,1:T(8,128)} %fusion.42) | data formatting | bytes 2097152
  91.5 1.6 %fusion.46 = bf16[256,1,1,128]{0,3,2,1:T(8,128)(2,1)S(1)} fusion(bf16[256,8,128]{2,1,0:T(8,128)(2,1)S(1)} %bitcast.349, bf16[256,8,256]{2,1,0:T(8,128)(2,1)} %copy.94), kind=kOutput, calls=%fused_computation.85 | convolution fusion | flops 134283264 | bytes 1638400 | tf_op jit(solution)/shard_map/tgru,tgrd->ugd/dot_general | solution.py:138
  93.1 2.7 %copy.95 = bf16[256,8,256]{2,1,0:T(8,128)(2,1)} copy(bf16[256,8,256]{0,2,1:T(8,128)(2,1)} %fusion.49) | data formatting | bytes 2097152 | tf_op jit(solution)/shard_map/reshape.53
  95.8 1.6 %convolution_bitcast_fusion.4 = bf16[256,1,1,128]{0,3,2,1:T(8,128)(2,1)S(1)} fusion(bf16[256,8,128]{2,1,0:T(8,128)(2,1)S(1)} %bitcast.353, bf16[256,8,256]{2,1,0:T(8,128)(2,1)} %copy.95), kind=kOutput, calls=%fused_computation.82 | convolution fusion | flops 134217728 | bytes 1638400 | tf_op jit(solution)/shard_map/tgru,tgrd->ugd/dot_general | solution.py:121
  97.6 28.3 %while.43 = (s32[]{:T(128)}, bf16[256,2,1,128]{3,0,2,1:T(8,128)(2,1)S(1)}, bf16[256,2,1,128]{3,0,2,1:T(8,128)(2,1)S(1)}, f32[256,1,8,128]{3,0,2,1:T(8,128)S(1)},...) while((s32[]{:T(128)}, ...), condition=%wide.region_16.18_spmd.clone, body=%wide.region_13.17_spmd.clone.sunk | while | flops 675780928 | bytes 16085530 | solution.py:155
  98.4 6.0 %collective-permute-done.1 = bf16[256,2,1,128]{3,0,2,1:T(8,128)(2,1)S(1)} collective-permute-done((bf16[256,2,1,128]{3,0,2,1:T(8,128)(2,1)S(1)}, bf16[256,2,1,128]{3,0,2,1:T(8,128)(2,1)S(1)}, u32[]{:S(2)}, u32[]{:S(2)}) %collective-permute-start.1) | collective-permute-done | bytes 131104 | tf_op jit(solution)/shard_map/while/body/eval_jaxpr/ppermute | solution.py:11
  107.8 6.0 %collective-permute-done.1 = bf16[256,2,1,128]{3,0,2,1:T(8,128)(2,1)S(1)} collective-permute-done((bf16[256,2,1,128]{3,0,2,1:T(8,128)(2,1)S(1)}, bf16[256,2,1,128]{3,0,2,1:T(8,128)(2,1)S(1)}, u32[]{:S(2)}, u32[]{:S(2)}) %collective-permute-start.1) | collective-permute-done | bytes 131104 | tf_op jit(solution)/shard_map/while/body/eval_jaxpr/ppermute | solution.py:11
  117.3 6.0 %collective-permute-done.1 = bf16[256,2,1,128]{3,0,2,1:T(8,128)(2,1)S(1)} collective-permute-done((bf16[256,2,1,128]{3,0,2,1:T(8,128)(2,1)S(1)}, bf16[256,2,1,128]{3,0,2,1:T(8,128)(2,1)S(1)}, u32[]{:S(2)}, u32[]{:S(2)}) %collective-permute-start.1) | collective-permute-done | bytes 131104 | tf_op jit(solution)/shard_map/while/body/eval_jaxpr/ppermute | solution.py:11
  126.0 1.4 %copy.131 = bf16[256,1,8,128]{3,2,0,1:T(8,128)(2,1)} copy(f32[256,1,8,128]{3,0,2,1:T(8,128)S(1)} %get-tuple-element.589) | data formatting | bytes 1572864 | tf_op jit(solution)/shard_map/while | solution.py:155
  127.4 5.3 %collective-permute-done.3 = bf16[256,2,1,128]{3,0,2,1:T(8,128)(2,1)S(1)} collective-permute-done((bf16[256,2,1,128]{3,0,2,1:T(8,128)(2,1)S(1)}, bf16[256,2,1,128]{3,0,2,1:T(8,128)(2,1)S(1)}, u32[]{:S(2)}, u32[]{:S(2)}) %collective-permute-start.3) | collective-permute-done | bytes 131104 | tf_op jit(solution)/shard_map/ppermute | solution.py:11
  (179 shorter events, 30.9 us)
Async XLA Ops:
  0.6 11.7 %copy-start.11 = (bf16[256,8,128]{2,1,0:T(8,128)(2,1)S(1)}, bf16[256,8,128]{2,1,0:T(8,128)(2,1)}, u32[]{:S(2)}) copy-start(bf16[256,8,128]{2,1,0:T(8,128)(2,1)} %param.12) | copy-start | bytes 1572868
  3.9 12.4 %all-to-all-start = ((bf16[4,64,256]{2,1,0:T(8,128)(2,1)}), bf16[4,64,256]{2,1,0:T(8,128)(2,1)S(1)}, u32[]{:S(2)}, u32[]{:S(2)}) async-start(bf16[4,64,256]{2,1,0:T(8,128)(2,1)} %broadcast_select_fusion.2), calls=%async_computation | async-start | bytes 262144 | tf_op jit(solution)/shard_map/all_to_all | solution.py:49
  13.1 7.0 %copy-start.14 = (s32[8]{0:T(128)S(1)}, s32[8]{0:T(128)}, u32[]{:S(2)}) copy-start(s32[8]{0:T(128)} %param.16) | copy-start | bytes 100
  16.3 17.6 %all-to-all-start.1 = ((bf16[4,64,1024]{2,1,0:T(8,128)(2,1)}), bf16[4,64,1024]{2,1,0:T(8,128)(2,1)S(1)}, u32[]{:S(2)}, u32[]{:S(2)}) async-start(bf16[4,64,1024]{2,1,0:T(8,128)(2,1)} %get-tuple-element.800), calls=%async_computation.1 | async-start | bytes 1048576 | tf_op jit(solution)/shard_map/all_to_all | solution.py:48
  20.6 18.0 %copy-start.8 = (bf16[256,2,1,128]{3,0,2,1:T(8,128)(2,1)}, bf16[256,2,1,128]{3,0,2,1:T(8,128)(2,1)S(1)}, u32[]{:S(2)}) copy-start(bf16[256,2,1,128]{3,0,2,1:T(8,128)(2,1)S(1)} %copy.86) | copy-start | bytes 393220
  33.9 43.1 %all-to-all-start.2 = ((bf16[4,64,1024]{2,1,0:T(8,128)(2,1)}), bf16[4,64,1024]{2,1,0:T(8,128)(2,1)}, u32[]{:S(2)}, u32[]{:S(2)}) async-start(bf16[4,64,1024]{2,1,0:T(8,128)(2,1)} %get-tuple-element.801), calls=%async_computation.2 | async-start | bytes 1048576 | tf_op jit(solution)/shard_map/all_to_all | solution.py:50
  38.1 5.4 %copy-start = (bf16[32,8,8,128]{3,2,1,0:T(8,128)(2,1)}, bf16[32,8,8,128]{3,2,1,0:T(8,128)(2,1)S(1)}, u32[]{:S(2)}) copy-start(bf16[32,8,8,128]{3,2,1,0:T(8,128)(2,1)S(1)} %copy.114) | copy-start | bytes 1572868
  40.9 2.7 %copy-start.10 = (bf16[256,2,1,128]{3,0,2,1:T(8,128)(2,1)S(1)}, bf16[256,2,1,128]{3,0,2,1:T(8,128)(2,1)}, u32[]{:S(2)}) copy-start(bf16[256,2,1,128]{3,0,2,1:T(8,128)(2,1)} %copy-done.8) | copy-start | bytes 393220
  40.9 2.7 %copy-start.12 = (s32[4,4]{1,0:T(4,128)S(1)}, s32[4,4]{1,0:T(4,128)}, u32[]{:S(2)}) copy-start(s32[4,4]{1,0:T(4,128)} %param.17) | copy-start | bytes 196
  43.6 9.3 %collective-permute-start = (bf16[256,2,1,128]{3,0,2,1:T(8,128)(2,1)S(1)}, bf16[256,2,1,128]{3,0,2,1:T(8,128)(2,1)S(1)}, u32[]{:S(2)}, u32[]{:S(2)}) collective-permute-start(bf16[256,2,1,128]{3,0,2,1:T(8,128)(2,1)S(1)} %get-tuple-element.974), channel_id=1, source_target_pairs={{0,4},{4,8},{8,12},{12,0},{1,5},{5,9},{9,13},{13,1},{2,6},{6,10},{... | collective-permute-start | bytes 393224 | tf_op jit(solution)/shard_map/while/body/eval_jaxpr/ppermute | solution.py:11
  53.0 1.2 copy-start.5
  55.2 1.0 copy-start.6
  56.2 6.8 %collective-permute-start = (bf16[256,2,1,128]{3,0,2,1:T(8,128)(2,1)S(1)}, bf16[256,2,1,128]{3,0,2,1:T(8,128)(2,1)S(1)}, u32[]{:S(2)}, u32[]{:S(2)}) collective-permute-start(bf16[256,2,1,128]{3,0,2,1:T(8,128)(2,1)S(1)} %get-tuple-element.974), channel_id=1, source_target_pairs={{0,4},{4,8},{8,12},{12,0},{1,5},{5,9},{9,13},{13,1},{2,6},{6,10},{... | collective-permute-start | bytes 393224 | tf_op jit(solution)/shard_map/while/body/eval_jaxpr/ppermute | solution.py:11
  63.0 1.2 copy-start.5
  65.3 1.0 copy-start.6
  66.3 6.8 %collective-permute-start = (bf16[256,2,1,128]{3,0,2,1:T(8,128)(2,1)S(1)}, bf16[256,2,1,128]{3,0,2,1:T(8,128)(2,1)S(1)}, u32[]{:S(2)}, u32[]{:S(2)}) collective-permute-start(bf16[256,2,1,128]{3,0,2,1:T(8,128)(2,1)S(1)} %get-tuple-element.974), channel_id=1, source_target_pairs={{0,4},{4,8},{8,12},{12,0},{1,5},{5,9},{9,13},{13,1},{2,6},{6,10},{... | collective-permute-start | bytes 393224 | tf_op jit(solution)/shard_map/while/body/eval_jaxpr/ppermute | solution.py:11
  73.0 1.2 copy-start.5
  75.3 1.0 copy-start.6
  78.2 5.2 %copy-start.2 = (bf16[32,8,8,128]{3,2,1,0:T(8,128)(2,1)}, bf16[32,8,8,128]{3,2,1,0:T(8,128)(2,1)S(1)}, u32[]{:S(2)}) copy-start(bf16[32,8,8,128]{3,2,1,0:T(8,128)(2,1)S(1)} %copy.116) | copy-start | bytes 1572868
  81.9 2.5 %copy-start.9 = (bf16[256,2,1,128]{3,0,2,1:T(8,128)(2,1)S(1)}, bf16[256,2,1,128]{3,0,2,1:T(8,128)(2,1)}, u32[]{:S(2)}) copy-start(bf16[256,2,1,128]{3,0,2,1:T(8,128)(2,1)} %copy-done.8) | copy-start | bytes 393220
  83.4 1.0 copy-start.7
  84.4 4.0 %copy-start.13 = (f32[256,1,8]{0,2,1:T(8,128)S(1)}, f32[256,1,8]{0,2,1:T(8,128)}, u32[]{:S(2)}) copy-start(f32[256,1,8]{0,2,1:T(8,128)} %log_add_fusion) | copy-start | bytes 24580
  88.4 1.4 %copy-start.3 = (bf16[32,8,8,128]{3,2,1,0:T(8,128)(2,1)S(1)}, bf16[32,8,8,128]{3,2,1,0:T(8,128)(2,1)}, u32[]{:S(2)}) copy-start(bf16[32,8,8,128]{3,2,1,0:T(8,128)(2,1)} %copy-done.2) | copy-start | bytes 1572868
  89.8 1.7 %copy-start.1 = (bf16[32,8,8,128]{3,2,1,0:T(8,128)(2,1)S(1)}, bf16[32,8,8,128]{3,2,1,0:T(8,128)(2,1)}, u32[]{:S(2)}) copy-start(bf16[32,8,8,128]{3,2,1,0:T(8,128)(2,1)} %copy-done) | copy-start | bytes 1572868
  91.5 4.3 %copy-start.4 = (bf16[32,8,8,128]{3,2,1,0:T(8,128)(2,1)S(1)}, bf16[32,8,8,128]{3,2,1,0:T(8,128)(2,1)}, u32[]{:S(2)}) copy-start(bf16[32,8,8,128]{3,2,1,0:T(8,128)(2,1)} %copy-done.2) | copy-start | bytes 1572868
  97.6 6.8 %collective-permute-start.1 = (bf16[256,2,1,128]{3,0,2,1:T(8,128)(2,1)S(1)}, bf16[256,2,1,128]{3,0,2,1:T(8,128)(2,1)S(1)}, u32[]{:S(2)}, u32[]{:S(2)}) collective-permute-start(bf16[256,2,1,128]{3,0,2,1:T(8,128)(2,1)S(1)} %get-tuple-element.1021), channel_id=1, source_target_pairs={{0,4},{4,8},{8,12},{12,0},{1,5},{5,9},{9,13},{13,1},{2,6},{6,10},{... | collective-permute-start | bytes 393224 | tf_op jit(solution)/shard_map/while/body/eval_jaxpr/ppermute | solution.py:11
  97.6 9.3 %collective-permute-start.2 = (bf16[256,2,1,128]{3,0,2,1:T(8,128)(2,1)S(1)}, bf16[256,2,1,128]{3,0,2,1:T(8,128)(2,1)S(1)}, u32[]{:S(2)}, u32[]{:S(2)}) collective-permute-start(bf16[256,2,1,128]{3,0,2,1:T(8,128)(2,1)S(1)} %get-tuple-element.1022), channel_id=1, source_target_pairs={{0,4},{4,8},{8,12},{12,0},{1,5},{5,9},{9,13},{13,1},{2,6},{6,10},{... | collective-permute-start | bytes 393224 | tf_op jit(solution)/shard_map/while/body/eval_jaxpr/ppermute | solution.py:11
  107.0 6.8 %collective-permute-start.1 = (bf16[256,2,1,128]{3,0,2,1:T(8,128)(2,1)S(1)}, bf16[256,2,1,128]{3,0,2,1:T(8,128)(2,1)S(1)}, u32[]{:S(2)}, u32[]{:S(2)}) collective-permute-start(bf16[256,2,1,128]{3,0,2,1:T(8,128)(2,1)S(1)} %get-tuple-element.1021), channel_id=1, source_target_pairs={{0,4},{4,8},{8,12},{12,0},{1,5},{5,9},{9,13},{13,1},{2,6},{6,10},{... | collective-permute-start | bytes 393224 | tf_op jit(solution)/shard_map/while/body/eval_jaxpr/ppermute | solution.py:11
  107.1 9.3 %collective-permute-start.2 = (bf16[256,2,1,128]{3,0,2,1:T(8,128)(2,1)S(1)}, bf16[256,2,1,128]{3,0,2,1:T(8,128)(2,1)S(1)}, u32[]{:S(2)}, u32[]{:S(2)}) collective-permute-start(bf16[256,2,1,128]{3,0,2,1:T(8,128)(2,1)S(1)} %get-tuple-element.1022), channel_id=1, source_target_pairs={{0,4},{4,8},{8,12},{12,0},{1,5},{5,9},{9,13},{13,1},{2,6},{6,10},{... | collective-permute-start | bytes 393224 | tf_op jit(solution)/shard_map/while/body/eval_jaxpr/ppermute | solution.py:11
  116.5 6.8 %collective-permute-start.1 = (bf16[256,2,1,128]{3,0,2,1:T(8,128)(2,1)S(1)}, bf16[256,2,1,128]{3,0,2,1:T(8,128)(2,1)S(1)}, u32[]{:S(2)}, u32[]{:S(2)}) collective-permute-start(bf16[256,2,1,128]{3,0,2,1:T(8,128)(2,1)S(1)} %get-tuple-element.1021), channel_id=1, source_target_pairs={{0,4},{4,8},{8,12},{12,0},{1,5},{5,9},{9,13},{13,1},{2,6},{6,10},{... | collective-permute-start | bytes 393224 | tf_op jit(solution)/shard_map/while/body/eval_jaxpr/ppermute | solution.py:11
  116.5 9.3 %collective-permute-start.2 = (bf16[256,2,1,128]{3,0,2,1:T(8,128)(2,1)S(1)}, bf16[256,2,1,128]{3,0,2,1:T(8,128)(2,1)S(1)}, u32[]{:S(2)}, u32[]{:S(2)}) collective-permute-start(bf16[256,2,1,128]{3,0,2,1:T(8,128)(2,1)S(1)} %get-tuple-element.1022), channel_id=1, source_target_pairs={{0,4},{4,8},{8,12},{12,0},{1,5},{5,9},{9,13},{13,1},{2,6},{6,10},{... | collective-permute-start | bytes 393224 | tf_op jit(solution)/shard_map/while/body/eval_jaxpr/ppermute | solution.py:11
  125.9 6.8 %collective-permute-start.3 = (bf16[256,2,1,128]{3,0,2,1:T(8,128)(2,1)S(1)}, bf16[256,2,1,128]{3,0,2,1:T(8,128)(2,1)S(1)}, u32[]{:S(2)}, u32[]{:S(2)}) collective-permute-start(bf16[256,2,1,128]{3,0,2,1:T(8,128)(2,1)S(1)} %get-tuple-element.590), channel_id=1, source_target_pairs={{0,4},{4,8},{8,12},{12,0},{1,5},{5,9},{9,13},{13,1},{2,6},{6,10},{... | collective-permute-start | bytes 393224 | tf_op jit(solution)/shard_map/ppermute | solution.py:11
where the time goes:
time: 134 us; the launch traced here: 133 us
  waiting for transfers between devices  56.2 us (42%)
  local copies, waits for them, and re-layouts  24 us (18%)
  matrix products  20.3 us (15%)
  starting transfers between devices  17 us (13%)
  other arithmetic  14.4 us (11%)
    ppermute x10, waiting for transfers between devices, passed_along(): lax.ppermute(array, axis, [(i, (i + by) % size) for i in range(size)])  41.7 us
    all_to_all x1, waiting for transfers between devices, on_device(): lax.all_to_all(arrange(query), 'ctx', split_axis=0, concat_axis=0, tiled=...  13 us
    unnamed x36, local copies, waits for them, and re-layouts  6.89 us
    all_to_all x1, starting transfers between devices, on_device(): lax.all_to_all(arrange(loaded_pairs), 'ctx', split_axis=0, concat_axis=0,...  6.32 us
    another operation x2, local copies, waits for them, and re-layouts  5.32 us
    dot_general x4, matrix products, forward_tile(): jnp.einsum('tgru,ugd->tgrd', weights.astype(jnp.bfloat16), pair_rows[:, 1...  4.81 us
    all_to_all x1, starting transfers between devices, on_device(): lax.all_to_all(arrange(output_gradient), 'ctx', split_axis=0, concat_axis...  4.14 us
    all_to_all x1, starting transfers between devices, on_device(): lax.all_to_all(arrange(query), 'ctx', split_axis=0, concat_axis=0, tiled=...  3.66 us
  transfers between devices with their start and end apart: 13, of which 9 were waited for; matrix products, arithmetic and copies ran while one was open for 23% of the time, Pallas kernels for 0%

commit v1 on v0

v1 whole, which is shorter than its diff:
```python
import functools
import jax
import jax.numpy as jnp
from jax import lax
from jax.experimental import pallas as pl
from jax.experimental.pallas import tpu as pltpu
from jax.sharding import PartitionSpec as P

MASKED = -1e30
LOG2_E = 1.4426950408889634
VMEM_LIMIT = 48 * 1024 * 1024


def dot(a, b, contract):
    return lax.dot_general(a, b, ((contract[0], contract[1]), ((), ())), preferred_element_type=jnp.float32)


def attend_block(first_row, ends, q, g, k, v, reach, heads, scale):
    cols = q.shape[0]
    key_rows = k.shape[0]
    token = lax.broadcasted_iota(jnp.int32, (1, cols), 1) // heads
    query_pos = first_row + token
    doc_start = jnp.zeros((1, cols), jnp.int32)
    for end in ends:
        doc_start = jnp.maximum(doc_start, jnp.where(end <= query_pos, end, 0))
    low = doc_start - (first_row - reach)
    raw = dot(k, q, ((1,), (1,)))
    index = lax.broadcasted_iota(jnp.int32, (key_rows, cols), 0)
    allowed = index >= low
    allowed_late = jnp.logical_and(allowed[reach:], index[reach:] - reach <= token)
    raw = jnp.concatenate(
        [jnp.where(allowed[:reach], raw[:reach], MASKED), jnp.where(allowed_late, raw[reach:], MASKED)], axis=0
    )
    row_max = jnp.max(raw, axis=0, keepdims=True)
    weights = jnp.exp2((raw - row_max) * (scale * LOG2_E))
    inverse = 1.0 / jnp.sum(weights, axis=0, keepdims=True)
    attended_t = (dot(v, weights.astype(jnp.bfloat16), ((0,), (0,))) * inverse).astype(jnp.bfloat16)
    attended = attended_t.T
    g_t = g.T.astype(jnp.float32)
    delta = jnp.sum(g_t * attended_t.astype(jnp.float32), axis=0, keepdims=True)
    probs = weights * inverse
    products = dot(v, g, ((1,), (1,)))
    slopes = (probs * (products - delta)).astype(jnp.bfloat16)
    value_part = dot(probs.astype(jnp.bfloat16), g, ((1,), (0,)))
    key_part = dot(slopes, q, ((1,), (0,)))
    query_grad = (dot(k, slopes, ((0,), (0,))) * scale).astype(jnp.bfloat16).T
    return attended, query_grad, key_part, value_part


def work_kernel(layout, shifts, meta, *refs):
    n, reach_ranges, rows, heads, scale, ndocs, carried, final = layout
    block = rows // n
    reach = reach_ranges * rows
    q_ref, g_ref = refs[:2]
    refs = refs[2:]
    k_refs, v_refs = refs[: reach_ranges + 1], refs[reach_ranges + 1 : 2 * reach_ranges + 2]
    refs = refs[2 * reach_ranges + 2 :]
    if carried:
        acc_in, refs = refs[0], refs[1:]
    pay_refs, refs = refs[: len(shifts)], refs[len(shifts) :]
    if final:
        grad_refs, refs = refs[:n], refs[n:]
        k_win, v_win, acc = refs
    else:
        acc, k_win, v_win = refs
    step = pl.program_id(0)

    @pl.when(step == 0)
    def _():
        for i in range(reach_ranges + 1):
            k_win[pl.ds((reach_ranges - i) * rows, rows), :] = k_refs[i][...]
            v_win[pl.ds((reach_ranges - i) * rows, rows), :] = v_refs[i][...]
        acc[...] = acc_in[...] if carried else jnp.zeros_like(acc)

    own = meta[0]
    ends = [meta[1 + i] for i in range(ndocs)]
    table = 1 + ndocs
    shift = step + 1 if len(shifts) > 1 else shifts[0]
    if len(shifts) > 1:
        shift = jnp.int32(shifts[0])
        for i, value in enumerate(shifts):
            shift = jnp.where(step == i, value, shift)
    slot = meta[table + shift]
    start = pl.multiple_of(slot * block, block)
    keys_here = pl.ds(start, reach + block)
    width = q_ref.shape[1]
    attended, query_grad, key_part, value_part = attend_block(
        own * rows + slot * block, ends, q_ref[...], g_ref[...], k_win[keys_here, :], v_win[keys_here, :],
        reach, heads, scale,
    )
    acc[keys_here, :width] = acc[keys_here, :width] + key_part
    acc[keys_here, width:] = acc[keys_here, width:] + value_part
    for i in range(len(shifts)):

        @pl.when(step == i)
        def _():
            pay_refs[i][0] = attended
            pay_refs[i][1] = query_grad

    if final:

        @pl.when(step == len(shifts) - 1)
        def _():
            for to in range(n):
                for back in range(reach_ranges + 1):
                    at = meta[table + back * n + to] * block + (reach_ranges - back) * rows
                    part = acc[pl.ds(pl.multiple_of(at, block), block), :]
                    grad_refs[to][back, :, :width] = (part[:, :width] * scale).astype(grad_refs[to].dtype)
                    grad_refs[to][back, :, width:] = part[:, width:].astype(grad_refs[to].dtype)


def work(layout, shifts, meta, q, g, k_list, v_list, acc):
    n, reach_ranges, rows, heads, scale, ndocs, carried, final = layout
    width = q.shape[1]
    block = rows // n
    cols = block * heads
    table = 1 + ndocs
    window = (reach_ranges + 1) * rows

    def of_shift(step, meta):
        shift = jnp.int32(shifts[0])
        for i, value in enumerate(shifts):
            shift = jnp.where(step == i, value, shift)
        return (meta[table + shift], 0)

    def whole(shape):
        return pl.BlockSpec(shape, lambda step, meta: (0,) * len(shape))

    in_specs = [pl.BlockSpec((cols, width), of_shift)] * 2
    in_specs += [whole((rows, width))] * (2 * reach_ranges + 2)
    operands = [q, g, *k_list, *v_list]
    if carried:
        in_specs.append(whole((window, 2 * width)))
        operands.append(acc)
    out_shape = [jax.ShapeDtypeStruct((2, cols, width), jnp.bfloat16)] * len(shifts)
    scratch = [pltpu.VMEM((window, width), jnp.bfloat16)] * 2
    if final:
        grad_shape = (reach_ranges + 1, block, 2 * width)
        out_shape += [jax.ShapeDtypeStruct(grad_shape, jnp.bfloat16 if i else jnp.float32) for i in range(n)]
        scratch.append(pltpu.VMEM((window, 2 * width), jnp.float32))
    else:
        out_shape.append(jax.ShapeDtypeStruct((window, 2 * width), jnp.float32))
    return pl.pallas_call(
        functools.partial(work_kernel, layout, shifts),
        out_shape=out_shape,
        grid_spec=pltpu.PrefetchScalarGridSpec(
            num_scalar_prefetch=1,
            grid=(len(shifts),),
            in_specs=in_specs,
            out_specs=[whole(s.shape) for s in out_shape],
            scratch_shapes=scratch,
        ),
        compiler_params=pltpu.CompilerParams(vmem_limit_bytes=VMEM_LIMIT),
        name="attend_" + ("last" if final else "first"),
    )(meta, *operands)


def place_kernel(n, reach_ranges, meta, *refs):
    own = meta[0]
    pay_refs, grad_refs = refs[:n], refs[n : 2 * n]
    attended, query_grad, key_grad, value_grad, acc = refs[2 * n :]
    cols = pay_refs[0].shape[1]
    block = grad_refs[0].shape[1]
    width = key_grad.shape[1]
    for shift in range(n):
        source = lax.rem(own - shift + n, n)
        to = pl.ds(pl.multiple_of(source * cols, cols), cols)
        attended[to, :] = pay_refs[shift][0]
        query_grad[to, :] = pay_refs[shift][1]
    acc[...] = jnp.zeros_like(acc)
    for shift in range(n):
        for back in range(reach_ranges + 1):
            source = lax.rem(own - shift - back + 2 * n, n)
            to = pl.ds(pl.multiple_of(source * block, block), block)
            acc[to, :] = acc[to, :] + grad_refs[shift][back].astype(jnp.float32)
    key_grad[...] = acc[:, :width].astype(jnp.bfloat16)
    value_grad[...] = acc[:, width:].astype(jnp.bfloat16)


def place(n, reach_ranges, rows, heads, width, meta, payloads, grads):
    vmem = pl.BlockSpec(memory_space=pltpu.VMEM)
    big = jax.ShapeDtypeStruct((rows * heads, width), jnp.bfloat16)
    small = jax.ShapeDtypeStruct((rows, width), jnp.bfloat16)
    return pl.pallas_call(
        functools.partial(place_kernel, n, reach_ranges),
        out_shape=[big, big, small, small],
        in_specs=[pl.BlockSpec(memory_space=pltpu.SMEM)] + [vmem] * (2 * n),
        out_specs=[vmem] * 4,
        scratch_shapes=[pltpu.VMEM((rows, 2 * width), jnp.float32)],
        compiler_params=pltpu.CompilerParams(vmem_limit_bytes=VMEM_LIMIT),
        name="place",
    )(meta, *payloads, *grads)


def on_device(query, keys, values, output_gradient, doc_lengths, block_owner):
    n = lax.axis_size("ctx")
    own = lax.axis_index("ctx")
    rows, heads, width = query.shape
    scale = width ** (-0.5)
    ndocs = doc_lengths.shape[0]
    reach_ranges = n // 2

    def passed(array, by):
        return lax.ppermute(array, "ctx", [(i, (i + by) % n) for i in range(n)])

    k = keys.reshape(rows, width)
    v = values.reshape(rows, width)
    k_list = [k] + [passed(k, i) for i in range(1, reach_ranges + 1)]
    v_list = [v] + [passed(v, i) for i in range(1, reach_ranges + 1)]
    q = query.reshape(rows * heads, width)
    g = output_gradient.reshape(rows * heads, width)

    ranges = (own - jnp.arange(reach_ranges + 1)) % n
    targets = (own + jnp.arange(n)) % n
    slots = jnp.arange(n, dtype=jnp.int32)
    match = block_owner[ranges][:, None, :] == targets[None, :, None]
    table = jnp.sum(jnp.where(match, slots, 0), axis=2)
    meta = jnp.concatenate(
        [own.reshape(1).astype(jnp.int32), jnp.cumsum(doc_lengths).astype(jnp.int32), table.reshape(-1)]
    )

    first = [n // 2]
    rest = [i for i in range(1, n) if i != n // 2] + [0]
    layout = (n, reach_ranges, rows, heads, scale, ndocs)
    out = work(layout + (False, False), first, meta, q, g, k_list, v_list, None)
    payloads = {first[0]: passed(out[0], first[0])}
    out = work(layout + (True, True), rest, meta, q, g, k_list, v_list, out[1])
    for i, shift in enumerate(rest):
        payloads[shift] = passed(out[i], shift) if shift else out[i]
    grads = [passed(grad, i) if i else grad for i, grad in enumerate(out[len(rest) :])]
    attended, query_grad, key_grad, value_grad = place(
        n, reach_ranges, rows, heads, width, meta, [payloads[i] for i in range(n)], grads
    )
    return (
        attended.reshape(rows, heads, width),
        query_grad.reshape(rows, heads, width),
        key_grad.reshape(rows, 1, width),
        value_grad.reshape(rows, 1, width),
    )


def solution(mesh):
    rows = P(("dp", "ctx"), "tp", None)
    return jax.shard_map(
        on_device,
        mesh=mesh,
        in_specs=(rows, rows, rows, rows, P("dp"), P("dp", None)),
        out_specs=(rows, rows, rows, rows),
        check_vma=False,
    )
```

time: 134 us -> 62.5 us (0.47)
  waiting for transfers between devices: 56.2 us -> 31.9 us
  matrix products: 20.3 us -> 0 us
  local copies, waits for them, and re-layouts: 24 us -> 5.08 us
  other arithmetic: 14.4 us -> 0.5 us
  Pallas kernels: 0 us -> 8.77 us
  starting transfers between devices: 17 us -> 15.3 us
    dot_general x27 -> x0, matrix products: 20.3 us -> none  [the longest x4 4.81 us: forward_tile(): jnp.einsum('tgru,ugd->tgrd', weights.astype(jnp.bfloat16), pair_rows[:, 1...]
    all_to_all x3 -> x0, waiting for transfers between devices: 14.4 us -> none  [the longest x1 13 us: on_device(): lax.all_to_all(arrange(query), 'ctx', split_axis=0, concat_axis=0, tiled=...]
    all_to_all x3 -> x0, starting transfers between devices: 14.1 us -> none  [the longest x1 6.32 us: on_device(): lax.all_to_all(arrange(loaded_pairs), 'ctx', split_axis=0, concat_axis=0,...]
    ppermute x10, starting transfers between devices: 2.88 us -> 15.3 us  [passed(): return lax.ppermute(array, 'ctx', [(i, (i + by) % n) for i in range(n)])]
    ppermute x10, waiting for transfers between devices: 41.7 us -> 31.9 us  [passed(): return lax.ppermute(array, 'ctx', [(i, (i + by) % n) for i in range(n)])]
    pallas_call x0 -> x3, Pallas kernels: none -> 8.77 us  [the longest x2 7.17 us: work(): pl.pallas_call(functools.partial(work_kernel, layout, shifts), out_shape=...]
    reduce_sum x20 -> x1, other arithmetic: 7.24 us -> 0.21 us  [on_device(): table = jnp.sum(jnp.where(match, slots, 0), axis=2)]
    another operation x3 -> x0, local copies, waits for them, and re-layouts: 5.45 us -> none
  transfers between devices with their start and end apart: 13 -> 10, of which waited for: 9 -> 5; matrix products, arithmetic and copies ran while one was open for 23% -> 2% of each run, Pallas kernels for 0% -> 0%
where the time goes in v1:
time: 62.5 us; the launch traced here: 62.2 us
  waiting for transfers between devices  31.9 us (51%)
  starting transfers between devices  15.3 us (24%)
  Pallas kernels  8.77 us (14%)
  local copies, waits for them, and re-layouts  5.08 us (8%)
  between operations  0.69 us (1%)
    ppermute x10, waiting for transfers between devices, passed(): return lax.ppermute(array, 'ctx', [(i, (i + by) % n) for i in range(n)])  31.9 us
    ppermute x10, starting transfers between devices, passed(): return lax.ppermute(array, 'ctx', [(i, (i + by) % n) for i in range(n)])  15.3 us
    pallas_call x2, Pallas kernels, work(): pl.pallas_call(functools.partial(work_kernel, layout, shifts), out_shape=...  7.17 us
    unnamed x12, local copies, waits for them, and re-layouts  4.44 us
    pallas_call x1, Pallas kernels, place(): pl.pallas_call(functools.partial(place_kernel, n, reach_ranges), out_shap...  1.6 us
  transfers between devices with their start and end apart: 10, of which 5 were waited for; matrix products, arithmetic and copies ran while one was open for 2% of the time, Pallas kernels for 0%

profile of v1, /device:TPU:0, one launch (start us, length us, event | category | flops | bytes accessed | tf_op | source)
XLA Modules:
  0.0 62.2 jit_solution(16107293880430894599)
XLA Ops:
  0.6 0.0 copy-start
  0.6 4.1 %collective-permute-start.1 = (bf16[256,128]{1,0:T(8,128)(2,1)}, bf16[256,128]{1,0:T(8,128)(2,1)S(1)}, u32[]{:S(2)}, u32[]{:S(2)}) collective-permute-start(bf16[256,128]{1,0:T(8,128)(2,1)} %bitcast.17), channel_id=1, source_target_pairs={{0,8},{4,12},{8,0},{12,4},{1,9},{5,13},{9,1},{13,5},{2,10},{6,14},... | collective-permute-start | bytes 196616 | tf_op jit(solution)/shard_map/ppermute | solution.py:204
  4.7 1.6 %collective-permute-start = (bf16[256,128]{1,0:T(8,128)(2,1)}, bf16[256,128]{1,0:T(8,128)(2,1)S(1)}, u32[]{:S(2)}, u32[]{:S(2)}) collective-permute-start(bf16[256,128]{1,0:T(8,128)(2,1)} %bitcast.18), channel_id=1, source_target_pairs={{0,4},{4,8},{8,12},{12,0},{1,5},{5,9},{9,13},{13,1},{2,6},{6,10},{... | collective-permute-start | bytes 196616 | tf_op jit(solution)/shard_map/ppermute | solution.py:204
  6.3 0.3 collective-permute-start.3
  6.7 2.5 %collective-permute-start.2 = (bf16[256,128]{1,0:T(8,128)(2,1)}, bf16[256,128]{1,0:T(8,128)(2,1)S(1)}, u32[]{:S(2)}, u32[]{:S(2)}) collective-permute-start(bf16[256,128]{1,0:T(8,128)(2,1)} %bitcast.22), channel_id=1, source_target_pairs={{0,4},{4,8},{8,12},{12,0},{1,5},{5,9},{9,13},{13,1},{2,6},{6,10},{... | collective-permute-start | bytes 196616 | tf_op jit(solution)/shard_map/ppermute | solution.py:204
  9.2 0.6 gather_fusion
  9.7 0.2 select_reduce_fusion
  10.0 0.1 reshape.132
  10.0 0.7 %copy-done.5 = s32[8]{0:T(128)S(1)} copy-done((s32[8]{0:T(128)S(1)}, s32[8]{0:T(128)}, u32[]{:S(2)}) %copy-start.5) | copy-done | bytes 56
  10.7 0.2 reduce-window.9
  10.9 0.1 pad_add_fusion.meta
  11.0 0.0 collective-permute-done.1.refs_4_
  11.0 0.7 %collective-permute-done.refs_3_ = bf16[256,128]{1,0:T(8,128)(2,1)S(1)} collective-permute-done((bf16[256,128]{1,0:T(8,128)(2,1)}, bf16[256,128]{1,0:T(8,128)(2,1)S(1)}, u32[]{:S(2)}, u32[]{:S(2)}) %collective-permute-start) | collective-permute-done | bytes 65568 | tf_op jit(solution)/shard_map/ppermute | solution.py:204
  11.7 2.8 %collective-permute-done.3.refs_7_ = bf16[256,128]{1,0:T(8,128)(2,1)S(1)} collective-permute-done((bf16[256,128]{1,0:T(8,128)(2,1)}, bf16[256,128]{1,0:T(8,128)(2,1)S(1)}, u32[]{:S(2)}, u32[]{:S(2)}) %collective-permute-start.3) | collective-permute-done | bytes 65568 | tf_op jit(solution)/shard_map/ppermute | solution.py:204
  14.5 1.0 %copy-done.1 = bf16[256,8,128]{2,1,0:T(8,128)(2,1)S(1)} copy-done((bf16[256,8,128]{2,1,0:T(8,128)(2,1)S(1)}, bf16[256,8,128]{2,1,0:T(8,128)(2,1)}, u32[]{:S(2)}) %copy-start.1) | copy-done | bytes 524312
  15.6 1.0 %copy-done.2 = bf16[256,8,128]{2,1,0:T(8,128)(2,1)S(1)} copy-done((bf16[256,8,128]{2,1,0:T(8,128)(2,1)S(1)}, bf16[256,8,128]{2,1,0:T(8,128)(2,1)}, u32[]{:S(2)}) %copy-start.2) | copy-done | bytes 524312
  16.6 0.8 %copy-done.3 = bf16[256,1,128]{2,0,1:T(8,128)(2,1)S(1)} copy-done((bf16[256,1,128]{2,0,1:T(8,128)(2,1)S(1)}, bf16[256,1,128]{2,0,1:T(8,128)(2,1)}, u32[]{:S(2)}) %copy-start.3) | copy-done | bytes 65560
  17.4 0.8 %copy-done.4 = bf16[256,1,128]{2,0,1:T(8,128)(2,1)S(1)} copy-done((bf16[256,1,128]{2,0,1:T(8,128)(2,1)S(1)}, bf16[256,1,128]{2,0,1:T(8,128)(2,1)}, u32[]{:S(2)}) %copy-start.4) | copy-done | bytes 65560
  18.3 2.0 %attend_first.1 = (bf16[2,512,128]{2,1,0:T(8,128)(2,1)S(1)}, f32[768,256]{1,0:T(8,128)S(1)}) custom-call(s32[21]{0:T(128)S(1)} %pad_add_fusion.meta, bf16[2048,128]{1,0:T(8,128)(2,1)S(1)} %bitcast.13, bf16[2048,128]{1,0:T(8,128)(2,1)S(1)} %bitcast.15, bf16[256,128]{1,0:T(8,128)(2,1)S(1)} %bitcast.19, bf16[256,128]{1,0:T(8,128)(2,1)S(1)} %collective-permute-done.refs_3_, ...), custom_call_target="tpu_custom_call" | custom-call | tf_op jit(solution)/shard_map/attend_first/pallas_call | solution.py:143
  20.3 5.1 %attend_last.1 = (bf16[2,512,128]{2,1,0:T(8,128)(2,1)S(1)}, bf16[2,512,128]{2,1,0:T(8,128)(2,1)S(1)}, bf16[2,512,128]{2,1,0:T(8,128)(2,1)S(1)}, f32[3,64,256]{2,...) custom-call(s32[21]{0:T(128)S(1)} %pad_add_fusion.meta, ...), custom_call_target="tpu_custom_call" | custom-call | tf_op jit(solution)/shard_map/attend_last/pallas_call | solution.py:143
  25.5 0.5 collective-permute-start.4
  25.9 3.4 %collective-permute-start.6 = (bf16[2,512,128]{2,1,0:T(8,128)(2,1)S(1)}, bf16[2,512,128]{2,1,0:T(8,128)(2,1)S(1)}, u32[]{:S(2)}, u32[]{:S(2)}) collective-permute-start(bf16[2,512,128]{2,1,0:T(8,128)(2,1)S(1)} %get-tuple-element.21), channel_id=1, source_target_pairs={{0,12},{4,0},{8,4},{12,8},{1,13},{5,1},{9,5},{13,9},{2,14},{6,2},{... | collective-permute-start | bytes 786440 | tf_op jit(solution)/shard_map/ppermute | solution.py:204
  29.4 0.4 collective-permute-start.5
  29.7 0.5 collective-permute-start.7
  30.3 2.0 %collective-permute-start.8 = (bf16[3,64,256]{2,1,0:T(8,128)(2,1)S(1)}, bf16[3,64,256]{2,1,0:T(8,128)(2,1)S(1)}, u32[]{:S(2)}, u32[]{:S(2)}) collective-permute-start(bf16[3,64,256]{2,1,0:T(8,128)(2,1)S(1)} %get-tuple-element.24), channel_id=1, source_target_pairs={{0,8},{4,12},{8,0},{12,4},{1,9},{5,13},{9,1},{13,5},{2,10},{6,14},... | collective-permute-start | bytes 294920 | tf_op jit(solution)/shard_map/ppermute | solution.py:204
  32.3 17.7 %collective-permute-done.7.refs_5_ = bf16[3,64,256]{2,1,0:T(8,128)(2,1)S(1)} collective-permute-done((bf16[3,64,256]{2,1,0:T(8,128)(2,1)S(1)}, bf16[3,64,256]{2,1,0:T(8,128)(2,1)S(1)}, u32[]{:S(2)}, u32[]{:S(2)}) %collective-permute-start.7) | collective-permute-done | bytes 98336 | tf_op jit(solution)/shard_map/ppermute | solution.py:204
  50.0 8.9 %collective-permute-done.8.refs_6_ = bf16[3,64,256]{2,1,0:T(8,128)(2,1)S(1)} collective-permute-done((bf16[3,64,256]{2,1,0:T(8,128)(2,1)S(1)}, bf16[3,64,256]{2,1,0:T(8,128)(2,1)S(1)}, u32[]{:S(2)}, u32[]{:S(2)}) %collective-permute-start.8) | collective-permute-done | bytes 98336 | tf_op jit(solution)/shard_map/ppermute | solution.py:204
  58.9 1.8 %collective-permute-done.9.refs_7_ = bf16[3,64,256]{2,1,0:T(8,128)(2,1)S(1)} collective-permute-done((bf16[3,64,256]{2,1,0:T(8,128)(2,1)S(1)}, bf16[3,64,256]{2,1,0:T(8,128)(2,1)S(1)}, u32[]{:S(2)}, u32[]{:S(2)}) %collective-permute-start.9) | collective-permute-done | bytes 98336 | tf_op jit(solution)/shard_map/ppermute | solution.py:204
  60.6 0.0 collective-permute-done.4.refs_1_
  60.6 0.0 collective-permute-done.6.refs_3_
  60.6 0.0 collective-permute-done.5.refs_2_
  60.6 1.6 %place.1 = (bf16[2048,128]{1,0:T(8,128)(2,1)}, bf16[2048,128]{1,0:T(8,128)(2,1)}, bf16[256,128]{1,0:T(8,128)(2,1)}, bf16[256,128]{1,0:T(8,128)(2,1)}) custom-call(s32[21]{0:T(128)S(1)} %pad_add_fusion.meta, bf16[2,512,128]{2,1,0:T(8,128)(2,1)S(1)} %get-tuple-element.18.refs_0_, bf16[2,512,128]{2,1,0:T(8,128)(2,1)S(1)} %collective-permute-done.4.refs_1_, ...), custom_call_target="tpu_custom_call" | custom-call | tf_op jit(solution)/shard_map/place/pallas_call | solution.py:184
  (11 shorter events, 0.0 us)
Async XLA Ops:
  0.6 8.5 %copy-start = (s32[4,4]{1,0:T(4,128)S(1)}, s32[4,4]{1,0:T(4,128)}, u32[]{:S(2)}) copy-start(s32[4,4]{1,0:T(4,128)} %param.11) | copy-start | bytes 196
  0.6 10.3 %collective-permute-start.1 = (bf16[256,128]{1,0:T(8,128)(2,1)}, bf16[256,128]{1,0:T(8,128)(2,1)S(1)}, u32[]{:S(2)}, u32[]{:S(2)}) collective-permute-start(bf16[256,128]{1,0:T(8,128)(2,1)} %bitcast.17), channel_id=1, source_target_pairs={{0,8},{4,12},{8,0},{12,4},{1,9},{5,13},{9,1},{13,5},{2,10},{6,14},... | collective-permute-start | bytes 196616 | tf_op jit(solution)/shard_map/ppermute | solution.py:204
  4.7 7.0 %collective-permute-start = (bf16[256,128]{1,0:T(8,128)(2,1)}, bf16[256,128]{1,0:T(8,128)(2,1)S(1)}, u32[]{:S(2)}, u32[]{:S(2)}) collective-permute-start(bf16[256,128]{1,0:T(8,128)(2,1)} %bitcast.18), channel_id=1, source_target_pairs={{0,4},{4,8},{8,12},{12,0},{1,5},{5,9},{9,13},{13,1},{2,6},{6,10},{... | collective-permute-start | bytes 196616 | tf_op jit(solution)/shard_map/ppermute | solution.py:204
  6.3 8.2 %collective-permute-start.3 = (bf16[256,128]{1,0:T(8,128)(2,1)}, bf16[256,128]{1,0:T(8,128)(2,1)S(1)}, u32[]{:S(2)}, u32[]{:S(2)}) collective-permute-start(bf16[256,128]{1,0:T(8,128)(2,1)} %bitcast.21), channel_id=1, source_target_pairs={{0,8},{4,12},{8,0},{12,4},{1,9},{5,13},{9,1},{13,5},{2,10},{6,14},... | collective-permute-start | bytes 196616 | tf_op jit(solution)/shard_map/ppermute | solution.py:204
  6.7 7.9 %collective-permute-start.2 = (bf16[256,128]{1,0:T(8,128)(2,1)}, bf16[256,128]{1,0:T(8,128)(2,1)S(1)}, u32[]{:S(2)}, u32[]{:S(2)}) collective-permute-start(bf16[256,128]{1,0:T(8,128)(2,1)} %bitcast.22), channel_id=1, source_target_pairs={{0,4},{4,8},{8,12},{12,0},{1,5},{5,9},{9,13},{13,1},{2,6},{6,10},{... | collective-permute-start | bytes 196616 | tf_op jit(solution)/shard_map/ppermute | solution.py:204
  10.0 0.7 %copy-start.5 = (s32[8]{0:T(128)S(1)}, s32[8]{0:T(128)}, u32[]{:S(2)}) copy-start(s32[8]{0:T(128)} %param.10) | copy-start | bytes 100
  14.5 1.0 %copy-start.1 = (bf16[256,8,128]{2,1,0:T(8,128)(2,1)S(1)}, bf16[256,8,128]{2,1,0:T(8,128)(2,1)}, u32[]{:S(2)}) copy-start(bf16[256,8,128]{2,1,0:T(8,128)(2,1)} %param.6) | copy-start | bytes 1572868
  15.6 1.0 %copy-start.2 = (bf16[256,8,128]{2,1,0:T(8,128)(2,1)S(1)}, bf16[256,8,128]{2,1,0:T(8,128)(2,1)}, u32[]{:S(2)}) copy-start(bf16[256,8,128]{2,1,0:T(8,128)(2,1)} %param.9) | copy-start | bytes 1572868
  16.6 0.8 %copy-start.3 = (bf16[256,1,128]{2,0,1:T(8,128)(2,1)S(1)}, bf16[256,1,128]{2,0,1:T(8,128)(2,1)}, u32[]{:S(2)}) copy-start(bf16[256,1,128]{2,0,1:T(8,128)(2,1)} %param.7) | copy-start | bytes 196612
  17.4 0.8 %copy-start.4 = (bf16[256,1,128]{2,0,1:T(8,128)(2,1)S(1)}, bf16[256,1,128]{2,0,1:T(8,128)(2,1)}, u32[]{:S(2)}) copy-start(bf16[256,1,128]{2,0,1:T(8,128)(2,1)} %param.8) | copy-start | bytes 196612
  25.5 35.1 %collective-permute-start.4 = (bf16[2,512,128]{2,1,0:T(8,128)(2,1)S(1)}, bf16[2,512,128]{2,1,0:T(8,128)(2,1)S(1)}, u32[]{:S(2)}, u32[]{:S(2)}) collective-permute-start(bf16[2,512,128]{2,1,0:T(8,128)(2,1)S(1)} %get-tuple-element.19), channel_id=1, source_target_pairs={{0,4},{4,8},{8,12},{12,0},{1,5},{5,9},{9,13},{13,1},{2,6},{6,10},{... | collective-permute-start | bytes 786440 | tf_op jit(solution)/shard_map/ppermute | solution.py:204
  25.9 34.7 %collective-permute-start.6 = (bf16[2,512,128]{2,1,0:T(8,128)(2,1)S(1)}, bf16[2,512,128]{2,1,0:T(8,128)(2,1)S(1)}, u32[]{:S(2)}, u32[]{:S(2)}) collective-permute-start(bf16[2,512,128]{2,1,0:T(8,128)(2,1)S(1)} %get-tuple-element.21), channel_id=1, source_target_pairs={{0,12},{4,0},{8,4},{12,8},{1,13},{5,1},{9,5},{13,9},{2,14},{6,2},{... | collective-permute-start | bytes 786440 | tf_op jit(solution)/shard_map/ppermute | solution.py:204
  29.4 31.3 %collective-permute-start.5 = (bf16[2,512,128]{2,1,0:T(8,128)(2,1)S(1)}, bf16[2,512,128]{2,1,0:T(8,128)(2,1)S(1)}, u32[]{:S(2)}, u32[]{:S(2)}) collective-permute-start(bf16[2,512,128]{2,1,0:T(8,128)(2,1)S(1)} %get-tuple-element.20), channel_id=1, source_target_pairs={{0,8},{4,12},{8,0},{12,4},{1,9},{5,13},{9,1},{13,5},{2,10},{6,14},... | collective-permute-start | bytes 786440 | tf_op jit(solution)/shard_map/ppermute | solution.py:204
  29.7 20.2 %collective-permute-start.7 = (bf16[3,64,256]{2,1,0:T(8,128)(2,1)S(1)}, bf16[3,64,256]{2,1,0:T(8,128)(2,1)S(1)}, u32[]{:S(2)}, u32[]{:S(2)}) collective-permute-start(bf16[3,64,256]{2,1,0:T(8,128)(2,1)S(1)} %get-tuple-element.23), channel_id=1, source_target_pairs={{0,4},{4,8},{8,12},{12,0},{1,5},{5,9},{9,13},{13,1},{2,6},{6,10},{... | collective-permute-start | bytes 294920 | tf_op jit(solution)/shard_map/ppermute | solution.py:204
  30.3 28.6 %collective-permute-start.8 = (bf16[3,64,256]{2,1,0:T(8,128)(2,1)S(1)}, bf16[3,64,256]{2,1,0:T(8,128)(2,1)S(1)}, u32[]{:S(2)}, u32[]{:S(2)}) collective-permute-start(bf16[3,64,256]{2,1,0:T(8,128)(2,1)S(1)} %get-tuple-element.24), channel_id=1, source_target_pairs={{0,8},{4,12},{8,0},{12,4},{1,9},{5,13},{9,1},{13,5},{2,10},{6,14},... | collective-permute-start | bytes 294920 | tf_op jit(solution)/shard_map/ppermute | solution.py:204
  50.0 10.6 %collective-permute-start.9 = (bf16[3,64,256]{2,1,0:T(8,128)(2,1)S(1)}, bf16[3,64,256]{2,1,0:T(8,128)(2,1)S(1)}, u32[]{:S(2)}, u32[]{:S(2)}) collective-permute-start(bf16[3,64,256]{2,1,0:T(8,128)(2,1)S(1)} %get-tuple-element.25), channel_id=1, source_target_pairs={{0,12},{4,0},{8,4},{12,8},{1,13},{5,1},{9,5},{13,9},{2,14},{6,2},{... | collective-permute-start | bytes 294920 | tf_op jit(solution)/shard_map/ppermute | solution.py:204

commit v2 on v1

v2 whole, which is shorter than its diff:
```python
import functools
import jax
import jax.numpy as jnp
from jax import lax
from jax.experimental import pallas as pl
from jax.experimental.pallas import tpu as pltpu
from jax.sharding import PartitionSpec as P

MASKED = -1e30
LOG2_E = 1.4426950408889634
VMEM_LIMIT = 32 * 1024 * 1024
EARLY = False


def dot(a, b, contract):
    return lax.dot_general(a, b, ((contract[0], contract[1]), ((), ())), preferred_element_type=jnp.float32)


def attend_block(first_row, ends, q, g, k, v, reach, heads, scale):
    cols = q.shape[0]
    key_rows = k.shape[0]
    token = lax.broadcasted_iota(jnp.int32, (1, cols), 1) // heads
    query_pos = first_row + token
    doc_start = jnp.zeros((1, cols), jnp.int32)
    for end in ends:
        doc_start = jnp.maximum(doc_start, jnp.where(end <= query_pos, end, 0))
    low = doc_start - (first_row - reach)
    raw = dot(k, q, ((1,), (1,)))
    index = lax.broadcasted_iota(jnp.int32, (key_rows, cols), 0)
    allowed = index >= low
    allowed_late = jnp.logical_and(allowed[reach:], index[reach:] - reach <= token)
    raw = jnp.concatenate(
        [jnp.where(allowed[:reach], raw[:reach], MASKED), jnp.where(allowed_late, raw[reach:], MASKED)], axis=0
    )
    row_max = jnp.max(raw, axis=0, keepdims=True)
    weights = jnp.exp2((raw - row_max) * (scale * LOG2_E))
    inverse = 1.0 / jnp.sum(weights, axis=0, keepdims=True)
    attended_t = (dot(v, weights.astype(jnp.bfloat16), ((0,), (0,))) * inverse).astype(jnp.bfloat16)
    attended = attended_t.T
    g_t = g.T.astype(jnp.float32)
    delta = jnp.sum(g_t * attended_t.astype(jnp.float32), axis=0, keepdims=True)
    probs = weights * inverse
    products = dot(v, g, ((1,), (1,)))
    slopes = (probs * (products - delta)).astype(jnp.bfloat16)
    value_part = dot(probs.astype(jnp.bfloat16), g, ((1,), (0,)))
    key_part = dot(slopes, q, ((1,), (0,))) * scale
    query_grad = (dot(k, slopes, ((0,), (0,))) * scale).astype(jnp.bfloat16).T
    return attended, query_grad, key_part, value_part


class Plan:
    def __init__(self, n, rows, heads, width, ndocs):
        self.n, self.rows, self.heads, self.width, self.ndocs = n, rows, heads, width, ndocs
        self.back = n // 2
        self.block = rows // n
        self.cols = self.block * heads
        self.reach = self.back * rows
        self.scale = width ** (-0.5)
        self.window_ranges = self.back + 3

    def ends(self, meta):
        return [meta[1 + i] for i in range(self.ndocs)]

    def slot(self, meta, loader, owner):
        return meta[1 + self.ndocs + loader * self.n + owner]

    def cost(self, blocks):
        return pl.CostEstimate(
            flops=14 * blocks * self.cols * (self.reach + self.block) * self.width * 8,
            bytes_accessed=blocks * self.cols * self.width * 16,
            transcendentals=blocks * self.cols * (self.reach + self.block),
        )


def fill_window(plan, refs, k_win, v_win):
    rows, width = plan.rows, plan.width
    k_win[pl.ds((plan.back + 1) * rows, rows), :] = refs[0][0]
    v_win[pl.ds((plan.back + 1) * rows, rows), :] = refs[0][1]
    for i in range(1, (len(refs) + 1) // 2):
        place = plan.back + 1 - i if i <= plan.back else plan.back + 2
        k_win[pl.ds(place * rows, rows), :] = refs[2 * i - 1][...]
        v_win[pl.ds(place * rows, rows), :] = refs[2 * i][...]
    if len(refs) > 2 * plan.back + 1:
        k_win[pl.ds(0, rows), :] = jnp.zeros((rows, width), k_win.dtype)
        v_win[pl.ds(0, rows), :] = jnp.zeros((rows, width), v_win.dtype)


def attend_at(plan, meta, loader, slot, q, g, k_win, v_win):
    start = (loader - meta[0] + 1) * plan.rows + slot * plan.block
    keys_here = pl.ds(pl.multiple_of(start, plan.block), plan.reach + plan.block)
    out = attend_block(
        loader * plan.rows + slot * plan.block, plan.ends(meta), q, g, k_win[keys_here, :], v_win[keys_here, :],
        plan.reach, plan.heads, plan.scale,
    )
    return keys_here, out


def pack_kernel(plan, meta, q_ref, g_ref, k_ref, v_ref, *refs):
    blocks, kv, sems, kv_sems = refs[: plan.n], refs[plan.n], refs[plan.n + 1], refs[plan.n + 2]
    own = meta[0]
    copies = [
        pltpu.make_async_copy(k_ref, kv.at[0], kv_sems.at[0]),
        pltpu.make_async_copy(v_ref, kv.at[1], kv_sems.at[1]),
    ]
    for shift, block in enumerate(blocks):
        slot = plan.slot(meta, own, lax.rem(own + shift, plan.n))
        at = pl.ds(pl.multiple_of(slot * plan.cols, plan.cols), plan.cols)
        copies.append(pltpu.make_async_copy(q_ref.at[at, :], block.at[0], sems.at[shift, 0]))
        copies.append(pltpu.make_async_copy(g_ref.at[at, :], block.at[1], sems.at[shift, 1]))
    for copy in copies:
        copy.start()
    for copy in copies:
        copy.wait()


def first_kernel(plan, shift, meta, qg, *refs):
    kv_refs, (pay_ref, grad_ref, k_win, v_win) = refs[:-4], refs[-4:]
    own = meta[0]
    slot = plan.slot(meta, own, lax.rem(own + shift, plan.n))
    fill_window(plan, kv_refs, k_win, v_win)
    _, (attended, query_grad, key_part, value_part) = attend_at(
        plan, meta, own, slot, qg[0], qg[1], k_win, v_win
    )
    pay_ref[0] = attended
    pay_ref[1] = query_grad
    grad_ref[:, : plan.width] = key_part
    grad_ref[:, plan.width :] = value_part


def last_kernel(plan, first_shift, items, meta, *refs):
    n, width, rows, block = plan.n, plan.width, plan.rows, plan.block
    qg_refs, refs = refs[: len(items)], refs[len(items) :]
    first_grad, refs = refs[0], refs[1:]
    kv_refs, refs = refs[: -(len(items) + 5)], refs[-(len(items) + 5) :]
    pay_refs, (send_ref, keep_ref, k_win, v_win, acc) = refs[: len(items)], refs[len(items) :]
    step = pl.program_id(0)
    own = meta[0]

    def valid(item):
        if item == "ahead":
            return own < n - 1
        if item == "behind":
            return jnp.logical_and(own >= 1, own <= plan.back)
        if EARLY and item == 1:
            return own >= plan.back
        if EARLY and item == n - 1:
            return own == 0
        return own >= 0

    @pl.when(step == 0)
    def _():
        fill_window(plan, kv_refs, k_win, v_win)
        acc[...] = jnp.zeros_like(acc)
        slot = plan.slot(meta, own, lax.rem(own + first_shift, n))
        keys_here = pl.ds(pl.multiple_of(rows + slot * block, block), plan.reach + block)
        acc[keys_here, :] = first_grad[...]

    for i, item in enumerate(items):

        @pl.when(jnp.logical_and(step == i, valid(item)))
        def _():
            loader = own + {"ahead": 1, "behind": -1}.get(item, 0)
            owner = own if item in ("ahead", "behind") else lax.rem(own + item, n)
            slot = plan.slot(meta, loader, owner)
            qg = qg_refs[i]
            keys_here, (attended, query_grad, key_part, value_part) = attend_at(
                plan, meta, loader, slot, qg[0], qg[1], k_win, v_win
            )
            acc[keys_here, :width] = acc[keys_here, :width] + key_part
            acc[keys_here, width:] = acc[keys_here, width:] + value_part
            pay_refs[i][0] = attended
            pay_refs[i][1] = query_grad

    @pl.when(step == len(items) - 1)
    def _():
        def of_range(key_range, carry):
            at = (lax.rem(key_range - own + plan.back + n, n) + 1) * rows
            for apart in range(n):
                slot = plan.slot(meta, key_range, own ^ apart)
                part = acc[pl.ds(pl.multiple_of(at + slot * block, block), block), :]
                to = keep_ref if apart % 2 == 0 else send_ref
                to[apart // 2, key_range] = part.astype(to.dtype)
            return carry

        lax.fori_loop(0, n, of_range, 0)


def spec_of(space):
    return pl.BlockSpec(memory_space=space)


def kernel_call(body, name, operands, spaces, out_shape, scratch, **more):
    return pl.pallas_call(
        body,
        out_shape=out_shape,
        in_specs=[spec_of(space) for space in spaces],
        compiler_params=pltpu.CompilerParams(vmem_limit_bytes=VMEM_LIMIT),
        scratch_shapes=scratch,
        name=name,
        **more,
    )(*operands)


def pack(plan, meta, q, g, k, v):
    out_shape = [jax.ShapeDtypeStruct((2, plan.cols, plan.width), jnp.bfloat16)] * plan.n
    out_shape.append(jax.ShapeDtypeStruct((2, plan.rows, plan.width), jnp.bfloat16))
    return kernel_call(
        functools.partial(pack_kernel, plan), "pack", (meta, q, g, k, v), [pltpu.SMEM] + [pl.ANY] * 4, out_shape,
        [pltpu.SemaphoreType.DMA((plan.n, 2)), pltpu.SemaphoreType.DMA((2,))],
        out_specs=[spec_of(pltpu.VMEM)] * len(out_shape),
    )


def attend_first(plan, shift, meta, qg, kv_list):
    window = pltpu.VMEM((plan.window_ranges * plan.rows, plan.width), jnp.bfloat16)
    out_shape = [
        jax.ShapeDtypeStruct((2, plan.cols, plan.width), jnp.bfloat16),
        jax.ShapeDtypeStruct((plan.reach + plan.block, 2 * plan.width), jnp.float32),
    ]
    operands = (meta, qg, *kv_list)
    return kernel_call(
        functools.partial(first_kernel, plan, shift), "attend_first", operands,
        [pltpu.SMEM] + [pltpu.VMEM] * (len(operands) - 1), out_shape, [window, window],
        out_specs=[spec_of(pltpu.VMEM)] * 2, cost_estimate=plan.cost(1),
    )


def attend_last(plan, first_shift, items, meta, qg_list, first_grad, kv_list):
    n = plan.n
    window = pltpu.VMEM((plan.window_ranges * plan.rows, plan.width), jnp.bfloat16)
    grads = (n // 2, n, plan.block, 2 * plan.width)
    out_shape = [jax.ShapeDtypeStruct((2, plan.cols, plan.width), jnp.bfloat16)] * len(items)
    out_shape += [jax.ShapeDtypeStruct(grads, jnp.bfloat16), jax.ShapeDtypeStruct(grads, jnp.float32)]
    operands = (meta, *qg_list, first_grad, *kv_list)
    return kernel_call(
        functools.partial(last_kernel, plan, first_shift, items), "attend_last", operands,
        [pltpu.SMEM] + [pltpu.VMEM] * (len(operands) - 1), out_shape,
        [window, window, pltpu.VMEM(((n + 1) * plan.rows, 2 * plan.width), jnp.float32)],
        out_specs=[spec_of(pltpu.VMEM)] * len(out_shape), cost_estimate=plan.cost(len(items)), grid=(len(items),),
    )


def place_kernel(plan, items, final, meta, *refs):
    n, cols, width, own = plan.n, plan.cols, plan.width, meta[0]
    pay_refs, refs = dict(zip(items, refs[: len(items)])), refs[len(items) :]
    if final:
        keep, arrived, _, _, attended, query_grad, key_grad, value_grad, sems = refs
    else:
        attended, query_grad, sems = refs

    def copies(i, item):
        if item == "ahead":
            source, here = own + 1, own < n - 1
        elif item == "behind":
            source, here = own - 1, jnp.logical_and(own >= 1, own <= plan.back)
        else:
            source = lax.rem(own - item + n, n)
            here = own >= 0
            if EARLY and item == 1:
                here = source >= plan.back
            if EARLY and item == n - 1:
                here = own == n - 1
        to = pl.ds(pl.multiple_of(source * cols, cols), cols)
        return here, [
            pltpu.make_async_copy(pay_refs[item].at[0], attended.at[to, :], sems.at[i, 0]),
            pltpu.make_async_copy(pay_refs[item].at[1], query_grad.at[to, :], sems.at[i, 1]),
        ]

    def each(act):
        for i, item in enumerate(items):
            here, pair = copies(i, item)

            @pl.when(here)
            def _():
                for copy in pair:
                    act(copy)

    each(lambda copy: copy.start())
    if final:
        total = keep[...] + arrived[...].astype(jnp.float32)
        key_grad[...] = total[:, :width].astype(jnp.bfloat16)
        value_grad[...] = total[:, width:].astype(jnp.bfloat16)
    each(lambda copy: copy.wait())


def place(plan, meta, payloads, grads=(), filled=()):
    items = tuple(payloads)
    big = jax.ShapeDtypeStruct((plan.rows * plan.heads, plan.width), jnp.bfloat16)
    small = jax.ShapeDtypeStruct((plan.rows, plan.width), jnp.bfloat16)
    final = len(filled) > 0
    at = 1 + len(items) + len(grads)
    return kernel_call(
        functools.partial(place_kernel, plan, items, final), "place_last" if final else "place_first",
        (meta, *payloads.values(), *grads, *filled),
        [pltpu.SMEM] + [pl.ANY] * len(items) + [pltpu.VMEM] * len(grads) + [pl.ANY] * len(filled),
        [big, big] + [small, small] * final, [pltpu.SemaphoreType.DMA((len(items), 2))],
        out_specs=[spec_of(pl.ANY)] * 2 + [spec_of(pltpu.VMEM)] * (2 * final),
        input_output_aliases={at: 0, at + 1: 1} if final else {},
        cost_estimate=plan.cost(len(items)),
    )


def on_device(query, keys, values, output_gradient, doc_lengths, block_owner):
    n = lax.axis_size("ctx")
    own = lax.axis_index("ctx")
    rows, heads, width = query.shape
    plan = Plan(n, rows, heads, width, doc_lengths.shape[0])

    def passed(array, by):
        return lax.ppermute(array, "ctx", [(i, (i + by) % n) for i in range(n)])

    k = keys.reshape(rows, width)
    v = values.reshape(rows, width)
    kv_list = []
    for i in range(1, plan.back + 1):
        kv_list += [passed(k, i), passed(v, i)]
    owners = jnp.arange(n, dtype=jnp.int32)
    match = block_owner[:, None, :] == owners[None, :, None]
    table = jnp.sum(jnp.where(match, owners, 0), axis=2)
    meta = jnp.concatenate(
        [own.reshape(1).astype(jnp.int32), jnp.cumsum(doc_lengths).astype(jnp.int32), table.reshape(-1)]
    )

    blocks = pack(plan, meta, query.reshape(rows * heads, width), output_gradient.reshape(rows * heads, width), k, v)
    kv_list = [blocks[n], *kv_list]
    first = n // 2
    items = tuple([i for i in range(1, n) if i != first] + [0])
    first_pay, first_grad = attend_first(plan, first, meta, blocks[first], kv_list)
    first_pay = passed(first_pay, first)
    out = attend_last(plan, first, items, meta, [blocks[i] for i in items], first_grad, kv_list)
    stay = {first: first_pay}
    late = {}
    for item, pay in zip(items, out):
        if item:
            late[item] = passed(pay, item)
        else:
            stay[item] = pay
    send, keep = out[len(items) :]
    bit = 1
    while True:
        arrived = lax.ppermute(send, "ctx", [(i, i ^ bit) for i in range(n)])
        bit *= 2
        if bit == n:
            break
        total = keep + arrived.astype(jnp.float32)
        send, keep = total[1::2].astype(jnp.bfloat16), total[0::2]
    grads = [keep.reshape(rows, 2 * width), arrived.reshape(rows, 2 * width)]
    attended, query_grad, key_grad, value_grad = place(plan, meta, late, grads, place(plan, meta, stay))
    return (
        attended.reshape(rows, heads, width),
        query_grad.reshape(rows, heads, width),
        key_grad.reshape(rows, 1, width),
        value_grad.reshape(rows, 1, width),
    )


def solution(mesh):
    rows = P(("dp", "ctx"), "tp", None)
    return jax.shard_map(
        on_device,
        mesh=mesh,
        in_specs=(rows, rows, rows, rows, P("dp"), P("dp", None)),
        out_specs=(rows, rows, rows, rows),
        check_vma=False,
    )
```

time: 62.5 us -> 57 us (0.912)
  waiting for transfers between devices: 31.9 us -> 23.5 us
  Pallas kernels: 8.77 us -> 12.4 us
  starting transfers between devices: 15.3 us -> 14.4 us
    ppermute x10 -> x7, waiting for transfers between devices: 31.9 us -> 9.17 us  [passed(): return lax.ppermute(array, 'ctx', [(i, (i + by) % n) for i in range(n)])]
    ppermute x0 -> x2, waiting for transfers between devices: none -> 14.3 us  [on_device(): arrived = lax.ppermute(send, 'ctx', [(i, i ^ bit) for i in range(n)])]
    pallas_call x3 -> x5, Pallas kernels: 8.77 us -> 12.4 us  [kernel_call(): pl.pallas_call(body, out_shape=out_shape, in_specs=[spec_of(space) for sp...]
    ppermute x10 -> x7, starting transfers between devices: 15.3 us -> 13.6 us  [passed(): return lax.ppermute(array, 'ctx', [(i, (i + by) % n) for i in range(n)])]
    ppermute x0 -> x2, starting transfers between devices: none -> 0.8 us  [on_device(): arrived = lax.ppermute(send, 'ctx', [(i, i ^ bit) for i in range(n)])]
    unnamed x12, local copies, waits for them, and re-layouts: 4.44 us -> 5.11 us
  transfers between devices with their start and end apart: 10 -> 9, of which waited for: 5 -> 4; matrix products, arithmetic and copies ran while one was open for 2% -> 1% of each run, Pallas kernels for 0% -> 6%
where the time goes in v2:
time: 57 us; the launch traced here: 56.7 us
  waiting for transfers between devices  23.5 us (41%)
  starting transfers between devices  14.4 us (25%)
  Pallas kernels  12.4 us (22%)
  local copies, waits for them, and re-layouts  5.23 us (9%)
  between operations  0.75 us (1%)
    ppermute x2, waiting for transfers between devices, on_device(): arrived = lax.ppermute(send, 'ctx', [(i, i ^ bit) for i in range(n)])  14.3 us
    ppermute x7, starting transfers between devices, passed(): return lax.ppermute(array, 'ctx', [(i, (i + by) % n) for i in range(n)])  13.6 us
    pallas_call x5, Pallas kernels, kernel_call(): pl.pallas_call(body, out_shape=out_shape, in_specs=[spec_of(space) for sp...  12.4 us
    ppermute x7, waiting for transfers between devices, passed(): return lax.ppermute(array, 'ctx', [(i, (i + by) % n) for i in range(n)])  9.17 us
    unnamed x12, local copies, waits for them, and re-layouts  5.11 us
  transfers between devices with their start and end apart: 9, of which 4 were waited for; matrix products, arithmetic and copies ran while one was open for 1% of the time, Pallas kernels for 6%

profile of v2, /device:TPU:0, one launch (start us, length us, event | category | flops | bytes accessed | tf_op | source)
XLA Modules:
  0.0 56.7 jit_solution(13701634792752301349)
XLA Ops:
  0.6 4.1 %collective-permute-start.2 = (bf16[256,128]{1,0:T(8,128)(2,1)}, bf16[256,128]{1,0:T(8,128)(2,1)S(1)}, u32[]{:S(2)}, u32[]{:S(2)}) collective-permute-start(bf16[256,128]{1,0:T(8,128)(2,1)} %bitcast.16), channel_id=1, source_target_pairs={{0,8},{4,12},{8,0},{12,4},{1,9},{5,13},{9,1},{13,5},{2,10},{6,14},... | collective-permute-start | bytes 196616 | tf_op jit(solution)/shard_map/ppermute | solution.py:310
  4.7 1.6 %collective-permute-start = (bf16[256,128]{1,0:T(8,128)(2,1)}, bf16[256,128]{1,0:T(8,128)(2,1)S(1)}, u32[]{:S(2)}, u32[]{:S(2)}) collective-permute-start(bf16[256,128]{1,0:T(8,128)(2,1)} %bitcast.17), channel_id=1, source_target_pairs={{0,4},{4,8},{8,12},{12,0},{1,5},{5,9},{9,13},{13,1},{2,6},{6,10},{... | collective-permute-start | bytes 196616 | tf_op jit(solution)/shard_map/ppermute | solution.py:310
  6.3 0.3 collective-permute-start.3
  6.6 2.5 %collective-permute-start.1 = (bf16[256,128]{1,0:T(8,128)(2,1)}, bf16[256,128]{1,0:T(8,128)(2,1)S(1)}, u32[]{:S(2)}, u32[]{:S(2)}) collective-permute-start(bf16[256,128]{1,0:T(8,128)(2,1)} %bitcast.20), channel_id=1, source_target_pairs={{0,4},{4,8},{8,12},{12,0},{1,5},{5,9},{9,13},{13,1},{2,6},{6,10},{... | collective-permute-start | bytes 196616 | tf_op jit(solution)/shard_map/ppermute | solution.py:310
  9.1 0.7 %copy-done.4 = s32[4,4]{1,0:T(4,128)S(1)} copy-done((s32[4,4]{1,0:T(4,128)S(1)}, s32[4,4]{1,0:T(4,128)}, u32[]{:S(2)}) %copy-start.4) | copy-done | bytes 88
  9.8 0.1 select_reduce_fusion
  9.9 0.1 reshape.74
  10.0 0.7 %copy-done.5 = s32[8]{0:T(128)S(1)} copy-done((s32[8]{0:T(128)S(1)}, s32[8]{0:T(128)}, u32[]{:S(2)}) %copy-start.5) | copy-done | bytes 56
  10.7 0.2 reduce-window.9
  10.9 0.1 pad_add_fusion.meta
  11.0 1.0 %copy-done = bf16[256,8,128]{2,1,0:T(8,128)(2,1)S(1)} copy-done((bf16[256,8,128]{2,1,0:T(8,128)(2,1)S(1)}, bf16[256,8,128]{2,1,0:T(8,128)(2,1)}, u32[]{:S(2)}) %copy-start) | copy-done | bytes 524312
  12.0 1.0 %copy-done.1 = bf16[256,8,128]{2,1,0:T(8,128)(2,1)S(1)} copy-done((bf16[256,8,128]{2,1,0:T(8,128)(2,1)S(1)}, bf16[256,8,128]{2,1,0:T(8,128)(2,1)}, u32[]{:S(2)}) %copy-start.1) | copy-done | bytes 524312
  13.0 0.8 %copy-done.2 = bf16[256,1,128]{2,0,1:T(8,128)(2,1)S(1)} copy-done((bf16[256,1,128]{2,0,1:T(8,128)(2,1)S(1)}, bf16[256,1,128]{2,0,1:T(8,128)(2,1)}, u32[]{:S(2)}) %copy-start.2) | copy-done | bytes 65560
  13.9 0.8 %copy-done.3 = bf16[256,1,128]{2,0,1:T(8,128)(2,1)S(1)} copy-done((bf16[256,1,128]{2,0,1:T(8,128)(2,1)S(1)}, bf16[256,1,128]{2,0,1:T(8,128)(2,1)}, u32[]{:S(2)}) %copy-start.3) | copy-done | bytes 65560
  14.7 2.2 %pack.1 = (bf16[2,512,128]{2,1,0:T(8,128)(2,1)S(1)}, bf16[2,512,128]{2,1,0:T(8,128)(2,1)S(1)}, bf16[2,512,128]{2,1,0:T(8,128)(2,1)S(1)}, bf16[2,512,128]{2,1,0:T(8,128)(2,1)S(1)}, bf16[2,256,128]{2,1,0:T(8,128)(2,1)S(1)}) custom-call(s32[25]{0:T(128)S(1)} %pad_add_fusion.meta, bf16[2048,128]{1,0:T(8,128)(2,1)S(1)} %bitcast.13, ...), custom_call_target="tpu_custom_call" | custom-call | tf_op jit(solution)/shard_map/pack/pallas_call | solution.py:193
  16.9 0.0 collective-permute-done.2.refs_3_.refs_7_
  16.9 0.0 collective-permute-done.3.refs_4_.refs_8_
  16.9 0.0 collective-permute-done.1.refs_2_.refs_6_
  17.0 2.0 %attend_first.1 = (bf16[2,512,128]{2,1,0:T(8,128)(2,1)S(1)}, f32[576,256]{1,0:T(8,128)S(1)}) custom-call(s32[25]{0:T(128)S(1)} %pad_add_fusion.meta, bf16[2,512,128]{2,1,0:T(8,128)(2,1)S(1)} %get-tuple-element.25.qg, bf16[2,256,128]{2,1,0:T(8,128)(2,1)S(1)} %get-tuple-element.26.refs_0_.refs_4_, bf16[256,128]{1,0:T(8,128)(2,1)S(1)} %collective-permute-done.refs_1_.refs_5_, ...), custom_call_target="tpu_custom_call" | custom-call | flops 4227858432 | bytes 1048576 | tf_op jit(solution)/shard_map/attend_first/pallas_call | solution.py:193
  18.9 4.9 %attend_last.1 = (bf16[2,512,128]{2,1,0:T(8,128)(2,1)S(1)}, bf16[2,512,128]{2,1,0:T(8,128)(2,1)S(1)}, bf16[2,512,128]{2,1,0:T(8,128)(2,1)S(1)}, bf16[2,4,64,256]{3,2,1,0:T(8,128)(2,1)S(1)}, f32[2,4,64,256]{3,2,1,0:T(8,128)S(1)}) custom-call(s32[25]{0:T(128)S(1)} %pad_add_fusion.meta, bf16[2,512,128]{2,1,0:T(8,128)(2,1)S(1)} %get-tuple-element.22.refs_0_, ...), custom_call_target="tpu_custom_call" | custom-call | flops 12683575296 | bytes 3145728 | tf_op jit(solution)/shard_map/attend_last/pallas_call | solution.py:193
  23.8 0.7 %collective-permute-start.6 = (bf16[2,4,64,256]{3,2,1,0:T(8,128)(2,1)S(1)}, bf16[2,4,64,256]{3,2,1,0:T(8,128)(2,1)S(1)}, u32[]{:S(2)}, u32[]{:S(2)}) collective-permute-start(bf16[2,4,64,256]{3,2,1,0:T(8,128)(2,1)S(1)} %get-tuple-element.31), channel_id=1, source_target_pairs={{0,4},{4,0},{8,12},{12,8},{1,5},{5,1},{9,13},{13,9},{2,6},{6,2},{1... | collective-permute-start | bytes 786440 | tf_op jit(solution)/shard_map/ppermute | solution.py:341
  24.6 1.2 %collective-permute-start.8 = (bf16[2,512,128]{2,1,0:T(8,128)(2,1)S(1)}, bf16[2,512,128]{2,1,0:T(8,128)(2,1)S(1)}, u32[]{:S(2)}, u32[]{:S(2)}) collective-permute-start(bf16[2,512,128]{2,1,0:T(8,128)(2,1)S(1)} %get-tuple-element.32), channel_id=1, source_target_pairs={{0,8},{4,12},{8,0},{12,4},{1,9},{5,13},{9,1},{13,5},{2,10},{6,14},... | collective-permute-start | bytes 786440 | tf_op jit(solution)/shard_map/ppermute | solution.py:310
  25.8 0.2 collective-permute-start.4
  26.0 3.6 %collective-permute-start.5 = (bf16[2,512,128]{2,1,0:T(8,128)(2,1)S(1)}, bf16[2,512,128]{2,1,0:T(8,128)(2,1)S(1)}, u32[]{:S(2)}, u32[]{:S(2)}) collective-permute-start(bf16[2,512,128]{2,1,0:T(8,128)(2,1)S(1)} %get-tuple-element.29), channel_id=1, source_target_pairs={{0,12},{4,0},{8,4},{12,8},{1,13},{5,1},{9,5},{13,9},{2,14},{6,2},{... | collective-permute-start | bytes 786440 | tf_op jit(solution)/shard_map/ppermute | solution.py:310
  29.6 7.6 %collective-permute-done.6 = bf16[2,4,64,256]{3,2,1,0:T(8,128)(2,1)S(1)} collective-permute-done((bf16[2,4,64,256]{3,2,1,0:T(8,128)(2,1)S(1)}, bf16[2,4,64,256]{3,2,1,0:T(8,128)(2,1)S(1)}, u32[]{:S(2)}, u32[]{:S(2)}) %collective-permute-start.6) | collective-permute-done | bytes 262176 | tf_op jit(solution)/shard_map/ppermute | solution.py:341
  37.2 0.1 convert_add_fusion
  37.3 0.1 collective-permute-start.7
  37.4 8.6 %collective-permute-done.8.refs_0_ = bf16[2,512,128]{2,1,0:T(8,128)(2,1)S(1)} collective-permute-done((bf16[2,512,128]{2,1,0:T(8,128)(2,1)S(1)}, bf16[2,512,128]{2,1,0:T(8,128)(2,1)S(1)}, u32[]{:S(2)}, u32[]{:S(2)}) %collective-permute-start.8) | collective-permute-done | bytes 262176 | tf_op jit(solution)/shard_map/ppermute | solution.py:310
  46.0 1.4 %place_first.1 = (bf16[2048,128]{1,0:T(8,128)(2,1)}, bf16[2048,128]{1,0:T(8,128)(2,1)}) custom-call(s32[25]{0:T(128)S(1)} %pad_add_fusion.meta, bf16[2,512,128]{2,1,0:T(8,128)(2,1)S(1)} %collective-permute-done.8.refs_0_, bf16[2,512,128]{2,1,0:T(8,128)(2,1)S(1)} %get-tuple-element.33.refs_1_), custom_call_target="tpu_custom_call" | custom-call | flops 8455716864 | bytes 2097152 | tf_op jit(solution)/shard_map/place_first/pallas_call | solution.py:193
  47.4 0.5 collective-permute-done.5.refs_1_
  47.9 6.7 %collective-permute-done.7 = bf16[1,4,64,256]{3,2,1,0:T(8,128)(2,1)S(1)} collective-permute-done((bf16[1,4,64,256]{3,2,1,0:T(8,128)(2,1)S(1)}, bf16[1,4,64,256]{3,2,1,0:T(8,128)(2,1)S(1)}, u32[]{:S(2)}, u32[]{:S(2)}) %collective-permute-start.7) | collective-permute-done | bytes 131104 | tf_op jit(solution)/shard_map/ppermute | solution.py:341
  54.7 2.0 %place_last.1 = (bf16[2048,128]{1,0:T(8,128)(2,1)}, bf16[2048,128]{1,0:T(8,128)(2,1)}, bf16[256,128]{1,0:T(8,128)(2,1)}, bf16[256,128]{1,0:T(8,128)(2,1)}) custom-call(s32[25]{0:T(128)S(1)} %pad_add_fusion.meta, bf16[2,512,128]{2,1,0:T(8,128)(2,1)S(1)} %collective-permute-done.4.refs_0_, ...), custom_call_target="tpu_custom_call", output_to_operand_aliasing={{0}: (5, {}), {1}: (6, {})} | custom-call | flops 8455716864 | bytes 2097152 | tf_op jit(solution)/shard_map/place_last/pallas_call | solution.py:193
  (10 shorter events, 0.0 us)
Async XLA Ops:
  0.6 16.3 %collective-permute-start.2 = (bf16[256,128]{1,0:T(8,128)(2,1)}, bf16[256,128]{1,0:T(8,128)(2,1)S(1)}, u32[]{:S(2)}, u32[]{:S(2)}) collective-permute-start(bf16[256,128]{1,0:T(8,128)(2,1)} %bitcast.16), channel_id=1, source_target_pairs={{0,8},{4,12},{8,0},{12,4},{1,9},{5,13},{9,1},{13,5},{2,10},{6,14},... | collective-permute-start | bytes 196616 | tf_op jit(solution)/shard_map/ppermute | solution.py:310
  4.7 12.2 %collective-permute-start = (bf16[256,128]{1,0:T(8,128)(2,1)}, bf16[256,128]{1,0:T(8,128)(2,1)S(1)}, u32[]{:S(2)}, u32[]{:S(2)}) collective-permute-start(bf16[256,128]{1,0:T(8,128)(2,1)} %bitcast.17), channel_id=1, source_target_pairs={{0,4},{4,8},{8,12},{12,0},{1,5},{5,9},{9,13},{13,1},{2,6},{6,10},{... | collective-permute-start | bytes 196616 | tf_op jit(solution)/shard_map/ppermute | solution.py:310
  6.3 10.6 %collective-permute-start.3 = (bf16[256,128]{1,0:T(8,128)(2,1)}, bf16[256,128]{1,0:T(8,128)(2,1)S(1)}, u32[]{:S(2)}, u32[]{:S(2)}) collective-permute-start(bf16[256,128]{1,0:T(8,128)(2,1)} %bitcast.19), channel_id=1, source_target_pairs={{0,8},{4,12},{8,0},{12,4},{1,9},{5,13},{9,1},{13,5},{2,10},{6,14},... | collective-permute-start | bytes 196616 | tf_op jit(solution)/shard_map/ppermute | solution.py:310
  6.6 10.3 %collective-permute-start.1 = (bf16[256,128]{1,0:T(8,128)(2,1)}, bf16[256,128]{1,0:T(8,128)(2,1)S(1)}, u32[]{:S(2)}, u32[]{:S(2)}) collective-permute-start(bf16[256,128]{1,0:T(8,128)(2,1)} %bitcast.20), channel_id=1, source_target_pairs={{0,4},{4,8},{8,12},{12,0},{1,5},{5,9},{9,13},{13,1},{2,6},{6,10},{... | collective-permute-start | bytes 196616 | tf_op jit(solution)/shard_map/ppermute | solution.py:310
  9.1 0.7 %copy-start.4 = (s32[4,4]{1,0:T(4,128)S(1)}, s32[4,4]{1,0:T(4,128)}, u32[]{:S(2)}) copy-start(s32[4,4]{1,0:T(4,128)} %param.11) | copy-start | bytes 196
  10.0 0.7 %copy-start.5 = (s32[8]{0:T(128)S(1)}, s32[8]{0:T(128)}, u32[]{:S(2)}) copy-start(s32[8]{0:T(128)} %param.10) | copy-start | bytes 100
  11.0 1.0 %copy-start = (bf16[256,8,128]{2,1,0:T(8,128)(2,1)S(1)}, bf16[256,8,128]{2,1,0:T(8,128)(2,1)}, u32[]{:S(2)}) copy-start(bf16[256,8,128]{2,1,0:T(8,128)(2,1)} %param.6) | copy-start | bytes 1572868
  12.0 1.0 %copy-start.1 = (bf16[256,8,128]{2,1,0:T(8,128)(2,1)S(1)}, bf16[256,8,128]{2,1,0:T(8,128)(2,1)}, u32[]{:S(2)}) copy-start(bf16[256,8,128]{2,1,0:T(8,128)(2,1)} %param.9) | copy-start | bytes 1572868
  13.0 0.8 %copy-start.2 = (bf16[256,1,128]{2,0,1:T(8,128)(2,1)S(1)}, bf16[256,1,128]{2,0,1:T(8,128)(2,1)}, u32[]{:S(2)}) copy-start(bf16[256,1,128]{2,0,1:T(8,128)(2,1)} %param.7) | copy-start | bytes 196612
  13.9 0.8 %copy-start.3 = (bf16[256,1,128]{2,0,1:T(8,128)(2,1)S(1)}, bf16[256,1,128]{2,0,1:T(8,128)(2,1)}, u32[]{:S(2)}) copy-start(bf16[256,1,128]{2,0,1:T(8,128)(2,1)} %param.8) | copy-start | bytes 196612
  23.8 13.4 %collective-permute-start.6 = (bf16[2,4,64,256]{3,2,1,0:T(8,128)(2,1)S(1)}, bf16[2,4,64,256]{3,2,1,0:T(8,128)(2,1)S(1)}, u32[]{:S(2)}, u32[]{:S(2)}) collective-permute-start(bf16[2,4,64,256]{3,2,1,0:T(8,128)(2,1)S(1)} %get-tuple-element.31), channel_id=1, source_target_pairs={{0,4},{4,0},{8,12},{12,8},{1,5},{5,1},{9,13},{13,9},{2,6},{6,2},{1... | collective-permute-start | bytes 786440 | tf_op jit(solution)/shard_map/ppermute | solution.py:341
  24.6 21.4 %collective-permute-start.8 = (bf16[2,512,128]{2,1,0:T(8,128)(2,1)S(1)}, bf16[2,512,128]{2,1,0:T(8,128)(2,1)S(1)}, u32[]{:S(2)}, u32[]{:S(2)}) collective-permute-start(bf16[2,512,128]{2,1,0:T(8,128)(2,1)S(1)} %get-tuple-element.32), channel_id=1, source_target_pairs={{0,8},{4,12},{8,0},{12,4},{1,9},{5,13},{9,1},{13,5},{2,10},{6,14},... | collective-permute-start | bytes 786440 | tf_op jit(solution)/shard_map/ppermute | solution.py:310
  25.8 21.6 %collective-permute-start.4 = (bf16[2,512,128]{2,1,0:T(8,128)(2,1)S(1)}, bf16[2,512,128]{2,1,0:T(8,128)(2,1)S(1)}, u32[]{:S(2)}, u32[]{:S(2)}) collective-permute-start(bf16[2,512,128]{2,1,0:T(8,128)(2,1)S(1)} %get-tuple-element.28), channel_id=1, source_target_pairs={{0,4},{4,8},{8,12},{12,0},{1,5},{5,9},{9,13},{13,1},{2,6},{6,10},{... | collective-permute-start | bytes 786440 | tf_op jit(solution)/shard_map/ppermute | solution.py:310
  26.0 21.9 %collective-permute-start.5 = (bf16[2,512,128]{2,1,0:T(8,128)(2,1)S(1)}, bf16[2,512,128]{2,1,0:T(8,128)(2,1)S(1)}, u32[]{:S(2)}, u32[]{:S(2)}) collective-permute-start(bf16[2,512,128]{2,1,0:T(8,128)(2,1)S(1)} %get-tuple-element.29), channel_id=1, source_target_pairs={{0,12},{4,0},{8,4},{12,8},{1,13},{5,1},{9,5},{13,9},{2,14},{6,2},{... | collective-permute-start | bytes 786440 | tf_op jit(solution)/shard_map/ppermute | solution.py:310
  37.3 17.4 %collective-permute-start.7 = (bf16[1,4,64,256]{3,2,1,0:T(8,128)(2,1)S(1)}, bf16[1,4,64,256]{3,2,1,0:T(8,128)(2,1)S(1)}, u32[]{:S(2)}, u32[]{:S(2)}) collective-permute-start(bf16[1,4,64,256]{3,2,1,0:T(8,128)(2,1)S(1)} %slice.14), channel_id=1, source_target_pairs={{0,8},{4,12},{8,0},{12,4},{1,9},{5,13},{9,1},{13,5},{2,10},{6,14},... | collective-permute-start | bytes 393224 | tf_op jit(solution)/shard_map/ppermute | solution.py:341

commit v3 on v2

--- a/solution.py
+++ b/solution.py
@@ -131,8 +131,8 @@
     n, width, rows, block = plan.n, plan.width, plan.rows, plan.block
     qg_refs, refs = refs[: len(items)], refs[len(items) :]
     first_grad, refs = refs[0], refs[1:]
-    kv_refs, refs = refs[: -(len(items) + 5)], refs[-(len(items) + 5) :]
-    pay_refs, (send_ref, keep_ref, k_win, v_win, acc) = refs[: len(items)], refs[len(items) :]
+    kv_refs, refs = refs[: -(len(items) + 7)], refs[-(len(items) + 7) :]
+    pay_refs, grad_refs, (k_win, v_win, acc) = refs[: len(items)], refs[len(items) : -3], refs[-3:]
     step = pl.program_id(0)
     own = meta[0]
 
@@ -178,8 +178,8 @@
             for apart in range(n):
                 slot = plan.slot(meta, key_range, own ^ apart)
                 part = acc[pl.ds(pl.multiple_of(at + slot * block, block), block), :]
-                to = keep_ref if apart % 2 == 0 else send_ref
-                to[apart // 2, key_range] = part.astype(to.dtype)
+                to = grad_refs[apart % 4]
+                to[apart // 4, key_range] = part.astype(to.dtype)
             return carry
 
         lax.fori_loop(0, n, of_range, 0)
@@ -208,6 +208,7 @@
         functools.partial(pack_kernel, plan), "pack", (meta, q, g, k, v), [pltpu.SMEM] + [pl.ANY] * 4, out_shape,
         [pltpu.SemaphoreType.DMA((plan.n, 2)), pltpu.SemaphoreType.DMA((2,))],
         out_specs=[spec_of(pltpu.VMEM)] * len(out_shape),
+        cost_estimate=pl.CostEstimate(flops=0, bytes_accessed=1024, transcendentals=0),
     )
 
 
@@ -228,9 +229,9 @@
 def attend_last(plan, first_shift, items, meta, qg_list, first_grad, kv_list):
     n = plan.n
     window = pltpu.VMEM((plan.window_ranges * plan.rows, plan.width), jnp.bfloat16)
-    grads = (n // 2, n, plan.block, 2 * plan.width)
+    grads = (n // 4, n, plan.block, 2 * plan.width)
     out_shape = [jax.ShapeDtypeStruct((2, plan.cols, plan.width), jnp.bfloat16)] * len(items)
-    out_shape += [jax.ShapeDtypeStruct(grads, jnp.bfloat16), jax.ShapeDtypeStruct(grads, jnp.float32)]
+    out_shape += [jax.ShapeDtypeStruct(grads, jnp.bfloat16 if apart % 2 else jnp.float32) for apart in range(4)]
     operands = (meta, *qg_list, first_grad, *kv_list)
     return kernel_call(
         functools.partial(last_kernel, plan, first_shift, items), "attend_last", operands,
@@ -244,9 +245,9 @@
     n, cols, width, own = plan.n, plan.cols, plan.width, meta[0]
     pay_refs, refs = dict(zip(items, refs[: len(items)])), refs[len(items) :]
     if final:
-        keep, arrived, _, _, attended, query_grad, key_grad, value_grad, sems = refs
+        grads, (_, _, attended, query_grad, key_grad, value_grad, sems) = refs[:-7], refs[-7:]
     else:
-        attended, query_grad, sems = refs
+        grads, (attended, query_grad, send, sems) = refs[:-4], refs[-4:]
 
     def copies(i, item):
         if item == "ahead":
@@ -276,8 +277,10 @@
                     act(copy)
 
     each(lambda copy: copy.start())
+    total = sum(grad[...].astype(jnp.float32) for grad in grads)
+    if not final:
+        send[...] = total.astype(jnp.bfloat16)
     if final:
-        total = keep[...] + arrived[...].astype(jnp.float32)
         key_grad[...] = total[:, :width].astype(jnp.bfloat16)
         value_grad[...] = total[:, width:].astype(jnp.bfloat16)
     each(lambda copy: copy.wait())
@@ -293,8 +296,8 @@
         functools.partial(place_kernel, plan, items, final), "place_last" if final else "place_first",
         (meta, *payloads.values(), *grads, *filled),
         [pltpu.SMEM] + [pl.ANY] * len(items) + [pltpu.VMEM] * len(grads) + [pl.ANY] * len(filled),
-        [big, big] + [small, small] * final, [pltpu.SemaphoreType.DMA((len(items), 2))],
-        out_specs=[spec_of(pl.ANY)] * 2 + [spec_of(pltpu.VMEM)] * (2 * final),
+        [big, big] + ([small, small] if final else [jax.ShapeDtypeStruct(grads[0].shape, jnp.bfloat16)]), [pltpu.SemaphoreType.DMA((len(items), 2))],
+        out_specs=[spec_of(pl.ANY)] * 2 + [spec_of(pltpu.VMEM)] * (1 + final),
         input_output_aliases={at: 0, at + 1: 1} if final else {},
         cost_estimate=plan.cost(len(items)),
     )
@@ -335,17 +338,21 @@
             late[item] = passed(pay, item)
         else:
             stay[item] = pay
-    send, keep = out[len(items) :]
-    bit = 1
-    while True:
-        arrived = lax.ppermute(send, "ctx", [(i, i ^ bit) for i in range(n)])
+    def across(array, bit):
+        return lax.ppermute(array, "ctx", [(i, i ^ bit) for i in range(n)])
+
+    keep, to_keep, pass_on, to_pass_on = out[len(items) :]
+    pass_on = (pass_on, across(to_pass_on, 1))
+    terms = (keep, across(to_keep, 1))
+    attended, query_grad, send = place(plan, meta, stay, pass_on)
+    terms += (across(send, 2),)
+    bit = 4
+    while bit < n:
+        total = sum(term.astype(jnp.float32) for term in terms)
+        terms = (total[0::2], across(total[1::2].astype(jnp.bfloat16), bit))
         bit *= 2
-        if bit == n:
-            break
-        total = keep + arrived.astype(jnp.float32)
-        send, keep = total[1::2].astype(jnp.bfloat16), total[0::2]
-    grads = [keep.reshape(rows, 2 * width), arrived.reshape(rows, 2 * width)]
-    attended, query_grad, key_grad, value_grad = place(plan, meta, late, grads, place(plan, meta, stay))
+    terms = [term.reshape(rows, 2 * width) for term in terms]
+    attended, query_grad, key_grad, value_grad = place(plan, meta, late, terms, (attended, query_grad))
     return (
         attended.reshape(rows, heads, width),
         query_grad.reshape(rows, heads, width),

time: 57 us -> 53.1 us (0.932)
  waiting for transfers between devices: 23.5 us -> 19.4 us
    ppermute x7, waiting for transfers between devices: 9.17 us -> 6.89 us  [passed(): return lax.ppermute(array, 'ctx', [(i, (i + by) % n) for i in range(n)])]
    ppermute x2 -> x3, waiting for transfers between devices: 14.3 us -> 12.5 us  [across(): return lax.ppermute(array, 'ctx', [(i, i ^ bit) for i in range(n)])]
    ppermute x2 -> x3, starting transfers between devices: 0.8 us -> 2.16 us  [across(): return lax.ppermute(array, 'ctx', [(i, i ^ bit) for i in range(n)])]
    ppermute x7, starting transfers between devices: 13.6 us -> 12.5 us  [passed(): return lax.ppermute(array, 'ctx', [(i, (i + by) % n) for i in range(n)])]
  transfers between devices with their start and end apart: 9 -> 10, of which waited for: 4 -> 3; matrix products, arithmetic and copies ran while one was open for 1% -> 1% of each run, Pallas kernels for 6% -> 16%
where the time goes in v3:
time: 53.1 us; the launch traced here: 52.7 us
  waiting for transfers between devices  19.4 us (37%)
  starting transfers between devices  14.7 us (28%)
  Pallas kernels  12.4 us (23%)
  local copies, waits for them, and re-layouts  5.19 us (10%)
  between operations  0.72 us (1%)
    ppermute x7, starting transfers between devices, passed(): return lax.ppermute(array, 'ctx', [(i, (i + by) % n) for i in range(n)])  12.5 us
    ppermute x3, waiting for transfers between devices, across(): return lax.ppermute(array, 'ctx', [(i, i ^ bit) for i in range(n)])  12.5 us
    pallas_call x5, Pallas kernels, kernel_call(): pl.pallas_call(body, out_shape=out_shape, in_specs=[spec_of(space) for sp...  12.4 us
    ppermute x7, waiting for transfers between devices, passed(): return lax.ppermute(array, 'ctx', [(i, (i + by) % n) for i in range(n)])  6.89 us
    unnamed x12, local copies, waits for them, and re-layouts  5.11 us
    ppermute x3, starting transfers between devices, across(): return lax.ppermute(array, 'ctx', [(i, i ^ bit) for i in range(n)])  2.16 us
  transfers between devices with their start and end apart: 10, of which 3 were waited for; matrix products, arithmetic and copies ran while one was open for 1% of the time, Pallas kernels for 16%

profile of v3, /device:TPU:0, one launch (start us, length us, event | category | flops | bytes accessed | tf_op | source)
XLA Modules:
  0.0 52.7 jit_solution(12685838226481239667)
XLA Ops:
  0.6 4.1 %collective-permute-start.2 = (bf16[256,128]{1,0:T(8,128)(2,1)}, bf16[256,128]{1,0:T(8,128)(2,1)S(1)}, u32[]{:S(2)}, u32[]{:S(2)}) collective-permute-start(bf16[256,128]{1,0:T(8,128)(2,1)} %bitcast.16), channel_id=1, source_target_pairs={{0,8},{4,12},{8,0},{12,4},{1,9},{5,13},{9,1},{13,5},{2,10},{6,14},... | collective-permute-start | bytes 196616 | tf_op jit(solution)/shard_map/ppermute | solution.py:313
  4.7 1.6 %collective-permute-start = (bf16[256,128]{1,0:T(8,128)(2,1)}, bf16[256,128]{1,0:T(8,128)(2,1)S(1)}, u32[]{:S(2)}, u32[]{:S(2)}) collective-permute-start(bf16[256,128]{1,0:T(8,128)(2,1)} %bitcast.17), channel_id=1, source_target_pairs={{0,4},{4,8},{8,12},{12,0},{1,5},{5,9},{9,13},{13,1},{2,6},{6,10},{... | collective-permute-start | bytes 196616 | tf_op jit(solution)/shard_map/ppermute | solution.py:313
  6.3 0.3 collective-permute-start.3
  6.6 2.5 %collective-permute-start.1 = (bf16[256,128]{1,0:T(8,128)(2,1)}, bf16[256,128]{1,0:T(8,128)(2,1)S(1)}, u32[]{:S(2)}, u32[]{:S(2)}) collective-permute-start(bf16[256,128]{1,0:T(8,128)(2,1)} %bitcast.20), channel_id=1, source_target_pairs={{0,4},{4,8},{8,12},{12,0},{1,5},{5,9},{9,13},{13,1},{2,6},{6,10},{... | collective-permute-start | bytes 196616 | tf_op jit(solution)/shard_map/ppermute | solution.py:313
  9.1 0.7 %copy-done.4 = s32[4,4]{1,0:T(4,128)S(1)} copy-done((s32[4,4]{1,0:T(4,128)S(1)}, s32[4,4]{1,0:T(4,128)}, u32[]{:S(2)}) %copy-start.4) | copy-done | bytes 88
  9.8 0.1 select_reduce_fusion
  9.9 0.1 reshape.77
  10.0 0.7 %copy-done.5 = s32[8]{0:T(128)S(1)} copy-done((s32[8]{0:T(128)S(1)}, s32[8]{0:T(128)}, u32[]{:S(2)}) %copy-start.5) | copy-done | bytes 56
  10.7 0.2 reduce-window.9
  10.9 0.1 pad_add_fusion.meta
  11.0 1.0 %copy-done = bf16[256,8,128]{2,1,0:T(8,128)(2,1)S(1)} copy-done((bf16[256,8,128]{2,1,0:T(8,128)(2,1)S(1)}, bf16[256,8,128]{2,1,0:T(8,128)(2,1)}, u32[]{:S(2)}) %copy-start) | copy-done | bytes 524312
  12.0 1.0 %copy-done.1 = bf16[256,8,128]{2,1,0:T(8,128)(2,1)S(1)} copy-done((bf16[256,8,128]{2,1,0:T(8,128)(2,1)S(1)}, bf16[256,8,128]{2,1,0:T(8,128)(2,1)}, u32[]{:S(2)}) %copy-start.1) | copy-done | bytes 524312
  13.0 0.8 %copy-done.2 = bf16[256,1,128]{2,0,1:T(8,128)(2,1)S(1)} copy-done((bf16[256,1,128]{2,0,1:T(8,128)(2,1)S(1)}, bf16[256,1,128]{2,0,1:T(8,128)(2,1)}, u32[]{:S(2)}) %copy-start.2) | copy-done | bytes 65560
  13.9 0.8 %copy-done.3 = bf16[256,1,128]{2,0,1:T(8,128)(2,1)S(1)} copy-done((bf16[256,1,128]{2,0,1:T(8,128)(2,1)S(1)}, bf16[256,1,128]{2,0,1:T(8,128)(2,1)}, u32[]{:S(2)}) %copy-start.3) | copy-done | bytes 65560
  14.7 2.2 %pack.1 = (bf16[2,512,128]{2,1,0:T(8,128)(2,1)S(1)}, bf16[2,512,128]{2,1,0:T(8,128)(2,1)S(1)}, bf16[2,512,128]{2,1,0:T(8,128)(2,1)S(1)}, bf16[2,512,128]{2,1,0:T(8,128)(2,1)S(1)}, bf16[2,256,128]{2,1,0:T(8,128)(2,1)S(1)}) custom-call(s32[25]{0:T(128)S(1)} %pad_add_fusion.meta, bf16[2048,128]{1,0:T(8,128)(2,1)S(1)} %bitcast.14, ...), custom_call_target="tpu_custom_call" | custom-call | bytes 1024 | tf_op jit(solution)/shard_map/pack/pallas_call | solution.py:193
  16.9 0.0 collective-permute-done.refs_1_.refs_5_
  16.9 0.0 collective-permute-done.3.refs_4_.refs_8_
  17.0 2.0 %attend_first.1 = (bf16[2,512,128]{2,1,0:T(8,128)(2,1)S(1)}, f32[576,256]{1,0:T(8,128)S(1)}) custom-call(s32[25]{0:T(128)S(1)} %pad_add_fusion.meta, bf16[2,512,128]{2,1,0:T(8,128)(2,1)S(1)} %get-tuple-element.28.qg, bf16[2,256,128]{2,1,0:T(8,128)(2,1)S(1)} %get-tuple-element.29.refs_0_.refs_4_, bf16[256,128]{1,0:T(8,128)(2,1)S(1)} %collective-permute-done.refs_1_.refs_5_, ...), custom_call_target="tpu_custom_call" | custom-call | flops 4227858432 | bytes 1048576 | tf_op jit(solution)/shard_map/attend_first/pallas_call | solution.py:193
  18.9 0.2 collective-permute-start.7
  19.1 4.9 %attend_last.1 = (bf16[2,512,128]{2,1,0:T(8,128)(2,1)S(1)}, bf16[2,512,128]{2,1,0:T(8,128)(2,1)S(1)}, bf16[2,512,128]{2,1,0:T(8,128)(2,1)S(1)}, f32[1,4,64,256]{...) custom-call(s32[25]{0:T(128)S(1)} %pad_add_fusion.meta, ...), custom_call_target="tpu_custom_call" | custom-call | flops 12683575296 | bytes 3145728 | tf_op jit(solution)/shard_map/attend_last/pallas_call | solution.py:193
  24.0 1.8 %collective-permute-start.8 = (bf16[1,4,64,256]{3,2,1,0:T(8,128)(2,1)S(1)}, bf16[1,4,64,256]{3,2,1,0:T(8,128)(2,1)S(1)}, u32[]{:S(2)}, u32[]{:S(2)}) collective-permute-start(bf16[1,4,64,256]{3,2,1,0:T(8,128)(2,1)S(1)} %get-tuple-element.38), channel_id=1, source_target_pairs={{0,4},{4,0},{8,12},{12,8},{1,5},{5,1},{9,13},{13,9},{2,6},{6,2},{1... | collective-permute-start | bytes 393224 | tf_op jit(solution)/shard_map/ppermute | solution.py:342
  25.8 0.2 collective-permute-start.6
  26.1 1.8 %collective-permute-start.4 = (bf16[2,512,128]{2,1,0:T(8,128)(2,1)S(1)}, bf16[2,512,128]{2,1,0:T(8,128)(2,1)S(1)}, u32[]{:S(2)}, u32[]{:S(2)}) collective-permute-start(bf16[2,512,128]{2,1,0:T(8,128)(2,1)S(1)} %get-tuple-element.31), channel_id=1, source_target_pairs={{0,4},{4,8},{8,12},{12,0},{1,5},{5,9},{9,13},{13,1},{2,6},{6,10},{... | collective-permute-start | bytes 786440 | tf_op jit(solution)/shard_map/ppermute | solution.py:313
  27.9 2.0 %collective-permute-start.5 = (bf16[2,512,128]{2,1,0:T(8,128)(2,1)S(1)}, bf16[2,512,128]{2,1,0:T(8,128)(2,1)S(1)}, u32[]{:S(2)}, u32[]{:S(2)}) collective-permute-start(bf16[2,512,128]{2,1,0:T(8,128)(2,1)S(1)} %get-tuple-element.32), channel_id=1, source_target_pairs={{0,12},{4,0},{8,4},{12,8},{1,13},{5,1},{9,5},{13,9},{2,14},{6,2},{... | collective-permute-start | bytes 786440 | tf_op jit(solution)/shard_map/ppermute | solution.py:313
  29.9 11.0 %collective-permute-done.8.refs_3_ = bf16[1,4,64,256]{3,2,1,0:T(8,128)(2,1)S(1)} collective-permute-done((bf16[1,4,64,256]{3,2,1,0:T(8,128)(2,1)S(1)}, bf16[1,4,64,256]{3,2,1,0:T(8,128)(2,1)S(1)}, u32[]{:S(2)}, u32[]{:S(2)}) %collective-permute-start.8) | collective-permute-done | bytes 131104 | tf_op jit(solution)/shard_map/ppermute | solution.py:342
  40.9 0.0 collective-permute-done.7.refs_0_
  40.9 1.4 %place_first.1 = (bf16[2048,128]{1,0:T(8,128)(2,1)}, bf16[2048,128]{1,0:T(8,128)(2,1)}, bf16[1,4,64,256]{3,2,1,0:T(8,128)(2,1)S(1)}) custom-call(s32[25]{0:T(128)S(1)} %pad_add_fusion.meta, bf16[2,512,128]{2,1,0:T(8,128)(2,1)S(1)} %collective-permute-done.7.refs_0_, bf16[2,512,128]{2,1,0:T(8,128)(2,1)S(1)} %get-tuple-element.36.refs_1_, ...), custom_call_target="tpu_custom_call" | custom-call | flops 8455716864 | bytes 2097152 | tf_op jit(solution)/shard_map/place_first/pallas_call | solution.py:193
  42.3 0.1 collective-permute-start.9
  42.3 1.5 %collective-permute-done.6 = bf16[1,4,64,256]{3,2,1,0:T(8,128)(2,1)S(1)} collective-permute-done((bf16[1,4,64,256]{3,2,1,0:T(8,128)(2,1)S(1)}, bf16[1,4,64,256]{3,2,1,0:T(8,128)(2,1)S(1)}, u32[]{:S(2)}, u32[]{:S(2)}) %collective-permute-start.6) | collective-permute-done | bytes 131104 | tf_op jit(solution)/shard_map/ppermute | solution.py:342
  43.8 0.0 collective-permute-done.4.refs_0_
  43.8 6.9 %collective-permute-done.5.refs_1_ = bf16[2,512,128]{2,1,0:T(8,128)(2,1)S(1)} collective-permute-done((bf16[2,512,128]{2,1,0:T(8,128)(2,1)S(1)}, bf16[2,512,128]{2,1,0:T(8,128)(2,1)S(1)}, u32[]{:S(2)}, u32[]{:S(2)}) %collective-permute-start.5) | collective-permute-done | bytes 262176 | tf_op jit(solution)/shard_map/ppermute | solution.py:313
  50.7 2.0 %place_last.1 = (bf16[2048,128]{1,0:T(8,128)(2,1)}, bf16[2048,128]{1,0:T(8,128)(2,1)}, bf16[256,128]{1,0:T(8,128)(2,1)}, bf16[256,128]{1,0:T(8,128)(2,1)}) custom-call(s32[25]{0:T(128)S(1)} %pad_add_fusion.meta, bf16[2,512,128]{2,1,0:T(8,128)(2,1)S(1)} %collective-permute-done.4.refs_0_, ...), custom_call_target="tpu_custom_call", output_to_operand_aliasing={{0}: (6, {}), {1}: (7, {})} | custom-call | flops 8455716864 | bytes 2097152 | tf_op jit(solution)/shard_map/place_last/pallas_call | solution.py:193
  (9 shorter events, 0.0 us)
Async XLA Ops:
  0.6 16.3 %collective-permute-start.2 = (bf16[256,128]{1,0:T(8,128)(2,1)}, bf16[256,128]{1,0:T(8,128)(2,1)S(1)}, u32[]{:S(2)}, u32[]{:S(2)}) collective-permute-start(bf16[256,128]{1,0:T(8,128)(2,1)} %bitcast.16), channel_id=1, source_target_pairs={{0,8},{4,12},{8,0},{12,4},{1,9},{5,13},{9,1},{13,5},{2,10},{6,14},... | collective-permute-start | bytes 196616 | tf_op jit(solution)/shard_map/ppermute | solution.py:313
  4.7 12.2 %collective-permute-start = (bf16[256,128]{1,0:T(8,128)(2,1)}, bf16[256,128]{1,0:T(8,128)(2,1)S(1)}, u32[]{:S(2)}, u32[]{:S(2)}) collective-permute-start(bf16[256,128]{1,0:T(8,128)(2,1)} %bitcast.17), channel_id=1, source_target_pairs={{0,4},{4,8},{8,12},{12,0},{1,5},{5,9},{9,13},{13,1},{2,6},{6,10},{... | collective-permute-start | bytes 196616 | tf_op jit(solution)/shard_map/ppermute | solution.py:313
  6.3 10.6 %collective-permute-start.3 = (bf16[256,128]{1,0:T(8,128)(2,1)}, bf16[256,128]{1,0:T(8,128)(2,1)S(1)}, u32[]{:S(2)}, u32[]{:S(2)}) collective-permute-start(bf16[256,128]{1,0:T(8,128)(2,1)} %bitcast.19), channel_id=1, source_target_pairs={{0,8},{4,12},{8,0},{12,4},{1,9},{5,13},{9,1},{13,5},{2,10},{6,14},... | collective-permute-start | bytes 196616 | tf_op jit(solution)/shard_map/ppermute | solution.py:313
  6.6 10.3 %collective-permute-start.1 = (bf16[256,128]{1,0:T(8,128)(2,1)}, bf16[256,128]{1,0:T(8,128)(2,1)S(1)}, u32[]{:S(2)}, u32[]{:S(2)}) collective-permute-start(bf16[256,128]{1,0:T(8,128)(2,1)} %bitcast.20), channel_id=1, source_target_pairs={{0,4},{4,8},{8,12},{12,0},{1,5},{5,9},{9,13},{13,1},{2,6},{6,10},{... | collective-permute-start | bytes 196616 | tf_op jit(solution)/shard_map/ppermute | solution.py:313
  9.1 0.7 %copy-start.4 = (s32[4,4]{1,0:T(4,128)S(1)}, s32[4,4]{1,0:T(4,128)}, u32[]{:S(2)}) copy-start(s32[4,4]{1,0:T(4,128)} %param.11) | copy-start | bytes 196
  10.0 0.7 %copy-start.5 = (s32[8]{0:T(128)S(1)}, s32[8]{0:T(128)}, u32[]{:S(2)}) copy-start(s32[8]{0:T(128)} %param.10) | copy-start | bytes 100
  11.0 1.0 %copy-start = (bf16[256,8,128]{2,1,0:T(8,128)(2,1)S(1)}, bf16[256,8,128]{2,1,0:T(8,128)(2,1)}, u32[]{:S(2)}) copy-start(bf16[256,8,128]{2,1,0:T(8,128)(2,1)} %param.6) | copy-start | bytes 1572868
  12.0 1.0 %copy-start.1 = (bf16[256,8,128]{2,1,0:T(8,128)(2,1)S(1)}, bf16[256,8,128]{2,1,0:T(8,128)(2,1)}, u32[]{:S(2)}) copy-start(bf16[256,8,128]{2,1,0:T(8,128)(2,1)} %param.9) | copy-start | bytes 1572868
  13.0 0.8 %copy-start.2 = (bf16[256,1,128]{2,0,1:T(8,128)(2,1)S(1)}, bf16[256,1,128]{2,0,1:T(8,128)(2,1)}, u32[]{:S(2)}) copy-start(bf16[256,1,128]{2,0,1:T(8,128)(2,1)} %param.7) | copy-start | bytes 196612
  13.9 0.8 %copy-start.3 = (bf16[256,1,128]{2,0,1:T(8,128)(2,1)S(1)}, bf16[256,1,128]{2,0,1:T(8,128)(2,1)}, u32[]{:S(2)}) copy-start(bf16[256,1,128]{2,0,1:T(8,128)(2,1)} %param.8) | copy-start | bytes 196612
  18.9 22.0 %collective-permute-start.7 = (bf16[2,512,128]{2,1,0:T(8,128)(2,1)S(1)}, bf16[2,512,128]{2,1,0:T(8,128)(2,1)S(1)}, u32[]{:S(2)}, u32[]{:S(2)}) collective-permute-start(bf16[2,512,128]{2,1,0:T(8,128)(2,1)S(1)} %get-tuple-element.35), channel_id=1, source_target_pairs={{0,8},{4,12},{8,0},{12,4},{1,9},{5,13},{9,1},{13,5},{2,10},{6,14},... | collective-permute-start | bytes 786440 | tf_op jit(solution)/shard_map/ppermute | solution.py:313
  24.0 16.9 %collective-permute-start.8 = (bf16[1,4,64,256]{3,2,1,0:T(8,128)(2,1)S(1)}, bf16[1,4,64,256]{3,2,1,0:T(8,128)(2,1)S(1)}, u32[]{:S(2)}, u32[]{:S(2)}) collective-permute-start(bf16[1,4,64,256]{3,2,1,0:T(8,128)(2,1)S(1)} %get-tuple-element.38), channel_id=1, source_target_pairs={{0,4},{4,0},{8,12},{12,8},{1,5},{5,1},{9,13},{13,9},{2,6},{6,2},{1... | collective-permute-start | bytes 393224 | tf_op jit(solution)/shard_map/ppermute | solution.py:342
  25.8 18.0 %collective-permute-start.6 = (bf16[1,4,64,256]{3,2,1,0:T(8,128)(2,1)S(1)}, bf16[1,4,64,256]{3,2,1,0:T(8,128)(2,1)S(1)}, u32[]{:S(2)}, u32[]{:S(2)}) collective-permute-start(bf16[1,4,64,256]{3,2,1,0:T(8,128)(2,1)S(1)} %get-tuple-element.34), channel_id=1, source_target_pairs={{0,4},{4,0},{8,12},{12,8},{1,5},{5,1},{9,13},{13,9},{2,6},{6,2},{1... | collective-permute-start | bytes 393224 | tf_op jit(solution)/shard_map/ppermute | solution.py:342
  26.1 17.8 %collective-permute-start.4 = (bf16[2,512,128]{2,1,0:T(8,128)(2,1)S(1)}, bf16[2,512,128]{2,1,0:T(8,128)(2,1)S(1)}, u32[]{:S(2)}, u32[]{:S(2)}) collective-permute-start(bf16[2,512,128]{2,1,0:T(8,128)(2,1)S(1)} %get-tuple-element.31), channel_id=1, source_target_pairs={{0,4},{4,8},{8,12},{12,0},{1,5},{5,9},{9,13},{13,1},{2,6},{6,10},{... | collective-permute-start | bytes 786440 | tf_op jit(solution)/shard_map/ppermute | solution.py:313
  27.9 22.9 %collective-permute-start.5 = (bf16[2,512,128]{2,1,0:T(8,128)(2,1)S(1)}, bf16[2,512,128]{2,1,0:T(8,128)(2,1)S(1)}, u32[]{:S(2)}, u32[]{:S(2)}) collective-permute-start(bf16[2,512,128]{2,1,0:T(8,128)(2,1)S(1)} %get-tuple-element.32), channel_id=1, source_target_pairs={{0,12},{4,0},{8,4},{12,8},{1,13},{5,1},{9,5},{13,9},{2,14},{6,2},{... | collective-permute-start | bytes 786440 | tf_op jit(solution)/shard_map/ppermute | solution.py:313
  42.3 8.5 %collective-permute-start.9 = (bf16[1,4,64,256]{3,2,1,0:T(8,128)(2,1)S(1)}, bf16[1,4,64,256]{3,2,1,0:T(8,128)(2,1)S(1)}, u32[]{:S(2)}, u32[]{:S(2)}) collective-permute-start(bf16[1,4,64,256]{3,2,1,0:T(8,128)(2,1)S(1)} %get-tuple-element.39), channel_id=1, source_target_pairs={{0,8},{4,12},{8,0},{12,4},{1,9},{5,13},{9,1},{13,5},{2,10},{6,14},... | collective-permute-start | bytes 393224 | tf_op jit(solution)/shard_map/ppermute | solution.py:342

commit v4 on v3

--- a/solution.py
+++ b/solution.py
@@ -9,7 +9,6 @@
 MASKED = -1e30
 LOG2_E = 1.4426950408889634
 VMEM_LIMIT = 32 * 1024 * 1024
-EARLY = False
 
 
 def dot(a, b, contract):
@@ -73,16 +72,14 @@
 
 
 def fill_window(plan, refs, k_win, v_win):
-    rows, width = plan.rows, plan.width
-    k_win[pl.ds((plan.back + 1) * rows, rows), :] = refs[0][0]
-    v_win[pl.ds((plan.back + 1) * rows, rows), :] = refs[0][1]
-    for i in range(1, (len(refs) + 1) // 2):
+    rows = plan.rows
+    for i, ref in enumerate(refs):
         place = plan.back + 1 - i if i <= plan.back else plan.back + 2
-        k_win[pl.ds(place * rows, rows), :] = refs[2 * i - 1][...]
-        v_win[pl.ds(place * rows, rows), :] = refs[2 * i][...]
-    if len(refs) > 2 * plan.back + 1:
-        k_win[pl.ds(0, rows), :] = jnp.zeros((rows, width), k_win.dtype)
-        v_win[pl.ds(0, rows), :] = jnp.zeros((rows, width), v_win.dtype)
+        k_win[pl.ds(place * rows, rows), :] = ref[pl.ds(0, rows), :]
+        v_win[pl.ds(place * rows, rows), :] = ref[pl.ds(rows, rows), :]
+    if len(refs) > plan.back + 1:
+        k_win[pl.ds(0, rows), :] = jnp.zeros((rows, plan.width), k_win.dtype)
+        v_win[pl.ds(0, rows), :] = jnp.zeros((rows, plan.width), v_win.dtype)
 
 
 def attend_at(plan, meta, loader, slot, q, g, k_win, v_win):
@@ -95,13 +92,10 @@
     return keys_here, out
 
 
-def pack_kernel(plan, meta, q_ref, g_ref, k_ref, v_ref, *refs):
-    blocks, kv, sems, kv_sems = refs[: plan.n], refs[plan.n], refs[plan.n + 1], refs[plan.n + 2]
+def pack_kernel(plan, meta, q_ref, g_ref, *refs):
+    blocks, sems = refs[: plan.n], refs[plan.n]
     own = meta[0]
-    copies = [
-        pltpu.make_async_copy(k_ref, kv.at[0], kv_sems.at[0]),
-        pltpu.make_async_copy(v_ref, kv.at[1], kv_sems.at[1]),
-    ]
+    copies = []
     for shift, block in enumerate(blocks):
         slot = plan.slot(meta, own, lax.rem(own + shift, plan.n))
         at = pl.ds(pl.multiple_of(slot * plan.cols, plan.cols), plan.cols)
@@ -141,9 +135,9 @@
             return own < n - 1
         if item == "behind":
             return jnp.logical_and(own >= 1, own <= plan.back)
-        if EARLY and item == 1:
+        if item == 1:
             return own >= plan.back
-        if EARLY and item == n - 1:
+        if item == n - 1:
             return own == 0
         return own >= 0
 
@@ -201,14 +195,13 @@
     )(*operands)
 
 
-def pack(plan, meta, q, g, k, v):
+def pack(plan, meta, q, g):
     out_shape = [jax.ShapeDtypeStruct((2, plan.cols, plan.width), jnp.bfloat16)] * plan.n
-    out_shape.append(jax.ShapeDtypeStruct((2, plan.rows, plan.width), jnp.bfloat16))
+    q, g = (pltpu.with_memory_space_constraint(x, pltpu.HBM) for x in (q, g))
     return kernel_call(
-        functools.partial(pack_kernel, plan), "pack", (meta, q, g, k, v), [pltpu.SMEM] + [pl.ANY] * 4, out_shape,
-        [pltpu.SemaphoreType.DMA((plan.n, 2)), pltpu.SemaphoreType.DMA((2,))],
+        functools.partial(pack_kernel, plan), "pack", (meta, q, g), [pltpu.SMEM] + [pl.ANY] * 2, out_shape,
+        [pltpu.SemaphoreType.DMA((plan.n, 2))],
         out_specs=[spec_of(pltpu.VMEM)] * len(out_shape),
-        cost_estimate=pl.CostEstimate(flops=0, bytes_accessed=1024, transcendentals=0),
     )
 
 
@@ -257,9 +250,9 @@
         else:
             source = lax.rem(own - item + n, n)
             here = own >= 0
-            if EARLY and item == 1:
+            if item == 1:
                 here = source >= plan.back
-            if EARLY and item == n - 1:
+            if item == n - 1:
                 here = own == n - 1
         to = pl.ds(pl.multiple_of(source * cols, cols), cols)
         return here, [
@@ -309,14 +302,13 @@
     rows, heads, width = query.shape
     plan = Plan(n, rows, heads, width, doc_lengths.shape[0])
 
-    def passed(array, by):
-        return lax.ppermute(array, "ctx", [(i, (i + by) % n) for i in range(n)])
-
-    k = keys.reshape(rows, width)
-    v = values.reshape(rows, width)
-    kv_list = []
-    for i in range(1, plan.back + 1):
-        kv_list += [passed(k, i), passed(v, i)]
+    def passed(array, by, sources=range(n)):
+        return lax.ppermute(array, "ctx", [(i, (i + by) % n) for i in sources])
+
+    kv = jnp.concatenate([keys.reshape(rows, width), values.reshape(rows, width)])
+    kv_back = [passed(kv, i, range(n - i)) for i in range(1, plan.back + 1)]
+    kv_ahead = passed(kv, -1, range(1, n))
+
     owners = jnp.arange(n, dtype=jnp.int32)
     match = block_owner[:, None, :] == owners[None, :, None]
     table = jnp.sum(jnp.where(match, owners, 0), axis=2)
@@ -324,18 +316,23 @@
         [own.reshape(1).astype(jnp.int32), jnp.cumsum(doc_lengths).astype(jnp.int32), table.reshape(-1)]
     )
 
-    blocks = pack(plan, meta, query.reshape(rows * heads, width), output_gradient.reshape(rows * heads, width), k, v)
-    kv_list = [blocks[n], *kv_list]
+    blocks = pack(plan, meta, query.reshape(rows * heads, width), output_gradient.reshape(rows * heads, width))
+    from_ahead = passed(blocks[n - 1], -1, range(1, n))
+    from_behind = passed(blocks[1], 1, range(plan.back))
+    kv_list = [kv, *kv_back]
     first = n // 2
-    items = tuple([i for i in range(1, n) if i != first] + [0])
     first_pay, first_grad = attend_first(plan, first, meta, blocks[first], kv_list)
     first_pay = passed(first_pay, first)
-    out = attend_last(plan, first, items, meta, [blocks[i] for i in items], first_grad, kv_list)
+    sent = [i for i in range(1, n) if i != first]
+    items = (*sent, 0, "ahead", "behind")
+    qg_list = [blocks[i] for i in sent] + [blocks[0], from_ahead, from_behind]
+    out = attend_last(plan, first, items, meta, qg_list, first_grad, [*kv_list, kv_ahead])
     stay = {first: first_pay}
     late = {}
     for item, pay in zip(items, out):
-        if item:
-            late[item] = passed(pay, item)
+        if item in sent:
+            sources = range(plan.back, n) if item == 1 else range(1) if item == n - 1 else range(n)
+            late[item] = passed(pay, item, sources)
         else:
             stay[item] = pay
     def across(array, bit):

time: 53.1 us -> 58.4 us (1.100)
  starting transfers between devices: 14.7 us -> 32.8 us
  waiting for transfers between devices: 19.4 us -> 10.1 us
  local copies, waits for them, and re-layouts: 5.19 us -> 0.75 us
  other arithmetic: 0.4 us -> 1.29 us
    ppermute x7 -> x8, starting transfers between devices: 12.5 us -> 24.8 us  [passed(): return lax.ppermute(array, 'ctx', [(i, (i + by) % n) for i in sources])]
    ppermute x3, waiting for transfers between devices: 12.5 us -> 4.32 us  [across(): return lax.ppermute(array, 'ctx', [(i, i ^ bit) for i in range(n)])]
    ppermute x3, starting transfers between devices: 2.16 us -> 8.02 us  [across(): return lax.ppermute(array, 'ctx', [(i, i ^ bit) for i in range(n)])]
    unnamed x12 -> x4, local copies, waits for them, and re-layouts: 5.11 us -> 0.67 us
    ppermute x7 -> x8, waiting for transfers between devices: 6.89 us -> 5.8 us  [passed(): return lax.ppermute(array, 'ctx', [(i, (i + by) % n) for i in sources])]
    concatenate x0 -> x1, other arithmetic: none -> 0.89 us  [on_device(): jnp.concatenate([keys.reshape(rows, width), values.reshape(rows, width)])]
  transfers between devices with their start and end apart: 10 -> 11, of which waited for: 3 -> 4; matrix products, arithmetic and copies ran while one was open for 1% -> 1% of each run, Pallas kernels for 16% -> 18%
where the time goes in v4:
time: 58.4 us; the launch traced here: 58.1 us
  starting transfers between devices  32.8 us (56%)
  Pallas kernels  12.3 us (21%)
  waiting for transfers between devices  10.1 us (17%)
  other arithmetic  1.29 us (2%)
  between operations  0.78 us (1%)
  local copies, waits for them, and re-layouts  0.75 us (1%)
    ppermute x8, starting transfers between devices, passed(): return lax.ppermute(array, 'ctx', [(i, (i + by) % n) for i in sources])  24.8 us
    pallas_call x5, Pallas kernels, kernel_call(): pl.pallas_call(body, out_shape=out_shape, in_specs=[spec_of(space) for sp...  12.3 us
    ppermute x3, starting transfers between devices, across(): return lax.ppermute(array, 'ctx', [(i, i ^ bit) for i in range(n)])  8.02 us
    ppermute x8, waiting for transfers between devices, passed(): return lax.ppermute(array, 'ctx', [(i, (i + by) % n) for i in sources])  5.8 us
    ppermute x3, waiting for transfers between devices, across(): return lax.ppermute(array, 'ctx', [(i, i ^ bit) for i in range(n)])  4.32 us
  transfers between devices with their start and end apart: 11, of which 4 were waited for; matrix products, arithmetic and copies ran while one was open for 1% of the time, Pallas kernels for 18%

profile of v4, /device:TPU:0, one launch (start us, length us, event | category | flops | bytes accessed | tf_op | source)
XLA Modules:
  0.0 58.1 jit_solution(10794019872988571379)
XLA Ops:
  0.6 0.9 %pad_maximum_fusion.refs_0_.refs_6_ = bf16[512,128]{1,0:T(8,128)(2,1)S(1)} fusion(bf16[256,128]{1,0:T(8,128)(2,1)} %bitcast.19, bf16[256,128]{1,0:T(8,128)(2,1)} %bitcast.20), kind=kLoop, calls=%fused_computation | loop fusion | flops 262144 | bytes 262144 | tf_op jit(solution)/shard_map/concatenate | solution.py:308
  1.5 1.3 %collective-permute-start.4 = (bf16[512,128]{1,0:T(8,128)(2,1)S(1)}, bf16[512,128]{1,0:T(8,128)(2,1)S(1)}, u32[]{:S(2)}, u32[]{:S(2)}) collective-permute-start(bf16[512,128]{1,0:T(8,128)(2,1)S(1)} %pad_maximum_fusion.refs_0_.refs_6_), channel_id=1, source_target_pairs={{4,0},{8,4},{12,8},{5,1},{9,5},{13,9},{6,2},{10,6},{14,10},{7,3},{... | collective-permute-start | bytes 393224 | tf_op jit(solution)/shard_map/ppermute | solution.py:306
  2.8 7.0 %collective-permute-start.3 = (bf16[512,128]{1,0:T(8,128)(2,1)S(1)}, bf16[512,128]{1,0:T(8,128)(2,1)S(1)}, u32[]{:S(2)}, u32[]{:S(2)}) collective-permute-start(bf16[512,128]{1,0:T(8,128)(2,1)S(1)} %pad_maximum_fusion.refs_0_.refs_6_), channel_id=1, source_target_pairs={{0,8},{4,12},{1,9},{5,13},{2,10},{6,14},{3,11},{7,15},{16,24},{20,... | collective-permute-start | bytes 393224 | tf_op jit(solution)/shard_map/ppermute | solution.py:306
  9.9 3.5 %collective-permute-start.2 = (bf16[512,128]{1,0:T(8,128)(2,1)S(1)}, bf16[512,128]{1,0:T(8,128)(2,1)S(1)}, u32[]{:S(2)}, u32[]{:S(2)}) collective-permute-start(bf16[512,128]{1,0:T(8,128)(2,1)S(1)} %pad_maximum_fusion.refs_0_.refs_6_), channel_id=1, source_target_pairs={{0,4},{4,8},{8,12},{1,5},{5,9},{9,13},{2,6},{6,10},{10,14},{3,7},{... | collective-permute-start | bytes 393224 | tf_op jit(solution)/shard_map/ppermute | solution.py:306
  13.4 0.1 select_reduce_fusion
  13.5 0.1 reshape.77
  13.6 0.7 %copy-done.1 = s32[8]{0:T(128)S(1)} copy-done((s32[8]{0:T(128)S(1)}, s32[8]{0:T(128)}, u32[]{:S(2)}) %copy-start.1) | copy-done | bytes 56
  14.3 0.2 reduce-window.9
  14.4 0.1 pad_add_fusion.meta
  14.5 1.9 %pack.1 = (bf16[2,512,128]{2,1,0:T(8,128)(2,1)S(1)}, bf16[2,512,128]{2,1,0:T(8,128)(2,1)S(1)}, bf16[2,512,128]{2,1,0:T(8,128)(2,1)S(1)}, bf16[2,512,128]{2,1,0:T(8,128)(2,1)S(1)}) custom-call(s32[25]{0:T(128)S(1)} %pad_add_fusion.meta, bf16[2048,128]{1,0:T(8,128)(2,1)} %bitcast.17, bf16[2048,128]{1,0:T(8,128)(2,1)} %bitcast.18), custom_call_target="tpu_custom_call" | custom-call | tf_op jit(solution)/shard_map/pack/pallas_call | solution.py:187
  16.4 1.9 %collective-permute-start.1 = (bf16[2,512,128]{2,1,0:T(8,128)(2,1)S(1)}, bf16[2,512,128]{2,1,0:T(8,128)(2,1)S(1)}, u32[]{:S(2)}, u32[]{:S(2)}) collective-permute-start(bf16[2,512,128]{2,1,0:T(8,128)(2,1)S(1)} %get-tuple-element.26.refs_0_), channel_id=1, source_target_pairs={{0,4},{4,8},{1,5},{5,9},{2,6},{6,10},{3,7},{7,11},{16,20},{20,24},... | collective-permute-start | bytes 786440 | tf_op jit(solution)/shard_map/ppermute | solution.py:306
  18.4 1.3 %collective-permute-start = (bf16[2,512,128]{2,1,0:T(8,128)(2,1)S(1)}, bf16[2,512,128]{2,1,0:T(8,128)(2,1)S(1)}, u32[]{:S(2)}, u32[]{:S(2)}) collective-permute-start(bf16[2,512,128]{2,1,0:T(8,128)(2,1)S(1)} %get-tuple-element.27.refs_1_), channel_id=1, source_target_pairs={{4,0},{8,4},{12,8},{5,1},{9,5},{13,9},{6,2},{10,6},{14,10},{7,3},{... | collective-permute-start | bytes 786440 | tf_op jit(solution)/shard_map/ppermute | solution.py:306
  19.7 0.0 collective-permute-done.3.refs_2_.refs_8_
  19.7 0.0 collective-permute-done.2.refs_1_.refs_7_
  19.7 2.0 %attend_first.1 = (bf16[2,512,128]{2,1,0:T(8,128)(2,1)S(1)}, f32[576,256]{1,0:T(8,128)S(1)}) custom-call(s32[25]{0:T(128)S(1)} %pad_add_fusion.meta, bf16[2,512,128]{2,1,0:T(8,128)(2,1)S(1)} %get-tuple-element.29.qg, bf16[512,128]{1,0:T(8,128)(2,1)S(1)} %pad_maximum_fusion.refs_0_.refs_6_, bf16[512,128]{1,0:T(8,128)(2,1)S(1)} %collective-permute-done.2.refs_1_.refs_7_, ...), custom_call_target="tpu_custom_call" | custom-call | flops 4227858432 | bytes 1048576 | tf_op jit(solution)/shard_map/attend_first/pallas_call | solution.py:187
  21.7 2.1 %collective-permute-start.8 = (bf16[2,512,128]{2,1,0:T(8,128)(2,1)S(1)}, bf16[2,512,128]{2,1,0:T(8,128)(2,1)S(1)}, u32[]{:S(2)}, u32[]{:S(2)}) collective-permute-start(bf16[2,512,128]{2,1,0:T(8,128)(2,1)S(1)} %get-tuple-element.35), channel_id=1, source_target_pairs={{0,8},{4,12},{8,0},{12,4},{1,9},{5,13},{9,1},{13,5},{2,10},{6,14},... | collective-permute-start | bytes 786440 | tf_op jit(solution)/shard_map/ppermute | solution.py:306
  23.8 0.0 collective-permute-done.4.refs_9_
  23.8 0.0 collective-permute-done.1.refs_4_
  23.8 4.0 %collective-permute-done.refs_3_ = bf16[2,512,128]{2,1,0:T(8,128)(2,1)S(1)} collective-permute-done((bf16[2,512,128]{2,1,0:T(8,128)(2,1)S(1)}, bf16[2,512,128]{2,1,0:T(8,128)(2,1)S(1)}, u32[]{:S(2)}, u32[]{:S(2)}) %collective-permute-start) | collective-permute-done | bytes 262176 | tf_op jit(solution)/shard_map/ppermute | solution.py:306
  27.8 5.1 %attend_last.1 = (bf16[2,512,128]{2,1,0:T(8,128)(2,1)S(1)}, bf16[2,512,128]{2,1,0:T(8,128)(2,1)S(1)}, bf16[2,512,128]{2,1,0:T(8,128)(2,1)S(1)}, bf16[2,512,128]{...) custom-call(s32[25]{0:T(128)S(1)} %pad_add_fusion.meta, ...), custom_call_target="tpu_custom_call" | custom-call | flops 21139292160 | bytes 5242880 | tf_op jit(solution)/shard_map/attend_last/pallas_call | solution.py:187
  32.9 7.4 %collective-permute-start.9 = (bf16[1,4,64,256]{3,2,1,0:T(8,128)(2,1)S(1)}, bf16[1,4,64,256]{3,2,1,0:T(8,128)(2,1)S(1)}, u32[]{:S(2)}, u32[]{:S(2)}) collective-permute-start(bf16[1,4,64,256]{3,2,1,0:T(8,128)(2,1)S(1)} %get-tuple-element.40), channel_id=1, source_target_pairs={{0,4},{4,0},{8,12},{12,8},{1,5},{5,1},{9,13},{13,9},{2,6},{6,2},{1... | collective-permute-start | bytes 393224 | tf_op jit(solution)/shard_map/ppermute | solution.py:339
  40.3 0.1 collective-permute-start.7
  40.3 1.3 %collective-permute-start.5 = (bf16[2,512,128]{2,1,0:T(8,128)(2,1)S(1)}, bf16[2,512,128]{2,1,0:T(8,128)(2,1)S(1)}, u32[]{:S(2)}, u32[]{:S(2)}) collective-permute-start(bf16[2,512,128]{2,1,0:T(8,128)(2,1)S(1)} %get-tuple-element.31), channel_id=1, source_target_pairs={{8,12},{12,0},{9,13},{13,1},{10,14},{14,2},{11,15},{15,3},{24,28},... | collective-permute-start | bytes 786440 | tf_op jit(solution)/shard_map/ppermute | solution.py:306
  41.6 6.4 %collective-permute-start.6 = (bf16[2,512,128]{2,1,0:T(8,128)(2,1)S(1)}, bf16[2,512,128]{2,1,0:T(8,128)(2,1)S(1)}, u32[]{:S(2)}, u32[]{:S(2)}) collective-permute-start(bf16[2,512,128]{2,1,0:T(8,128)(2,1)S(1)} %get-tuple-element.32), channel_id=1, source_target_pairs={{0,12},{1,13},{2,14},{3,15},{16,28},{17,29},{18,30},{19,31}} | collective-permute-start | bytes 786440 | tf_op jit(solution)/shard_map/ppermute | solution.py:306
  48.0 0.0 collective-permute-done.9.refs_5_
  48.0 0.0 collective-permute-done.8.refs_0_
  48.0 1.5 %place_first.1 = (bf16[2048,128]{1,0:T(8,128)(2,1)}, bf16[2048,128]{1,0:T(8,128)(2,1)}, bf16[1,4,64,256]{3,2,1,0:T(8,128)(2,1)S(1)}) custom-call(s32[25]{0:T(128)S(1)} %pad_add_fusion.meta, bf16[2,512,128]{2,1,0:T(8,128)(2,1)S(1)} %collective-permute-done.8.refs_0_, bf16[2,512,128]{2,1,0:T(8,128)(2,1)S(1)} %get-tuple-element.36.refs_1_, ...), custom_call_target="tpu_custom_call" | custom-call | flops 16911433728 | bytes 4194304 | tf_op jit(solution)/shard_map/place_first/pallas_call | solution.py:187
  49.5 0.6 collective-permute-start.10
  50.1 0.6 %collective-permute-done.5.refs_0_ = bf16[2,512,128]{2,1,0:T(8,128)(2,1)S(1)} collective-permute-done((bf16[2,512,128]{2,1,0:T(8,128)(2,1)S(1)}, bf16[2,512,128]{2,1,0:T(8,128)(2,1)S(1)}, u32[]{:S(2)}, u32[]{:S(2)}) %collective-permute-start.5) | collective-permute-done | bytes 262176 | tf_op jit(solution)/shard_map/ppermute | solution.py:306
  50.7 1.2 %collective-permute-done.6.refs_1_ = bf16[2,512,128]{2,1,0:T(8,128)(2,1)S(1)} collective-permute-done((bf16[2,512,128]{2,1,0:T(8,128)(2,1)S(1)}, bf16[2,512,128]{2,1,0:T(8,128)(2,1)S(1)}, u32[]{:S(2)}, u32[]{:S(2)}) %collective-permute-start.6) | collective-permute-done | bytes 262176 | tf_op jit(solution)/shard_map/ppermute | solution.py:306
  51.9 4.3 %collective-permute-done.10 = bf16[1,4,64,256]{3,2,1,0:T(8,128)(2,1)S(1)} collective-permute-done((bf16[1,4,64,256]{3,2,1,0:T(8,128)(2,1)S(1)}, bf16[1,4,64,256]{3,2,1,0:T(8,128)(2,1)S(1)}, u32[]{:S(2)}, u32[]{:S(2)}) %collective-permute-start.10) | collective-permute-done | bytes 131104 | tf_op jit(solution)/shard_map/ppermute | solution.py:339
  56.2 1.9 %place_last.1 = (bf16[2048,128]{1,0:T(8,128)(2,1)}, bf16[2048,128]{1,0:T(8,128)(2,1)}, bf16[256,128]{1,0:T(8,128)(2,1)}, bf16[256,128]{1,0:T(8,128)(2,1)}) custom-call(s32[25]{0:T(128)S(1)} %pad_add_fusion.meta, bf16[2,512,128]{2,1,0:T(8,128)(2,1)S(1)} %collective-permute-done.5.refs_0_, ...), custom_call_target="tpu_custom_call", output_to_operand_aliasing={{0}: (6, {}), {1}: (7, {})} | custom-call | flops 8455716864 | bytes 2097152 | tf_op jit(solution)/shard_map/place_last/pallas_call | solution.py:187
  (4 shorter events, 0.0 us)
Async XLA Ops:
  0.6 12.7 %copy-start = (s32[4,4]{1,0:T(4,128)S(1)}, s32[4,4]{1,0:T(4,128)}, u32[]{:S(2)}) copy-start(s32[4,4]{1,0:T(4,128)} %param.11) | copy-start | bytes 196
  1.5 22.3 %collective-permute-start.4 = (bf16[512,128]{1,0:T(8,128)(2,1)S(1)}, bf16[512,128]{1,0:T(8,128)(2,1)S(1)}, u32[]{:S(2)}, u32[]{:S(2)}) collective-permute-start(bf16[512,128]{1,0:T(8,128)(2,1)S(1)} %pad_maximum_fusion.refs_0_.refs_6_), channel_id=1, source_target_pairs={{4,0},{8,4},{12,8},{5,1},{9,5},{13,9},{6,2},{10,6},{14,10},{7,3},{... | collective-permute-start | bytes 393224 | tf_op jit(solution)/shard_map/ppermute | solution.py:306
  2.8 16.8 %collective-permute-start.3 = (bf16[512,128]{1,0:T(8,128)(2,1)S(1)}, bf16[512,128]{1,0:T(8,128)(2,1)S(1)}, u32[]{:S(2)}, u32[]{:S(2)}) collective-permute-start(bf16[512,128]{1,0:T(8,128)(2,1)S(1)} %pad_maximum_fusion.refs_0_.refs_6_), channel_id=1, source_target_pairs={{0,8},{4,12},{1,9},{5,13},{2,10},{6,14},{3,11},{7,15},{16,24},{20,... | collective-permute-start | bytes 393224 | tf_op jit(solution)/shard_map/ppermute | solution.py:306
  9.9 9.8 %collective-permute-start.2 = (bf16[512,128]{1,0:T(8,128)(2,1)S(1)}, bf16[512,128]{1,0:T(8,128)(2,1)S(1)}, u32[]{:S(2)}, u32[]{:S(2)}) collective-permute-start(bf16[512,128]{1,0:T(8,128)(2,1)S(1)} %pad_maximum_fusion.refs_0_.refs_6_), channel_id=1, source_target_pairs={{0,4},{4,8},{8,12},{1,5},{5,9},{9,13},{2,6},{6,10},{10,14},{3,7},{... | collective-permute-start | bytes 393224 | tf_op jit(solution)/shard_map/ppermute | solution.py:306
  13.6 0.7 %copy-start.1 = (s32[8]{0:T(128)S(1)}, s32[8]{0:T(128)}, u32[]{:S(2)}) copy-start(s32[8]{0:T(128)} %param.10) | copy-start | bytes 100
  16.4 7.4 %collective-permute-start.1 = (bf16[2,512,128]{2,1,0:T(8,128)(2,1)S(1)}, bf16[2,512,128]{2,1,0:T(8,128)(2,1)S(1)}, u32[]{:S(2)}, u32[]{:S(2)}) collective-permute-start(bf16[2,512,128]{2,1,0:T(8,128)(2,1)S(1)} %get-tuple-element.26.refs_0_), channel_id=1, source_target_pairs={{0,4},{4,8},{1,5},{5,9},{2,6},{6,10},{3,7},{7,11},{16,20},{20,24},... | collective-permute-start | bytes 786440 | tf_op jit(solution)/shard_map/ppermute | solution.py:306
  18.4 9.4 %collective-permute-start = (bf16[2,512,128]{2,1,0:T(8,128)(2,1)S(1)}, bf16[2,512,128]{2,1,0:T(8,128)(2,1)S(1)}, u32[]{:S(2)}, u32[]{:S(2)}) collective-permute-start(bf16[2,512,128]{2,1,0:T(8,128)(2,1)S(1)} %get-tuple-element.27.refs_1_), channel_id=1, source_target_pairs={{4,0},{8,4},{12,8},{5,1},{9,5},{13,9},{6,2},{10,6},{14,10},{7,3},{... | collective-permute-start | bytes 786440 | tf_op jit(solution)/shard_map/ppermute | solution.py:306
  21.7 26.4 %collective-permute-start.8 = (bf16[2,512,128]{2,1,0:T(8,128)(2,1)S(1)}, bf16[2,512,128]{2,1,0:T(8,128)(2,1)S(1)}, u32[]{:S(2)}, u32[]{:S(2)}) collective-permute-start(bf16[2,512,128]{2,1,0:T(8,128)(2,1)S(1)} %get-tuple-element.35), channel_id=1, source_target_pairs={{0,8},{4,12},{8,0},{12,4},{1,9},{5,13},{9,1},{13,5},{2,10},{6,14},... | collective-permute-start | bytes 786440 | tf_op jit(solution)/shard_map/ppermute | solution.py:306
  32.9 15.1 %collective-permute-start.9 = (bf16[1,4,64,256]{3,2,1,0:T(8,128)(2,1)S(1)}, bf16[1,4,64,256]{3,2,1,0:T(8,128)(2,1)S(1)}, u32[]{:S(2)}, u32[]{:S(2)}) collective-permute-start(bf16[1,4,64,256]{3,2,1,0:T(8,128)(2,1)S(1)} %get-tuple-element.40), channel_id=1, source_target_pairs={{0,4},{4,0},{8,12},{12,8},{1,5},{5,1},{9,13},{13,9},{2,6},{6,2},{1... | collective-permute-start | bytes 393224 | tf_op jit(solution)/shard_map/ppermute | solution.py:339
  40.3 9.8 %collective-permute-start.7 = (bf16[1,4,64,256]{3,2,1,0:T(8,128)(2,1)S(1)}, bf16[1,4,64,256]{3,2,1,0:T(8,128)(2,1)S(1)}, u32[]{:S(2)}, u32[]{:S(2)}) collective-permute-start(bf16[1,4,64,256]{3,2,1,0:T(8,128)(2,1)S(1)} %get-tuple-element.34), channel_id=1, source_target_pairs={{0,4},{4,0},{8,12},{12,8},{1,5},{5,1},{9,13},{13,9},{2,6},{6,2},{1... | collective-permute-start | bytes 393224 | tf_op jit(solution)/shard_map/ppermute | solution.py:339
  40.3 10.3 %collective-permute-start.5 = (bf16[2,512,128]{2,1,0:T(8,128)(2,1)S(1)}, bf16[2,512,128]{2,1,0:T(8,128)(2,1)S(1)}, u32[]{:S(2)}, u32[]{:S(2)}) collective-permute-start(bf16[2,512,128]{2,1,0:T(8,128)(2,1)S(1)} %get-tuple-element.31), channel_id=1, source_target_pairs={{8,12},{12,0},{9,13},{13,1},{10,14},{14,2},{11,15},{15,3},{24,28},... | collective-permute-start | bytes 786440 | tf_op jit(solution)/shard_map/ppermute | solution.py:306
  41.6 10.2 %collective-permute-start.6 = (bf16[2,512,128]{2,1,0:T(8,128)(2,1)S(1)}, bf16[2,512,128]{2,1,0:T(8,128)(2,1)S(1)}, u32[]{:S(2)}, u32[]{:S(2)}) collective-permute-start(bf16[2,512,128]{2,1,0:T(8,128)(2,1)S(1)} %get-tuple-element.32), channel_id=1, source_target_pairs={{0,12},{1,13},{2,14},{3,15},{16,28},{17,29},{18,30},{19,31}} | collective-permute-start | bytes 786440 | tf_op jit(solution)/shard_map/ppermute | solution.py:306
  49.5 6.7 %collective-permute-start.10 = (bf16[1,4,64,256]{3,2,1,0:T(8,128)(2,1)S(1)}, bf16[1,4,64,256]{3,2,1,0:T(8,128)(2,1)S(1)}, u32[]{:S(2)}, u32[]{:S(2)}) collective-permute-start(bf16[1,4,64,256]{3,2,1,0:T(8,128)(2,1)S(1)} %get-tuple-element.41), channel_id=1, source_target_pairs={{0,8},{4,12},{8,0},{12,4},{1,9},{5,13},{9,1},{13,5},{2,10},{6,14},... | collective-permute-start | bytes 393224 | tf_op jit(solution)/shard_map/ppermute | solution.py:339

commit v5 on v4

--- a/solution.py
+++ b/solution.py
@@ -96,21 +96,21 @@
     blocks, sems = refs[: plan.n], refs[plan.n]
     own = meta[0]
     copies = []
-    for shift, block in enumerate(blocks):
-        slot = plan.slot(meta, own, lax.rem(own + shift, plan.n))
+    for apart, block in enumerate(blocks):
+        slot = plan.slot(meta, own, own ^ apart)
         at = pl.ds(pl.multiple_of(slot * plan.cols, plan.cols), plan.cols)
-        copies.append(pltpu.make_async_copy(q_ref.at[at, :], block.at[0], sems.at[shift, 0]))
-        copies.append(pltpu.make_async_copy(g_ref.at[at, :], block.at[1], sems.at[shift, 1]))
+        copies.append(pltpu.make_async_copy(q_ref.at[at, :], block.at[0], sems.at[apart, 0]))
+        copies.append(pltpu.make_async_copy(g_ref.at[at, :], block.at[1], sems.at[apart, 1]))
     for copy in copies:
         copy.start()
     for copy in copies:
         copy.wait()
 
 
-def first_kernel(plan, shift, meta, qg, *refs):
+def first_kernel(plan, apart, meta, qg, *refs):
     kv_refs, (pay_ref, grad_ref, k_win, v_win) = refs[:-4], refs[-4:]
     own = meta[0]
-    slot = plan.slot(meta, own, lax.rem(own + shift, plan.n))
+    slot = plan.slot(meta, own, own ^ apart)
     fill_window(plan, kv_refs, k_win, v_win)
     _, (attended, query_grad, key_part, value_part) = attend_at(
         plan, meta, own, slot, qg[0], qg[1], k_win, v_win
@@ -121,7 +121,7 @@
     grad_ref[:, plan.width :] = value_part
 
 
-def last_kernel(plan, first_shift, items, meta, *refs):
+def last_kernel(plan, first, items, meta, *refs):
     n, width, rows, block = plan.n, plan.width, plan.rows, plan.block
     qg_refs, refs = refs[: len(items)], refs[len(items) :]
     first_grad, refs = refs[0], refs[1:]
@@ -130,35 +130,22 @@
     step = pl.program_id(0)
     own = meta[0]
 
-    def valid(item):
-        if item == "ahead":
-            return own < n - 1
-        if item == "behind":
-            return jnp.logical_and(own >= 1, own <= plan.back)
-        if item == 1:
-            return own >= plan.back
-        if item == n - 1:
-            return own == 0
-        return own >= 0
-
     @pl.when(step == 0)
     def _():
         fill_window(plan, kv_refs, k_win, v_win)
         acc[...] = jnp.zeros_like(acc)
-        slot = plan.slot(meta, own, lax.rem(own + first_shift, n))
+        slot = plan.slot(meta, own, own ^ first)
         keys_here = pl.ds(pl.multiple_of(rows + slot * block, block), plan.reach + block)
         acc[keys_here, :] = first_grad[...]
 
     for i, item in enumerate(items):
 
-        @pl.when(jnp.logical_and(step == i, valid(item)))
+        @pl.when(step == i)
         def _():
-            loader = own + {"ahead": 1, "behind": -1}.get(item, 0)
-            owner = own if item in ("ahead", "behind") else lax.rem(own + item, n)
-            slot = plan.slot(meta, loader, owner)
+            slot = plan.slot(meta, own, own ^ item)
             qg = qg_refs[i]
             keys_here, (attended, query_grad, key_part, value_part) = attend_at(
-                plan, meta, loader, slot, qg[0], qg[1], k_win, v_win
+                plan, meta, own, slot, qg[0], qg[1], k_win, v_win
             )
             acc[keys_here, :width] = acc[keys_here, :width] + key_part
             acc[keys_here, width:] = acc[keys_here, width:] + value_part
@@ -205,7 +192,7 @@
     )
 
 
-def attend_first(plan, shift, meta, qg, kv_list):
+def attend_first(plan, apart, meta, qg, kv_list):
     window = pltpu.VMEM((plan.window_ranges * plan.rows, plan.width), jnp.bfloat16)
     out_shape = [
         jax.ShapeDtypeStruct((2, plan.cols, plan.width), jnp.bfloat16),
@@ -213,13 +200,13 @@
     ]
     operands = (meta, qg, *kv_list)
     return kernel_call(
-        functools.partial(first_kernel, plan, shift), "attend_first", operands,
+        functools.partial(first_kernel, plan, apart), "attend_first", operands,
         [pltpu.SMEM] + [pltpu.VMEM] * (len(operands) - 1), out_shape, [window, window],
         out_specs=[spec_of(pltpu.VMEM)] * 2, cost_estimate=plan.cost(1),
     )
 
 
-def attend_last(plan, first_shift, items, meta, qg_list, first_grad, kv_list):
+def attend_last(plan, first, items, meta, qg_list, first_grad, kv_list):
     n = plan.n
     window = pltpu.VMEM((plan.window_ranges * plan.rows, plan.width), jnp.bfloat16)
     grads = (n // 4, n, plan.block, 2 * plan.width)
@@ -227,70 +214,56 @@
     out_shape += [jax.ShapeDtypeStruct(grads, jnp.bfloat16 if apart % 2 else jnp.float32) for apart in range(4)]
     operands = (meta, *qg_list, first_grad, *kv_list)
     return kernel_call(
-        functools.partial(last_kernel, plan, first_shift, items), "attend_last", operands,
+        functools.partial(last_kernel, plan, first, items), "attend_last", operands,
         [pltpu.SMEM] + [pltpu.VMEM] * (len(operands) - 1), out_shape,
         [window, window, pltpu.VMEM(((n + 1) * plan.rows, 2 * plan.width), jnp.float32)],
         out_specs=[spec_of(pltpu.VMEM)] * len(out_shape), cost_estimate=plan.cost(len(items)), grid=(len(items),),
     )
 
 
-def place_kernel(plan, items, final, meta, *refs):
-    n, cols, width, own = plan.n, plan.cols, plan.width, meta[0]
-    pay_refs, refs = dict(zip(items, refs[: len(items)])), refs[len(items) :]
+def place_kernel(plan, items, final, *refs):
+    n, cols, width = plan.n, plan.cols, plan.width
+    own = lax.axis_index("ctx")
+    pay_refs, refs = refs[: len(items)], refs[len(items) :]
     if final:
-        grads, (_, _, attended, query_grad, key_grad, value_grad, sems) = refs[:-7], refs[-7:]
+        grads, (_, _, attended, query_grad, key_grad, value_grad, sums, sems, sum_sems) = refs[:-9], refs[-9:]
     else:
         grads, (attended, query_grad, send, sems) = refs[:-4], refs[-4:]
-
-    def copies(i, item):
-        if item == "ahead":
-            source, here = own + 1, own < n - 1
-        elif item == "behind":
-            source, here = own - 1, jnp.logical_and(own >= 1, own <= plan.back)
-        else:
-            source = lax.rem(own - item + n, n)
-            here = own >= 0
-            if item == 1:
-                here = source >= plan.back
-            if item == n - 1:
-                here = own == n - 1
-        to = pl.ds(pl.multiple_of(source * cols, cols), cols)
-        return here, [
-            pltpu.make_async_copy(pay_refs[item].at[0], attended.at[to, :], sems.at[i, 0]),
-            pltpu.make_async_copy(pay_refs[item].at[1], query_grad.at[to, :], sems.at[i, 1]),
-        ]
-
-    def each(act):
-        for i, item in enumerate(items):
-            here, pair = copies(i, item)
-
-            @pl.when(here)
-            def _():
-                for copy in pair:
-                    act(copy)
-
-    each(lambda copy: copy.start())
-    total = sum(grad[...].astype(jnp.float32) for grad in grads)
-    if not final:
-        send[...] = total.astype(jnp.bfloat16)
+    copies = []
+    for i, item in enumerate(items):
+        to = pl.ds(pl.multiple_of((own ^ item) * cols, cols), cols)
+        copies.append(pltpu.make_async_copy(pay_refs[i].at[0], attended.at[to, :], sems.at[i, 0]))
+        copies.append(pltpu.make_async_copy(pay_refs[i].at[1], query_grad.at[to, :], sems.at[i, 1]))
+    for copy in copies:
+        copy.start()
+    total = sum(grad[...].astype(jnp.float32) for grad in grads).astype(jnp.bfloat16)
     if final:
-        key_grad[...] = total[:, :width].astype(jnp.bfloat16)
-        value_grad[...] = total[:, width:].astype(jnp.bfloat16)
-    each(lambda copy: copy.wait())
-
-
-def place(plan, meta, payloads, grads=(), filled=()):
+        sums[0] = total[:, :width]
+        sums[1] = total[:, width:]
+        for i, ref in enumerate((key_grad, value_grad)):
+            copies.append(pltpu.make_async_copy(sums.at[i], ref, sum_sems.at[i]))
+            copies[-1].start()
+    else:
+        send[...] = total
+    for copy in copies:
+        copy.wait()
+
+
+def place(plan, payloads, grads, filled=()):
     items = tuple(payloads)
     big = jax.ShapeDtypeStruct((plan.rows * plan.heads, plan.width), jnp.bfloat16)
     small = jax.ShapeDtypeStruct((plan.rows, plan.width), jnp.bfloat16)
     final = len(filled) > 0
-    at = 1 + len(items) + len(grads)
+    at = len(items) + len(grads)
+    scratch = [pltpu.SemaphoreType.DMA((len(items), 2))]
+    if final:
+        scratch = [pltpu.VMEM((2, plan.rows, plan.width), jnp.bfloat16), *scratch, pltpu.SemaphoreType.DMA((2,))]
     return kernel_call(
         functools.partial(place_kernel, plan, items, final), "place_last" if final else "place_first",
-        (meta, *payloads.values(), *grads, *filled),
-        [pltpu.SMEM] + [pl.ANY] * len(items) + [pltpu.VMEM] * len(grads) + [pl.ANY] * len(filled),
-        [big, big] + ([small, small] if final else [jax.ShapeDtypeStruct(grads[0].shape, jnp.bfloat16)]), [pltpu.SemaphoreType.DMA((len(items), 2))],
-        out_specs=[spec_of(pl.ANY)] * 2 + [spec_of(pltpu.VMEM)] * (1 + final),
+        (*payloads.values(), *grads, *filled),
+        [pl.ANY] * len(items) + [pltpu.VMEM] * len(grads) + [pl.ANY] * len(filled),
+        [big, big] + ([small, small] if final else [jax.ShapeDtypeStruct(grads[0].shape, jnp.bfloat16)]), scratch,
+        out_specs=[spec_of(pl.ANY)] * 2 + [spec_of(pl.ANY)] * 2 if final else [spec_of(pl.ANY)] * 2 + [spec_of(pltpu.VMEM)],
         input_output_aliases={at: 0, at + 1: 1} if final else {},
         cost_estimate=plan.cost(len(items)),
     )
@@ -302,12 +275,14 @@
     rows, heads, width = query.shape
     plan = Plan(n, rows, heads, width, doc_lengths.shape[0])
 
-    def passed(array, by, sources=range(n)):
-        return lax.ppermute(array, "ctx", [(i, (i + by) % n) for i in sources])
+    def permuted(array, pairs):
+        return lax.ppermute(array, "ctx", pairs)
+
+    def across(array, bits):
+        return permuted(array, [(i, i ^ bits) for i in range(n)])
 
     kv = jnp.concatenate([keys.reshape(rows, width), values.reshape(rows, width)])
-    kv_back = [passed(kv, i, range(n - i)) for i in range(1, plan.back + 1)]
-    kv_ahead = passed(kv, -1, range(1, n))
+    kv_list = [kv] + [permuted(kv, [(i, i + by) for i in range(n - by)]) for by in range(1, plan.back + 1)]
 
     owners = jnp.arange(n, dtype=jnp.int32)
     match = block_owner[:, None, :] == owners[None, :, None]
@@ -317,31 +292,18 @@
     )
 
     blocks = pack(plan, meta, query.reshape(rows * heads, width), output_gradient.reshape(rows * heads, width))
-    from_ahead = passed(blocks[n - 1], -1, range(1, n))
-    from_behind = passed(blocks[1], 1, range(plan.back))
-    kv_list = [kv, *kv_back]
     first = n // 2
     first_pay, first_grad = attend_first(plan, first, meta, blocks[first], kv_list)
-    first_pay = passed(first_pay, first)
-    sent = [i for i in range(1, n) if i != first]
-    items = (*sent, 0, "ahead", "behind")
-    qg_list = [blocks[i] for i in sent] + [blocks[0], from_ahead, from_behind]
-    out = attend_last(plan, first, items, meta, qg_list, first_grad, [*kv_list, kv_ahead])
-    stay = {first: first_pay}
-    late = {}
-    for item, pay in zip(items, out):
-        if item in sent:
-            sources = range(plan.back, n) if item == 1 else range(1) if item == n - 1 else range(n)
-            late[item] = passed(pay, item, sources)
-        else:
-            stay[item] = pay
-    def across(array, bit):
-        return lax.ppermute(array, "ctx", [(i, i ^ bit) for i in range(n)])
-
+    stay = {first: across(first_pay, first)}
+    sent = [x for x in range(n - 1, 0, -1) if x != first]
+    items = (*sent, 0)
+    out = attend_last(plan, first, items, meta, [blocks[x] for x in items], first_grad, kv_list)
+    late = {x: across(pay, x) for x, pay in zip(sent, out)}
+    stay[0] = out[len(sent)]
     keep, to_keep, pass_on, to_pass_on = out[len(items) :]
     pass_on = (pass_on, across(to_pass_on, 1))
     terms = (keep, across(to_keep, 1))
-    attended, query_grad, send = place(plan, meta, stay, pass_on)
+    attended, query_grad, send = place(plan, stay, pass_on)
     terms += (across(send, 2),)
     bit = 4
     while bit < n:
@@ -349,7 +311,7 @@
         terms = (total[0::2], across(total[1::2].astype(jnp.bfloat16), bit))
         bit *= 2
     terms = [term.reshape(rows, 2 * width) for term in terms]
-    attended, query_grad, key_grad, value_grad = place(plan, meta, late, terms, (attended, query_grad))
+    attended, query_grad, key_grad, value_grad = place(plan, late, terms, (attended, query_grad))
     return (
         attended.reshape(rows, heads, width),
         query_grad.reshape(rows, heads, width),

time: 58.4 us -> 54.2 us (0.928)
  starting transfers between devices: 32.8 us -> 17.4 us
  waiting for transfers between devices: 10.1 us -> 23.3 us
  Pallas kernels: 12.3 us -> 10.4 us
    ppermute x11 -> x8, starting transfers between devices: 32.8 us -> 17.4 us  [permuted(): return lax.ppermute(array, 'ctx', pairs)]
    ppermute x11 -> x8, waiting for transfers between devices: 10.1 us -> 23.3 us  [permuted(): return lax.ppermute(array, 'ctx', pairs)]
    pallas_call x5, Pallas kernels: 12.3 us -> 10.4 us  [kernel_call(): pl.pallas_call(body, out_shape=out_shape, in_specs=[spec_of(space) for sp...]
  transfers between devices with their start and end apart: 11 -> 8, of which waited for: 4 -> 3; matrix products, arithmetic and copies ran while one was open for 1% -> 1% of each run, Pallas kernels for 18% -> 14%
where the time goes in v5:
time: 54.2 us; the launch traced here: 54 us
  waiting for transfers between devices  23.3 us (43%)
  starting transfers between devices  17.4 us (32%)
  Pallas kernels  10.4 us (19%)
  other arithmetic  1.29 us (2%)
  local copies, waits for them, and re-layouts  0.75 us (1%)
  between operations  0.74 us (1%)
    ppermute x8, waiting for transfers between devices, permuted(): return lax.ppermute(array, 'ctx', pairs)  23.3 us
    ppermute x8, starting transfers between devices, permuted(): return lax.ppermute(array, 'ctx', pairs)  17.4 us
    pallas_call x5, Pallas kernels, kernel_call(): pl.pallas_call(body, out_shape=out_shape, in_specs=[spec_of(space) for sp...  10.4 us
  transfers between devices with their start and end apart: 8, of which 3 were waited for; matrix products, arithmetic and copies ran while one was open for 1% of the time, Pallas kernels for 14%

profile of v5, /device:TPU:0, one launch (start us, length us, event | category | flops | bytes accessed | tf_op | source)
XLA Modules:
  0.0 54.0 jit_solution(13825546510288880090)
XLA Ops:
  0.6 0.0 copy-start
  0.6 0.9 %pad_maximum_fusion.refs_0_.refs_4_ = bf16[512,128]{1,0:T(8,128)(2,1)S(1)} fusion(bf16[256,128]{1,0:T(8,128)(2,1)} %bitcast.19, bf16[256,128]{1,0:T(8,128)(2,1)} %bitcast.20), kind=kLoop, calls=%fused_computation | loop fusion | flops 262144 | bytes 262144 | tf_op jit(solution)/shard_map/concatenate | solution.py:284
  1.5 5.9 %collective-permute-start.1 = (bf16[512,128]{1,0:T(8,128)(2,1)S(1)}, bf16[512,128]{1,0:T(8,128)(2,1)S(1)}, u32[]{:S(2)}, u32[]{:S(2)}) collective-permute-start(bf16[512,128]{1,0:T(8,128)(2,1)S(1)} %pad_maximum_fusion.refs_0_.refs_4_), channel_id=1, source_target_pairs={{0,8},{4,12},{1,9},{5,13},{2,10},{6,14},{3,11},{7,15},{16,24},{20,... | collective-permute-start | bytes 393224 | tf_op jit(solution)/shard_map/ppermute | solution.py:279
  7.5 3.5 %collective-permute-start = (bf16[512,128]{1,0:T(8,128)(2,1)S(1)}, bf16[512,128]{1,0:T(8,128)(2,1)S(1)}, u32[]{:S(2)}, u32[]{:S(2)}) collective-permute-start(bf16[512,128]{1,0:T(8,128)(2,1)S(1)} %pad_maximum_fusion.refs_0_.refs_4_), channel_id=1, source_target_pairs={{0,4},{4,8},{8,12},{1,5},{5,9},{9,13},{2,6},{6,10},{10,14},{3,7},{... | collective-permute-start | bytes 393224 | tf_op jit(solution)/shard_map/ppermute | solution.py:279
  11.0 0.0 copy-done
  11.0 0.1 select_reduce_fusion
  11.1 0.1 reshape.77
  11.2 0.0 copy-start.1
  11.2 0.7 %copy-done.1 = s32[8]{0:T(128)S(1)} copy-done((s32[8]{0:T(128)S(1)}, s32[8]{0:T(128)}, u32[]{:S(2)}) %copy-start.1) | copy-done | bytes 56
  11.9 0.2 reduce-window.9
  12.1 0.1 pad_add_fusion.meta
  12.1 1.9 %pack.1 = (bf16[2,512,128]{2,1,0:T(8,128)(2,1)S(1)}, bf16[2,512,128]{2,1,0:T(8,128)(2,1)S(1)}, bf16[2,512,128]{2,1,0:T(8,128)(2,1)S(1)}, bf16[2,512,128]{2,1,0:T(8,128)(2,1)S(1)}) custom-call(s32[25]{0:T(128)S(1)} %pad_add_fusion.meta, bf16[2048,128]{1,0:T(8,128)(2,1)} %bitcast.17, bf16[2048,128]{1,0:T(8,128)(2,1)} %bitcast.18), custom_call_target="tpu_custom_call" | custom-call | tf_op jit(solution)/shard_map/pack/pallas_call | solution.py:174
  14.1 0.0 collective-permute-done.1.refs_2_.refs_6_
  14.1 0.0 collective-permute-done.refs_1_.refs_5_
  14.1 2.0 %attend_first.1 = (bf16[2,512,128]{2,1,0:T(8,128)(2,1)S(1)}, f32[576,256]{1,0:T(8,128)S(1)}) custom-call(s32[25]{0:T(128)S(1)} %pad_add_fusion.meta, bf16[2,512,128]{2,1,0:T(8,128)(2,1)S(1)} %get-tuple-element.27.qg, bf16[512,128]{1,0:T(8,128)(2,1)S(1)} %pad_maximum_fusion.refs_0_.refs_4_, bf16[512,128]{1,0:T(8,128)(2,1)S(1)} %collective-permute-done.refs_1_.refs_5_, ...), custom_call_target="tpu_custom_call" | custom-call | flops 4227858432 | bytes 1048576 | tf_op jit(solution)/shard_map/attend_first/pallas_call | solution.py:174
  16.0 5.2 %collective-permute-start.5 = (bf16[2,512,128]{2,1,0:T(8,128)(2,1)S(1)}, bf16[2,512,128]{2,1,0:T(8,128)(2,1)S(1)}, u32[]{:S(2)}, u32[]{:S(2)}) collective-permute-start(bf16[2,512,128]{2,1,0:T(8,128)(2,1)S(1)} %get-tuple-element.33), channel_id=1, source_target_pairs={{0,8},{4,12},{8,0},{12,4},{1,9},{5,13},{9,1},{13,5},{2,10},{6,14},... | collective-permute-start | bytes 786440 | tf_op jit(solution)/shard_map/ppermute | solution.py:279
  21.3 4.8 %attend_last.1 = (bf16[2,512,128]{2,1,0:T(8,128)(2,1)S(1)}, bf16[2,512,128]{2,1,0:T(8,128)(2,1)S(1)}, bf16[2,512,128]{2,1,0:T(8,128)(2,1)S(1)}, f32[1,4,64,256]{...) custom-call(s32[25]{0:T(128)S(1)} %pad_add_fusion.meta, ...), custom_call_target="tpu_custom_call" | custom-call | flops 12683575296 | bytes 3145728 | tf_op jit(solution)/shard_map/attend_last/pallas_call | solution.py:174
  26.1 0.1 collective-permute-start.6
  26.2 2.0 %collective-permute-start.4 = (bf16[1,4,64,256]{3,2,1,0:T(8,128)(2,1)S(1)}, bf16[1,4,64,256]{3,2,1,0:T(8,128)(2,1)S(1)}, u32[]{:S(2)}, u32[]{:S(2)}) collective-permute-start(bf16[1,4,64,256]{3,2,1,0:T(8,128)(2,1)S(1)} %get-tuple-element.32), channel_id=1, source_target_pairs={{0,4},{4,0},{8,12},{12,8},{1,5},{5,1},{9,13},{13,9},{2,6},{6,2},{1... | collective-permute-start | bytes 393224 | tf_op jit(solution)/shard_map/ppermute | solution.py:279
  28.2 0.4 collective-permute-start.2
  28.7 0.2 collective-permute-start.3
  28.8 13.1 %collective-permute-done.6.refs_3_ = bf16[1,4,64,256]{3,2,1,0:T(8,128)(2,1)S(1)} collective-permute-done((bf16[1,4,64,256]{3,2,1,0:T(8,128)(2,1)S(1)}, bf16[1,4,64,256]{3,2,1,0:T(8,128)(2,1)S(1)}, u32[]{:S(2)}, u32[]{:S(2)}) %collective-permute-start.6) | collective-permute-done | bytes 131104 | tf_op jit(solution)/shard_map/ppermute | solution.py:279
  41.9 0.0 collective-permute-done.5.refs_0_
  41.9 0.8 %place_first.1 = (bf16[2048,128]{1,0:T(8,128)(2,1)}, bf16[2048,128]{1,0:T(8,128)(2,1)}, bf16[1,4,64,256]{3,2,1,0:T(8,128)(2,1)S(1)}) custom-call(bf16[2,512,128]{2,1,0:T(8,128)(2,1)S(1)} %collective-permute-done.5.refs_0_, bf16[2,512,128]{2,1,0:T(8,128)(2,1)S(1)} %get-tuple-element.34.refs_1_, f32[1,4,64,256]{3,2,1,0:T(8,128)S(1)} %get-tuple-element.35.refs_2_, ...), custom_call_target="tpu_custom_call" | custom-call | flops 8455716864 | bytes 2097152 | tf_op jit(solution)/shard_map/place_first/pallas_call | solution.py:174
  42.8 0.1 collective-permute-start.7
  42.8 1.9 %collective-permute-done.4 = bf16[1,4,64,256]{3,2,1,0:T(8,128)(2,1)S(1)} collective-permute-done((bf16[1,4,64,256]{3,2,1,0:T(8,128)(2,1)S(1)}, bf16[1,4,64,256]{3,2,1,0:T(8,128)(2,1)S(1)}, u32[]{:S(2)}, u32[]{:S(2)}) %collective-permute-start.4) | collective-permute-done | bytes 131104 | tf_op jit(solution)/shard_map/ppermute | solution.py:279
  44.7 0.0 collective-permute-done.2.refs_0_
  44.7 8.3 %collective-permute-done.3.refs_1_ = bf16[2,512,128]{2,1,0:T(8,128)(2,1)S(1)} collective-permute-done((bf16[2,512,128]{2,1,0:T(8,128)(2,1)S(1)}, bf16[2,512,128]{2,1,0:T(8,128)(2,1)S(1)}, u32[]{:S(2)}, u32[]{:S(2)}) %collective-permute-start.3) | collective-permute-done | bytes 262176 | tf_op jit(solution)/shard_map/ppermute | solution.py:279
  53.1 0.0 collective-permute-done.7
  53.1 0.9 %place_last.1 = (bf16[2048,128]{1,0:T(8,128)(2,1)}, bf16[2048,128]{1,0:T(8,128)(2,1)}, bf16[256,128]{1,0:T(8,128)(2,1)}, bf16[256,128]{1,0:T(8,128)(2,1)}) custom-call(bf16[2,512,128]{2,1,0:T(8,128)(2,1)S(1)} %collective-permute-done.2.refs_0_, ...), custom_call_target="tpu_custom_call", output_to_operand_aliasing={{0}: (5, {}), {1}: (6, {})} | custom-call | flops 8455716864 | bytes 2097152 | tf_op jit(solution)/shard_map/place_last/pallas_call | solution.py:174
Async XLA Ops:
  0.6 10.4 %copy-start = (s32[4,4]{1,0:T(4,128)S(1)}, s32[4,4]{1,0:T(4,128)}, u32[]{:S(2)}) copy-start(s32[4,4]{1,0:T(4,128)} %param.11) | copy-start | bytes 196
  1.5 12.5 %collective-permute-start.1 = (bf16[512,128]{1,0:T(8,128)(2,1)S(1)}, bf16[512,128]{1,0:T(8,128)(2,1)S(1)}, u32[]{:S(2)}, u32[]{:S(2)}) collective-permute-start(bf16[512,128]{1,0:T(8,128)(2,1)S(1)} %pad_maximum_fusion.refs_0_.refs_4_), channel_id=1, source_target_pairs={{0,8},{4,12},{1,9},{5,13},{2,10},{6,14},{3,11},{7,15},{16,24},{20,... | collective-permute-start | bytes 393224 | tf_op jit(solution)/shard_map/ppermute | solution.py:279
  7.5 6.6 %collective-permute-start = (bf16[512,128]{1,0:T(8,128)(2,1)S(1)}, bf16[512,128]{1,0:T(8,128)(2,1)S(1)}, u32[]{:S(2)}, u32[]{:S(2)}) collective-permute-start(bf16[512,128]{1,0:T(8,128)(2,1)S(1)} %pad_maximum_fusion.refs_0_.refs_4_), channel_id=1, source_target_pairs={{0,4},{4,8},{8,12},{1,5},{5,9},{9,13},{2,6},{6,10},{10,14},{3,7},{... | collective-permute-start | bytes 393224 | tf_op jit(solution)/shard_map/ppermute | solution.py:279
  11.2 0.7 %copy-start.1 = (s32[8]{0:T(128)S(1)}, s32[8]{0:T(128)}, u32[]{:S(2)}) copy-start(s32[8]{0:T(128)} %param.10) | copy-start | bytes 100
  16.0 25.9 %collective-permute-start.5 = (bf16[2,512,128]{2,1,0:T(8,128)(2,1)S(1)}, bf16[2,512,128]{2,1,0:T(8,128)(2,1)S(1)}, u32[]{:S(2)}, u32[]{:S(2)}) collective-permute-start(bf16[2,512,128]{2,1,0:T(8,128)(2,1)S(1)} %get-tuple-element.33), channel_id=1, source_target_pairs={{0,8},{4,12},{8,0},{12,4},{1,9},{5,13},{9,1},{13,5},{2,10},{6,14},... | collective-permute-start | bytes 786440 | tf_op jit(solution)/shard_map/ppermute | solution.py:279
  26.1 15.8 %collective-permute-start.6 = (bf16[1,4,64,256]{3,2,1,0:T(8,128)(2,1)S(1)}, bf16[1,4,64,256]{3,2,1,0:T(8,128)(2,1)S(1)}, u32[]{:S(2)}, u32[]{:S(2)}) collective-permute-start(bf16[1,4,64,256]{3,2,1,0:T(8,128)(2,1)S(1)} %get-tuple-element.36), channel_id=1, source_target_pairs={{0,4},{4,0},{8,12},{12,8},{1,5},{5,1},{9,13},{13,9},{2,6},{6,2},{1... | collective-permute-start | bytes 393224 | tf_op jit(solution)/shard_map/ppermute | solution.py:279
  26.2 18.5 %collective-permute-start.4 = (bf16[1,4,64,256]{3,2,1,0:T(8,128)(2,1)S(1)}, bf16[1,4,64,256]{3,2,1,0:T(8,128)(2,1)S(1)}, u32[]{:S(2)}, u32[]{:S(2)}) collective-permute-start(bf16[1,4,64,256]{3,2,1,0:T(8,128)(2,1)S(1)} %get-tuple-element.32), channel_id=1, source_target_pairs={{0,4},{4,0},{8,12},{12,8},{1,5},{5,1},{9,13},{13,9},{2,6},{6,2},{1... | collective-permute-start | bytes 393224 | tf_op jit(solution)/shard_map/ppermute | solution.py:279
  28.2 16.5 %collective-permute-start.2 = (bf16[2,512,128]{2,1,0:T(8,128)(2,1)S(1)}, bf16[2,512,128]{2,1,0:T(8,128)(2,1)S(1)}, u32[]{:S(2)}, u32[]{:S(2)}) collective-permute-start(bf16[2,512,128]{2,1,0:T(8,128)(2,1)S(1)} %get-tuple-element.29), channel_id=1, source_target_pairs={{0,12},{4,8},{8,4},{12,0},{1,13},{5,9},{9,5},{13,1},{2,14},{6,10},... | collective-permute-start | bytes 786440 | tf_op jit(solution)/shard_map/ppermute | solution.py:279
  28.7 24.4 %collective-permute-start.3 = (bf16[2,512,128]{2,1,0:T(8,128)(2,1)S(1)}, bf16[2,512,128]{2,1,0:T(8,128)(2,1)S(1)}, u32[]{:S(2)}, u32[]{:S(2)}) collective-permute-start(bf16[2,512,128]{2,1,0:T(8,128)(2,1)S(1)} %get-tuple-element.30), channel_id=1, source_target_pairs={{0,4},{4,0},{8,12},{12,8},{1,5},{5,1},{9,13},{13,9},{2,6},{6,2},{1... | collective-permute-start | bytes 786440 | tf_op jit(solution)/shard_map/ppermute | solution.py:279
  42.8 10.3 %collective-permute-start.7 = (bf16[1,4,64,256]{3,2,1,0:T(8,128)(2,1)S(1)}, bf16[1,4,64,256]{3,2,1,0:T(8,128)(2,1)S(1)}, u32[]{:S(2)}, u32[]{:S(2)}) collective-permute-start(bf16[1,4,64,256]{3,2,1,0:T(8,128)(2,1)S(1)} %get-tuple-element.37), channel_id=1, source_target_pairs={{0,8},{4,12},{8,0},{12,4},{1,9},{5,13},{9,1},{13,5},{2,10},{6,14},... | collective-permute-start | bytes 393224 | tf_op jit(solution)/shard_map/ppermute | solution.py:279

commit v6 on v5

--- a/solution.py
+++ b/solution.py
@@ -56,6 +56,13 @@
         self.reach = self.back * rows
         self.scale = width ** (-0.5)
         self.window_ranges = self.back + 3
+        self.grad_rows = 2 * (self.back + 1) * self.block
+
+    def is_middle(self, own):
+        return jnp.logical_or(own == self.back - 1, own == self.back)
+
+    def first_range(self, own):
+        return jnp.maximum(own - self.back, 0)
 
     def ends(self, meta):
         return [meta[1 + i] for i in range(self.ndocs)]
@@ -71,15 +78,19 @@
         )
 
 
-def fill_window(plan, refs, k_win, v_win):
+def fill_window(plan, own, refs, k_win, v_win):
     rows = plan.rows
+    empty = jnp.zeros((rows, plan.width), k_win.dtype)
+    for place in (0, 1):
+        k_win[pl.ds(place * rows, rows), :] = empty
+        v_win[pl.ds(place * rows, rows), :] = empty
     for i, ref in enumerate(refs):
-        place = plan.back + 1 - i if i <= plan.back else plan.back + 2
-        k_win[pl.ds(place * rows, rows), :] = ref[pl.ds(0, rows), :]
-        v_win[pl.ds(place * rows, rows), :] = ref[pl.ds(rows, rows), :]
-    if len(refs) > plan.back + 1:
-        k_win[pl.ds(0, rows), :] = jnp.zeros((rows, plan.width), k_win.dtype)
-        v_win[pl.ds(0, rows), :] = jnp.zeros((rows, plan.width), v_win.dtype)
+        place = plan.back + 1 - i
+        if i == plan.back:
+            place = jnp.where(own == plan.back - 1, plan.back + 2, place)
+        to = pl.ds(pl.multiple_of(place * rows, rows), rows)
+        k_win[to, :] = ref[pl.ds(0, rows), :]
+        v_win[to, :] = ref[pl.ds(rows, rows), :]
 
 
 def attend_at(plan, meta, loader, slot, q, g, k_win, v_win):
@@ -111,28 +122,30 @@
     kv_refs, (pay_ref, grad_ref, k_win, v_win) = refs[:-4], refs[-4:]
     own = meta[0]
     slot = plan.slot(meta, own, own ^ apart)
-    fill_window(plan, kv_refs, k_win, v_win)
+    fill_window(plan, own, kv_refs, k_win, v_win)
     _, (attended, query_grad, key_part, value_part) = attend_at(
         plan, meta, own, slot, qg[0], qg[1], k_win, v_win
     )
-    pay_ref[0] = attended
-    pay_ref[1] = query_grad
+    pay_ref[pl.ds(0, plan.cols), :] = attended
+    pay_ref[pl.ds(plan.cols, plan.cols), :] = query_grad
     grad_ref[:, : plan.width] = key_part
     grad_ref[:, plan.width :] = value_part
 
 
 def last_kernel(plan, first, items, meta, *refs):
     n, width, rows, block = plan.n, plan.width, plan.rows, plan.block
-    qg_refs, refs = refs[: len(items)], refs[len(items) :]
-    first_grad, refs = refs[0], refs[1:]
-    kv_refs, refs = refs[: -(len(items) + 7)], refs[-(len(items) + 7) :]
-    pay_refs, grad_refs, (k_win, v_win, acc) = refs[: len(items)], refs[len(items) : -3], refs[-3:]
+    qg_refs, (got_ref, first_grad), refs = refs[: len(items)], refs[len(items) : len(items) + 2], refs[len(items) + 2 :]
+    outs = len(items) + n - 1 + 4
+    kv_refs, refs = refs[:-outs], refs[-outs:]
+    pay_refs, grad_refs, (k_win, v_win, acc, qg) = refs[: len(items)], refs[len(items) : -4], refs[-4:]
+    grad_refs = [grad_refs[0], pay_refs[items.index(1)].at[pl.ds(2 * plan.cols, plan.grad_rows), :], *grad_refs[1:]]
     step = pl.program_id(0)
     own = meta[0]
+    middle = plan.is_middle(own)
 
     @pl.when(step == 0)
     def _():
-        fill_window(plan, kv_refs, k_win, v_win)
+        fill_window(plan, own, kv_refs, k_win, v_win)
         acc[...] = jnp.zeros_like(acc)
         slot = plan.slot(meta, own, own ^ first)
         keys_here = pl.ds(pl.multiple_of(rows + slot * block, block), plan.reach + block)
@@ -142,28 +155,43 @@
 
         @pl.when(step == i)
         def _():
-            slot = plan.slot(meta, own, own ^ item)
-            qg = qg_refs[i]
+            loader, owner, source = own, own ^ item, qg_refs[i]
+            if item == n - 1:
+                loader, owner, source = jnp.where(middle, owner, own), jnp.where(middle, own, owner), qg
+
+                @pl.when(middle)
+                def _():
+                    qg[...] = got_ref[...]
+
+                @pl.when(jnp.logical_not(middle))
+                def _():
+                    qg[...] = qg_refs[i][...]
+
+            slot = plan.slot(meta, loader, owner)
             keys_here, (attended, query_grad, key_part, value_part) = attend_at(
-                plan, meta, own, slot, qg[0], qg[1], k_win, v_win
+                plan, meta, loader, slot, source[0], source[1], k_win, v_win
             )
             acc[keys_here, :width] = acc[keys_here, :width] + key_part
             acc[keys_here, width:] = acc[keys_here, width:] + value_part
-            pay_refs[i][0] = attended
-            pay_refs[i][1] = query_grad
+            pay_refs[i][pl.ds(0, plan.cols), :] = attended
+            pay_refs[i][pl.ds(plan.cols, plan.cols), :] = query_grad
 
     @pl.when(step == len(items) - 1)
     def _():
-        def of_range(key_range, carry):
-            at = (lax.rem(key_range - own + plan.back + n, n) + 1) * rows
+        def of_range(i, carry):
+            key_range = plan.first_range(own) + i
+            at = (key_range - own + plan.back + 1) * rows
             for apart in range(n):
                 slot = plan.slot(meta, key_range, own ^ apart)
                 part = acc[pl.ds(pl.multiple_of(at + slot * block, block), block), :]
-                to = grad_refs[apart % 4]
-                to[apart // 4, key_range] = part.astype(to.dtype)
+                part = part.astype(grad_refs[apart].dtype)
+                to = pl.multiple_of(i * block, block)
+                grad_refs[apart][pl.ds(to, block), :] = part[:, :width]
+                to = pl.multiple_of(i * block + plan.grad_rows // 2, block)
+                grad_refs[apart][pl.ds(to, block), :] = part[:, width:]
             return carry
 
-        lax.fori_loop(0, n, of_range, 0)
+        lax.fori_loop(0, plan.back + 1, of_range, 0)
 
 
 def spec_of(space):
@@ -195,7 +223,7 @@
 def attend_first(plan, apart, meta, qg, kv_list):
     window = pltpu.VMEM((plan.window_ranges * plan.rows, plan.width), jnp.bfloat16)
     out_shape = [
-        jax.ShapeDtypeStruct((2, plan.cols, plan.width), jnp.bfloat16),
+        jax.ShapeDtypeStruct((2 * plan.cols, plan.width), jnp.bfloat16),
         jax.ShapeDtypeStruct((plan.reach + plan.block, 2 * plan.width), jnp.float32),
     ]
     operands = (meta, qg, *kv_list)
@@ -206,66 +234,98 @@
     )
 
 
-def attend_last(plan, first, items, meta, qg_list, first_grad, kv_list):
+def attend_last(plan, first, items, meta, qg_list, got, first_grad, kv_list):
     n = plan.n
-    window = pltpu.VMEM((plan.window_ranges * plan.rows, plan.width), jnp.bfloat16)
-    grads = (n // 4, n, plan.block, 2 * plan.width)
-    out_shape = [jax.ShapeDtypeStruct((2, plan.cols, plan.width), jnp.bfloat16)] * len(items)
-    out_shape += [jax.ShapeDtypeStruct(grads, jnp.bfloat16 if apart % 2 else jnp.float32) for apart in range(4)]
-    operands = (meta, *qg_list, first_grad, *kv_list)
+    rows = plan.window_ranges * plan.rows
+    window = pltpu.VMEM((rows, plan.width), jnp.bfloat16)
+    sum_rows = (2 * plan.back + 2) * plan.rows
+    block = (2, plan.cols, plan.width)
+    pay_rows = [2 * plan.cols + (plan.grad_rows if x == 1 else 0) for x in items]
+    out_shape = [jax.ShapeDtypeStruct((size, plan.width), jnp.bfloat16) for size in pay_rows]
+    grads = (plan.grad_rows, plan.width)
+    out_shape += [jax.ShapeDtypeStruct(grads, jnp.bfloat16 if i else jnp.float32) for i in range(n - 1)]
+    operands = (meta, *qg_list, got, first_grad, *kv_list)
     return kernel_call(
         functools.partial(last_kernel, plan, first, items), "attend_last", operands,
         [pltpu.SMEM] + [pltpu.VMEM] * (len(operands) - 1), out_shape,
-        [window, window, pltpu.VMEM(((n + 1) * plan.rows, 2 * plan.width), jnp.float32)],
+        [window, window, pltpu.VMEM((sum_rows, 2 * plan.width), jnp.float32), pltpu.VMEM(block, jnp.bfloat16)],
         out_specs=[spec_of(pltpu.VMEM)] * len(out_shape), cost_estimate=plan.cost(len(items)), grid=(len(items),),
     )
 
 
-def place_kernel(plan, items, final, *refs):
+def place_kernel(plan, late, *refs):
     n, cols, width = plan.n, plan.cols, plan.width
     own = lax.axis_index("ctx")
-    pay_refs, refs = refs[: len(items)], refs[len(items) :]
-    if final:
-        grads, (_, _, attended, query_grad, key_grad, value_grad, sums, sems, sum_sems) = refs[:-9], refs[-9:]
+    middle = plan.is_middle(own)
+
+    def copies(i, x, pay, attended, query_grad, sems):
+        to = pl.ds(pl.multiple_of((own ^ x) * cols, cols), cols)
+        return [
+            pltpu.make_async_copy(pay.at[pl.ds(0, cols), :], attended.at[to, :], sems.at[i, 0]),
+            pltpu.make_async_copy(pay.at[pl.ds(cols, cols), :], query_grad.at[to, :], sems.at[i, 1]),
+        ]
+
+    if late:
+        pay_refs, grad_refs, refs = refs[: len(late)], refs[len(late) : len(late) + n - 1], refs[len(late) + n - 1 :]
+        grad_refs = [grad_refs[0], pay_refs[late.index(1)].at[pl.ds(2 * cols, plan.grad_rows), :], *grad_refs[1:]]
+        _, _, attended, query_grad, key_grad, value_grad, acc, sums, sems, sum_sems = refs
+        items = late
     else:
-        grads, (attended, query_grad, send, sems) = refs[:-4], refs[-4:]
-    copies = []
-    for i, item in enumerate(items):
-        to = pl.ds(pl.multiple_of((own ^ item) * cols, cols), cols)
-        copies.append(pltpu.make_async_copy(pay_refs[i].at[0], attended.at[to, :], sems.at[i, 0]))
-        copies.append(pltpu.make_async_copy(pay_refs[i].at[1], query_grad.at[to, :], sems.at[i, 1]))
-    for copy in copies:
-        copy.start()
-    total = sum(grad[...].astype(jnp.float32) for grad in grads).astype(jnp.bfloat16)
-    if final:
-        sums[0] = total[:, :width]
-        sums[1] = total[:, width:]
+        items = (n // 2, 0, n - 1)
+        pay_refs, (attended, query_grad, sems) = refs[:3], refs[3:]
+
+    def each(act):
+        for i, item in enumerate(items):
+            here = middle if not late else jnp.logical_not(middle)
+
+            def run():
+                for copy in copies(i, item, pay_refs[i], attended, query_grad, sems):
+                    act(copy)
+
+            if item == n - 1:
+                pl.when(here)(run)
+            else:
+                run()
+
+    each(lambda copy: copy.start())
+    if late:
+        acc[...] = jnp.zeros_like(acc)
+        for x in range(n):
+            for i in range(plan.back + 1):
+                at = (plan.first_range(own ^ x) + i) * plan.block
+                to = pl.ds(pl.multiple_of(at, plan.block), plan.block)
+                for part in range(2):
+                    term = grad_refs[x][pl.ds(i * plan.block + part * plan.grad_rows // 2, plan.block), :]
+                    acc[part, to, :] = acc[part, to, :] + term.astype(jnp.float32)
         for i, ref in enumerate((key_grad, value_grad)):
-            copies.append(pltpu.make_async_copy(sums.at[i], ref, sum_sems.at[i]))
-            copies[-1].start()
-    else:
-        send[...] = total
-    for copy in copies:
-        copy.wait()
-
-
-def place(plan, payloads, grads, filled=()):
-    items = tuple(payloads)
+            sums[i] = acc[i].astype(jnp.bfloat16)
+            pltpu.make_async_copy(sums.at[i], ref, sum_sems.at[i]).start()
+        for i, ref in enumerate((key_grad, value_grad)):
+            pltpu.make_async_copy(sums.at[i], ref, sum_sems.at[i]).wait()
+    each(lambda copy: copy.wait())
+
+
+def place(plan, payloads, late=(), grads=(), filled=()):
     big = jax.ShapeDtypeStruct((plan.rows * plan.heads, plan.width), jnp.bfloat16)
     small = jax.ShapeDtypeStruct((plan.rows, plan.width), jnp.bfloat16)
-    final = len(filled) > 0
-    at = len(items) + len(grads)
-    scratch = [pltpu.SemaphoreType.DMA((len(items), 2))]
-    if final:
-        scratch = [pltpu.VMEM((2, plan.rows, plan.width), jnp.bfloat16), *scratch, pltpu.SemaphoreType.DMA((2,))]
+    out_shape, scratch = [big, big], [pltpu.SemaphoreType.DMA((len(payloads), 2))]
+    if late:
+        out_shape += [small, small]
+        scratch = [
+            pltpu.VMEM((2, plan.rows, plan.width), jnp.float32),
+            pltpu.VMEM((2, plan.rows, plan.width), jnp.bfloat16),
+            *scratch,
+            pltpu.SemaphoreType.DMA((2,)),
+        ]
+    at = len(payloads) + len(grads)
     return kernel_call(
-        functools.partial(place_kernel, plan, items, final), "place_last" if final else "place_first",
-        (*payloads.values(), *grads, *filled),
-        [pl.ANY] * len(items) + [pltpu.VMEM] * len(grads) + [pl.ANY] * len(filled),
-        [big, big] + ([small, small] if final else [jax.ShapeDtypeStruct(grads[0].shape, jnp.bfloat16)]), scratch,
-        out_specs=[spec_of(pl.ANY)] * 2 + [spec_of(pl.ANY)] * 2 if final else [spec_of(pl.ANY)] * 2 + [spec_of(pltpu.VMEM)],
-        input_output_aliases={at: 0, at + 1: 1} if final else {},
-        cost_estimate=plan.cost(len(items)),
+        functools.partial(place_kernel, plan, late), "place_last" if late else "place_first",
+        (*payloads, *grads, *filled),
+        [pltpu.VMEM] * (len(payloads) + len(grads)) + [pl.ANY] * len(filled),
+        out_shape, scratch,
+        out_specs=[spec_of(pl.ANY)] * len(out_shape),
+        input_output_aliases={at: 0, at + 1: 1} if late else {},
+        cost_estimate=plan.cost(len(payloads)),
     )
 
 
@@ -282,7 +342,10 @@
         return permuted(array, [(i, i ^ bits) for i in range(n)])
 
     kv = jnp.concatenate([keys.reshape(rows, width), values.reshape(rows, width)])
-    kv_list = [kv] + [permuted(kv, [(i, i + by) for i in range(n - by)]) for by in range(1, plan.back + 1)]
+    kv_list = [kv]
+    for by in range(1, plan.back + 1):
+        pairs = [(i, i + by) for i in range(n - by)]
+        kv_list.append(permuted(kv, pairs + [(n // 2, n // 2 - 1)] if by == plan.back else pairs))
 
     owners = jnp.arange(n, dtype=jnp.int32)
     match = block_owner[:, None, :] == owners[None, :, None]
@@ -292,26 +355,20 @@
     )
 
     blocks = pack(plan, meta, query.reshape(rows * heads, width), output_gradient.reshape(rows * heads, width))
+    middle = (n // 2 - 1, n // 2)
+    got = permuted(blocks[n - 1], [middle, middle[::-1]])
     first = n // 2
     first_pay, first_grad = attend_first(plan, first, meta, blocks[first], kv_list)
-    stay = {first: across(first_pay, first)}
-    sent = [x for x in range(n - 1, 0, -1) if x != first]
+    first_pay = across(first_pay, first)
+    sent = tuple(x for x in range(n - 1, 0, -1) if x != first)
     items = (*sent, 0)
-    out = attend_last(plan, first, items, meta, [blocks[x] for x in items], first_grad, kv_list)
-    late = {x: across(pay, x) for x, pay in zip(sent, out)}
-    stay[0] = out[len(sent)]
-    keep, to_keep, pass_on, to_pass_on = out[len(items) :]
-    pass_on = (pass_on, across(to_pass_on, 1))
-    terms = (keep, across(to_keep, 1))
-    attended, query_grad, send = place(plan, stay, pass_on)
-    terms += (across(send, 2),)
-    bit = 4
-    while bit < n:
-        total = sum(term.astype(jnp.float32) for term in terms)
-        terms = (total[0::2], across(total[1::2].astype(jnp.bfloat16), bit))
-        bit *= 2
-    terms = [term.reshape(rows, 2 * width) for term in terms]
-    attended, query_grad, key_grad, value_grad = place(plan, late, terms, (attended, query_grad))
+    out = attend_last(plan, first, items, meta, [blocks[x] for x in items], got, first_grad, kv_list)
+    pays, grads = out[: len(items)], out[len(items) :]
+    late = [permuted(pays[0], [(i, i ^ (n - 1)) for i in range(n) if i not in middle])]
+    late += [across(pay, x) for x, pay in zip(sent[1:], pays[1:])]
+    grads = [across(grad, i + 1) if i else grad for i, grad in enumerate(grads)]
+    filled = place(plan, [first_pay, pays[-1], pays[0]])
+    attended, query_grad, key_grad, value_grad = place(plan, late, sent, grads, filled)
     return (
         attended.reshape(rows, heads, width),
         query_grad.reshape(rows, heads, width),

time: 54.2 us -> 54.2 us (level)
  waiting for transfers between devices: 23.3 us -> 10.8 us
  starting transfers between devices: 17.4 us -> 29.8 us
    ppermute x8, waiting for transfers between devices: 23.3 us -> 10.8 us  [permuted(): return lax.ppermute(array, 'ctx', pairs)]
    ppermute x8, starting transfers between devices: 17.4 us -> 29.8 us  [permuted(): return lax.ppermute(array, 'ctx', pairs)]
  transfers between devices with their start and end apart: 8 -> 8, of which waited for: 3 -> 3; matrix products, arithmetic and copies ran while one was open for 1% -> 1% of each run, Pallas kernels for 14% -> 18%
where the time goes in v6:
time: 54.2 us; the launch traced here: 53.9 us
  starting transfers between devices  29.8 us (55%)
  waiting for transfers between devices  10.8 us (20%)
  Pallas kernels  10.5 us (19%)
  other arithmetic  1.29 us (2%)
  between operations  0.76 us (1%)
  local copies, waits for them, and re-layouts  0.75 us (1%)
    ppermute x8, starting transfers between devices, permuted(): return lax.ppermute(array, 'ctx', pairs)  29.8 us
    ppermute x8, waiting for transfers between devices, permuted(): return lax.ppermute(array, 'ctx', pairs)  10.8 us
    pallas_call x5, Pallas kernels, kernel_call(): pl.pallas_call(body, out_shape=out_shape, in_specs=[spec_of(space) for sp...  10.5 us
  transfers between devices with their start and end apart: 8, of which 3 were waited for; matrix products, arithmetic and copies ran while one was open for 1% of the time, Pallas kernels for 18%

profile of v6, /device:TPU:0, one launch (start us, length us, event | category | flops | bytes accessed | tf_op | source)
XLA Modules:
  0.0 53.9 jit_solution(11665300122044100920)
XLA Ops:
  0.6 0.0 copy-start
  0.6 0.9 %pad_maximum_fusion.refs_0_.refs_5_ = bf16[512,128]{1,0:T(8,128)(2,1)S(1)} fusion(bf16[256,128]{1,0:T(8,128)(2,1)} %bitcast.13, bf16[256,128]{1,0:T(8,128)(2,1)} %bitcast.14), kind=kLoop, calls=%fused_computation | loop fusion | flops 262144 | bytes 262144 | tf_op jit(solution)/shard_map/concatenate | solution.py:344
  1.5 5.9 %collective-permute-start.2 = (bf16[512,128]{1,0:T(8,128)(2,1)S(1)}, bf16[512,128]{1,0:T(8,128)(2,1)S(1)}, u32[]{:S(2)}, u32[]{:S(2)}) collective-permute-start(bf16[512,128]{1,0:T(8,128)(2,1)S(1)} %pad_maximum_fusion.refs_0_.refs_5_), channel_id=1, source_target_pairs={{0,8},{4,12},{8,4},{1,9},{5,13},{9,5},{2,10},{6,14},{10,6},{3,11},... | collective-permute-start | bytes 393224 | tf_op jit(solution)/shard_map/ppermute | solution.py:339
  7.5 3.5 %collective-permute-start.1 = (bf16[512,128]{1,0:T(8,128)(2,1)S(1)}, bf16[512,128]{1,0:T(8,128)(2,1)S(1)}, u32[]{:S(2)}, u32[]{:S(2)}) collective-permute-start(bf16[512,128]{1,0:T(8,128)(2,1)S(1)} %pad_maximum_fusion.refs_0_.refs_5_), channel_id=1, source_target_pairs={{0,4},{4,8},{8,12},{1,5},{5,9},{9,13},{2,6},{6,10},{10,14},{3,7},{... | collective-permute-start | bytes 393224 | tf_op jit(solution)/shard_map/ppermute | solution.py:339
  11.0 0.0 copy-done
  11.0 0.1 select_reduce_fusion
  11.1 0.1 reshape.68
  11.2 0.0 copy-start.1
  11.2 0.7 %copy-done.1 = s32[8]{0:T(128)S(1)} copy-done((s32[8]{0:T(128)S(1)}, s32[8]{0:T(128)}, u32[]{:S(2)}) %copy-start.1) | copy-done | bytes 56
  11.9 0.2 reduce-window.9
  12.1 0.1 pad_add_fusion.meta
  12.1 1.9 %pack.1 = (bf16[2,512,128]{2,1,0:T(8,128)(2,1)S(1)}, bf16[2,512,128]{2,1,0:T(8,128)(2,1)S(1)}, bf16[2,512,128]{2,1,0:T(8,128)(2,1)S(1)}, bf16[2,512,128]{2,1,0:T(8,128)(2,1)S(1)}) custom-call(s32[25]{0:T(128)S(1)} %pad_add_fusion.meta, bf16[2048,128]{1,0:T(8,128)(2,1)} %bitcast.11, bf16[2048,128]{1,0:T(8,128)(2,1)} %bitcast.12), custom_call_target="tpu_custom_call" | custom-call | tf_op jit(solution)/shard_map/pack/pallas_call | solution.py:202
  14.1 0.7 %collective-permute-start = (bf16[2,512,128]{2,1,0:T(8,128)(2,1)S(1)}, bf16[2,512,128]{2,1,0:T(8,128)(2,1)S(1)}, u32[]{:S(2)}, u32[]{:S(2)}) collective-permute-start(bf16[2,512,128]{2,1,0:T(8,128)(2,1)S(1)} %get-tuple-element.22.refs_0_), channel_id=1, source_target_pairs={{4,8},{8,4},{5,9},{9,5},{6,10},{10,6},{7,11},{11,7},{20,24},{24,20... | collective-permute-start | bytes 786440 | tf_op jit(solution)/shard_map/ppermute | solution.py:339
  14.7 0.0 collective-permute-done.2.refs_2_.refs_7_
  14.8 0.0 collective-permute-done.1.refs_1_.refs_6_
  14.8 2.0 %attend_first.1 = (bf16[1024,128]{1,0:T(8,128)(2,1)S(1)}, f32[576,256]{1,0:T(8,128)S(1)}) custom-call(s32[25]{0:T(128)S(1)} %pad_add_fusion.meta, bf16[2,512,128]{2,1,0:T(8,128)(2,1)S(1)} %get-tuple-element.25.qg, bf16[512,128]{1,0:T(8,128)(2,1)S(1)} %pad_maximum_fusion.refs_0_.refs_5_, bf16[512,128]{1,0:T(8,128)(2,1)S(1)} %collective-permute-done.1.refs_1_.refs_6_, ...), custom_call_target="tpu_custom_call" | custom-call | flops 4227858432 | bytes 1048576 | tf_op jit(solution)/shard_map/attend_first/pallas_call | solution.py:202
  16.8 4.6 %collective-permute-start.7 = (bf16[1024,128]{1,0:T(8,128)(2,1)S(1)}, bf16[1024,128]{1,0:T(8,128)(2,1)S(1)}, u32[]{:S(2)}, u32[]{:S(2)}) collective-permute-start(bf16[1024,128]{1,0:T(8,128)(2,1)S(1)} %get-tuple-element.32), channel_id=1, source_target_pairs={{0,8},{4,12},{8,0},{12,4},{1,9},{5,13},{9,1},{13,5},{2,10},{6,14},... | collective-permute-start | bytes 786440 | tf_op jit(solution)/shard_map/ppermute | solution.py:339
  21.4 0.0 collective-permute-done.refs_3_
  21.4 4.9 %attend_last.1 = (bf16[1024,128]{1,0:T(8,128)(2,1)S(1)}, bf16[1408,128]{1,0:T(8,128)(2,1)S(1)}, bf16[1024,128]{1,0:T(8,128)(2,1)S(1)}, f32[384,128]{1,0:T(8,128)...) custom-call(s32[25]{0:T(128)S(1)} %pad_add_fusion.meta, ...), custom_call_target="tpu_custom_call" | custom-call | flops 12683575296 | bytes 3145728 | tf_op jit(solution)/shard_map/attend_last/pallas_call | solution.py:202
  26.3 9.2 %collective-permute-start.5 = (bf16[384,128]{1,0:T(8,128)(2,1)S(1)}, bf16[384,128]{1,0:T(8,128)(2,1)S(1)}, u32[]{:S(2)}, u32[]{:S(2)}) collective-permute-start(bf16[384,128]{1,0:T(8,128)(2,1)S(1)} %get-tuple-element.30), channel_id=1, source_target_pairs={{0,8},{4,12},{8,0},{12,4},{1,9},{5,13},{9,1},{13,5},{2,10},{6,14},... | collective-permute-start | bytes 294920 | tf_op jit(solution)/shard_map/ppermute | solution.py:339
  35.6 2.0 %collective-permute-start.6 = (bf16[384,128]{1,0:T(8,128)(2,1)S(1)}, bf16[384,128]{1,0:T(8,128)(2,1)S(1)}, u32[]{:S(2)}, u32[]{:S(2)}) collective-permute-start(bf16[384,128]{1,0:T(8,128)(2,1)S(1)} %get-tuple-element.31), channel_id=1, source_target_pairs={{0,12},{4,8},{8,4},{12,0},{1,13},{5,9},{9,5},{13,1},{2,14},{6,10},... | collective-permute-start | bytes 294920 | tf_op jit(solution)/shard_map/ppermute | solution.py:339
  37.6 3.7 %collective-permute-start.3 = (bf16[1024,128]{1,0:T(8,128)(2,1)S(1)}, bf16[1024,128]{1,0:T(8,128)(2,1)S(1)}, u32[]{:S(2)}, u32[]{:S(2)}) collective-permute-start(bf16[1024,128]{1,0:T(8,128)(2,1)S(1)} %get-tuple-element.27.refs_2_), channel_id=1, source_target_pairs={{0,12},{12,0},{1,13},{13,1},{2,14},{14,2},{3,15},{15,3},{16,28},{2... | collective-permute-start | bytes 786440 | tf_op jit(solution)/shard_map/ppermute | solution.py:339
  41.3 0.1 collective-permute-start.4
  41.4 0.0 collective-permute-done.7.refs_0_
  41.4 0.8 %place_first.1 = (bf16[2048,128]{1,0:T(8,128)(2,1)}, bf16[2048,128]{1,0:T(8,128)(2,1)}) custom-call(bf16[1024,128]{1,0:T(8,128)(2,1)S(1)} %collective-permute-done.7.refs_0_, bf16[1024,128]{1,0:T(8,128)(2,1)S(1)} %get-tuple-element.33.refs_1_, bf16[1024,128]{1,0:T(8,128)(2,1)S(1)} %get-tuple-element.27.refs_2_), custom_call_target="tpu_custom_call" | custom-call | flops 12683575296 | bytes 3145728 | tf_op jit(solution)/shard_map/place_first/pallas_call | solution.py:202
  42.3 2.2 %collective-permute-done.5.refs_3_ = bf16[384,128]{1,0:T(8,128)(2,1)S(1)} collective-permute-done((bf16[384,128]{1,0:T(8,128)(2,1)S(1)}, bf16[384,128]{1,0:T(8,128)(2,1)S(1)}, u32[]{:S(2)}, u32[]{:S(2)}) %collective-permute-start.5) | collective-permute-done | bytes 98336 | tf_op jit(solution)/shard_map/ppermute | solution.py:339
  44.5 0.0 collective-permute-done.6.refs_4_
  44.5 3.4 %collective-permute-done.3.refs_0_ = bf16[1024,128]{1,0:T(8,128)(2,1)S(1)} collective-permute-done((bf16[1024,128]{1,0:T(8,128)(2,1)S(1)}, bf16[1024,128]{1,0:T(8,128)(2,1)S(1)}, u32[]{:S(2)}, u32[]{:S(2)}) %collective-permute-start.3) | collective-permute-done | bytes 262176 | tf_op jit(solution)/shard_map/ppermute | solution.py:339
  47.8 5.2 %collective-permute-done.4.refs_1_ = bf16[1408,128]{1,0:T(8,128)(2,1)S(1)} collective-permute-done((bf16[1408,128]{1,0:T(8,128)(2,1)S(1)}, bf16[1408,128]{1,0:T(8,128)(2,1)S(1)}, u32[]{:S(2)}, u32[]{:S(2)}) %collective-permute-start.4) | collective-permute-done | bytes 360480 | tf_op jit(solution)/shard_map/ppermute | solution.py:339
  53.0 0.9 %place_last.1 = (bf16[2048,128]{1,0:T(8,128)(2,1)}, bf16[2048,128]{1,0:T(8,128)(2,1)}, bf16[256,128]{1,0:T(8,128)(2,1)}, bf16[256,128]{1,0:T(8,128)(2,1)}) custom-call(bf16[1024,128]{1,0:T(8,128)(2,1)S(1)} %collective-permute-done.3.refs_0_, bf16[1408,128]{1,0:T(8,128)(2,1)S(1)} %collective-permute-done.4.refs_1_, ...), custom_call_target="tpu_custom_call", output_to_operand_aliasing={{0}: (5, {}), {1}: (6, {})} | custom-call | flops 8455716864 | bytes 2097152 | tf_op jit(solution)/shard_map/place_last/pallas_call | solution.py:202
Async XLA Ops:
  0.6 10.3 %copy-start = (s32[4,4]{1,0:T(4,128)S(1)}, s32[4,4]{1,0:T(4,128)}, u32[]{:S(2)}) copy-start(s32[4,4]{1,0:T(4,128)} %param.11) | copy-start | bytes 196
  1.5 13.2 %collective-permute-start.2 = (bf16[512,128]{1,0:T(8,128)(2,1)S(1)}, bf16[512,128]{1,0:T(8,128)(2,1)S(1)}, u32[]{:S(2)}, u32[]{:S(2)}) collective-permute-start(bf16[512,128]{1,0:T(8,128)(2,1)S(1)} %pad_maximum_fusion.refs_0_.refs_5_), channel_id=1, source_target_pairs={{0,8},{4,12},{8,4},{1,9},{5,13},{9,5},{2,10},{6,14},{10,6},{3,11},... | collective-permute-start | bytes 393224 | tf_op jit(solution)/shard_map/ppermute | solution.py:339
  7.5 7.3 %collective-permute-start.1 = (bf16[512,128]{1,0:T(8,128)(2,1)S(1)}, bf16[512,128]{1,0:T(8,128)(2,1)S(1)}, u32[]{:S(2)}, u32[]{:S(2)}) collective-permute-start(bf16[512,128]{1,0:T(8,128)(2,1)S(1)} %pad_maximum_fusion.refs_0_.refs_5_), channel_id=1, source_target_pairs={{0,4},{4,8},{8,12},{1,5},{5,9},{9,13},{2,6},{6,10},{10,14},{3,7},{... | collective-permute-start | bytes 393224 | tf_op jit(solution)/shard_map/ppermute | solution.py:339
  11.2 0.7 %copy-start.1 = (s32[8]{0:T(128)S(1)}, s32[8]{0:T(128)}, u32[]{:S(2)}) copy-start(s32[8]{0:T(128)} %param.10) | copy-start | bytes 100
  14.1 7.3 %collective-permute-start = (bf16[2,512,128]{2,1,0:T(8,128)(2,1)S(1)}, bf16[2,512,128]{2,1,0:T(8,128)(2,1)S(1)}, u32[]{:S(2)}, u32[]{:S(2)}) collective-permute-start(bf16[2,512,128]{2,1,0:T(8,128)(2,1)S(1)} %get-tuple-element.22.refs_0_), channel_id=1, source_target_pairs={{4,8},{8,4},{5,9},{9,5},{6,10},{10,6},{7,11},{11,7},{20,24},{24,20... | collective-permute-start | bytes 786440 | tf_op jit(solution)/shard_map/ppermute | solution.py:339
  16.8 24.6 %collective-permute-start.7 = (bf16[1024,128]{1,0:T(8,128)(2,1)S(1)}, bf16[1024,128]{1,0:T(8,128)(2,1)S(1)}, u32[]{:S(2)}, u32[]{:S(2)}) collective-permute-start(bf16[1024,128]{1,0:T(8,128)(2,1)S(1)} %get-tuple-element.32), channel_id=1, source_target_pairs={{0,8},{4,12},{8,0},{12,4},{1,9},{5,13},{9,1},{13,5},{2,10},{6,14},... | collective-permute-start | bytes 786440 | tf_op jit(solution)/shard_map/ppermute | solution.py:339
  26.3 18.1 %collective-permute-start.5 = (bf16[384,128]{1,0:T(8,128)(2,1)S(1)}, bf16[384,128]{1,0:T(8,128)(2,1)S(1)}, u32[]{:S(2)}, u32[]{:S(2)}) collective-permute-start(bf16[384,128]{1,0:T(8,128)(2,1)S(1)} %get-tuple-element.30), channel_id=1, source_target_pairs={{0,8},{4,12},{8,0},{12,4},{1,9},{5,13},{9,1},{13,5},{2,10},{6,14},... | collective-permute-start | bytes 294920 | tf_op jit(solution)/shard_map/ppermute | solution.py:339
  35.6 8.9 %collective-permute-start.6 = (bf16[384,128]{1,0:T(8,128)(2,1)S(1)}, bf16[384,128]{1,0:T(8,128)(2,1)S(1)}, u32[]{:S(2)}, u32[]{:S(2)}) collective-permute-start(bf16[384,128]{1,0:T(8,128)(2,1)S(1)} %get-tuple-element.31), channel_id=1, source_target_pairs={{0,12},{4,8},{8,4},{12,0},{1,13},{5,9},{9,5},{13,1},{2,14},{6,10},... | collective-permute-start | bytes 294920 | tf_op jit(solution)/shard_map/ppermute | solution.py:339
  37.6 10.2 %collective-permute-start.3 = (bf16[1024,128]{1,0:T(8,128)(2,1)S(1)}, bf16[1024,128]{1,0:T(8,128)(2,1)S(1)}, u32[]{:S(2)}, u32[]{:S(2)}) collective-permute-start(bf16[1024,128]{1,0:T(8,128)(2,1)S(1)} %get-tuple-element.27.refs_2_), channel_id=1, source_target_pairs={{0,12},{12,0},{1,13},{13,1},{2,14},{14,2},{3,15},{15,3},{16,28},{2... | collective-permute-start | bytes 786440 | tf_op jit(solution)/shard_map/ppermute | solution.py:339
  41.3 11.7 %collective-permute-start.4 = (bf16[1408,128]{1,0:T(8,128)(2,1)S(1)}, bf16[1408,128]{1,0:T(8,128)(2,1)S(1)}, u32[]{:S(2)}, u32[]{:S(2)}) collective-permute-start(bf16[1408,128]{1,0:T(8,128)(2,1)S(1)} %get-tuple-element.28), channel_id=1, source_target_pairs={{0,4},{4,0},{8,12},{12,8},{1,5},{5,1},{9,13},{13,9},{2,6},{6,2},{1... | collective-permute-start | bytes 1081352 | tf_op jit(solution)/shard_map/ppermute | solution.py:339

commit v7 on v6

--- a/solution.py
+++ b/solution.py
@@ -84,13 +84,15 @@
     for place in (0, 1):
         k_win[pl.ds(place * rows, rows), :] = empty
         v_win[pl.ds(place * rows, rows), :] = empty
-    for i, ref in enumerate(refs):
+    k_win[pl.ds((plan.back + 1) * rows, rows), :] = refs[0][pl.ds(0, rows), :]
+    v_win[pl.ds((plan.back + 1) * rows, rows), :] = refs[0][pl.ds(rows, rows), :]
+    for i in range(1, plan.back + 1):
         place = plan.back + 1 - i
         if i == plan.back:
             place = jnp.where(own == plan.back - 1, plan.back + 2, place)
         to = pl.ds(pl.multiple_of(place * rows, rows), rows)
-        k_win[to, :] = ref[pl.ds(0, rows), :]
-        v_win[to, :] = ref[pl.ds(rows, rows), :]
+        k_win[to, :] = refs[2 * i - 1][...]
+        v_win[to, :] = refs[2 * i][...]
 
 
 def attend_at(plan, meta, loader, slot, q, g, k_win, v_win):
@@ -103,8 +105,8 @@
     return keys_here, out
 
 
-def pack_kernel(plan, meta, q_ref, g_ref, *refs):
-    blocks, sems = refs[: plan.n], refs[plan.n]
+def pack_kernel(plan, meta, q_ref, g_ref, k_ref, v_ref, *refs):
+    blocks, (kv, sems, kv_sems) = refs[: plan.n], refs[plan.n :]
     own = meta[0]
     copies = []
     for apart, block in enumerate(blocks):
@@ -112,6 +114,9 @@
         at = pl.ds(pl.multiple_of(slot * plan.cols, plan.cols), plan.cols)
         copies.append(pltpu.make_async_copy(q_ref.at[at, :], block.at[0], sems.at[apart, 0]))
         copies.append(pltpu.make_async_copy(g_ref.at[at, :], block.at[1], sems.at[apart, 1]))
+    for i, ref in enumerate((k_ref, v_ref)):
+        to = kv.at[pl.ds(i * plan.rows, plan.rows), :]
+        copies.append(pltpu.make_async_copy(ref, to, kv_sems.at[i]))
     for copy in copies:
         copy.start()
     for copy in copies:
@@ -126,72 +131,91 @@
     _, (attended, query_grad, key_part, value_part) = attend_at(
         plan, meta, own, slot, qg[0], qg[1], k_win, v_win
     )
+    put_rows(plan, pay_ref, attended, query_grad)
+    grad_ref[:, : plan.width] = key_part
+    grad_ref[:, plan.width :] = value_part
+
+
+def add_parts(plan, acc, keys_here, key_part, value_part):
+    acc[keys_here, : plan.width] = acc[keys_here, : plan.width] + key_part
+    acc[keys_here, plan.width :] = acc[keys_here, plan.width :] + value_part
+
+
+def put_rows(plan, pay_ref, attended, query_grad):
     pay_ref[pl.ds(0, plan.cols), :] = attended
     pay_ref[pl.ds(plan.cols, plan.cols), :] = query_grad
-    grad_ref[:, : plan.width] = key_part
-    grad_ref[:, plan.width :] = value_part
-
-
-def last_kernel(plan, first, items, meta, *refs):
-    n, width, rows, block = plan.n, plan.width, plan.rows, plan.block
-    qg_refs, (got_ref, first_grad), refs = refs[: len(items)], refs[len(items) : len(items) + 2], refs[len(items) + 2 :]
-    outs = len(items) + n - 1 + 4
-    kv_refs, refs = refs[:-outs], refs[-outs:]
-    pay_refs, grad_refs, (k_win, v_win, acc, qg) = refs[: len(items)], refs[len(items) : -4], refs[-4:]
-    grad_refs = [grad_refs[0], pay_refs[items.index(1)].at[pl.ds(2 * plan.cols, plan.grad_rows), :], *grad_refs[1:]]
+
+
+def next_kernel(plan, first, items, meta, *refs):
+    qg_refs, first_grad, refs = refs[: len(items)], refs[len(items)], refs[len(items) + 1 :]
+    outs = len(items) + 3
+    kv_refs, pay_refs, (acc, k_win, v_win) = refs[:-outs], refs[-outs:-3], refs[-3:]
     step = pl.program_id(0)
     own = meta[0]
-    middle = plan.is_middle(own)
 
     @pl.when(step == 0)
     def _():
         fill_window(plan, own, kv_refs, k_win, v_win)
         acc[...] = jnp.zeros_like(acc)
         slot = plan.slot(meta, own, own ^ first)
-        keys_here = pl.ds(pl.multiple_of(rows + slot * block, block), plan.reach + block)
-        acc[keys_here, :] = first_grad[...]
+        start = pl.multiple_of(plan.rows + slot * plan.block, plan.block)
+        acc[pl.ds(start, plan.reach + plan.block), :] = first_grad[...]
 
     for i, item in enumerate(items):
 
         @pl.when(step == i)
         def _():
-            loader, owner, source = own, own ^ item, qg_refs[i]
-            if item == n - 1:
-                loader, owner, source = jnp.where(middle, owner, own), jnp.where(middle, own, owner), qg
-
-                @pl.when(middle)
-                def _():
-                    qg[...] = got_ref[...]
-
-                @pl.when(jnp.logical_not(middle))
-                def _():
-                    qg[...] = qg_refs[i][...]
-
-            slot = plan.slot(meta, loader, owner)
-            keys_here, (attended, query_grad, key_part, value_part) = attend_at(
-                plan, meta, loader, slot, source[0], source[1], k_win, v_win
+            slot = plan.slot(meta, own, own ^ item)
+            keys_here, (attended, query_grad, *parts) = attend_at(
+                plan, meta, own, slot, qg_refs[i][0], qg_refs[i][1], k_win, v_win
             )
-            acc[keys_here, :width] = acc[keys_here, :width] + key_part
-            acc[keys_here, width:] = acc[keys_here, width:] + value_part
-            pay_refs[i][pl.ds(0, plan.cols), :] = attended
-            pay_refs[i][pl.ds(plan.cols, plan.cols), :] = query_grad
-
-    @pl.when(step == len(items) - 1)
+            add_parts(plan, acc, keys_here, *parts)
+            put_rows(plan, pay_refs[i], attended, query_grad)
+
+
+def last_kernel(plan, meta, *refs):
+    n, width, block, rows = plan.n, plan.width, plan.block, plan.rows
+    qg_ref, got_ref, near_ref, acc_ref, refs = *refs[:4], refs[4:]
+    outs = 2 + n - 1 + 4
+    kv_refs, (pay_ref, near_pay_ref, *grad_refs), (k_win, v_win, acc, qg) = refs[:-outs], refs[-outs:-4], refs[-4:]
+    own = meta[0]
+    middle = plan.is_middle(own)
+
+    @pl.when(middle)
     def _():
-        def of_range(i, carry):
-            key_range = plan.first_range(own) + i
-            at = (key_range - own + plan.back + 1) * rows
-            for apart in range(n):
-                slot = plan.slot(meta, key_range, own ^ apart)
-                part = acc[pl.ds(pl.multiple_of(at + slot * block, block), block), :]
-                part = part.astype(grad_refs[apart].dtype)
-                to = pl.multiple_of(i * block, block)
-                grad_refs[apart][pl.ds(to, block), :] = part[:, :width]
-                to = pl.multiple_of(i * block + plan.grad_rows // 2, block)
-                grad_refs[apart][pl.ds(to, block), :] = part[:, width:]
-            return carry
-
-        lax.fori_loop(0, plan.back + 1, of_range, 0)
+        qg[...] = got_ref[...]
+
+    @pl.when(jnp.logical_not(middle))
+    def _():
+        qg[...] = qg_ref[...]
+
+    fill_window(plan, own, kv_refs, k_win, v_win)
+    size = acc_ref.shape[0]
+    acc[pl.ds(0, size), :] = acc_ref[...]
+    acc[pl.ds(size, acc.shape[0] - size), :] = jnp.zeros((acc.shape[0] - size, 2 * width), jnp.float32)
+    loader, owner = jnp.where(middle, own ^ (n - 1), own), jnp.where(middle, own, own ^ (n - 1))
+    keys_here, (attended, query_grad, *parts) = attend_at(
+        plan, meta, loader, plan.slot(meta, loader, owner), qg[0], qg[1], k_win, v_win
+    )
+    add_parts(plan, acc, keys_here, *parts)
+    put_rows(plan, pay_ref, attended, query_grad)
+
+    near_pay_ref[pl.ds(0, 2 * plan.cols), :] = near_ref[...]
+    grad_refs = [grad_refs[0], near_pay_ref.at[pl.ds(2 * plan.cols, plan.grad_rows), :], *grad_refs[1:]]
+
+    def of_range(i, carry):
+        key_range = plan.first_range(own) + i
+        at = (key_range - own + plan.back + 1) * rows
+        for apart in range(n):
+            slot = plan.slot(meta, key_range, own ^ apart)
+            part = acc[pl.ds(pl.multiple_of(at + slot * block, block), block), :].astype(grad_refs[apart].dtype)
+            to = pl.multiple_of(i * block, block)
+            grad_refs[apart][pl.ds(to, block), :] = part[:, :width]
+            to = pl.multiple_of(i * block + plan.grad_rows // 2, block)
+            grad_refs[apart][pl.ds(to, block), :] = part[:, width:]
+        return carry
+
+    lax.fori_loop(0, plan.back + 1, of_range, 0)
 
 
 def spec_of(space):
@@ -210,12 +234,13 @@
     )(*operands)
 
 
-def pack(plan, meta, q, g):
+def pack(plan, meta, *operands):
     out_shape = [jax.ShapeDtypeStruct((2, plan.cols, plan.width), jnp.bfloat16)] * plan.n
-    q, g = (pltpu.with_memory_space_constraint(x, pltpu.HBM) for x in (q, g))
+    out_shape.append(jax.ShapeDtypeStruct((2 * plan.rows, plan.width), jnp.bfloat16))
+    operands = [pltpu.with_memory_space_constraint(x, pltpu.HBM) for x in operands]
     return kernel_call(
-        functools.partial(pack_kernel, plan), "pack", (meta, q, g), [pltpu.SMEM] + [pl.ANY] * 2, out_shape,
-        [pltpu.SemaphoreType.DMA((plan.n, 2))],
+        functools.partial(pack_kernel, plan), "pack", (meta, *operands), [pltpu.SMEM] + [pl.ANY] * 4, out_shape,
+        [pltpu.SemaphoreType.DMA((plan.n, 2)), pltpu.SemaphoreType.DMA((2,))],
         out_specs=[spec_of(pltpu.VMEM)] * len(out_shape),
     )
 
@@ -234,22 +259,34 @@
     )
 
 
-def attend_last(plan, first, items, meta, qg_list, got, first_grad, kv_list):
-    n = plan.n
+def attend_next(plan, first, items, meta, qg_list, first_grad, kv_list):
     rows = plan.window_ranges * plan.rows
     window = pltpu.VMEM((rows, plan.width), jnp.bfloat16)
+    out_shape = [jax.ShapeDtypeStruct((2 * plan.cols, plan.width), jnp.bfloat16)] * len(items)
+    out_shape.append(jax.ShapeDtypeStruct((rows, 2 * plan.width), jnp.float32))
+    operands = (meta, *qg_list, first_grad, *kv_list)
+    return kernel_call(
+        functools.partial(next_kernel, plan, first, items), "attend_next", operands,
+        [pltpu.SMEM] + [pltpu.VMEM] * (len(operands) - 1), out_shape, [window, window],
+        out_specs=[spec_of(pltpu.VMEM)] * len(out_shape), cost_estimate=plan.cost(len(items)), grid=(len(items),),
+    )
+
+
+def attend_last(plan, meta, qg, got, near_pay, sums, kv_list):
+    n = plan.n
+    window = pltpu.VMEM((plan.window_ranges * plan.rows, plan.width), jnp.bfloat16)
     sum_rows = (2 * plan.back + 2) * plan.rows
-    block = (2, plan.cols, plan.width)
-    pay_rows = [2 * plan.cols + (plan.grad_rows if x == 1 else 0) for x in items]
-    out_shape = [jax.ShapeDtypeStruct((size, plan.width), jnp.bfloat16) for size in pay_rows]
+    out_shape = [
+        jax.ShapeDtypeStruct((size, plan.width), jnp.bfloat16) for size in (2 * plan.cols, 2 * plan.cols + plan.grad_rows)
+    ]
     grads = (plan.grad_rows, plan.width)
     out_shape += [jax.ShapeDtypeStruct(grads, jnp.bfloat16 if i else jnp.float32) for i in range(n - 1)]
-    operands = (meta, *qg_list, got, first_grad, *kv_list)
+    operands = (meta, qg, got, near_pay, sums, *kv_list)
     return kernel_call(
-        functools.partial(last_kernel, plan, first, items), "attend_last", operands,
+        functools.partial(last_kernel, plan), "attend_last", operands,
         [pltpu.SMEM] + [pltpu.VMEM] * (len(operands) - 1), out_shape,
-        [window, window, pltpu.VMEM((sum_rows, 2 * plan.width), jnp.float32), pltpu.VMEM(block, jnp.bfloat16)],
-        out_specs=[spec_of(pltpu.VMEM)] * len(out_shape), cost_estimate=plan.cost(len(items)), grid=(len(items),),
+        [window, window, pltpu.VMEM((sum_rows, 2 * plan.width), jnp.float32), pltpu.VMEM(qg.shape, jnp.bfloat16)],
+        out_specs=[spec_of(pltpu.VMEM)] * len(out_shape), cost_estimate=plan.cost(1),
     )
 
 
@@ -341,11 +378,14 @@
     def across(array, bits):
         return permuted(array, [(i, i ^ bits) for i in range(n)])
 
-    kv = jnp.concatenate([keys.reshape(rows, width), values.reshape(rows, width)])
-    kv_list = [kv]
+    k = keys.reshape(rows, width)
+    v = values.reshape(rows, width)
+    kv_list = []
     for by in range(1, plan.back + 1):
         pairs = [(i, i + by) for i in range(n - by)]
-        kv_list.append(permuted(kv, pairs + [(n // 2, n // 2 - 1)] if by == plan.back else pairs))
+        if by == plan.back:
+            pairs.append((n // 2, n // 2 - 1))
+        kv_list += [permuted(k, pairs), permuted(v, pairs)]
 
     owners = jnp.arange(n, dtype=jnp.int32)
     match = block_owner[:, None, :] == owners[None, :, None]
@@ -354,20 +394,23 @@
         [own.reshape(1).astype(jnp.int32), jnp.cumsum(doc_lengths).astype(jnp.int32), table.reshape(-1)]
     )
 
-    blocks = pack(plan, meta, query.reshape(rows * heads, width), output_gradient.reshape(rows * heads, width))
+    q, g = (x.reshape(rows * heads, width) for x in (query, output_gradient))
+    *blocks, kv = pack(plan, meta, q, g, k, v)
+    kv_list = [kv, *kv_list]
     middle = (n // 2 - 1, n // 2)
     got = permuted(blocks[n - 1], [middle, middle[::-1]])
     first = n // 2
     first_pay, first_grad = attend_first(plan, first, meta, blocks[first], kv_list)
     first_pay = across(first_pay, first)
-    sent = tuple(x for x in range(n - 1, 0, -1) if x != first)
-    items = (*sent, 0)
-    out = attend_last(plan, first, items, meta, [blocks[x] for x in items], got, first_grad, kv_list)
-    pays, grads = out[: len(items)], out[len(items) :]
-    late = [permuted(pays[0], [(i, i ^ (n - 1)) for i in range(n) if i not in middle])]
-    late += [across(pay, x) for x, pay in zip(sent[1:], pays[1:])]
+    items = tuple(x for x in range(n - 1) if x != first)
+    *pays, sums = attend_next(plan, first, items, meta, [blocks[x] for x in items], first_grad, kv_list)
+    pays = dict(zip(items, pays))
+    last_pay, pays[1], *grads = attend_last(plan, meta, blocks[n - 1], got, pays[1], sums, kv_list)
+    late = [permuted(last_pay, [(i, i ^ (n - 1)) for i in range(n) if i not in middle])]
+    sent = (n - 1, *items[1:])
+    late += [across(pays[x], x) for x in sent[1:]]
     grads = [across(grad, i + 1) if i else grad for i, grad in enumerate(grads)]
-    filled = place(plan, [first_pay, pays[-1], pays[0]])
+    filled = place(plan, [first_pay, pays[0], last_pay])
     attended, query_grad, key_grad, value_grad = place(plan, late, sent, grads, filled)
     return (
         attended.reshape(rows, heads, width),

time: 54.2 us -> 55.4 us (1.022)
  starting transfers between devices: 29.8 us -> 31.5 us
  waiting for transfers between devices: 10.8 us -> 9.92 us
  local copies, waits for them, and re-layouts: 0.75 us -> 0.08 us
  Pallas kernels: 10.5 us -> 11.1 us
    ppermute x8 -> x10, starting transfers between devices: 29.8 us -> 31.5 us  [permuted(): return lax.ppermute(array, 'ctx', pairs)]
    concatenate x1 -> x0, other arithmetic: 0.89 us -> none  [on_device(): jnp.concatenate([keys.reshape(rows, width), values.reshape(rows, width)])]
    ppermute x8 -> x10, waiting for transfers between devices: 10.8 us -> 9.92 us  [permuted(): return lax.ppermute(array, 'ctx', pairs)]
    reduce_sum x1, other arithmetic: 0.14 us -> 0.82 us  [on_device(): table = jnp.sum(jnp.where(match, owners, 0), axis=2)]
    unnamed x4 -> x0, local copies, waits for them, and re-layouts: 0.67 us -> none
    another operation x1, other arithmetic: 0.18 us -> 0.84 us
    pallas_call x5 -> x6, Pallas kernels: 10.5 us -> 11.1 us  [kernel_call(): pl.pallas_call(body, out_shape=out_shape, in_specs=[spec_of(space) for sp...]
  transfers between devices with their start and end apart: 8 -> 10, of which waited for: 3 -> 2; matrix products, arithmetic and copies ran while one was open for 1% -> 3% of each run, Pallas kernels for 18% -> 18%
where the time goes in v7:
time: 55.4 us; the launch traced here: 55.1 us
  starting transfers between devices  31.5 us (57%)
  Pallas kernels  11.1 us (20%)
  waiting for transfers between devices  9.92 us (18%)
  other arithmetic  1.74 us (3%)
  between operations  0.78 us (1%)
    ppermute x10, starting transfers between devices, permuted(): return lax.ppermute(array, 'ctx', pairs)  31.5 us
    pallas_call x6, Pallas kernels, kernel_call(): pl.pallas_call(body, out_shape=out_shape, in_specs=[spec_of(space) for sp...  11.1 us
    ppermute x10, waiting for transfers between devices, permuted(): return lax.ppermute(array, 'ctx', pairs)  9.92 us
  transfers between devices with their start and end apart: 10, of which 2 were waited for; matrix products, arithmetic and copies ran while one was open for 3% of the time, Pallas kernels for 18%

profile of v7, /device:TPU:0, one launch (start us, length us, event | category | flops | bytes accessed | tf_op | source)
XLA Modules:
  0.0 55.1 jit_solution(10452019950836833812)
XLA Ops:
  0.6 4.9 %collective-permute-start.1 = (bf16[256,128]{1,0:T(8,128)(2,1)}, bf16[256,128]{1,0:T(8,128)(2,1)S(1)}, u32[]{:S(2)}, u32[]{:S(2)}) collective-permute-start(bf16[256,128]{1,0:T(8,128)(2,1)} %bitcast.13), channel_id=1, source_target_pairs={{0,4},{4,8},{8,12},{1,5},{5,9},{9,13},{2,6},{6,10},{10,14},{3,7},{... | collective-permute-start | bytes 196616 | tf_op jit(solution)/shard_map/ppermute | solution.py:376
  5.6 4.5 %collective-permute-start.3 = (bf16[256,128]{1,0:T(8,128)(2,1)}, bf16[256,128]{1,0:T(8,128)(2,1)S(1)}, u32[]{:S(2)}, u32[]{:S(2)}) collective-permute-start(bf16[256,128]{1,0:T(8,128)(2,1)} %bitcast.14), channel_id=1, source_target_pairs={{0,8},{4,12},{8,4},{1,9},{5,13},{9,5},{2,10},{6,14},{10,6},{3,11},... | collective-permute-start | bytes 196616 | tf_op jit(solution)/shard_map/ppermute | solution.py:376
  10.1 1.3 %collective-permute-start.2 = (bf16[256,128]{1,0:T(8,128)(2,1)}, bf16[256,128]{1,0:T(8,128)(2,1)S(1)}, u32[]{:S(2)}, u32[]{:S(2)}) collective-permute-start(bf16[256,128]{1,0:T(8,128)(2,1)} %bitcast.16), channel_id=1, source_target_pairs={{0,4},{4,8},{8,12},{1,5},{5,9},{9,13},{2,6},{6,10},{10,14},{3,7},{... | collective-permute-start | bytes 196616 | tf_op jit(solution)/shard_map/ppermute | solution.py:376
  11.4 3.0 %collective-permute-start.4 = (bf16[256,128]{1,0:T(8,128)(2,1)}, bf16[256,128]{1,0:T(8,128)(2,1)S(1)}, u32[]{:S(2)}, u32[]{:S(2)}) collective-permute-start(bf16[256,128]{1,0:T(8,128)(2,1)} %bitcast.17), channel_id=1, source_target_pairs={{0,8},{4,12},{8,4},{1,9},{5,13},{9,5},{2,10},{6,14},{10,6},{3,11},... | collective-permute-start | bytes 196616 | tf_op jit(solution)/shard_map/ppermute | solution.py:376
  14.4 0.8 %select_reduce_fusion = s32[4,4]{1,0:T(4,128)S(1)} fusion(s32[4,4]{1,0:T(4,128)} %param.11), kind=kLoop, calls=%fused_computation | loop fusion | flops 176 | bytes 128 | tf_op jit(solution)/shard_map/reduce_sum | solution.py:392
  15.2 0.1 reshape.68
  15.3 0.8 %reduce-window.9 = s32[8,1]{0,1:T(1,128)S(1)} reduce-window(s32[8,1]{0,1:T(1,128)} %bitcast.20, s32[]{:T(128)} %constant.9.clone.1), window={size=8x1 pad=7_0x0_0}, to_apply=%region_0.1 | reduce-window | flops 56 | bytes 68 | tf_op jit(solution)/shard_map/reduce-window.4
  16.1 0.1 pad_add_fusion.meta
  16.2 1.9 %pack.1 = (bf16[2,512,128]{2,1,0:T(8,128)(2,1)S(1)}, bf16[2,512,128]{2,1,0:T(8,128)(2,1)S(1)}, bf16[2,512,128]{2,1,0:T(8,128)(2,1)S(1)}, bf16[2,512,128]{2,1,0:T(8,128)(2,1)S(1)}, bf16[512,128]{1,0:T(8,128)(2,1)S(1)}) custom-call(s32[25]{0:T(128)S(1)} %pad_add_fusion.meta, bf16[2048,128]{1,0:T(8,128)(2,1)} %bitcast.11, bf16[2048,128]{1,0:T(8,128)(2,1)} %bitcast.12, ...), custom_call_target="tpu_custom_call" | custom-call | tf_op jit(solution)/shard_map/pack/pallas_call | solution.py:226
  18.2 0.7 %collective-permute-start = (bf16[2,512,128]{2,1,0:T(8,128)(2,1)S(1)}, bf16[2,512,128]{2,1,0:T(8,128)(2,1)S(1)}, u32[]{:S(2)}, u32[]{:S(2)}) collective-permute-start(bf16[2,512,128]{2,1,0:T(8,128)(2,1)S(1)} %get-tuple-element.25.refs_0_), channel_id=1, source_target_pairs={{4,8},{8,4},{5,9},{9,5},{6,10},{10,6},{7,11},{11,7},{20,24},{24,20... | collective-permute-start | bytes 786440 | tf_op jit(solution)/shard_map/ppermute | solution.py:376
  18.8 0.0 collective-permute-done.1.refs_1_.refs_4_.refs_5_
  18.9 0.0 collective-permute-done.2.refs_2_.refs_5_.refs_6_
  18.9 0.0 collective-permute-done.3.refs_3_.refs_6_.refs_7_
  18.9 0.0 collective-permute-done.4.refs_4_.refs_7_.refs_8_
  18.9 2.0 %attend_first.1 = (bf16[1024,128]{1,0:T(8,128)(2,1)S(1)}, f32[576,256]{1,0:T(8,128)S(1)}) custom-call(s32[25]{0:T(128)S(1)} %pad_add_fusion.meta, bf16[2,512,128]{2,1,0:T(8,128)(2,1)S(1)} %get-tuple-element.28.qg, bf16[512,128]{1,0:T(8,128)(2,1)S(1)} %get-tuple-element.29.refs_0_.refs_3_.refs_4_, ...), custom_call_target="tpu_custom_call" | custom-call | flops 4227858432 | bytes 1048576 | tf_op jit(solution)/shard_map/attend_first/pallas_call | solution.py:226
  20.9 3.3 %collective-permute-start.9 = (bf16[1024,128]{1,0:T(8,128)(2,1)S(1)}, bf16[1024,128]{1,0:T(8,128)(2,1)S(1)}, u32[]{:S(2)}, u32[]{:S(2)}) collective-permute-start(bf16[1024,128]{1,0:T(8,128)(2,1)S(1)} %get-tuple-element.38), channel_id=1, source_target_pairs={{0,8},{4,12},{8,0},{12,4},{1,9},{5,13},{9,1},{13,5},{2,10},{6,14},... | collective-permute-start | bytes 786440 | tf_op jit(solution)/shard_map/ppermute | solution.py:376
  24.2 3.4 %attend_next.1 = (bf16[1024,128]{1,0:T(8,128)(2,1)S(1)}, bf16[1024,128]{1,0:T(8,128)(2,1)S(1)}, f32[1280,256]{1,0:T(8,128)S(1)}) custom-call(s32[25]{0:T(128)S(1)} %pad_add_fusion.meta, bf16[2,512,128]{2,1,0:T(8,128)(2,1)S(1)} %get-tuple-element.26.refs_0_, bf16[2,512,128]{2,1,0:T(8,128)(2,1)S(1)} %get-tuple-element.27.refs_1_, ...), custom_call_target="tpu_custom_call" | custom-call | flops 8455716864 | bytes 2097152 | tf_op jit(solution)/shard_map/attend_next/pallas_call | solution.py:226
  27.6 0.0 collective-permute-done.refs_1_
  27.6 2.1 %attend_last.1 = (bf16[1024,128]{1,0:T(8,128)(2,1)S(1)}, bf16[1408,128]{1,0:T(8,128)(2,1)S(1)}, f32[384,128]{1,0:T(8,128)S(1)}, bf16[384,128]{1,0:T(8,128)(2,1)S(1)}, bf16[384,128]{1,0:T(8,128)(2,1)S(1)}) custom-call(s32[25]{0:T(128)S(1)} %pad_add_fusion.meta, bf16[2,512,128]{2,1,0:T(8,128)(2,1)S(1)} %get-tuple-element.25.refs_0_, ...), custom_call_target="tpu_custom_call" | custom-call | flops 4227858432 | bytes 1048576 | tf_op jit(solution)/shard_map/attend_last/pallas_call | solution.py:226
  29.7 8.0 %collective-permute-start.6 = (bf16[1408,128]{1,0:T(8,128)(2,1)S(1)}, bf16[1408,128]{1,0:T(8,128)(2,1)S(1)}, u32[]{:S(2)}, u32[]{:S(2)}) collective-permute-start(bf16[1408,128]{1,0:T(8,128)(2,1)S(1)} %get-tuple-element.34), channel_id=1, source_target_pairs={{0,4},{4,0},{8,12},{12,8},{1,5},{5,1},{9,13},{13,9},{2,6},{6,2},{1... | collective-permute-start | bytes 1081352 | tf_op jit(solution)/shard_map/ppermute | solution.py:376
  37.6 4.8 %collective-permute-start.5 = (bf16[1024,128]{1,0:T(8,128)(2,1)S(1)}, bf16[1024,128]{1,0:T(8,128)(2,1)S(1)}, u32[]{:S(2)}, u32[]{:S(2)}) collective-permute-start(bf16[1024,128]{1,0:T(8,128)(2,1)S(1)} %get-tuple-element.33.refs_2_), channel_id=1, source_target_pairs={{0,12},{12,0},{1,13},{13,1},{2,14},{14,2},{3,15},{15,3},{16,28},{2... | collective-permute-start | bytes 786440 | tf_op jit(solution)/shard_map/ppermute | solution.py:376
  42.4 0.1 collective-permute-start.7
  42.5 1.0 %collective-permute-start.8 = (bf16[384,128]{1,0:T(8,128)(2,1)S(1)}, bf16[384,128]{1,0:T(8,128)(2,1)S(1)}, u32[]{:S(2)}, u32[]{:S(2)}) collective-permute-start(bf16[384,128]{1,0:T(8,128)(2,1)S(1)} %get-tuple-element.37), channel_id=1, source_target_pairs={{0,12},{4,8},{8,4},{12,0},{1,13},{5,9},{9,5},{13,1},{2,14},{6,10},... | collective-permute-start | bytes 294920 | tf_op jit(solution)/shard_map/ppermute | solution.py:376
  43.5 0.0 collective-permute-done.9.refs_0_
  43.5 0.8 %place_first.1 = (bf16[2048,128]{1,0:T(8,128)(2,1)}, bf16[2048,128]{1,0:T(8,128)(2,1)}) custom-call(bf16[1024,128]{1,0:T(8,128)(2,1)S(1)} %collective-permute-done.9.refs_0_, bf16[1024,128]{1,0:T(8,128)(2,1)S(1)} %get-tuple-element.39.refs_1_, bf16[1024,128]{1,0:T(8,128)(2,1)S(1)} %get-tuple-element.33.refs_2_), custom_call_target="tpu_custom_call" | custom-call | flops 12683575296 | bytes 3145728 | tf_op jit(solution)/shard_map/place_first/pallas_call | solution.py:226
  44.3 6.1 %collective-permute-done.7.refs_3_ = bf16[384,128]{1,0:T(8,128)(2,1)S(1)} collective-permute-done((bf16[384,128]{1,0:T(8,128)(2,1)S(1)}, bf16[384,128]{1,0:T(8,128)(2,1)S(1)}, u32[]{:S(2)}, u32[]{:S(2)}) %collective-permute-start.7) | collective-permute-done | bytes 98336 | tf_op jit(solution)/shard_map/ppermute | solution.py:376
  50.4 3.8 %collective-permute-done.8.refs_4_ = bf16[384,128]{1,0:T(8,128)(2,1)S(1)} collective-permute-done((bf16[384,128]{1,0:T(8,128)(2,1)S(1)}, bf16[384,128]{1,0:T(8,128)(2,1)S(1)}, u32[]{:S(2)}, u32[]{:S(2)}) %collective-permute-start.8) | collective-permute-done | bytes 98336 | tf_op jit(solution)/shard_map/ppermute | solution.py:376
  54.2 0.0 collective-permute-done.5.refs_0_
  54.2 0.0 collective-permute-done.6.refs_1_
  54.2 0.9 %place_last.1 = (bf16[2048,128]{1,0:T(8,128)(2,1)}, bf16[2048,128]{1,0:T(8,128)(2,1)}, bf16[256,128]{1,0:T(8,128)(2,1)}, bf16[256,128]{1,0:T(8,128)(2,1)}) custom-call(bf16[1024,128]{1,0:T(8,128)(2,1)S(1)} %collective-permute-done.5.refs_0_, bf16[1408,128]{1,0:T(8,128)(2,1)S(1)} %collective-permute-done.6.refs_1_, ...), custom_call_target="tpu_custom_call", output_to_operand_aliasing={{0}: (5, {}), {1}: (6, {})} | custom-call | flops 8455716864 | bytes 2097152 | tf_op jit(solution)/shard_map/place_last/pallas_call | solution.py:226
Async XLA Ops:
  0.6 18.2 %collective-permute-start.1 = (bf16[256,128]{1,0:T(8,128)(2,1)}, bf16[256,128]{1,0:T(8,128)(2,1)S(1)}, u32[]{:S(2)}, u32[]{:S(2)}) collective-permute-start(bf16[256,128]{1,0:T(8,128)(2,1)} %bitcast.13), channel_id=1, source_target_pairs={{0,4},{4,8},{8,12},{1,5},{5,9},{9,13},{2,6},{6,10},{10,14},{3,7},{... | collective-permute-start | bytes 196616 | tf_op jit(solution)/shard_map/ppermute | solution.py:376
  5.6 13.3 %collective-permute-start.3 = (bf16[256,128]{1,0:T(8,128)(2,1)}, bf16[256,128]{1,0:T(8,128)(2,1)S(1)}, u32[]{:S(2)}, u32[]{:S(2)}) collective-permute-start(bf16[256,128]{1,0:T(8,128)(2,1)} %bitcast.14), channel_id=1, source_target_pairs={{0,8},{4,12},{8,4},{1,9},{5,13},{9,5},{2,10},{6,14},{10,6},{3,11},... | collective-permute-start | bytes 196616 | tf_op jit(solution)/shard_map/ppermute | solution.py:376
  10.1 8.8 %collective-permute-start.2 = (bf16[256,128]{1,0:T(8,128)(2,1)}, bf16[256,128]{1,0:T(8,128)(2,1)S(1)}, u32[]{:S(2)}, u32[]{:S(2)}) collective-permute-start(bf16[256,128]{1,0:T(8,128)(2,1)} %bitcast.16), channel_id=1, source_target_pairs={{0,4},{4,8},{8,12},{1,5},{5,9},{9,13},{2,6},{6,10},{10,14},{3,7},{... | collective-permute-start | bytes 196616 | tf_op jit(solution)/shard_map/ppermute | solution.py:376
  11.4 7.5 %collective-permute-start.4 = (bf16[256,128]{1,0:T(8,128)(2,1)}, bf16[256,128]{1,0:T(8,128)(2,1)S(1)}, u32[]{:S(2)}, u32[]{:S(2)}) collective-permute-start(bf16[256,128]{1,0:T(8,128)(2,1)} %bitcast.17), channel_id=1, source_target_pairs={{0,8},{4,12},{8,4},{1,9},{5,13},{9,5},{2,10},{6,14},{10,6},{3,11},... | collective-permute-start | bytes 196616 | tf_op jit(solution)/shard_map/ppermute | solution.py:376
  18.2 9.4 %collective-permute-start = (bf16[2,512,128]{2,1,0:T(8,128)(2,1)S(1)}, bf16[2,512,128]{2,1,0:T(8,128)(2,1)S(1)}, u32[]{:S(2)}, u32[]{:S(2)}) collective-permute-start(bf16[2,512,128]{2,1,0:T(8,128)(2,1)S(1)} %get-tuple-element.25.refs_0_), channel_id=1, source_target_pairs={{4,8},{8,4},{5,9},{9,5},{6,10},{10,6},{7,11},{11,7},{20,24},{24,20... | collective-permute-start | bytes 786440 | tf_op jit(solution)/shard_map/ppermute | solution.py:376
  20.9 22.6 %collective-permute-start.9 = (bf16[1024,128]{1,0:T(8,128)(2,1)S(1)}, bf16[1024,128]{1,0:T(8,128)(2,1)S(1)}, u32[]{:S(2)}, u32[]{:S(2)}) collective-permute-start(bf16[1024,128]{1,0:T(8,128)(2,1)S(1)} %get-tuple-element.38), channel_id=1, source_target_pairs={{0,8},{4,12},{8,0},{12,4},{1,9},{5,13},{9,1},{13,5},{2,10},{6,14},... | collective-permute-start | bytes 786440 | tf_op jit(solution)/shard_map/ppermute | solution.py:376
  29.7 24.6 %collective-permute-start.6 = (bf16[1408,128]{1,0:T(8,128)(2,1)S(1)}, bf16[1408,128]{1,0:T(8,128)(2,1)S(1)}, u32[]{:S(2)}, u32[]{:S(2)}) collective-permute-start(bf16[1408,128]{1,0:T(8,128)(2,1)S(1)} %get-tuple-element.34), channel_id=1, source_target_pairs={{0,4},{4,0},{8,12},{12,8},{1,5},{5,1},{9,13},{13,9},{2,6},{6,2},{1... | collective-permute-start | bytes 1081352 | tf_op jit(solution)/shard_map/ppermute | solution.py:376
  37.6 16.6 %collective-permute-start.5 = (bf16[1024,128]{1,0:T(8,128)(2,1)S(1)}, bf16[1024,128]{1,0:T(8,128)(2,1)S(1)}, u32[]{:S(2)}, u32[]{:S(2)}) collective-permute-start(bf16[1024,128]{1,0:T(8,128)(2,1)S(1)} %get-tuple-element.33.refs_2_), channel_id=1, source_target_pairs={{0,12},{12,0},{1,13},{13,1},{2,14},{14,2},{3,15},{15,3},{16,28},{2... | collective-permute-start | bytes 786440 | tf_op jit(solution)/shard_map/ppermute | solution.py:376
  42.4 8.0 %collective-permute-start.7 = (bf16[384,128]{1,0:T(8,128)(2,1)S(1)}, bf16[384,128]{1,0:T(8,128)(2,1)S(1)}, u32[]{:S(2)}, u32[]{:S(2)}) collective-permute-start(bf16[384,128]{1,0:T(8,128)(2,1)S(1)} %get-tuple-element.36), channel_id=1, source_target_pairs={{0,8},{4,12},{8,0},{12,4},{1,9},{5,13},{9,1},{13,5},{2,10},{6,14},... | collective-permute-start | bytes 294920 | tf_op jit(solution)/shard_map/ppermute | solution.py:376
  42.5 11.7 %collective-permute-start.8 = (bf16[384,128]{1,0:T(8,128)(2,1)S(1)}, bf16[384,128]{1,0:T(8,128)(2,1)S(1)}, u32[]{:S(2)}, u32[]{:S(2)}) collective-permute-start(bf16[384,128]{1,0:T(8,128)(2,1)S(1)} %get-tuple-element.37), channel_id=1, source_target_pairs={{0,12},{4,8},{8,4},{12,0},{1,13},{5,9},{9,5},{13,1},{2,14},{6,10},... | collective-permute-start | bytes 294920 | tf_op jit(solution)/shard_map/ppermute | solution.py:376

commit v8 on v5

--- a/solution.py
+++ b/solution.py
@@ -55,7 +55,7 @@
         self.cols = self.block * heads
         self.reach = self.back * rows
         self.scale = width ** (-0.5)
-        self.window_ranges = self.back + 3
+        self.window_ranges = self.back + 1
 
     def ends(self, meta):
         return [meta[1 + i] for i in range(self.ndocs)]
@@ -73,17 +73,16 @@
 
 def fill_window(plan, refs, k_win, v_win):
     rows = plan.rows
-    for i, ref in enumerate(refs):
-        place = plan.back + 1 - i if i <= plan.back else plan.back + 2
-        k_win[pl.ds(place * rows, rows), :] = ref[pl.ds(0, rows), :]
-        v_win[pl.ds(place * rows, rows), :] = ref[pl.ds(rows, rows), :]
-    if len(refs) > plan.back + 1:
-        k_win[pl.ds(0, rows), :] = jnp.zeros((rows, plan.width), k_win.dtype)
-        v_win[pl.ds(0, rows), :] = jnp.zeros((rows, plan.width), v_win.dtype)
+    k_win[pl.ds(plan.back * rows, rows), :] = refs[0][pl.ds(0, rows), :]
+    v_win[pl.ds(plan.back * rows, rows), :] = refs[0][pl.ds(rows, rows), :]
+    for i in range(1, plan.back + 1):
+        to = pl.ds((plan.back - i) * rows, rows)
+        k_win[to, :] = refs[2 * i - 1][...]
+        v_win[to, :] = refs[2 * i][...]
 
 
 def attend_at(plan, meta, loader, slot, q, g, k_win, v_win):
-    start = (loader - meta[0] + 1) * plan.rows + slot * plan.block
+    start = (loader - meta[0]) * plan.rows + slot * plan.block
     keys_here = pl.ds(pl.multiple_of(start, plan.block), plan.reach + plan.block)
     out = attend_block(
         loader * plan.rows + slot * plan.block, plan.ends(meta), q, g, k_win[keys_here, :], v_win[keys_here, :],
@@ -92,8 +91,8 @@
     return keys_here, out
 
 
-def pack_kernel(plan, meta, q_ref, g_ref, *refs):
-    blocks, sems = refs[: plan.n], refs[plan.n]
+def pack_kernel(plan, meta, q_ref, g_ref, k_ref, v_ref, *refs):
+    blocks, (kv, sems, kv_sems) = refs[: plan.n], refs[plan.n :]
     own = meta[0]
     copies = []
     for apart, block in enumerate(blocks):
@@ -101,6 +100,9 @@
         at = pl.ds(pl.multiple_of(slot * plan.cols, plan.cols), plan.cols)
         copies.append(pltpu.make_async_copy(q_ref.at[at, :], block.at[0], sems.at[apart, 0]))
         copies.append(pltpu.make_async_copy(g_ref.at[at, :], block.at[1], sems.at[apart, 1]))
+    for i, ref in enumerate((k_ref, v_ref)):
+        to = kv.at[pl.ds(i * plan.rows, plan.rows), :]
+        copies.append(pltpu.make_async_copy(ref, to, kv_sems.at[i]))
     for copy in copies:
         copy.start()
     for copy in copies:
@@ -135,7 +137,7 @@
         fill_window(plan, kv_refs, k_win, v_win)
         acc[...] = jnp.zeros_like(acc)
         slot = plan.slot(meta, own, own ^ first)
-        keys_here = pl.ds(pl.multiple_of(rows + slot * block, block), plan.reach + block)
+        keys_here = pl.ds(pl.multiple_of(slot * block, block), plan.reach + block)
         acc[keys_here, :] = first_grad[...]
 
     for i, item in enumerate(items):
@@ -155,7 +157,7 @@
     @pl.when(step == len(items) - 1)
     def _():
         def of_range(key_range, carry):
-            at = (lax.rem(key_range - own + plan.back + n, n) + 1) * rows
+            at = lax.rem(key_range - own + plan.back + n, n) * rows
             for apart in range(n):
                 slot = plan.slot(meta, key_range, own ^ apart)
                 part = acc[pl.ds(pl.multiple_of(at + slot * block, block), block), :]
@@ -182,12 +184,13 @@
     )(*operands)
 
 
-def pack(plan, meta, q, g):
+def pack(plan, meta, *operands):
     out_shape = [jax.ShapeDtypeStruct((2, plan.cols, plan.width), jnp.bfloat16)] * plan.n
-    q, g = (pltpu.with_memory_space_constraint(x, pltpu.HBM) for x in (q, g))
+    out_shape.append(jax.ShapeDtypeStruct((2 * plan.rows, plan.width), jnp.bfloat16))
+    operands = [pltpu.with_memory_space_constraint(x, pltpu.HBM) for x in operands]
     return kernel_call(
-        functools.partial(pack_kernel, plan), "pack", (meta, q, g), [pltpu.SMEM] + [pl.ANY] * 2, out_shape,
-        [pltpu.SemaphoreType.DMA((plan.n, 2))],
+        functools.partial(pack_kernel, plan), "pack", (meta, *operands), [pltpu.SMEM] + [pl.ANY] * 4, out_shape,
+        [pltpu.SemaphoreType.DMA((plan.n, 2)), pltpu.SemaphoreType.DMA((2,))],
         out_specs=[spec_of(pltpu.VMEM)] * len(out_shape),
     )
 
@@ -216,7 +219,7 @@
     return kernel_call(
         functools.partial(last_kernel, plan, first, items), "attend_last", operands,
         [pltpu.SMEM] + [pltpu.VMEM] * (len(operands) - 1), out_shape,
-        [window, window, pltpu.VMEM(((n + 1) * plan.rows, 2 * plan.width), jnp.float32)],
+        [window, window, pltpu.VMEM((n * plan.rows, 2 * plan.width), jnp.float32)],
         out_specs=[spec_of(pltpu.VMEM)] * len(out_shape), cost_estimate=plan.cost(len(items)), grid=(len(items),),
     )
 
@@ -263,7 +266,7 @@
         (*payloads.values(), *grads, *filled),
         [pl.ANY] * len(items) + [pltpu.VMEM] * len(grads) + [pl.ANY] * len(filled),
         [big, big] + ([small, small] if final else [jax.ShapeDtypeStruct(grads[0].shape, jnp.bfloat16)]), scratch,
-        out_specs=[spec_of(pl.ANY)] * 2 + [spec_of(pl.ANY)] * 2 if final else [spec_of(pl.ANY)] * 2 + [spec_of(pltpu.VMEM)],
+        out_specs=[spec_of(pl.ANY)] * 2 + ([spec_of(pl.ANY)] * 2 if final else [spec_of(pltpu.VMEM)]),
         input_output_aliases={at: 0, at + 1: 1} if final else {},
         cost_estimate=plan.cost(len(items)),
     )
@@ -281,8 +284,12 @@
     def across(array, bits):
         return permuted(array, [(i, i ^ bits) for i in range(n)])
 
-    kv = jnp.concatenate([keys.reshape(rows, width), values.reshape(rows, width)])
-    kv_list = [kv] + [permuted(kv, [(i, i + by) for i in range(n - by)]) for by in range(1, plan.back + 1)]
+    k = keys.reshape(rows, width)
+    v = values.reshape(rows, width)
+    kv_list = []
+    for by in range(1, plan.back + 1):
+        pairs = [(i, (i + by) % n) for i in range(n)]
+        kv_list += [permuted(k, pairs), permuted(v, pairs)]
 
     owners = jnp.arange(n, dtype=jnp.int32)
     match = block_owner[:, None, :] == owners[None, :, None]
@@ -291,7 +298,9 @@
         [own.reshape(1).astype(jnp.int32), jnp.cumsum(doc_lengths).astype(jnp.int32), table.reshape(-1)]
     )
 
-    blocks = pack(plan, meta, query.reshape(rows * heads, width), output_gradient.reshape(rows * heads, width))
+    q, g = (x.reshape(rows * heads, width) for x in (query, output_gradient))
+    *blocks, kv = pack(plan, meta, q, g, k, v)
+    kv_list = [kv, *kv_list]
     first = n // 2
     first_pay, first_grad = attend_first(plan, first, meta, blocks[first], kv_list)
     stay = {first: across(first_pay, first)}
@@ -301,10 +310,8 @@
     late = {x: across(pay, x) for x, pay in zip(sent, out)}
     stay[0] = out[len(sent)]
     keep, to_keep, pass_on, to_pass_on = out[len(items) :]
-    pass_on = (pass_on, across(to_pass_on, 1))
-    terms = (keep, across(to_keep, 1))
-    attended, query_grad, send = place(plan, stay, pass_on)
-    terms += (across(send, 2),)
+    attended, query_grad, send = place(plan, stay, (pass_on, across(to_pass_on, 1)))
+    terms = (keep, across(to_keep, 1), across(send, 2))
     bit = 4
     while bit < n:
         total = sum(term.astype(jnp.float32) for term in terms)

time: 54.2 us -> 51.5 us (0.950)
  starting transfers between devices: 17.4 us -> 14.2 us
  other arithmetic: 1.29 us -> 0.4 us
  waiting for transfers between devices: 23.3 us -> 24.1 us
  local copies, waits for them, and re-layouts: 0.75 us -> 1.43 us
    ppermute x8 -> x10, starting transfers between devices: 17.4 us -> 14.2 us  [permuted(): return lax.ppermute(array, 'ctx', pairs)]
    concatenate x1 -> x0, other arithmetic: 0.89 us -> none  [on_device(): jnp.concatenate([keys.reshape(rows, width), values.reshape(rows, width)])]
    ppermute x8 -> x10, waiting for transfers between devices: 23.3 us -> 24.1 us  [permuted(): return lax.ppermute(array, 'ctx', pairs)]
    unnamed x4, local copies, waits for them, and re-layouts: 0.67 us -> 1.35 us
  transfers between devices with their start and end apart: 8 -> 10, of which waited for: 3 -> 4; matrix products, arithmetic and copies ran while one was open for 1% -> 1% of each run, Pallas kernels for 14% -> 15%
where the time goes in v8:
time: 51.5 us; the launch traced here: 51.3 us
  waiting for transfers between devices  24.1 us (47%)
  starting transfers between devices  14.2 us (28%)
  Pallas kernels  10.4 us (20%)
  local copies, waits for them, and re-layouts  1.43 us (3%)
  between operations  0.7 us (1%)
    ppermute x10, waiting for transfers between devices, permuted(): return lax.ppermute(array, 'ctx', pairs)  24.1 us
    ppermute x10, starting transfers between devices, permuted(): return lax.ppermute(array, 'ctx', pairs)  14.2 us
    pallas_call x5, Pallas kernels, kernel_call(): pl.pallas_call(body, out_shape=out_shape, in_specs=[spec_of(space) for sp...  10.4 us
    unnamed x4, local copies, waits for them, and re-layouts  1.35 us
  transfers between devices with their start and end apart: 10, of which 4 were waited for; matrix products, arithmetic and copies ran while one was open for 1% of the time, Pallas kernels for 15%

profile of v8, /device:TPU:0, one launch (start us, length us, event | category | flops | bytes accessed | tf_op | source)
XLA Modules:
  0.0 51.3 jit_solution(5881074991644400160)
XLA Ops:
  0.6 4.1 %collective-permute-start.2 = (bf16[256,128]{1,0:T(8,128)(2,1)}, bf16[256,128]{1,0:T(8,128)(2,1)S(1)}, u32[]{:S(2)}, u32[]{:S(2)}) collective-permute-start(bf16[256,128]{1,0:T(8,128)(2,1)} %bitcast.19), channel_id=1, source_target_pairs={{0,8},{4,12},{8,0},{12,4},{1,9},{5,13},{9,1},{13,5},{2,10},{6,14},... | collective-permute-start | bytes 196616 | tf_op jit(solution)/shard_map/ppermute | solution.py:282
  4.7 1.6 %collective-permute-start = (bf16[256,128]{1,0:T(8,128)(2,1)}, bf16[256,128]{1,0:T(8,128)(2,1)S(1)}, u32[]{:S(2)}, u32[]{:S(2)}) collective-permute-start(bf16[256,128]{1,0:T(8,128)(2,1)} %bitcast.20), channel_id=1, source_target_pairs={{0,4},{4,8},{8,12},{12,0},{1,5},{5,9},{9,13},{13,1},{2,6},{6,10},{... | collective-permute-start | bytes 196616 | tf_op jit(solution)/shard_map/ppermute | solution.py:282
  6.3 0.3 collective-permute-start.3
  6.6 2.5 %collective-permute-start.1 = (bf16[256,128]{1,0:T(8,128)(2,1)}, bf16[256,128]{1,0:T(8,128)(2,1)S(1)}, u32[]{:S(2)}, u32[]{:S(2)}) collective-permute-start(bf16[256,128]{1,0:T(8,128)(2,1)} %bitcast.23), channel_id=1, source_target_pairs={{0,4},{4,8},{8,12},{12,0},{1,5},{5,9},{9,13},{13,1},{2,6},{6,10},{... | collective-permute-start | bytes 196616 | tf_op jit(solution)/shard_map/ppermute | solution.py:282
  9.1 0.0 copy-start
  9.1 0.7 %copy-done = s32[4,4]{1,0:T(4,128)S(1)} copy-done((s32[4,4]{1,0:T(4,128)S(1)}, s32[4,4]{1,0:T(4,128)}, u32[]{:S(2)}) %copy-start) | copy-done | bytes 88
  9.8 0.1 select_reduce_fusion
  9.9 0.1 reshape.77
  10.0 0.7 %copy-done.1 = s32[8]{0:T(128)S(1)} copy-done((s32[8]{0:T(128)S(1)}, s32[8]{0:T(128)}, u32[]{:S(2)}) %copy-start.1) | copy-done | bytes 56
  10.7 0.2 reduce-window.9
  10.9 0.1 pad_add_fusion.meta
  11.0 1.9 %pack.1 = (bf16[2,512,128]{2,1,0:T(8,128)(2,1)S(1)}, bf16[2,512,128]{2,1,0:T(8,128)(2,1)S(1)}, bf16[2,512,128]{2,1,0:T(8,128)(2,1)S(1)}, bf16[2,512,128]{2,1,0:T(8,128)(2,1)S(1)}, bf16[512,128]{1,0:T(8,128)(2,1)S(1)}) custom-call(s32[25]{0:T(128)S(1)} %pad_add_fusion.meta, bf16[2048,128]{1,0:T(8,128)(2,1)} %bitcast.17, bf16[2048,128]{1,0:T(8,128)(2,1)} %bitcast.18, ...), custom_call_target="tpu_custom_call" | custom-call | tf_op jit(solution)/shard_map/pack/pallas_call | solution.py:176
  12.9 0.0 collective-permute-done.2.refs_3_.refs_7_
  12.9 0.0 collective-permute-done.refs_1_.refs_5_
  12.9 1.6 %collective-permute-done.3.refs_4_.refs_8_ = bf16[256,128]{1,0:T(8,128)(2,1)S(1)} collective-permute-done((bf16[256,128]{1,0:T(8,128)(2,1)}, bf16[256,128]{1,0:T(8,128)(2,1)S(1)}, u32[]{:S(2)}, u32[]{:S(2)}) %collective-permute-start.3) | collective-permute-done | bytes 65568 | tf_op jit(solution)/shard_map/ppermute | solution.py:282
  14.5 0.0 collective-permute-done.1.refs_2_.refs_6_
  14.5 2.0 %attend_first.1 = (bf16[2,512,128]{2,1,0:T(8,128)(2,1)S(1)}, f32[576,256]{1,0:T(8,128)S(1)}) custom-call(s32[25]{0:T(128)S(1)} %pad_add_fusion.meta, bf16[2,512,128]{2,1,0:T(8,128)(2,1)S(1)} %get-tuple-element.28.qg, bf16[512,128]{1,0:T(8,128)(2,1)S(1)} %get-tuple-element.29.refs_0_.refs_4_, bf16[256,128]{1,0:T(8,128)(2,1)S(1)} %collective-permute-done.refs_1_.refs_5_, ...), custom_call_target="tpu_custom_call" | custom-call | flops 4227858432 | bytes 1048576 | tf_op jit(solution)/shard_map/attend_first/pallas_call | solution.py:176
  16.5 2.3 %collective-permute-start.7 = (bf16[2,512,128]{2,1,0:T(8,128)(2,1)S(1)}, bf16[2,512,128]{2,1,0:T(8,128)(2,1)S(1)}, u32[]{:S(2)}, u32[]{:S(2)}) collective-permute-start(bf16[2,512,128]{2,1,0:T(8,128)(2,1)S(1)} %get-tuple-element.35), channel_id=1, source_target_pairs={{0,8},{4,12},{8,0},{12,4},{1,9},{5,13},{9,1},{13,5},{2,10},{6,14},... | collective-permute-start | bytes 786440 | tf_op jit(solution)/shard_map/ppermute | solution.py:282
  18.7 4.8 %attend_last.1 = (bf16[2,512,128]{2,1,0:T(8,128)(2,1)S(1)}, bf16[2,512,128]{2,1,0:T(8,128)(2,1)S(1)}, bf16[2,512,128]{2,1,0:T(8,128)(2,1)S(1)}, f32[1,4,64,256]{...) custom-call(s32[25]{0:T(128)S(1)} %pad_add_fusion.meta, ...), custom_call_target="tpu_custom_call" | custom-call | flops 12683575296 | bytes 3145728 | tf_op jit(solution)/shard_map/attend_last/pallas_call | solution.py:176
  23.5 0.6 %collective-permute-start.8 = (bf16[1,4,64,256]{3,2,1,0:T(8,128)(2,1)S(1)}, bf16[1,4,64,256]{3,2,1,0:T(8,128)(2,1)S(1)}, u32[]{:S(2)}, u32[]{:S(2)}) collective-permute-start(bf16[1,4,64,256]{3,2,1,0:T(8,128)(2,1)S(1)} %get-tuple-element.38), channel_id=1, source_target_pairs={{0,4},{4,0},{8,12},{12,8},{1,5},{5,1},{9,13},{13,9},{2,6},{6,2},{1... | collective-permute-start | bytes 393224 | tf_op jit(solution)/shard_map/ppermute | solution.py:282
  24.1 1.5 %collective-permute-start.6 = (bf16[1,4,64,256]{3,2,1,0:T(8,128)(2,1)S(1)}, bf16[1,4,64,256]{3,2,1,0:T(8,128)(2,1)S(1)}, u32[]{:S(2)}, u32[]{:S(2)}) collective-permute-start(bf16[1,4,64,256]{3,2,1,0:T(8,128)(2,1)S(1)} %get-tuple-element.34), channel_id=1, source_target_pairs={{0,4},{4,0},{8,12},{12,8},{1,5},{5,1},{9,13},{13,9},{2,6},{6,2},{1... | collective-permute-start | bytes 393224 | tf_op jit(solution)/shard_map/ppermute | solution.py:282
  25.6 0.5 %collective-permute-start.4 = (bf16[2,512,128]{2,1,0:T(8,128)(2,1)S(1)}, bf16[2,512,128]{2,1,0:T(8,128)(2,1)S(1)}, u32[]{:S(2)}, u32[]{:S(2)}) collective-permute-start(bf16[2,512,128]{2,1,0:T(8,128)(2,1)S(1)} %get-tuple-element.31), channel_id=1, source_target_pairs={{0,12},{4,8},{8,4},{12,0},{1,13},{5,9},{9,5},{13,1},{2,14},{6,10},... | collective-permute-start | bytes 786440 | tf_op jit(solution)/shard_map/ppermute | solution.py:282
  26.2 0.8 %collective-permute-start.5 = (bf16[2,512,128]{2,1,0:T(8,128)(2,1)S(1)}, bf16[2,512,128]{2,1,0:T(8,128)(2,1)S(1)}, u32[]{:S(2)}, u32[]{:S(2)}) collective-permute-start(bf16[2,512,128]{2,1,0:T(8,128)(2,1)S(1)} %get-tuple-element.32), channel_id=1, source_target_pairs={{0,4},{4,0},{8,12},{12,8},{1,5},{5,1},{9,13},{13,9},{2,6},{6,2},{1... | collective-permute-start | bytes 786440 | tf_op jit(solution)/shard_map/ppermute | solution.py:282
  26.9 12.3 %collective-permute-done.8.refs_3_ = bf16[1,4,64,256]{3,2,1,0:T(8,128)(2,1)S(1)} collective-permute-done((bf16[1,4,64,256]{3,2,1,0:T(8,128)(2,1)S(1)}, bf16[1,4,64,256]{3,2,1,0:T(8,128)(2,1)S(1)}, u32[]{:S(2)}, u32[]{:S(2)}) %collective-permute-start.8) | collective-permute-done | bytes 131104 | tf_op jit(solution)/shard_map/ppermute | solution.py:282
  39.3 0.0 collective-permute-done.7.refs_0_
  39.3 0.8 %place_first.1 = (bf16[2048,128]{1,0:T(8,128)(2,1)}, bf16[2048,128]{1,0:T(8,128)(2,1)}, bf16[1,4,64,256]{3,2,1,0:T(8,128)(2,1)S(1)}) custom-call(bf16[2,512,128]{2,1,0:T(8,128)(2,1)S(1)} %collective-permute-done.7.refs_0_, bf16[2,512,128]{2,1,0:T(8,128)(2,1)S(1)} %get-tuple-element.36.refs_1_, f32[1,4,64,256]{3,2,1,0:T(8,128)S(1)} %get-tuple-element.37.refs_2_, ...), custom_call_target="tpu_custom_call" | custom-call | flops 8455716864 | bytes 2097152 | tf_op jit(solution)/shard_map/place_first/pallas_call | solution.py:176
  40.1 0.1 collective-permute-start.9
  40.2 1.9 %collective-permute-done.6 = bf16[1,4,64,256]{3,2,1,0:T(8,128)(2,1)S(1)} collective-permute-done((bf16[1,4,64,256]{3,2,1,0:T(8,128)(2,1)S(1)}, bf16[1,4,64,256]{3,2,1,0:T(8,128)(2,1)S(1)}, u32[]{:S(2)}, u32[]{:S(2)}) %collective-permute-start.6) | collective-permute-done | bytes 131104 | tf_op jit(solution)/shard_map/ppermute | solution.py:282
  42.1 0.0 collective-permute-done.4.refs_0_
  42.1 8.3 %collective-permute-done.5.refs_1_ = bf16[2,512,128]{2,1,0:T(8,128)(2,1)S(1)} collective-permute-done((bf16[2,512,128]{2,1,0:T(8,128)(2,1)S(1)}, bf16[2,512,128]{2,1,0:T(8,128)(2,1)S(1)}, u32[]{:S(2)}, u32[]{:S(2)}) %collective-permute-start.5) | collective-permute-done | bytes 262176 | tf_op jit(solution)/shard_map/ppermute | solution.py:282
  50.4 0.0 collective-permute-done.9
  50.4 0.9 %place_last.1 = (bf16[2048,128]{1,0:T(8,128)(2,1)}, bf16[2048,128]{1,0:T(8,128)(2,1)}, bf16[256,128]{1,0:T(8,128)(2,1)}, bf16[256,128]{1,0:T(8,128)(2,1)}) custom-call(bf16[2,512,128]{2,1,0:T(8,128)(2,1)S(1)} %collective-permute-done.4.refs_0_, ...), custom_call_target="tpu_custom_call", output_to_operand_aliasing={{0}: (5, {}), {1}: (6, {})} | custom-call | flops 8455716864 | bytes 2097152 | tf_op jit(solution)/shard_map/place_last/pallas_call | solution.py:176
  (1 shorter events, 0.0 us)
Async XLA Ops:
  0.6 12.3 %collective-permute-start.2 = (bf16[256,128]{1,0:T(8,128)(2,1)}, bf16[256,128]{1,0:T(8,128)(2,1)S(1)}, u32[]{:S(2)}, u32[]{:S(2)}) collective-permute-start(bf16[256,128]{1,0:T(8,128)(2,1)} %bitcast.19), channel_id=1, source_target_pairs={{0,8},{4,12},{8,0},{12,4},{1,9},{5,13},{9,1},{13,5},{2,10},{6,14},... | collective-permute-start | bytes 196616 | tf_op jit(solution)/shard_map/ppermute | solution.py:282
  4.7 8.2 %collective-permute-start = (bf16[256,128]{1,0:T(8,128)(2,1)}, bf16[256,128]{1,0:T(8,128)(2,1)S(1)}, u32[]{:S(2)}, u32[]{:S(2)}) collective-permute-start(bf16[256,128]{1,0:T(8,128)(2,1)} %bitcast.20), channel_id=1, source_target_pairs={{0,4},{4,8},{8,12},{12,0},{1,5},{5,9},{9,13},{13,1},{2,6},{6,10},{... | collective-permute-start | bytes 196616 | tf_op jit(solution)/shard_map/ppermute | solution.py:282
  6.3 8.2 %collective-permute-start.3 = (bf16[256,128]{1,0:T(8,128)(2,1)}, bf16[256,128]{1,0:T(8,128)(2,1)S(1)}, u32[]{:S(2)}, u32[]{:S(2)}) collective-permute-start(bf16[256,128]{1,0:T(8,128)(2,1)} %bitcast.22), channel_id=1, source_target_pairs={{0,8},{4,12},{8,0},{12,4},{1,9},{5,13},{9,1},{13,5},{2,10},{6,14},... | collective-permute-start | bytes 196616 | tf_op jit(solution)/shard_map/ppermute | solution.py:282
  6.6 7.9 %collective-permute-start.1 = (bf16[256,128]{1,0:T(8,128)(2,1)}, bf16[256,128]{1,0:T(8,128)(2,1)S(1)}, u32[]{:S(2)}, u32[]{:S(2)}) collective-permute-start(bf16[256,128]{1,0:T(8,128)(2,1)} %bitcast.23), channel_id=1, source_target_pairs={{0,4},{4,8},{8,12},{12,0},{1,5},{5,9},{9,13},{13,1},{2,6},{6,10},{... | collective-permute-start | bytes 196616 | tf_op jit(solution)/shard_map/ppermute | solution.py:282
  9.1 0.7 %copy-start = (s32[4,4]{1,0:T(4,128)S(1)}, s32[4,4]{1,0:T(4,128)}, u32[]{:S(2)}) copy-start(s32[4,4]{1,0:T(4,128)} %param.11) | copy-start | bytes 196
  10.0 0.7 %copy-start.1 = (s32[8]{0:T(128)S(1)}, s32[8]{0:T(128)}, u32[]{:S(2)}) copy-start(s32[8]{0:T(128)} %param.10) | copy-start | bytes 100
  16.5 22.8 %collective-permute-start.7 = (bf16[2,512,128]{2,1,0:T(8,128)(2,1)S(1)}, bf16[2,512,128]{2,1,0:T(8,128)(2,1)S(1)}, u32[]{:S(2)}, u32[]{:S(2)}) collective-permute-start(bf16[2,512,128]{2,1,0:T(8,128)(2,1)S(1)} %get-tuple-element.35), channel_id=1, source_target_pairs={{0,8},{4,12},{8,0},{12,4},{1,9},{5,13},{9,1},{13,5},{2,10},{6,14},... | collective-permute-start | bytes 786440 | tf_op jit(solution)/shard_map/ppermute | solution.py:282
  23.5 15.7 %collective-permute-start.8 = (bf16[1,4,64,256]{3,2,1,0:T(8,128)(2,1)S(1)}, bf16[1,4,64,256]{3,2,1,0:T(8,128)(2,1)S(1)}, u32[]{:S(2)}, u32[]{:S(2)}) collective-permute-start(bf16[1,4,64,256]{3,2,1,0:T(8,128)(2,1)S(1)} %get-tuple-element.38), channel_id=1, source_target_pairs={{0,4},{4,0},{8,12},{12,8},{1,5},{5,1},{9,13},{13,9},{2,6},{6,2},{1... | collective-permute-start | bytes 393224 | tf_op jit(solution)/shard_map/ppermute | solution.py:282
  24.1 18.0 %collective-permute-start.6 = (bf16[1,4,64,256]{3,2,1,0:T(8,128)(2,1)S(1)}, bf16[1,4,64,256]{3,2,1,0:T(8,128)(2,1)S(1)}, u32[]{:S(2)}, u32[]{:S(2)}) collective-permute-start(bf16[1,4,64,256]{3,2,1,0:T(8,128)(2,1)S(1)} %get-tuple-element.34), channel_id=1, source_target_pairs={{0,4},{4,0},{8,12},{12,8},{1,5},{5,1},{9,13},{13,9},{2,6},{6,2},{1... | collective-permute-start | bytes 393224 | tf_op jit(solution)/shard_map/ppermute | solution.py:282
  25.6 16.4 %collective-permute-start.4 = (bf16[2,512,128]{2,1,0:T(8,128)(2,1)S(1)}, bf16[2,512,128]{2,1,0:T(8,128)(2,1)S(1)}, u32[]{:S(2)}, u32[]{:S(2)}) collective-permute-start(bf16[2,512,128]{2,1,0:T(8,128)(2,1)S(1)} %get-tuple-element.31), channel_id=1, source_target_pairs={{0,12},{4,8},{8,4},{12,0},{1,13},{5,9},{9,5},{13,1},{2,14},{6,10},... | collective-permute-start | bytes 786440 | tf_op jit(solution)/shard_map/ppermute | solution.py:282
  26.2 24.2 %collective-permute-start.5 = (bf16[2,512,128]{2,1,0:T(8,128)(2,1)S(1)}, bf16[2,512,128]{2,1,0:T(8,128)(2,1)S(1)}, u32[]{:S(2)}, u32[]{:S(2)}) collective-permute-start(bf16[2,512,128]{2,1,0:T(8,128)(2,1)S(1)} %get-tuple-element.32), channel_id=1, source_target_pairs={{0,4},{4,0},{8,12},{12,8},{1,5},{5,1},{9,13},{13,9},{2,6},{6,2},{1... | collective-permute-start | bytes 786440 | tf_op jit(solution)/shard_map/ppermute | solution.py:282
  40.1 10.3 %collective-permute-start.9 = (bf16[1,4,64,256]{3,2,1,0:T(8,128)(2,1)S(1)}, bf16[1,4,64,256]{3,2,1,0:T(8,128)(2,1)S(1)}, u32[]{:S(2)}, u32[]{:S(2)}) collective-permute-start(bf16[1,4,64,256]{3,2,1,0:T(8,128)(2,1)S(1)} %get-tuple-element.39), channel_id=1, source_target_pairs={{0,8},{4,12},{8,0},{12,4},{1,9},{5,13},{9,1},{13,5},{2,10},{6,14},... | collective-permute-start | bytes 393224 | tf_op jit(solution)/shard_map/ppermute | solution.py:282

commit v9 on v8

--- a/solution.py
+++ b/solution.py
@@ -156,13 +156,25 @@
 
     @pl.when(step == len(items) - 1)
     def _():
+        def put_part(key_range, entry, part):
+            @pl.when(key_range < n // 2)
+            def _():
+                grad_refs[2][entry, key_range] = part.astype(jnp.bfloat16)
+
+            @pl.when(key_range >= n // 2)
+            def _():
+                grad_refs[3][entry, key_range - n // 2] = part.astype(jnp.bfloat16)
+
         def of_range(key_range, carry):
             at = lax.rem(key_range - own + plan.back + n, n) * rows
             for apart in range(n):
                 slot = plan.slot(meta, key_range, own ^ apart)
                 part = acc[pl.ds(pl.multiple_of(at + slot * block, block), block), :]
-                to = grad_refs[apart % 4]
-                to[apart // 4, key_range] = part.astype(to.dtype)
+                if apart % 2 == 0:
+                    to = grad_refs[apart % 4 // 2]
+                    to[apart // 4, key_range] = part
+                else:
+                    put_part(key_range, apart // 2, part)
             return carry
 
         lax.fori_loop(0, n, of_range, 0)
@@ -212,9 +224,10 @@
 def attend_last(plan, first, items, meta, qg_list, first_grad, kv_list):
     n = plan.n
     window = pltpu.VMEM((plan.window_ranges * plan.rows, plan.width), jnp.bfloat16)
-    grads = (n // 4, n, plan.block, 2 * plan.width)
+    keep = jax.ShapeDtypeStruct((n // 4, n, plan.block, 2 * plan.width), jnp.float32)
+    send = jax.ShapeDtypeStruct((n // 2, n // 2, plan.block, 2 * plan.width), jnp.bfloat16)
     out_shape = [jax.ShapeDtypeStruct((2, plan.cols, plan.width), jnp.bfloat16)] * len(items)
-    out_shape += [jax.ShapeDtypeStruct(grads, jnp.bfloat16 if apart % 2 else jnp.float32) for apart in range(4)]
+    out_shape += [keep, keep, send, send]
     operands = (meta, *qg_list, first_grad, *kv_list)
     return kernel_call(
         functools.partial(last_kernel, plan, first, items), "attend_last", operands,
@@ -231,7 +244,7 @@
     if final:
         grads, (_, _, attended, query_grad, key_grad, value_grad, sums, sems, sum_sems) = refs[:-9], refs[-9:]
     else:
-        grads, (attended, query_grad, send, sems) = refs[:-4], refs[-4:]
+        grads, (attended, query_grad, send, kept, sems) = refs[:-5], refs[-5:]
     copies = []
     for i, item in enumerate(items):
         to = pl.ds(pl.multiple_of((own ^ item) * cols, cols), cols)
@@ -239,15 +252,23 @@
         copies.append(pltpu.make_async_copy(pay_refs[i].at[1], query_grad.at[to, :], sems.at[i, 1]))
     for copy in copies:
         copy.start()
-    total = sum(grad[...].astype(jnp.float32) for grad in grads).astype(jnp.bfloat16)
     if final:
+        total = sum(grad[...].astype(jnp.float32) for grad in grads).astype(jnp.bfloat16)
         sums[0] = total[:, :width]
         sums[1] = total[:, width:]
         for i, ref in enumerate((key_grad, value_grad)):
             copies.append(pltpu.make_async_copy(sums.at[i], ref, sum_sems.at[i]))
             copies[-1].start()
     else:
-        send[...] = total
+        pass_on, keep, *arrived = grads
+        for entry in range(n // 2):
+            for half, ref in enumerate(arrived):
+                ranges = pl.ds(half * (n // 2), n // 2)
+                total = (keep, pass_on)[entry % 2][entry // 2, ranges] + ref[entry].astype(jnp.float32)
+                if entry % 2:
+                    send[entry // 2, ranges] = total.astype(jnp.bfloat16)
+                else:
+                    kept[entry // 2, ranges] = total
     for copy in copies:
         copy.wait()
 
@@ -265,8 +286,8 @@
         functools.partial(place_kernel, plan, items, final), "place_last" if final else "place_first",
         (*payloads.values(), *grads, *filled),
         [pl.ANY] * len(items) + [pltpu.VMEM] * len(grads) + [pl.ANY] * len(filled),
-        [big, big] + ([small, small] if final else [jax.ShapeDtypeStruct(grads[0].shape, jnp.bfloat16)]), scratch,
-        out_specs=[spec_of(pl.ANY)] * 2 + ([spec_of(pl.ANY)] * 2 if final else [spec_of(pltpu.VMEM)]),
+        [big, big] + ([small, small] if final else [jax.ShapeDtypeStruct(grads[0].shape, t) for t in (jnp.bfloat16, jnp.float32)]), scratch,
+        out_specs=[spec_of(pl.ANY)] * 2 + [spec_of(pl.ANY if final else pltpu.VMEM)] * 2,
         input_output_aliases={at: 0, at + 1: 1} if final else {},
         cost_estimate=plan.cost(len(items)),
     )
@@ -304,14 +325,15 @@
     first = n // 2
     first_pay, first_grad = attend_first(plan, first, meta, blocks[first], kv_list)
     stay = {first: across(first_pay, first)}
-    sent = [x for x in range(n - 1, 0, -1) if x != first]
+    sent = [x for x in range(1, n) if x != first]
     items = (*sent, 0)
     out = attend_last(plan, first, items, meta, [blocks[x] for x in items], first_grad, kv_list)
     late = {x: across(pay, x) for x, pay in zip(sent, out)}
     stay[0] = out[len(sent)]
-    keep, to_keep, pass_on, to_pass_on = out[len(items) :]
-    attended, query_grad, send = place(plan, stay, (pass_on, across(to_pass_on, 1)))
-    terms = (keep, across(to_keep, 1), across(send, 2))
+    keep, pass_on, lower, upper = out[len(items) :]
+    upper = permuted(upper, [(i, i ^ 1) for i in range(n // 2, n)])
+    attended, query_grad, send, keep = place(plan, stay, (pass_on, keep, across(lower, 1), upper))
+    terms = (keep, across(send, 2))
     bit = 4
     while bit < n:
         total = sum(term.astype(jnp.float32) for term in terms)

time: 51.5 us -> 49.6 us (0.963)
  waiting for transfers between devices: 24.1 us -> 17.1 us
  starting transfers between devices: 14.2 us -> 19.3 us
    ppermute x10, waiting for transfers between devices: 24.1 us -> 17.1 us  [permuted(): return lax.ppermute(array, 'ctx', pairs)]
    ppermute x10, starting transfers between devices: 14.2 us -> 19.3 us  [permuted(): return lax.ppermute(array, 'ctx', pairs)]
where the time goes in v9:
time: 49.6 us; the launch traced here: 49.5 us
  starting transfers between devices  19.3 us (39%)
  waiting for transfers between devices  17.1 us (34%)
  Pallas kernels  10.5 us (21%)
  local copies, waits for them, and re-layouts  1.43 us (3%)
  between operations  0.7 us (1%)
    ppermute x10, starting transfers between devices, permuted(): return lax.ppermute(array, 'ctx', pairs)  19.3 us
    ppermute x10, waiting for transfers between devices, permuted(): return lax.ppermute(array, 'ctx', pairs)  17.1 us
    pallas_call x5, Pallas kernels, kernel_call(): pl.pallas_call(body, out_shape=out_shape, in_specs=[spec_of(space) for sp...  10.5 us
    unnamed x4, local copies, waits for them, and re-layouts  1.35 us
  transfers between devices with their start and end apart: 10, of which 4 were waited for; matrix products, arithmetic and copies ran while one was open for 1% of the time, Pallas kernels for 15%

profile of v9, /device:TPU:0, one launch (start us, length us, event | category | flops | bytes accessed | tf_op | source)
XLA Modules:
  0.0 49.5 jit_solution(17917272966762360970)
XLA Ops:
  0.6 4.1 %collective-permute-start.2 = (bf16[256,128]{1,0:T(8,128)(2,1)}, bf16[256,128]{1,0:T(8,128)(2,1)S(1)}, u32[]{:S(2)}, u32[]{:S(2)}) collective-permute-start(bf16[256,128]{1,0:T(8,128)(2,1)} %bitcast.17), channel_id=1, source_target_pairs={{0,8},{4,12},{8,0},{12,4},{1,9},{5,13},{9,1},{13,5},{2,10},{6,14},... | collective-permute-start | bytes 196616 | tf_op jit(solution)/shard_map/ppermute | solution.py:303
  4.7 1.6 %collective-permute-start = (bf16[256,128]{1,0:T(8,128)(2,1)}, bf16[256,128]{1,0:T(8,128)(2,1)S(1)}, u32[]{:S(2)}, u32[]{:S(2)}) collective-permute-start(bf16[256,128]{1,0:T(8,128)(2,1)} %bitcast.18), channel_id=1, source_target_pairs={{0,4},{4,8},{8,12},{12,0},{1,5},{5,9},{9,13},{13,1},{2,6},{6,10},{... | collective-permute-start | bytes 196616 | tf_op jit(solution)/shard_map/ppermute | solution.py:303
  6.3 0.3 collective-permute-start.3
  6.6 2.5 %collective-permute-start.1 = (bf16[256,128]{1,0:T(8,128)(2,1)}, bf16[256,128]{1,0:T(8,128)(2,1)S(1)}, u32[]{:S(2)}, u32[]{:S(2)}) collective-permute-start(bf16[256,128]{1,0:T(8,128)(2,1)} %bitcast.21), channel_id=1, source_target_pairs={{0,4},{4,8},{8,12},{12,0},{1,5},{5,9},{9,13},{13,1},{2,6},{6,10},{... | collective-permute-start | bytes 196616 | tf_op jit(solution)/shard_map/ppermute | solution.py:303
  9.1 0.7 %copy-done = s32[4,4]{1,0:T(4,128)S(1)} copy-done((s32[4,4]{1,0:T(4,128)S(1)}, s32[4,4]{1,0:T(4,128)}, u32[]{:S(2)}) %copy-start) | copy-done | bytes 88
  9.8 0.1 select_reduce_fusion
  9.9 0.1 reshape.74
  10.0 0.0 copy-start.1
  10.0 0.7 %copy-done.1 = s32[8]{0:T(128)S(1)} copy-done((s32[8]{0:T(128)S(1)}, s32[8]{0:T(128)}, u32[]{:S(2)}) %copy-start.1) | copy-done | bytes 56
  10.7 0.2 reduce-window.9
  10.9 0.1 pad_add_fusion.meta
  11.0 1.9 %pack.1 = (bf16[2,512,128]{2,1,0:T(8,128)(2,1)S(1)}, bf16[2,512,128]{2,1,0:T(8,128)(2,1)S(1)}, bf16[2,512,128]{2,1,0:T(8,128)(2,1)S(1)}, bf16[2,512,128]{2,1,0:T(8,128)(2,1)S(1)}, bf16[512,128]{1,0:T(8,128)(2,1)S(1)}) custom-call(s32[25]{0:T(128)S(1)} %pad_add_fusion.meta, bf16[2048,128]{1,0:T(8,128)(2,1)} %bitcast.15, bf16[2048,128]{1,0:T(8,128)(2,1)} %bitcast.16, ...), custom_call_target="tpu_custom_call" | custom-call | tf_op jit(solution)/shard_map/pack/pallas_call | solution.py:188
  12.9 0.0 collective-permute-done.2.refs_3_.refs_7_
  12.9 0.0 collective-permute-done.refs_1_.refs_5_
  12.9 1.6 %collective-permute-done.3.refs_4_.refs_8_ = bf16[256,128]{1,0:T(8,128)(2,1)S(1)} collective-permute-done((bf16[256,128]{1,0:T(8,128)(2,1)}, bf16[256,128]{1,0:T(8,128)(2,1)S(1)}, u32[]{:S(2)}, u32[]{:S(2)}) %collective-permute-start.3) | collective-permute-done | bytes 65568 | tf_op jit(solution)/shard_map/ppermute | solution.py:303
  14.5 0.0 collective-permute-done.1.refs_2_.refs_6_
  14.5 2.0 %attend_first.1 = (bf16[2,512,128]{2,1,0:T(8,128)(2,1)S(1)}, f32[576,256]{1,0:T(8,128)S(1)}) custom-call(s32[25]{0:T(128)S(1)} %pad_add_fusion.meta, bf16[2,512,128]{2,1,0:T(8,128)(2,1)S(1)} %get-tuple-element.29.qg, bf16[512,128]{1,0:T(8,128)(2,1)S(1)} %get-tuple-element.30.refs_0_.refs_4_, bf16[256,128]{1,0:T(8,128)(2,1)S(1)} %collective-permute-done.refs_1_.refs_5_, ...), custom_call_target="tpu_custom_call" | custom-call | flops 4227858432 | bytes 1048576 | tf_op jit(solution)/shard_map/attend_first/pallas_call | solution.py:188
  16.5 2.3 %collective-permute-start.6 = (bf16[2,512,128]{2,1,0:T(8,128)(2,1)S(1)}, bf16[2,512,128]{2,1,0:T(8,128)(2,1)S(1)}, u32[]{:S(2)}, u32[]{:S(2)}) collective-permute-start(bf16[2,512,128]{2,1,0:T(8,128)(2,1)S(1)} %get-tuple-element.34), channel_id=1, source_target_pairs={{0,8},{4,12},{8,0},{12,4},{1,9},{5,13},{9,1},{13,5},{2,10},{6,14},... | collective-permute-start | bytes 786440 | tf_op jit(solution)/shard_map/ppermute | solution.py:303
  18.7 4.9 %attend_last.1 = (bf16[2,512,128]{2,1,0:T(8,128)(2,1)S(1)}, bf16[2,512,128]{2,1,0:T(8,128)(2,1)S(1)}, bf16[2,512,128]{2,1,0:T(8,128)(2,1)S(1)}, f32[1,4,64,256]{...) custom-call(s32[25]{0:T(128)S(1)} %pad_add_fusion.meta, ...), custom_call_target="tpu_custom_call" | custom-call | flops 12683575296 | bytes 3145728 | tf_op jit(solution)/shard_map/attend_last/pallas_call | solution.py:188
  23.6 0.6 %collective-permute-start.7 = (bf16[2,2,64,256]{3,2,1,0:T(8,128)(2,1)S(1)}, bf16[2,2,64,256]{3,2,1,0:T(8,128)(2,1)S(1)}, u32[]{:S(2)}, u32[]{:S(2)}) collective-permute-start(bf16[2,2,64,256]{3,2,1,0:T(8,128)(2,1)S(1)} %get-tuple-element.38), channel_id=1, source_target_pairs={{0,4},{4,0},{8,12},{12,8},{1,5},{5,1},{9,13},{13,9},{2,6},{6,2},{1... | collective-permute-start | bytes 393224 | tf_op jit(solution)/shard_map/ppermute | solution.py:303
  24.2 0.7 %collective-permute-start.8 = (bf16[2,2,64,256]{3,2,1,0:T(8,128)(2,1)S(1)}, bf16[2,2,64,256]{3,2,1,0:T(8,128)(2,1)S(1)}, u32[]{:S(2)}, u32[]{:S(2)}) collective-permute-start(bf16[2,2,64,256]{3,2,1,0:T(8,128)(2,1)S(1)} %get-tuple-element.39), channel_id=1, source_target_pairs={{8,12},{12,8},{9,13},{13,9},{10,14},{14,10},{11,15},{15,11},{24,28... | collective-permute-start | bytes 393224 | tf_op jit(solution)/shard_map/ppermute | solution.py:303
  24.9 1.6 %collective-permute-start.4 = (bf16[2,512,128]{2,1,0:T(8,128)(2,1)S(1)}, bf16[2,512,128]{2,1,0:T(8,128)(2,1)S(1)}, u32[]{:S(2)}, u32[]{:S(2)}) collective-permute-start(bf16[2,512,128]{2,1,0:T(8,128)(2,1)S(1)} %get-tuple-element.32), channel_id=1, source_target_pairs={{0,4},{4,0},{8,12},{12,8},{1,5},{5,1},{9,13},{13,9},{2,6},{6,2},{1... | collective-permute-start | bytes 786440 | tf_op jit(solution)/shard_map/ppermute | solution.py:303
  26.4 3.4 %collective-permute-start.5 = (bf16[2,512,128]{2,1,0:T(8,128)(2,1)S(1)}, bf16[2,512,128]{2,1,0:T(8,128)(2,1)S(1)}, u32[]{:S(2)}, u32[]{:S(2)}) collective-permute-start(bf16[2,512,128]{2,1,0:T(8,128)(2,1)S(1)} %get-tuple-element.33), channel_id=1, source_target_pairs={{0,12},{4,8},{8,4},{12,0},{1,13},{5,9},{9,5},{13,1},{2,14},{6,10},... | collective-permute-start | bytes 786440 | tf_op jit(solution)/shard_map/ppermute | solution.py:303
  29.9 3.8 %collective-permute-done.7.refs_4_ = bf16[2,2,64,256]{3,2,1,0:T(8,128)(2,1)S(1)} collective-permute-done((bf16[2,2,64,256]{3,2,1,0:T(8,128)(2,1)S(1)}, bf16[2,2,64,256]{3,2,1,0:T(8,128)(2,1)S(1)}, u32[]{:S(2)}, u32[]{:S(2)}) %collective-permute-start.7) | collective-permute-done | bytes 131104 | tf_op jit(solution)/shard_map/ppermute | solution.py:303
  33.6 0.0 collective-permute-done.8.refs_5_
  33.7 0.0 collective-permute-done.6.refs_0_
  33.7 0.8 %place_first.1 = (bf16[2048,128]{1,0:T(8,128)(2,1)}, bf16[2048,128]{1,0:T(8,128)(2,1)}, bf16[1,4,64,256]{3,2,1,0:T(8,128)(2,1)S(1)}, f32[1,4,64,256]{3,2,1,0:T(8,128)S(1)}) custom-call(bf16[2,512,128]{2,1,0:T(8,128)(2,1)S(1)} %collective-permute-done.6.refs_0_, bf16[2,512,128]{2,1,0:T(8,128)(2,1)S(1)} %get-tuple-element.35.refs_1_, ...), custom_call_target="tpu_custom_call" | custom-call | flops 8455716864 | bytes 2097152 | tf_op jit(solution)/shard_map/place_first/pallas_call | solution.py:188
  34.5 2.3 %collective-permute-start.9 = (bf16[1,4,64,256]{3,2,1,0:T(8,128)(2,1)S(1)}, bf16[1,4,64,256]{3,2,1,0:T(8,128)(2,1)S(1)}, u32[]{:S(2)}, u32[]{:S(2)}) collective-permute-start(bf16[1,4,64,256]{3,2,1,0:T(8,128)(2,1)S(1)} %get-tuple-element.41), channel_id=1, source_target_pairs={{0,8},{4,12},{8,0},{12,4},{1,9},{5,13},{9,1},{13,5},{2,10},{6,14},... | collective-permute-start | bytes 393224 | tf_op jit(solution)/shard_map/ppermute | solution.py:303
  36.8 8.3 %collective-permute-done.4.refs_0_ = bf16[2,512,128]{2,1,0:T(8,128)(2,1)S(1)} collective-permute-done((bf16[2,512,128]{2,1,0:T(8,128)(2,1)S(1)}, bf16[2,512,128]{2,1,0:T(8,128)(2,1)S(1)}, u32[]{:S(2)}, u32[]{:S(2)}) %collective-permute-start.4) | collective-permute-done | bytes 262176 | tf_op jit(solution)/shard_map/ppermute | solution.py:303
  45.1 0.0 collective-permute-done.5.refs_1_
  45.1 3.4 %collective-permute-done.9 = bf16[1,4,64,256]{3,2,1,0:T(8,128)(2,1)S(1)} collective-permute-done((bf16[1,4,64,256]{3,2,1,0:T(8,128)(2,1)S(1)}, bf16[1,4,64,256]{3,2,1,0:T(8,128)(2,1)S(1)}, u32[]{:S(2)}, u32[]{:S(2)}) %collective-permute-start.9) | collective-permute-done | bytes 131104 | tf_op jit(solution)/shard_map/ppermute | solution.py:303
  48.6 0.9 %place_last.1 = (bf16[2048,128]{1,0:T(8,128)(2,1)}, bf16[2048,128]{1,0:T(8,128)(2,1)}, bf16[256,128]{1,0:T(8,128)(2,1)}, bf16[256,128]{1,0:T(8,128)(2,1)}) custom-call(bf16[2,512,128]{2,1,0:T(8,128)(2,1)S(1)} %collective-permute-done.4.refs_0_, ...), custom_call_target="tpu_custom_call", output_to_operand_aliasing={{0}: (4, {}), {1}: (5, {})} | custom-call | flops 8455716864 | bytes 2097152 | tf_op jit(solution)/shard_map/place_last/pallas_call | solution.py:188
  (1 shorter events, 0.0 us)
Async XLA Ops:
  0.6 12.3 %collective-permute-start.2 = (bf16[256,128]{1,0:T(8,128)(2,1)}, bf16[256,128]{1,0:T(8,128)(2,1)S(1)}, u32[]{:S(2)}, u32[]{:S(2)}) collective-permute-start(bf16[256,128]{1,0:T(8,128)(2,1)} %bitcast.17), channel_id=1, source_target_pairs={{0,8},{4,12},{8,0},{12,4},{1,9},{5,13},{9,1},{13,5},{2,10},{6,14},... | collective-permute-start | bytes 196616 | tf_op jit(solution)/shard_map/ppermute | solution.py:303
  4.7 8.2 %collective-permute-start = (bf16[256,128]{1,0:T(8,128)(2,1)}, bf16[256,128]{1,0:T(8,128)(2,1)S(1)}, u32[]{:S(2)}, u32[]{:S(2)}) collective-permute-start(bf16[256,128]{1,0:T(8,128)(2,1)} %bitcast.18), channel_id=1, source_target_pairs={{0,4},{4,8},{8,12},{12,0},{1,5},{5,9},{9,13},{13,1},{2,6},{6,10},{... | collective-permute-start | bytes 196616 | tf_op jit(solution)/shard_map/ppermute | solution.py:303
  6.3 8.2 %collective-permute-start.3 = (bf16[256,128]{1,0:T(8,128)(2,1)}, bf16[256,128]{1,0:T(8,128)(2,1)S(1)}, u32[]{:S(2)}, u32[]{:S(2)}) collective-permute-start(bf16[256,128]{1,0:T(8,128)(2,1)} %bitcast.20), channel_id=1, source_target_pairs={{0,8},{4,12},{8,0},{12,4},{1,9},{5,13},{9,1},{13,5},{2,10},{6,14},... | collective-permute-start | bytes 196616 | tf_op jit(solution)/shard_map/ppermute | solution.py:303
  6.6 7.9 %collective-permute-start.1 = (bf16[256,128]{1,0:T(8,128)(2,1)}, bf16[256,128]{1,0:T(8,128)(2,1)S(1)}, u32[]{:S(2)}, u32[]{:S(2)}) collective-permute-start(bf16[256,128]{1,0:T(8,128)(2,1)} %bitcast.21), channel_id=1, source_target_pairs={{0,4},{4,8},{8,12},{12,0},{1,5},{5,9},{9,13},{13,1},{2,6},{6,10},{... | collective-permute-start | bytes 196616 | tf_op jit(solution)/shard_map/ppermute | solution.py:303
  9.1 0.7 %copy-start = (s32[4,4]{1,0:T(4,128)S(1)}, s32[4,4]{1,0:T(4,128)}, u32[]{:S(2)}) copy-start(s32[4,4]{1,0:T(4,128)} %param.11) | copy-start | bytes 196
  10.0 0.7 %copy-start.1 = (s32[8]{0:T(128)S(1)}, s32[8]{0:T(128)}, u32[]{:S(2)}) copy-start(s32[8]{0:T(128)} %param.10) | copy-start | bytes 100
  16.5 17.2 %collective-permute-start.6 = (bf16[2,512,128]{2,1,0:T(8,128)(2,1)S(1)}, bf16[2,512,128]{2,1,0:T(8,128)(2,1)S(1)}, u32[]{:S(2)}, u32[]{:S(2)}) collective-permute-start(bf16[2,512,128]{2,1,0:T(8,128)(2,1)S(1)} %get-tuple-element.34), channel_id=1, source_target_pairs={{0,8},{4,12},{8,0},{12,4},{1,9},{5,13},{9,1},{13,5},{2,10},{6,14},... | collective-permute-start | bytes 786440 | tf_op jit(solution)/shard_map/ppermute | solution.py:303
  23.6 10.0 %collective-permute-start.7 = (bf16[2,2,64,256]{3,2,1,0:T(8,128)(2,1)S(1)}, bf16[2,2,64,256]{3,2,1,0:T(8,128)(2,1)S(1)}, u32[]{:S(2)}, u32[]{:S(2)}) collective-permute-start(bf16[2,2,64,256]{3,2,1,0:T(8,128)(2,1)S(1)} %get-tuple-element.38), channel_id=1, source_target_pairs={{0,4},{4,0},{8,12},{12,8},{1,5},{5,1},{9,13},{13,9},{2,6},{6,2},{1... | collective-permute-start | bytes 393224 | tf_op jit(solution)/shard_map/ppermute | solution.py:303
  24.2 9.4 %collective-permute-start.8 = (bf16[2,2,64,256]{3,2,1,0:T(8,128)(2,1)S(1)}, bf16[2,2,64,256]{3,2,1,0:T(8,128)(2,1)S(1)}, u32[]{:S(2)}, u32[]{:S(2)}) collective-permute-start(bf16[2,2,64,256]{3,2,1,0:T(8,128)(2,1)S(1)} %get-tuple-element.39), channel_id=1, source_target_pairs={{8,12},{12,8},{9,13},{13,9},{10,14},{14,10},{11,15},{15,11},{24,28... | collective-permute-start | bytes 393224 | tf_op jit(solution)/shard_map/ppermute | solution.py:303
  24.9 20.3 %collective-permute-start.4 = (bf16[2,512,128]{2,1,0:T(8,128)(2,1)S(1)}, bf16[2,512,128]{2,1,0:T(8,128)(2,1)S(1)}, u32[]{:S(2)}, u32[]{:S(2)}) collective-permute-start(bf16[2,512,128]{2,1,0:T(8,128)(2,1)S(1)} %get-tuple-element.32), channel_id=1, source_target_pairs={{0,4},{4,0},{8,12},{12,8},{1,5},{5,1},{9,13},{13,9},{2,6},{6,2},{1... | collective-permute-start | bytes 786440 | tf_op jit(solution)/shard_map/ppermute | solution.py:303
  26.4 18.7 %collective-permute-start.5 = (bf16[2,512,128]{2,1,0:T(8,128)(2,1)S(1)}, bf16[2,512,128]{2,1,0:T(8,128)(2,1)S(1)}, u32[]{:S(2)}, u32[]{:S(2)}) collective-permute-start(bf16[2,512,128]{2,1,0:T(8,128)(2,1)S(1)} %get-tuple-element.33), channel_id=1, source_target_pairs={{0,12},{4,8},{8,4},{12,0},{1,13},{5,9},{9,5},{13,1},{2,14},{6,10},... | collective-permute-start | bytes 786440 | tf_op jit(solution)/shard_map/ppermute | solution.py:303
  34.5 14.1 %collective-permute-start.9 = (bf16[1,4,64,256]{3,2,1,0:T(8,128)(2,1)S(1)}, bf16[1,4,64,256]{3,2,1,0:T(8,128)(2,1)S(1)}, u32[]{:S(2)}, u32[]{:S(2)}) collective-permute-start(bf16[1,4,64,256]{3,2,1,0:T(8,128)(2,1)S(1)} %get-tuple-element.41), channel_id=1, source_target_pairs={{0,8},{4,12},{8,0},{12,4},{1,9},{5,13},{9,1},{13,5},{2,10},{6,14},... | collective-permute-start | bytes 393224 | tf_op jit(solution)/shard_map/ppermute | solution.py:303

commit v10 on v9

--- a/solution.py
+++ b/solution.py
@@ -55,7 +55,8 @@
         self.cols = self.block * heads
         self.reach = self.back * rows
         self.scale = width ** (-0.5)
-        self.window_ranges = self.back + 1
+        self.lower = self.back + 1
+        self.window_ranges = self.back + 2
 
     def ends(self, meta):
         return [meta[1 + i] for i in range(self.ndocs)]
@@ -71,12 +72,15 @@
         )
 
 
-def fill_window(plan, refs, k_win, v_win):
+def fill_window(plan, own, refs, k_win, v_win):
     rows = plan.rows
+    k_win[pl.ds(0, rows), :] = jnp.zeros((rows, plan.width), k_win.dtype)
+    v_win[pl.ds(0, rows), :] = jnp.zeros((rows, plan.width), v_win.dtype)
     k_win[pl.ds(plan.back * rows, rows), :] = refs[0][pl.ds(0, rows), :]
     v_win[pl.ds(plan.back * rows, rows), :] = refs[0][pl.ds(rows, rows), :]
     for i in range(1, plan.back + 1):
-        to = pl.ds((plan.back - i) * rows, rows)
+        place = plan.back - i if i < plan.back else jnp.where(own == plan.back - 1, plan.back + 1, 0)
+        to = pl.ds(pl.multiple_of(place * rows, rows), rows)
         k_win[to, :] = refs[2 * i - 1][...]
         v_win[to, :] = refs[2 * i][...]
 
@@ -113,7 +117,7 @@
     kv_refs, (pay_ref, grad_ref, k_win, v_win) = refs[:-4], refs[-4:]
     own = meta[0]
     slot = plan.slot(meta, own, own ^ apart)
-    fill_window(plan, kv_refs, k_win, v_win)
+    fill_window(plan, own, kv_refs, k_win, v_win)
     _, (attended, query_grad, key_part, value_part) = attend_at(
         plan, meta, own, slot, qg[0], qg[1], k_win, v_win
     )
@@ -123,61 +127,84 @@
     grad_ref[:, plan.width :] = value_part
 
 
-def last_kernel(plan, first, items, meta, *refs):
-    n, width, rows, block = plan.n, plan.width, plan.rows, plan.block
-    qg_refs, refs = refs[: len(items)], refs[len(items) :]
-    first_grad, refs = refs[0], refs[1:]
-    kv_refs, refs = refs[: -(len(items) + 7)], refs[-(len(items) + 7) :]
-    pay_refs, grad_refs, (k_win, v_win, acc) = refs[: len(items)], refs[len(items) : -3], refs[-3:]
+def add_parts(plan, acc, keys_here, key_part, value_part):
+    acc[keys_here, : plan.width] = acc[keys_here, : plan.width] + key_part
+    acc[keys_here, plan.width :] = acc[keys_here, plan.width :] + value_part
+
+
+def put_rows(plan, pay_ref, attended, query_grad):
+    pay_ref[0] = attended
+    pay_ref[1] = query_grad
+
+
+def next_kernel(plan, first, items, meta, *refs):
+    n = plan.n
+    qg_refs, first_grad, refs = refs[: len(items)], refs[len(items)], refs[len(items) + 1 :]
+    outs = len(items) + 3
+    kv_refs, pay_refs, (acc, k_win, v_win) = refs[:-outs], refs[-outs:-3], refs[-3:]
     step = pl.program_id(0)
     own = meta[0]
 
     @pl.when(step == 0)
     def _():
-        fill_window(plan, kv_refs, k_win, v_win)
+        fill_window(plan, own, kv_refs, k_win, v_win)
         acc[...] = jnp.zeros_like(acc)
         slot = plan.slot(meta, own, own ^ first)
-        keys_here = pl.ds(pl.multiple_of(slot * block, block), plan.reach + block)
-        acc[keys_here, :] = first_grad[...]
+        start = pl.multiple_of(slot * plan.block, plan.block)
+        acc[pl.ds(start, plan.reach + plan.block), :] = first_grad[...]
 
     for i, item in enumerate(items):
-
-        @pl.when(step == i)
+        here = step == i
+        if item == n - 1:
+            here = jnp.logical_and(here, own != plan.back)
+
+        @pl.when(here)
         def _():
             slot = plan.slot(meta, own, own ^ item)
-            qg = qg_refs[i]
-            keys_here, (attended, query_grad, key_part, value_part) = attend_at(
-                plan, meta, own, slot, qg[0], qg[1], k_win, v_win
+            keys_here, (attended, query_grad, *parts) = attend_at(
+                plan, meta, own, slot, qg_refs[i][0], qg_refs[i][1], k_win, v_win
             )
-            acc[keys_here, :width] = acc[keys_here, :width] + key_part
-            acc[keys_here, width:] = acc[keys_here, width:] + value_part
-            pay_refs[i][0] = attended
-            pay_refs[i][1] = query_grad
-
-    @pl.when(step == len(items) - 1)
+            add_parts(plan, acc, keys_here, *parts)
+            put_rows(plan, pay_refs[i], attended, query_grad)
+
+
+def last_kernel(plan, meta, got_ref, acc_ref, *refs):
+    n, block, rows = plan.n, plan.block, plan.rows
+    kv_refs, (pay_ref, *grad_refs), (k_win, v_win, acc) = refs[:-8], refs[-8:-3], refs[-3:]
+    own = meta[0]
+    acc[...] = acc_ref[...]
+
+    @pl.when(own == plan.back - 1)
     def _():
-        def put_part(key_range, entry, part):
-            @pl.when(key_range < n // 2)
-            def _():
-                grad_refs[2][entry, key_range] = part.astype(jnp.bfloat16)
-
-            @pl.when(key_range >= n // 2)
-            def _():
-                grad_refs[3][entry, key_range - n // 2] = part.astype(jnp.bfloat16)
-
-        def of_range(key_range, carry):
-            at = lax.rem(key_range - own + plan.back + n, n) * rows
-            for apart in range(n):
-                slot = plan.slot(meta, key_range, own ^ apart)
-                part = acc[pl.ds(pl.multiple_of(at + slot * block, block), block), :]
-                if apart % 2 == 0:
-                    to = grad_refs[apart % 4 // 2]
-                    to[apart // 4, key_range] = part
-                else:
-                    put_part(key_range, apart // 2, part)
-            return carry
-
-        lax.fori_loop(0, n, of_range, 0)
+        fill_window(plan, own, kv_refs, k_win, v_win)
+        keys_here, (attended, query_grad, *parts) = attend_at(
+            plan, meta, own + 1, plan.slot(meta, own + 1, own), got_ref[0], got_ref[1], k_win, v_win
+        )
+        add_parts(plan, acc, keys_here, *parts)
+        put_rows(plan, pay_ref, attended, query_grad)
+
+    def put_part(key_range, entry, part):
+        @pl.when(key_range < plan.lower)
+        def _():
+            grad_refs[2][entry, key_range] = part.astype(jnp.bfloat16)
+
+        @pl.when(key_range >= plan.lower)
+        def _():
+            grad_refs[3][entry, key_range - plan.lower] = part.astype(jnp.bfloat16)
+
+    def of_range(key_range, carry):
+        at = lax.rem(key_range - own + plan.back + n, n) * rows
+        for apart in range(n):
+            slot = plan.slot(meta, key_range, own ^ apart)
+            part = acc[pl.ds(pl.multiple_of(at + slot * block, block), block), :]
+            if apart % 2 == 0:
+                to = grad_refs[apart % 4 // 2]
+                to[apart // 4, key_range] = part
+            else:
+                put_part(key_range, apart // 2, part)
+        return carry
+
+    lax.fori_loop(0, n, of_range, 0)
 
 
 def spec_of(space):
@@ -221,19 +248,32 @@
     )
 
 
-def attend_last(plan, first, items, meta, qg_list, first_grad, kv_list):
+def attend_next(plan, first, items, meta, qg_list, first_grad, kv_list):
+    window = pltpu.VMEM((plan.window_ranges * plan.rows, plan.width), jnp.bfloat16)
+    out_shape = [jax.ShapeDtypeStruct((2, plan.cols, plan.width), jnp.bfloat16)] * len(items)
+    out_shape.append(jax.ShapeDtypeStruct((plan.n * plan.rows, 2 * plan.width), jnp.float32))
+    operands = (meta, *qg_list, first_grad, *kv_list)
+    return kernel_call(
+        functools.partial(next_kernel, plan, first, items), "attend_next", operands,
+        [pltpu.SMEM] + [pltpu.VMEM] * (len(operands) - 1), out_shape, [window, window],
+        out_specs=[spec_of(pltpu.VMEM)] * len(out_shape), cost_estimate=plan.cost(len(items)), grid=(len(items),),
+    )
+
+
+def attend_last(plan, meta, got, sums, kv_list):
     n = plan.n
     window = pltpu.VMEM((plan.window_ranges * plan.rows, plan.width), jnp.bfloat16)
-    keep = jax.ShapeDtypeStruct((n // 4, n, plan.block, 2 * plan.width), jnp.float32)
-    send = jax.ShapeDtypeStruct((n // 2, n // 2, plan.block, 2 * plan.width), jnp.bfloat16)
-    out_shape = [jax.ShapeDtypeStruct((2, plan.cols, plan.width), jnp.bfloat16)] * len(items)
-    out_shape += [keep, keep, send, send]
-    operands = (meta, *qg_list, first_grad, *kv_list)
+    part = (plan.block, 2 * plan.width)
+    keep = jax.ShapeDtypeStruct((n // 4, n, *part), jnp.float32)
+    lower = jax.ShapeDtypeStruct((n // 2, plan.lower, *part), jnp.bfloat16)
+    upper = jax.ShapeDtypeStruct((n // 2, n - plan.lower, *part), jnp.bfloat16)
+    out_shape = [jax.ShapeDtypeStruct((2, plan.cols, plan.width), jnp.bfloat16), keep, keep, lower, upper]
+    operands = (meta, got, sums, *kv_list)
     return kernel_call(
-        functools.partial(last_kernel, plan, first, items), "attend_last", operands,
+        functools.partial(last_kernel, plan), "attend_last", operands,
         [pltpu.SMEM] + [pltpu.VMEM] * (len(operands) - 1), out_shape,
-        [window, window, pltpu.VMEM((n * plan.rows, 2 * plan.width), jnp.float32)],
-        out_specs=[spec_of(pltpu.VMEM)] * len(out_shape), cost_estimate=plan.cost(len(items)), grid=(len(items),),
+        [window, window, pltpu.VMEM(sums.shape, jnp.float32)],
+        out_specs=[spec_of(pltpu.VMEM)] * len(out_shape), cost_estimate=plan.cost(1),
     )
 
 
@@ -247,30 +287,42 @@
         grads, (attended, query_grad, send, kept, sems) = refs[:-5], refs[-5:]
     copies = []
     for i, item in enumerate(items):
-        to = pl.ds(pl.multiple_of((own ^ item) * cols, cols), cols)
-        copies.append(pltpu.make_async_copy(pay_refs[i].at[0], attended.at[to, :], sems.at[i, 0]))
-        copies.append(pltpu.make_async_copy(pay_refs[i].at[1], query_grad.at[to, :], sems.at[i, 1]))
-    for copy in copies:
-        copy.start()
+        to = pl.ds(pl.multiple_of((own ^ (n - 1 if item == "got" else item)) * cols, cols), cols)
+        pair = [
+            pltpu.make_async_copy(pay_refs[i].at[0], attended.at[to, :], sems.at[i, 0]),
+            pltpu.make_async_copy(pay_refs[i].at[1], query_grad.at[to, :], sems.at[i, 1]),
+        ]
+        if item in ("got", n - 1):
+            copies += [(copy, (own == plan.back - 1) == (item == "got")) for copy in pair]
+        else:
+            copies += [(copy, None) for copy in pair]
+
+    def each(act):
+        for copy, here in copies:
+            if here is None:
+                act(copy)
+            else:
+                pl.when(here)(functools.partial(act, copy))
+
+    each(lambda copy: copy.start())
     if final:
         total = sum(grad[...].astype(jnp.float32) for grad in grads).astype(jnp.bfloat16)
         sums[0] = total[:, :width]
         sums[1] = total[:, width:]
         for i, ref in enumerate((key_grad, value_grad)):
-            copies.append(pltpu.make_async_copy(sums.at[i], ref, sum_sems.at[i]))
-            copies[-1].start()
+            copies.append((pltpu.make_async_copy(sums.at[i], ref, sum_sems.at[i]), None))
+            copies[-1][0].start()
     else:
         pass_on, keep, *arrived = grads
         for entry in range(n // 2):
             for half, ref in enumerate(arrived):
-                ranges = pl.ds(half * (n // 2), n // 2)
+                ranges = pl.ds(plan.lower, n - plan.lower) if half else pl.ds(0, plan.lower)
                 total = (keep, pass_on)[entry % 2][entry // 2, ranges] + ref[entry].astype(jnp.float32)
                 if entry % 2:
                     send[entry // 2, ranges] = total.astype(jnp.bfloat16)
                 else:
                     kept[entry // 2, ranges] = total
-    for copy in copies:
-        copy.wait()
+    each(lambda copy: copy.wait())
 
 
 def place(plan, payloads, grads, filled=()):
@@ -310,6 +362,8 @@
     kv_list = []
     for by in range(1, plan.back + 1):
         pairs = [(i, (i + by) % n) for i in range(n)]
+        if by == plan.back:
+            pairs = [(i, i + by if i < by else (i - by - 1) % by) for i in range(n)]
         kv_list += [permuted(k, pairs), permuted(v, pairs)]
 
     owners = jnp.arange(n, dtype=jnp.int32)
@@ -322,16 +376,18 @@
     q, g = (x.reshape(rows * heads, width) for x in (query, output_gradient))
     *blocks, kv = pack(plan, meta, q, g, k, v)
     kv_list = [kv, *kv_list]
+    got = permuted(blocks[n - 1], [(plan.back, plan.back - 1)])
     first = n // 2
     first_pay, first_grad = attend_first(plan, first, meta, blocks[first], kv_list)
     stay = {first: across(first_pay, first)}
-    sent = [x for x in range(1, n) if x != first]
-    items = (*sent, 0)
-    out = attend_last(plan, first, items, meta, [blocks[x] for x in items], first_grad, kv_list)
-    late = {x: across(pay, x) for x, pay in zip(sent, out)}
-    stay[0] = out[len(sent)]
-    keep, pass_on, lower, upper = out[len(items) :]
-    upper = permuted(upper, [(i, i ^ 1) for i in range(n // 2, n)])
+    items = tuple(x for x in range(n - 1, -1, -1) if x != first)
+    *pays, sums = attend_next(plan, first, items, meta, [blocks[x] for x in items], first_grad, kv_list)
+    stay["got"], *out = attend_last(plan, meta, got, sums, kv_list)
+    stay[0] = pays[-1]
+    late = {n - 1: permuted(pays[0], [(i, i ^ (n - 1)) for i in range(n) if i != plan.back])}
+    late.update({x: across(pay, x) for x, pay in zip(items[1:-1], pays[1:-1])})
+    keep, pass_on, lower, upper = out
+    upper = permuted(upper, [(i, i ^ 1) for i in range(plan.back, n)])
     attended, query_grad, send, keep = place(plan, stay, (pass_on, keep, across(lower, 1), upper))
     terms = (keep, across(send, 2))
     bit = 4

time: 49.6 us -> 50.8 us (1.024)
  starting transfers between devices: 19.3 us -> 24.2 us
  waiting for transfers between devices: 17.1 us -> 13.3 us
  Pallas kernels: 10.5 us -> 11.2 us
  local copies, waits for them, and re-layouts: 1.43 us -> 0.76 us
    ppermute x10 -> x11, starting transfers between devices: 19.3 us -> 24.2 us  [permuted(): return lax.ppermute(array, 'ctx', pairs)]
    ppermute x10 -> x11, waiting for transfers between devices: 17.1 us -> 13.3 us  [permuted(): return lax.ppermute(array, 'ctx', pairs)]
    unnamed x4, local copies, waits for them, and re-layouts: 1.35 us -> 0.67 us
    pallas_call x5 -> x6, Pallas kernels: 10.5 us -> 11.2 us  [kernel_call(): pl.pallas_call(body, out_shape=out_shape, in_specs=[spec_of(space) for sp...]
  transfers between devices with their start and end apart: 10 -> 11, of which waited for: 4 -> 5; matrix products, arithmetic and copies ran while one was open for 1% -> 1% of each run, Pallas kernels for 15% -> 20%
where the time goes in v10:
time: 50.8 us; the launch traced here: 50.6 us
  starting transfers between devices  24.2 us (48%)
  waiting for transfers between devices  13.3 us (26%)
  Pallas kernels  11.2 us (22%)
  local copies, waits for them, and re-layouts  0.76 us (1%)
  between operations  0.74 us (1%)
    ppermute x11, starting transfers between devices, permuted(): return lax.ppermute(array, 'ctx', pairs)  24.2 us
    ppermute x11, waiting for transfers between devices, permuted(): return lax.ppermute(array, 'ctx', pairs)  13.3 us
    pallas_call x6, Pallas kernels, kernel_call(): pl.pallas_call(body, out_shape=out_shape, in_specs=[spec_of(space) for sp...  11.2 us
  transfers between devices with their start and end apart: 11, of which 5 were waited for; matrix products, arithmetic and copies ran while one was open for 1% of the time, Pallas kernels for 20%

profile of v10, /device:TPU:0, one launch (start us, length us, event | category | flops | bytes accessed | tf_op | source)
XLA Modules:
  0.0 50.6 jit_solution(14619888353893250105)
XLA Ops:
  0.6 3.1 %collective-permute-start = (bf16[256,128]{1,0:T(8,128)(2,1)}, bf16[256,128]{1,0:T(8,128)(2,1)S(1)}, u32[]{:S(2)}, u32[]{:S(2)}) collective-permute-start(bf16[256,128]{1,0:T(8,128)(2,1)} %bitcast.17), channel_id=1, source_target_pairs={{0,4},{4,8},{8,12},{12,0},{1,5},{5,9},{9,13},{13,1},{2,6},{6,10},{... | collective-permute-start | bytes 196616 | tf_op jit(solution)/shard_map/ppermute | solution.py:355
  3.7 2.6 %collective-permute-start.2 = (bf16[256,128]{1,0:T(8,128)(2,1)}, bf16[256,128]{1,0:T(8,128)(2,1)S(1)}, u32[]{:S(2)}, u32[]{:S(2)}) collective-permute-start(bf16[256,128]{1,0:T(8,128)(2,1)} %bitcast.18), channel_id=1, source_target_pairs={{0,8},{4,12},{8,4},{12,0},{1,9},{5,13},{9,5},{13,1},{2,10},{6,14},... | collective-permute-start | bytes 196616 | tf_op jit(solution)/shard_map/ppermute | solution.py:355
  6.3 0.1 collective-permute-start.1
  6.4 1.7 %collective-permute-start.3 = (bf16[256,128]{1,0:T(8,128)(2,1)}, bf16[256,128]{1,0:T(8,128)(2,1)S(1)}, u32[]{:S(2)}, u32[]{:S(2)}) collective-permute-start(bf16[256,128]{1,0:T(8,128)(2,1)} %bitcast.21), channel_id=1, source_target_pairs={{0,8},{4,12},{8,4},{12,0},{1,9},{5,13},{9,5},{13,1},{2,10},{6,14},... | collective-permute-start | bytes 196616 | tf_op jit(solution)/shard_map/ppermute | solution.py:355
  8.1 0.1 select_reduce_fusion
  8.3 0.1 reshape.74
  8.3 0.7 %copy-done.1 = s32[8]{0:T(128)S(1)} copy-done((s32[8]{0:T(128)S(1)}, s32[8]{0:T(128)}, u32[]{:S(2)}) %copy-start.1) | copy-done | bytes 56
  9.0 0.2 reduce-window.9
  9.2 0.1 pad_add_fusion.meta
  9.3 1.9 %pack.1 = (bf16[2,512,128]{2,1,0:T(8,128)(2,1)S(1)}, bf16[2,512,128]{2,1,0:T(8,128)(2,1)S(1)}, bf16[2,512,128]{2,1,0:T(8,128)(2,1)S(1)}, bf16[2,512,128]{2,1,0:T(8,128)(2,1)S(1)}, bf16[512,128]{1,0:T(8,128)(2,1)S(1)}) custom-call(s32[25]{0:T(128)S(1)} %pad_add_fusion.meta, bf16[2048,128]{1,0:T(8,128)(2,1)} %bitcast.15, bf16[2048,128]{1,0:T(8,128)(2,1)} %bitcast.16, ...), custom_call_target="tpu_custom_call" | custom-call | tf_op jit(solution)/shard_map/pack/pallas_call | solution.py:215
  11.2 0.7 %collective-permute-start.7 = (bf16[2,512,128]{2,1,0:T(8,128)(2,1)S(1)}, bf16[2,512,128]{2,1,0:T(8,128)(2,1)S(1)}, u32[]{:S(2)}, u32[]{:S(2)}) collective-permute-start(bf16[2,512,128]{2,1,0:T(8,128)(2,1)S(1)} %get-tuple-element.28.refs_0_), channel_id=1, source_target_pairs={{8,4},{9,5},{10,6},{11,7},{24,20},{25,21},{26,22},{27,23}} | collective-permute-start | bytes 786440 | tf_op jit(solution)/shard_map/ppermute | solution.py:355
  11.9 0.0 collective-permute-done.refs_1_.refs_5_
  11.9 0.7 %collective-permute-done.1.refs_2_.refs_6_ = bf16[256,128]{1,0:T(8,128)(2,1)S(1)} collective-permute-done((bf16[256,128]{1,0:T(8,128)(2,1)}, bf16[256,128]{1,0:T(8,128)(2,1)S(1)}, u32[]{:S(2)}, u32[]{:S(2)}) %collective-permute-start.1) | collective-permute-done | bytes 65568 | tf_op jit(solution)/shard_map/ppermute | solution.py:355
  12.6 0.0 collective-permute-done.2.refs_3_.refs_7_
  12.6 0.7 %collective-permute-done.3.refs_4_.refs_8_ = bf16[256,128]{1,0:T(8,128)(2,1)S(1)} collective-permute-done((bf16[256,128]{1,0:T(8,128)(2,1)}, bf16[256,128]{1,0:T(8,128)(2,1)S(1)}, u32[]{:S(2)}, u32[]{:S(2)}) %collective-permute-start.3) | collective-permute-done | bytes 65568 | tf_op jit(solution)/shard_map/ppermute | solution.py:355
  13.3 2.0 %attend_first.1 = (bf16[2,512,128]{2,1,0:T(8,128)(2,1)S(1)}, f32[576,256]{1,0:T(8,128)S(1)}) custom-call(s32[25]{0:T(128)S(1)} %pad_add_fusion.meta, bf16[2,512,128]{2,1,0:T(8,128)(2,1)S(1)} %get-tuple-element.31.qg, bf16[512,128]{1,0:T(8,128)(2,1)S(1)} %get-tuple-element.32.refs_0_.refs_4_, bf16[256,128]{1,0:T(8,128)(2,1)S(1)} %collective-permute-done.refs_1_.refs_5_, ...), custom_call_target="tpu_custom_call" | custom-call | flops 4227858432 | bytes 1048576 | tf_op jit(solution)/shard_map/attend_first/pallas_call | solution.py:215
  15.3 4.0 %collective-permute-start.6 = (bf16[2,512,128]{2,1,0:T(8,128)(2,1)S(1)}, bf16[2,512,128]{2,1,0:T(8,128)(2,1)S(1)}, u32[]{:S(2)}, u32[]{:S(2)}) collective-permute-start(bf16[2,512,128]{2,1,0:T(8,128)(2,1)S(1)} %get-tuple-element.36), channel_id=1, source_target_pairs={{0,8},{4,12},{8,0},{12,4},{1,9},{5,13},{9,1},{13,5},{2,10},{6,14},... | collective-permute-start | bytes 786440 | tf_op jit(solution)/shard_map/ppermute | solution.py:355
  19.3 4.7 %attend_next.1 = (bf16[2,512,128]{2,1,0:T(8,128)(2,1)S(1)}, bf16[2,512,128]{2,1,0:T(8,128)(2,1)S(1)}, bf16[2,512,128]{2,1,0:T(8,128)(2,1)S(1)}, f32[1024,256]{1,0:T(8,128)S(1)}) custom-call(s32[25]{0:T(128)S(1)} %pad_add_fusion.meta, bf16[2,512,128]{2,1,0:T(8,128)(2,1)S(1)} %get-tuple-element.28.refs_0_, bf16[2,512,128]{2,1,0:T(8,128)(2,1)S(1)} %get-tuple-element.29.refs_1_, ...), custom_call_target="tpu_custom_call" | custom-call | flops 12683575296 | bytes 3145728 | tf_op jit(solution)/shard_map/attend_next/pallas_call | solution.py:215
  24.0 0.0 collective-permute-done.7.got_ref
  24.0 0.8 %attend_last.1 = (bf16[2,512,128]{2,1,0:T(8,128)(2,1)S(1)}, f32[1,4,64,256]{3,2,1,0:T(8,128)S(1)}, f32[1,4,64,256]{3,2,1,0:T(8,128)S(1)}, bf16[2,3,64,256]{3,2,1,0:T(8,128)(2,1)S(1)}, bf16[2,1,64,256]{3,2,1,0:T(8,128)(2,1)S(1)}) custom-call(s32[25]{0:T(128)S(1)} %pad_add_fusion.meta, bf16[2,512,128]{2,1,0:T(8,128)(2,1)S(1)} %collective-permute-done.7.got_ref, ...), custom_call_target="tpu_custom_call" | custom-call | flops 4227858432 | bytes 1048576 | tf_op jit(solution)/shard_map/attend_last/pallas_call | solution.py:215
  24.8 7.9 %collective-permute-start.8 = (bf16[2,3,64,256]{3,2,1,0:T(8,128)(2,1)S(1)}, bf16[2,3,64,256]{3,2,1,0:T(8,128)(2,1)S(1)}, u32[]{:S(2)}, u32[]{:S(2)}) collective-permute-start(bf16[2,3,64,256]{3,2,1,0:T(8,128)(2,1)S(1)} %get-tuple-element.42), channel_id=1, source_target_pairs={{0,4},{4,0},{8,12},{12,8},{1,5},{5,1},{9,13},{13,9},{2,6},{6,2},{1... | collective-permute-start | bytes 589832 | tf_op jit(solution)/shard_map/ppermute | solution.py:355
  32.8 0.7 %collective-permute-start.9 = (bf16[2,1,64,256]{3,2,1,0:T(8,128)(2,1)S(1)}, bf16[2,1,64,256]{3,2,1,0:T(8,128)(2,1)S(1)}, u32[]{:S(2)}, u32[]{:S(2)}) collective-permute-start(bf16[2,1,64,256]{3,2,1,0:T(8,128)(2,1)S(1)} %get-tuple-element.43), channel_id=1, source_target_pairs={{8,12},{12,8},{9,13},{13,9},{10,14},{14,10},{11,15},{15,11},{24,28... | collective-permute-start | bytes 196616 | tf_op jit(solution)/shard_map/ppermute | solution.py:355
  33.4 2.3 %collective-permute-start.4 = (bf16[2,512,128]{2,1,0:T(8,128)(2,1)S(1)}, bf16[2,512,128]{2,1,0:T(8,128)(2,1)S(1)}, u32[]{:S(2)}, u32[]{:S(2)}) collective-permute-start(bf16[2,512,128]{2,1,0:T(8,128)(2,1)S(1)} %get-tuple-element.34), channel_id=1, source_target_pairs={{0,12},{4,8},{12,0},{1,13},{5,9},{13,1},{2,14},{6,10},{14,2},{3,15... | collective-permute-start | bytes 786440 | tf_op jit(solution)/shard_map/ppermute | solution.py:355
  35.7 1.2 %collective-permute-start.5 = (bf16[2,512,128]{2,1,0:T(8,128)(2,1)S(1)}, bf16[2,512,128]{2,1,0:T(8,128)(2,1)S(1)}, u32[]{:S(2)}, u32[]{:S(2)}) collective-permute-start(bf16[2,512,128]{2,1,0:T(8,128)(2,1)S(1)} %get-tuple-element.35), channel_id=1, source_target_pairs={{0,4},{4,0},{8,12},{12,8},{1,5},{5,1},{9,13},{13,9},{2,6},{6,2},{1... | collective-permute-start | bytes 786440 | tf_op jit(solution)/shard_map/ppermute | solution.py:355
  36.9 0.0 collective-permute-done.9.refs_6_
  36.9 0.0 collective-permute-done.6.refs_0_
  36.9 3.6 %collective-permute-done.8.refs_5_ = bf16[2,3,64,256]{3,2,1,0:T(8,128)(2,1)S(1)} collective-permute-done((bf16[2,3,64,256]{3,2,1,0:T(8,128)(2,1)S(1)}, bf16[2,3,64,256]{3,2,1,0:T(8,128)(2,1)S(1)}, u32[]{:S(2)}, u32[]{:S(2)}) %collective-permute-start.8) | collective-permute-done | bytes 196640 | tf_op jit(solution)/shard_map/ppermute | solution.py:355
  40.5 0.9 %place_first.1 = (bf16[2048,128]{1,0:T(8,128)(2,1)}, bf16[2048,128]{1,0:T(8,128)(2,1)}, bf16[1,4,64,256]{3,2,1,0:T(8,128)(2,1)S(1)}, f32[1,4,64,256]{3,2,1,0:T(8,128)S(1)}) custom-call(bf16[2,512,128]{2,1,0:T(8,128)(2,1)S(1)} %collective-permute-done.6.refs_0_, bf16[2,512,128]{2,1,0:T(8,128)(2,1)S(1)} %get-tuple-element.38.refs_1_, ...), custom_call_target="tpu_custom_call" | custom-call | flops 12683575296 | bytes 3145728 | tf_op jit(solution)/shard_map/place_first/pallas_call | solution.py:215
  41.3 0.1 collective-permute-start.10
  41.4 3.1 %collective-permute-done.4.refs_0_ = bf16[2,512,128]{2,1,0:T(8,128)(2,1)S(1)} collective-permute-done((bf16[2,512,128]{2,1,0:T(8,128)(2,1)S(1)}, bf16[2,512,128]{2,1,0:T(8,128)(2,1)S(1)}, u32[]{:S(2)}, u32[]{:S(2)}) %collective-permute-start.4) | collective-permute-done | bytes 262176 | tf_op jit(solution)/shard_map/ppermute | solution.py:355
  44.5 5.2 %collective-permute-done.5.refs_1_ = bf16[2,512,128]{2,1,0:T(8,128)(2,1)S(1)} collective-permute-done((bf16[2,512,128]{2,1,0:T(8,128)(2,1)S(1)}, bf16[2,512,128]{2,1,0:T(8,128)(2,1)S(1)}, u32[]{:S(2)}, u32[]{:S(2)}) %collective-permute-start.5) | collective-permute-done | bytes 262176 | tf_op jit(solution)/shard_map/ppermute | solution.py:355
  49.7 0.9 %place_last.1 = (bf16[2048,128]{1,0:T(8,128)(2,1)}, bf16[2048,128]{1,0:T(8,128)(2,1)}, bf16[256,128]{1,0:T(8,128)(2,1)}, bf16[256,128]{1,0:T(8,128)(2,1)}) custom-call(bf16[2,512,128]{2,1,0:T(8,128)(2,1)S(1)} %collective-permute-done.4.refs_0_, ...), custom_call_target="tpu_custom_call", output_to_operand_aliasing={{0}: (4, {}), {1}: (5, {})} | custom-call | flops 8455716864 | bytes 2097152 | tf_op jit(solution)/shard_map/place_last/pallas_call | solution.py:215
  (4 shorter events, 0.0 us)
Async XLA Ops:
  0.6 7.5 %copy-start = (s32[4,4]{1,0:T(4,128)S(1)}, s32[4,4]{1,0:T(4,128)}, u32[]{:S(2)}) copy-start(s32[4,4]{1,0:T(4,128)} %param.11) | copy-start | bytes 196
  0.6 11.3 %collective-permute-start = (bf16[256,128]{1,0:T(8,128)(2,1)}, bf16[256,128]{1,0:T(8,128)(2,1)S(1)}, u32[]{:S(2)}, u32[]{:S(2)}) collective-permute-start(bf16[256,128]{1,0:T(8,128)(2,1)} %bitcast.17), channel_id=1, source_target_pairs={{0,4},{4,8},{8,12},{12,0},{1,5},{5,9},{9,13},{13,1},{2,6},{6,10},{... | collective-permute-start | bytes 196616 | tf_op jit(solution)/shard_map/ppermute | solution.py:355
  3.7 8.9 %collective-permute-start.2 = (bf16[256,128]{1,0:T(8,128)(2,1)}, bf16[256,128]{1,0:T(8,128)(2,1)S(1)}, u32[]{:S(2)}, u32[]{:S(2)}) collective-permute-start(bf16[256,128]{1,0:T(8,128)(2,1)} %bitcast.18), channel_id=1, source_target_pairs={{0,8},{4,12},{8,4},{12,0},{1,9},{5,13},{9,5},{13,1},{2,10},{6,14},... | collective-permute-start | bytes 196616 | tf_op jit(solution)/shard_map/ppermute | solution.py:355
  6.3 6.3 %collective-permute-start.1 = (bf16[256,128]{1,0:T(8,128)(2,1)}, bf16[256,128]{1,0:T(8,128)(2,1)S(1)}, u32[]{:S(2)}, u32[]{:S(2)}) collective-permute-start(bf16[256,128]{1,0:T(8,128)(2,1)} %bitcast.20), channel_id=1, source_target_pairs={{0,4},{4,8},{8,12},{12,0},{1,5},{5,9},{9,13},{13,1},{2,6},{6,10},{... | collective-permute-start | bytes 196616 | tf_op jit(solution)/shard_map/ppermute | solution.py:355
  6.4 7.0 %collective-permute-start.3 = (bf16[256,128]{1,0:T(8,128)(2,1)}, bf16[256,128]{1,0:T(8,128)(2,1)S(1)}, u32[]{:S(2)}, u32[]{:S(2)}) collective-permute-start(bf16[256,128]{1,0:T(8,128)(2,1)} %bitcast.21), channel_id=1, source_target_pairs={{0,8},{4,12},{8,4},{12,0},{1,9},{5,13},{9,5},{13,1},{2,10},{6,14},... | collective-permute-start | bytes 196616 | tf_op jit(solution)/shard_map/ppermute | solution.py:355
  8.3 0.7 %copy-start.1 = (s32[8]{0:T(128)S(1)}, s32[8]{0:T(128)}, u32[]{:S(2)}) copy-start(s32[8]{0:T(128)} %param.10) | copy-start | bytes 100
  11.2 12.8 %collective-permute-start.7 = (bf16[2,512,128]{2,1,0:T(8,128)(2,1)S(1)}, bf16[2,512,128]{2,1,0:T(8,128)(2,1)S(1)}, u32[]{:S(2)}, u32[]{:S(2)}) collective-permute-start(bf16[2,512,128]{2,1,0:T(8,128)(2,1)S(1)} %get-tuple-element.28.refs_0_), channel_id=1, source_target_pairs={{8,4},{9,5},{10,6},{11,7},{24,20},{25,21},{26,22},{27,23}} | collective-permute-start | bytes 786440 | tf_op jit(solution)/shard_map/ppermute | solution.py:355
  15.3 21.6 %collective-permute-start.6 = (bf16[2,512,128]{2,1,0:T(8,128)(2,1)S(1)}, bf16[2,512,128]{2,1,0:T(8,128)(2,1)S(1)}, u32[]{:S(2)}, u32[]{:S(2)}) collective-permute-start(bf16[2,512,128]{2,1,0:T(8,128)(2,1)S(1)} %get-tuple-element.36), channel_id=1, source_target_pairs={{0,8},{4,12},{8,0},{12,4},{1,9},{5,13},{9,1},{13,5},{2,10},{6,14},... | collective-permute-start | bytes 786440 | tf_op jit(solution)/shard_map/ppermute | solution.py:355
  24.8 15.7 %collective-permute-start.8 = (bf16[2,3,64,256]{3,2,1,0:T(8,128)(2,1)S(1)}, bf16[2,3,64,256]{3,2,1,0:T(8,128)(2,1)S(1)}, u32[]{:S(2)}, u32[]{:S(2)}) collective-permute-start(bf16[2,3,64,256]{3,2,1,0:T(8,128)(2,1)S(1)} %get-tuple-element.42), channel_id=1, source_target_pairs={{0,4},{4,0},{8,12},{12,8},{1,5},{5,1},{9,13},{13,9},{2,6},{6,2},{1... | collective-permute-start | bytes 589832 | tf_op jit(solution)/shard_map/ppermute | solution.py:355
  32.8 4.1 %collective-permute-start.9 = (bf16[2,1,64,256]{3,2,1,0:T(8,128)(2,1)S(1)}, bf16[2,1,64,256]{3,2,1,0:T(8,128)(2,1)S(1)}, u32[]{:S(2)}, u32[]{:S(2)}) collective-permute-start(bf16[2,1,64,256]{3,2,1,0:T(8,128)(2,1)S(1)} %get-tuple-element.43), channel_id=1, source_target_pairs={{8,12},{12,8},{9,13},{13,9},{10,14},{14,10},{11,15},{15,11},{24,28... | collective-permute-start | bytes 196616 | tf_op jit(solution)/shard_map/ppermute | solution.py:355
  33.4 11.1 %collective-permute-start.4 = (bf16[2,512,128]{2,1,0:T(8,128)(2,1)S(1)}, bf16[2,512,128]{2,1,0:T(8,128)(2,1)S(1)}, u32[]{:S(2)}, u32[]{:S(2)}) collective-permute-start(bf16[2,512,128]{2,1,0:T(8,128)(2,1)S(1)} %get-tuple-element.34), channel_id=1, source_target_pairs={{0,12},{4,8},{12,0},{1,13},{5,9},{13,1},{2,14},{6,10},{14,2},{3,15... | collective-permute-start | bytes 786440 | tf_op jit(solution)/shard_map/ppermute | solution.py:355
  35.7 14.0 %collective-permute-start.5 = (bf16[2,512,128]{2,1,0:T(8,128)(2,1)S(1)}, bf16[2,512,128]{2,1,0:T(8,128)(2,1)S(1)}, u32[]{:S(2)}, u32[]{:S(2)}) collective-permute-start(bf16[2,512,128]{2,1,0:T(8,128)(2,1)S(1)} %get-tuple-element.35), channel_id=1, source_target_pairs={{0,4},{4,0},{8,12},{12,8},{1,5},{5,1},{9,13},{13,9},{2,6},{6,2},{1... | collective-permute-start | bytes 786440 | tf_op jit(solution)/shard_map/ppermute | solution.py:355
  41.3 8.3 %collective-permute-start.10 = (bf16[1,4,64,256]{3,2,1,0:T(8,128)(2,1)S(1)}, bf16[1,4,64,256]{3,2,1,0:T(8,128)(2,1)S(1)}, u32[]{:S(2)}, u32[]{:S(2)}) collective-permute-start(bf16[1,4,64,256]{3,2,1,0:T(8,128)(2,1)S(1)} %get-tuple-element.45), channel_id=1, source_target_pairs={{0,8},{4,12},{8,0},{12,4},{1,9},{5,13},{9,1},{13,5},{2,10},{6,14},... | collective-permute-start | bytes 393224 | tf_op jit(solution)/shard_map/ppermute | solution.py:355

commit v11 on v10

--- a/solution.py
+++ b/solution.py
@@ -95,20 +95,35 @@
     return keys_here, out
 
 
-def pack_kernel(plan, meta, q_ref, g_ref, k_ref, v_ref, *refs):
-    blocks, (kv, sems, kv_sems) = refs[: plan.n], refs[plan.n :]
-    own = meta[0]
+def pack_kernel(plan, ends_ref, owners_ref, q_ref, g_ref, k_ref, v_ref, *refs):
+    n = plan.n
+    blocks, (kv, meta, sems, kv_sems) = refs[:n], refs[n:]
+    own = lax.axis_index("ctx")
     copies = []
-    for apart, block in enumerate(blocks):
-        slot = plan.slot(meta, own, own ^ apart)
-        at = pl.ds(pl.multiple_of(slot * plan.cols, plan.cols), plan.cols)
-        copies.append(pltpu.make_async_copy(q_ref.at[at, :], block.at[0], sems.at[apart, 0]))
-        copies.append(pltpu.make_async_copy(g_ref.at[at, :], block.at[1], sems.at[apart, 1]))
     for i, ref in enumerate((k_ref, v_ref)):
         to = kv.at[pl.ds(i * plan.rows, plan.rows), :]
         copies.append(pltpu.make_async_copy(ref, to, kv_sems.at[i]))
-    for copy in copies:
-        copy.start()
+        copies[-1].start()
+
+    def slots_of(loader):
+        for slot in range(n):
+            meta[1 + plan.ndocs + loader * n + owners_ref[loader, slot]] = slot
+
+    slots_of(own)
+    for apart in range(n - 1, -1, -1):
+        slot = plan.slot(meta, own, own ^ apart)
+        at = pl.ds(pl.multiple_of(slot * plan.cols, plan.cols), plan.cols)
+        copies.append(pltpu.make_async_copy(q_ref.at[at, :], blocks[apart].at[0], sems.at[apart, 0]))
+        copies.append(pltpu.make_async_copy(g_ref.at[at, :], blocks[apart].at[1], sems.at[apart, 1]))
+        copies[-2].start()
+        copies[-1].start()
+    meta[0] = own
+    end = jnp.int32(0)
+    for i in range(plan.ndocs):
+        end = end + ends_ref[i]
+        meta[1 + i] = end
+    for loader in range(n):
+        slots_of(loader)
     for copy in copies:
         copy.wait()
 
@@ -223,14 +238,17 @@
     )(*operands)
 
 
-def pack(plan, meta, *operands):
-    out_shape = [jax.ShapeDtypeStruct((2, plan.cols, plan.width), jnp.bfloat16)] * plan.n
+def pack(plan, doc_lengths, block_owner, *operands):
+    n = plan.n
+    out_shape = [jax.ShapeDtypeStruct((2, plan.cols, plan.width), jnp.bfloat16)] * n
     out_shape.append(jax.ShapeDtypeStruct((2 * plan.rows, plan.width), jnp.bfloat16))
+    out_shape.append(jax.ShapeDtypeStruct((1 + plan.ndocs + n * n,), jnp.int32))
     operands = [pltpu.with_memory_space_constraint(x, pltpu.HBM) for x in operands]
     return kernel_call(
-        functools.partial(pack_kernel, plan), "pack", (meta, *operands), [pltpu.SMEM] + [pl.ANY] * 4, out_shape,
-        [pltpu.SemaphoreType.DMA((plan.n, 2)), pltpu.SemaphoreType.DMA((2,))],
-        out_specs=[spec_of(pltpu.VMEM)] * len(out_shape),
+        functools.partial(pack_kernel, plan), "pack", (doc_lengths, block_owner, *operands),
+        [pltpu.SMEM] * 2 + [pl.ANY] * 4, out_shape,
+        [pltpu.SemaphoreType.DMA((n, 2)), pltpu.SemaphoreType.DMA((2,))],
+        out_specs=[spec_of(pltpu.VMEM)] * (n + 1) + [spec_of(pltpu.SMEM)],
     )
 
 
@@ -366,15 +384,8 @@
             pairs = [(i, i + by if i < by else (i - by - 1) % by) for i in range(n)]
         kv_list += [permuted(k, pairs), permuted(v, pairs)]
 
-    owners = jnp.arange(n, dtype=jnp.int32)
-    match = block_owner[:, None, :] == owners[None, :, None]
-    table = jnp.sum(jnp.where(match, owners, 0), axis=2)
-    meta = jnp.concatenate(
-        [own.reshape(1).astype(jnp.int32), jnp.cumsum(doc_lengths).astype(jnp.int32), table.reshape(-1)]
-    )
-
     q, g = (x.reshape(rows * heads, width) for x in (query, output_gradient))
-    *blocks, kv = pack(plan, meta, q, g, k, v)
+    *blocks, kv, meta = pack(plan, doc_lengths, block_owner, q, g, k, v)
     kv_list = [kv, *kv_list]
     got = permuted(blocks[n - 1], [(plan.back, plan.back - 1)])
     first = n // 2

time: 50.8 us -> 50.5 us (level)
  Pallas kernels: 11.2 us -> 11.8 us
    pallas_call x6, Pallas kernels: 11.2 us -> 11.8 us  [kernel_call(): pl.pallas_call(body, out_shape=out_shape, in_specs=[spec_of(space) for sp...]
  transfers between devices with their start and end apart: 11 -> 11, of which waited for: 5 -> 4; matrix products, arithmetic and copies ran while one was open for 1% -> 0% of each run, Pallas kernels for 20% -> 22%
where the time goes in v11:
time: 50.5 us; the launch traced here: 50.3 us
  starting transfers between devices  24.2 us (48%)
  waiting for transfers between devices  12.9 us (26%)
  Pallas kernels  11.8 us (23%)
  between operations  0.74 us (1%)
  local copies, waits for them, and re-layouts  0.66 us (1%)
    ppermute x11, starting transfers between devices, permuted(): return lax.ppermute(array, 'ctx', pairs)  24.2 us
    ppermute x11, waiting for transfers between devices, permuted(): return lax.ppermute(array, 'ctx', pairs)  12.9 us
    pallas_call x6, Pallas kernels, kernel_call(): pl.pallas_call(body, out_shape=out_shape, in_specs=[spec_of(space) for sp...  11.8 us
  transfers between devices with their start and end apart: 11, of which 4 were waited for; matrix products, arithmetic and copies ran while one was open for 0% of the time, Pallas kernels for 22%

profile of v11, /device:TPU:0, one launch (start us, length us, event | category | flops | bytes accessed | tf_op | source)
XLA Modules:
  0.0 50.3 jit_solution(16145371646604776848)
XLA Ops:
  0.6 3.1 %collective-permute-start = (bf16[256,128]{1,0:T(8,128)(2,1)}, bf16[256,128]{1,0:T(8,128)(2,1)S(1)}, u32[]{:S(2)}, u32[]{:S(2)}) collective-permute-start(bf16[256,128]{1,0:T(8,128)(2,1)} %bitcast.14), channel_id=1, source_target_pairs={{0,4},{4,8},{8,12},{12,0},{1,5},{5,9},{9,13},{13,1},{2,6},{6,10},{... | collective-permute-start | bytes 196616 | tf_op jit(solution)/shard_map/ppermute | solution.py:373
  3.7 0.0 copy-start
  3.7 1.6 %collective-permute-start.1 = (bf16[256,128]{1,0:T(8,128)(2,1)}, bf16[256,128]{1,0:T(8,128)(2,1)S(1)}, u32[]{:S(2)}, u32[]{:S(2)}) collective-permute-start(bf16[256,128]{1,0:T(8,128)(2,1)} %bitcast.17), channel_id=1, source_target_pairs={{0,4},{4,8},{8,12},{12,0},{1,5},{5,9},{9,13},{13,1},{2,6},{6,10},{... | collective-permute-start | bytes 196616 | tf_op jit(solution)/shard_map/ppermute | solution.py:373
  5.3 1.1 %collective-permute-start.2 = (bf16[256,128]{1,0:T(8,128)(2,1)}, bf16[256,128]{1,0:T(8,128)(2,1)S(1)}, u32[]{:S(2)}, u32[]{:S(2)}) collective-permute-start(bf16[256,128]{1,0:T(8,128)(2,1)} %bitcast.15), channel_id=1, source_target_pairs={{0,8},{4,12},{8,4},{12,0},{1,9},{5,13},{9,5},{13,1},{2,10},{6,14},... | collective-permute-start | bytes 196616 | tf_op jit(solution)/shard_map/ppermute | solution.py:373
  6.4 2.0 %collective-permute-start.3 = (bf16[256,128]{1,0:T(8,128)(2,1)}, bf16[256,128]{1,0:T(8,128)(2,1)S(1)}, u32[]{:S(2)}, u32[]{:S(2)}) collective-permute-start(bf16[256,128]{1,0:T(8,128)(2,1)} %bitcast.18), channel_id=1, source_target_pairs={{0,8},{4,12},{8,4},{12,0},{1,9},{5,13},{9,5},{13,1},{2,10},{6,14},... | collective-permute-start | bytes 196616 | tf_op jit(solution)/shard_map/ppermute | solution.py:373
  8.3 0.0 copy-start.1
  8.3 0.0 copy-done
  8.3 0.7 %copy-done.1 = s32[8]{0:T(128)S(1)} copy-done((s32[8]{0:T(128)S(1)}, s32[8]{0:T(128)}, u32[]{:S(2)}) %copy-start.1) | copy-done | bytes 56
  9.0 2.6 %pack.1 = (bf16[2,512,128]{2,1,0:T(8,128)(2,1)S(1)}, bf16[2,512,128]{2,1,0:T(8,128)(2,1)S(1)}, bf16[2,512,128]{2,1,0:T(8,128)(2,1)S(1)}, bf16[2,512,128]{2,1,0:T...) custom-call(s32[8]{0:T(128)S(1)} %copy-done.1, s32[4,4]{1,0:T(4,128)S(1)} %copy-done, ...), custom_call_target="tpu_custom_call" | custom-call | tf_op jit(solution)/shard_map/pack/pallas_call | solution.py:230
  11.6 0.7 %collective-permute-start.7 = (bf16[2,512,128]{2,1,0:T(8,128)(2,1)S(1)}, bf16[2,512,128]{2,1,0:T(8,128)(2,1)S(1)}, u32[]{:S(2)}, u32[]{:S(2)}) collective-permute-start(bf16[2,512,128]{2,1,0:T(8,128)(2,1)S(1)} %get-tuple-element.30.refs_0_), channel_id=1, source_target_pairs={{8,4},{9,5},{10,6},{11,7},{24,20},{25,21},{26,22},{27,23}} | collective-permute-start | bytes 786440 | tf_op jit(solution)/shard_map/ppermute | solution.py:373
  12.3 0.0 collective-permute-done.refs_1_.refs_5_
  12.3 0.0 collective-permute-done.1.refs_2_.refs_6_
  12.3 0.0 collective-permute-done.2.refs_3_.refs_7_
  12.3 0.4 collective-permute-done.3.refs_4_.refs_8_
  12.7 2.0 %attend_first.1 = (bf16[2,512,128]{2,1,0:T(8,128)(2,1)S(1)}, f32[576,256]{1,0:T(8,128)S(1)}) custom-call(s32[25]{0:T(128)S(1)} %get-tuple-element.29.meta, bf16[2,512,128]{2,1,0:T(8,128)(2,1)S(1)} %get-tuple-element.33.qg, bf16[512,128]{1,0:T(8,128)(2,1)S(1)} %get-tuple-element.34.refs_0_.refs_4_, bf16[256,128]{1,0:T(8,128)(2,1)S(1)} %collective-permute-done.refs_1_.refs_5_, ...), custom_call_target="tpu_custom_call" | custom-call | flops 4227858432 | bytes 1048576 | tf_op jit(solution)/shard_map/attend_first/pallas_call | solution.py:230
  14.7 3.7 %collective-permute-start.6 = (bf16[2,512,128]{2,1,0:T(8,128)(2,1)S(1)}, bf16[2,512,128]{2,1,0:T(8,128)(2,1)S(1)}, u32[]{:S(2)}, u32[]{:S(2)}) collective-permute-start(bf16[2,512,128]{2,1,0:T(8,128)(2,1)S(1)} %get-tuple-element.38), channel_id=1, source_target_pairs={{0,8},{4,12},{8,0},{12,4},{1,9},{5,13},{9,1},{13,5},{2,10},{6,14},... | collective-permute-start | bytes 786440 | tf_op jit(solution)/shard_map/ppermute | solution.py:373
  18.4 4.8 %attend_next.1 = (bf16[2,512,128]{2,1,0:T(8,128)(2,1)S(1)}, bf16[2,512,128]{2,1,0:T(8,128)(2,1)S(1)}, bf16[2,512,128]{2,1,0:T(8,128)(2,1)S(1)}, f32[1024,256]{1,0:T(8,128)S(1)}) custom-call(s32[25]{0:T(128)S(1)} %get-tuple-element.29.meta, bf16[2,512,128]{2,1,0:T(8,128)(2,1)S(1)} %get-tuple-element.30.refs_0_, ...), custom_call_target="tpu_custom_call" | custom-call | flops 12683575296 | bytes 3145728 | tf_op jit(solution)/shard_map/attend_next/pallas_call | solution.py:230
  23.2 0.0 collective-permute-done.7.got_ref
  23.2 0.8 %attend_last.1 = (bf16[2,512,128]{2,1,0:T(8,128)(2,1)S(1)}, f32[1,4,64,256]{3,2,1,0:T(8,128)S(1)}, f32[1,4,64,256]{3,2,1,0:T(8,128)S(1)}, bf16[2,3,64,256]{3,2,1,0:T(8,128)(2,1)S(1)}, bf16[2,1,64,256]{3,2,1,0:T(8,128)(2,1)S(1)}) custom-call(s32[25]{0:T(128)S(1)} %get-tuple-element.29.meta, bf16[2,512,128]{2,1,0:T(8,128)(2,1)S(1)} %collective-permute-done.7.got_ref, ...), custom_call_target="tpu_custom_call" | custom-call | flops 4227858432 | bytes 1048576 | tf_op jit(solution)/shard_map/attend_last/pallas_call | solution.py:230
  24.0 7.9 %collective-permute-start.8 = (bf16[2,3,64,256]{3,2,1,0:T(8,128)(2,1)S(1)}, bf16[2,3,64,256]{3,2,1,0:T(8,128)(2,1)S(1)}, u32[]{:S(2)}, u32[]{:S(2)}) collective-permute-start(bf16[2,3,64,256]{3,2,1,0:T(8,128)(2,1)S(1)} %get-tuple-element.44), channel_id=1, source_target_pairs={{0,4},{4,0},{8,12},{12,8},{1,5},{5,1},{9,13},{13,9},{2,6},{6,2},{1... | collective-permute-start | bytes 589832 | tf_op jit(solution)/shard_map/ppermute | solution.py:373
  31.9 0.7 %collective-permute-start.9 = (bf16[2,1,64,256]{3,2,1,0:T(8,128)(2,1)S(1)}, bf16[2,1,64,256]{3,2,1,0:T(8,128)(2,1)S(1)}, u32[]{:S(2)}, u32[]{:S(2)}) collective-permute-start(bf16[2,1,64,256]{3,2,1,0:T(8,128)(2,1)S(1)} %get-tuple-element.45), channel_id=1, source_target_pairs={{8,12},{12,8},{9,13},{13,9},{10,14},{14,10},{11,15},{15,11},{24,28... | collective-permute-start | bytes 196616 | tf_op jit(solution)/shard_map/ppermute | solution.py:373
  32.5 2.3 %collective-permute-start.4 = (bf16[2,512,128]{2,1,0:T(8,128)(2,1)S(1)}, bf16[2,512,128]{2,1,0:T(8,128)(2,1)S(1)}, u32[]{:S(2)}, u32[]{:S(2)}) collective-permute-start(bf16[2,512,128]{2,1,0:T(8,128)(2,1)S(1)} %get-tuple-element.36), channel_id=1, source_target_pairs={{0,12},{4,8},{12,0},{1,13},{5,9},{13,1},{2,14},{6,10},{14,2},{3,15... | collective-permute-start | bytes 786440 | tf_op jit(solution)/shard_map/ppermute | solution.py:373
  34.8 1.2 %collective-permute-start.5 = (bf16[2,512,128]{2,1,0:T(8,128)(2,1)S(1)}, bf16[2,512,128]{2,1,0:T(8,128)(2,1)S(1)}, u32[]{:S(2)}, u32[]{:S(2)}) collective-permute-start(bf16[2,512,128]{2,1,0:T(8,128)(2,1)S(1)} %get-tuple-element.37), channel_id=1, source_target_pairs={{0,4},{4,0},{8,12},{12,8},{1,5},{5,1},{9,13},{13,9},{2,6},{6,2},{1... | collective-permute-start | bytes 786440 | tf_op jit(solution)/shard_map/ppermute | solution.py:373
  36.0 0.0 collective-permute-done.9.refs_6_
  36.0 0.0 collective-permute-done.6.refs_0_
  36.0 4.0 %collective-permute-done.8.refs_5_ = bf16[2,3,64,256]{3,2,1,0:T(8,128)(2,1)S(1)} collective-permute-done((bf16[2,3,64,256]{3,2,1,0:T(8,128)(2,1)S(1)}, bf16[2,3,64,256]{3,2,1,0:T(8,128)(2,1)S(1)}, u32[]{:S(2)}, u32[]{:S(2)}) %collective-permute-start.8) | collective-permute-done | bytes 196640 | tf_op jit(solution)/shard_map/ppermute | solution.py:373
  40.0 0.9 %place_first.1 = (bf16[2048,128]{1,0:T(8,128)(2,1)}, bf16[2048,128]{1,0:T(8,128)(2,1)}, bf16[1,4,64,256]{3,2,1,0:T(8,128)(2,1)S(1)}, f32[1,4,64,256]{3,2,1,0:T(8,128)S(1)}) custom-call(bf16[2,512,128]{2,1,0:T(8,128)(2,1)S(1)} %collective-permute-done.6.refs_0_, bf16[2,512,128]{2,1,0:T(8,128)(2,1)S(1)} %get-tuple-element.40.refs_1_, ...), custom_call_target="tpu_custom_call" | custom-call | flops 12683575296 | bytes 3145728 | tf_op jit(solution)/shard_map/place_first/pallas_call | solution.py:230
  40.9 0.1 collective-permute-start.10
  41.0 3.7 %collective-permute-done.4.refs_0_ = bf16[2,512,128]{2,1,0:T(8,128)(2,1)S(1)} collective-permute-done((bf16[2,512,128]{2,1,0:T(8,128)(2,1)S(1)}, bf16[2,512,128]{2,1,0:T(8,128)(2,1)S(1)}, u32[]{:S(2)}, u32[]{:S(2)}) %collective-permute-start.4) | collective-permute-done | bytes 262176 | tf_op jit(solution)/shard_map/ppermute | solution.py:373
  44.7 4.7 %collective-permute-done.5.refs_1_ = bf16[2,512,128]{2,1,0:T(8,128)(2,1)S(1)} collective-permute-done((bf16[2,512,128]{2,1,0:T(8,128)(2,1)S(1)}, bf16[2,512,128]{2,1,0:T(8,128)(2,1)S(1)}, u32[]{:S(2)}, u32[]{:S(2)}) %collective-permute-start.5) | collective-permute-done | bytes 262176 | tf_op jit(solution)/shard_map/ppermute | solution.py:373
  49.4 0.0 collective-permute-done.10
  49.4 0.9 %place_last.1 = (bf16[2048,128]{1,0:T(8,128)(2,1)}, bf16[2048,128]{1,0:T(8,128)(2,1)}, bf16[256,128]{1,0:T(8,128)(2,1)}, bf16[256,128]{1,0:T(8,128)(2,1)}) custom-call(bf16[2,512,128]{2,1,0:T(8,128)(2,1)S(1)} %collective-permute-done.4.refs_0_, ...), custom_call_target="tpu_custom_call", output_to_operand_aliasing={{0}: (4, {}), {1}: (5, {})} | custom-call | flops 8455716864 | bytes 2097152 | tf_op jit(solution)/shard_map/place_last/pallas_call | solution.py:230
Async XLA Ops:
  0.6 11.6 %collective-permute-start = (bf16[256,128]{1,0:T(8,128)(2,1)}, bf16[256,128]{1,0:T(8,128)(2,1)S(1)}, u32[]{:S(2)}, u32[]{:S(2)}) collective-permute-start(bf16[256,128]{1,0:T(8,128)(2,1)} %bitcast.14), channel_id=1, source_target_pairs={{0,4},{4,8},{8,12},{12,0},{1,5},{5,9},{9,13},{13,1},{2,6},{6,10},{... | collective-permute-start | bytes 196616 | tf_op jit(solution)/shard_map/ppermute | solution.py:373
  3.7 4.6 %copy-start = (s32[4,4]{1,0:T(4,128)S(1)}, s32[4,4]{1,0:T(4,128)}, u32[]{:S(2)}) copy-start(s32[4,4]{1,0:T(4,128)} %owners_ref.1) | copy-start | bytes 196
  3.7 8.6 %collective-permute-start.1 = (bf16[256,128]{1,0:T(8,128)(2,1)}, bf16[256,128]{1,0:T(8,128)(2,1)S(1)}, u32[]{:S(2)}, u32[]{:S(2)}) collective-permute-start(bf16[256,128]{1,0:T(8,128)(2,1)} %bitcast.17), channel_id=1, source_target_pairs={{0,4},{4,8},{8,12},{12,0},{1,5},{5,9},{9,13},{13,1},{2,6},{6,10},{... | collective-permute-start | bytes 196616 | tf_op jit(solution)/shard_map/ppermute | solution.py:373
  5.3 7.0 %collective-permute-start.2 = (bf16[256,128]{1,0:T(8,128)(2,1)}, bf16[256,128]{1,0:T(8,128)(2,1)S(1)}, u32[]{:S(2)}, u32[]{:S(2)}) collective-permute-start(bf16[256,128]{1,0:T(8,128)(2,1)} %bitcast.15), channel_id=1, source_target_pairs={{0,8},{4,12},{8,4},{12,0},{1,9},{5,13},{9,5},{13,1},{2,10},{6,14},... | collective-permute-start | bytes 196616 | tf_op jit(solution)/shard_map/ppermute | solution.py:373
  6.4 6.4 %collective-permute-start.3 = (bf16[256,128]{1,0:T(8,128)(2,1)}, bf16[256,128]{1,0:T(8,128)(2,1)S(1)}, u32[]{:S(2)}, u32[]{:S(2)}) collective-permute-start(bf16[256,128]{1,0:T(8,128)(2,1)} %bitcast.18), channel_id=1, source_target_pairs={{0,8},{4,12},{8,4},{12,0},{1,9},{5,13},{9,5},{13,1},{2,10},{6,14},... | collective-permute-start | bytes 196616 | tf_op jit(solution)/shard_map/ppermute | solution.py:373
  8.3 0.7 %copy-start.1 = (s32[8]{0:T(128)S(1)}, s32[8]{0:T(128)}, u32[]{:S(2)}) copy-start(s32[8]{0:T(128)} %ends_ref.1) | copy-start | bytes 100
  11.6 11.6 %collective-permute-start.7 = (bf16[2,512,128]{2,1,0:T(8,128)(2,1)S(1)}, bf16[2,512,128]{2,1,0:T(8,128)(2,1)S(1)}, u32[]{:S(2)}, u32[]{:S(2)}) collective-permute-start(bf16[2,512,128]{2,1,0:T(8,128)(2,1)S(1)} %get-tuple-element.30.refs_0_), channel_id=1, source_target_pairs={{8,4},{9,5},{10,6},{11,7},{24,20},{25,21},{26,22},{27,23}} | collective-permute-start | bytes 786440 | tf_op jit(solution)/shard_map/ppermute | solution.py:373
  14.7 21.3 %collective-permute-start.6 = (bf16[2,512,128]{2,1,0:T(8,128)(2,1)S(1)}, bf16[2,512,128]{2,1,0:T(8,128)(2,1)S(1)}, u32[]{:S(2)}, u32[]{:S(2)}) collective-permute-start(bf16[2,512,128]{2,1,0:T(8,128)(2,1)S(1)} %get-tuple-element.38), channel_id=1, source_target_pairs={{0,8},{4,12},{8,0},{12,4},{1,9},{5,13},{9,1},{13,5},{2,10},{6,14},... | collective-permute-start | bytes 786440 | tf_op jit(solution)/shard_map/ppermute | solution.py:373
  24.0 16.1 %collective-permute-start.8 = (bf16[2,3,64,256]{3,2,1,0:T(8,128)(2,1)S(1)}, bf16[2,3,64,256]{3,2,1,0:T(8,128)(2,1)S(1)}, u32[]{:S(2)}, u32[]{:S(2)}) collective-permute-start(bf16[2,3,64,256]{3,2,1,0:T(8,128)(2,1)S(1)} %get-tuple-element.44), channel_id=1, source_target_pairs={{0,4},{4,0},{8,12},{12,8},{1,5},{5,1},{9,13},{13,9},{2,6},{6,2},{1... | collective-permute-start | bytes 589832 | tf_op jit(solution)/shard_map/ppermute | solution.py:373
  31.9 4.1 %collective-permute-start.9 = (bf16[2,1,64,256]{3,2,1,0:T(8,128)(2,1)S(1)}, bf16[2,1,64,256]{3,2,1,0:T(8,128)(2,1)S(1)}, u32[]{:S(2)}, u32[]{:S(2)}) collective-permute-start(bf16[2,1,64,256]{3,2,1,0:T(8,128)(2,1)S(1)} %get-tuple-element.45), channel_id=1, source_target_pairs={{8,12},{12,8},{9,13},{13,9},{10,14},{14,10},{11,15},{15,11},{24,28... | collective-permute-start | bytes 196616 | tf_op jit(solution)/shard_map/ppermute | solution.py:373
  32.5 12.1 %collective-permute-start.4 = (bf16[2,512,128]{2,1,0:T(8,128)(2,1)S(1)}, bf16[2,512,128]{2,1,0:T(8,128)(2,1)S(1)}, u32[]{:S(2)}, u32[]{:S(2)}) collective-permute-start(bf16[2,512,128]{2,1,0:T(8,128)(2,1)S(1)} %get-tuple-element.36), channel_id=1, source_target_pairs={{0,12},{4,8},{12,0},{1,13},{5,9},{13,1},{2,14},{6,10},{14,2},{3,15... | collective-permute-start | bytes 786440 | tf_op jit(solution)/shard_map/ppermute | solution.py:373
  34.8 14.6 %collective-permute-start.5 = (bf16[2,512,128]{2,1,0:T(8,128)(2,1)S(1)}, bf16[2,512,128]{2,1,0:T(8,128)(2,1)S(1)}, u32[]{:S(2)}, u32[]{:S(2)}) collective-permute-start(bf16[2,512,128]{2,1,0:T(8,128)(2,1)S(1)} %get-tuple-element.37), channel_id=1, source_target_pairs={{0,4},{4,0},{8,12},{12,8},{1,5},{5,1},{9,13},{13,9},{2,6},{6,2},{1... | collective-permute-start | bytes 786440 | tf_op jit(solution)/shard_map/ppermute | solution.py:373
  40.9 8.5 %collective-permute-start.10 = (bf16[1,4,64,256]{3,2,1,0:T(8,128)(2,1)S(1)}, bf16[1,4,64,256]{3,2,1,0:T(8,128)(2,1)S(1)}, u32[]{:S(2)}, u32[]{:S(2)}) collective-permute-start(bf16[1,4,64,256]{3,2,1,0:T(8,128)(2,1)S(1)} %get-tuple-element.47), channel_id=1, source_target_pairs={{0,8},{4,12},{8,0},{12,4},{1,9},{5,13},{9,1},{13,5},{2,10},{6,14},... | collective-permute-start | bytes 393224 | tf_op jit(solution)/shard_map/ppermute | solution.py:373

commit v12 on v11

--- a/solution.py
+++ b/solution.py
@@ -15,10 +15,10 @@
     return lax.dot_general(a, b, ((contract[0], contract[1]), ((), ())), preferred_element_type=jnp.float32)
 
 
-def attend_block(first_row, ends, q, g, k, v, reach, heads, scale):
+def attend_block(first_row, skipped, ends, q, g, k, v, reach, heads, scale):
     cols = q.shape[0]
     key_rows = k.shape[0]
-    token = lax.broadcasted_iota(jnp.int32, (1, cols), 1) // heads
+    token = lax.broadcasted_iota(jnp.int32, (1, cols), 1) // heads + skipped
     query_pos = first_row + token
     doc_start = jnp.zeros((1, cols), jnp.int32)
     for end in ends:
@@ -56,7 +56,11 @@
         self.reach = self.back * rows
         self.scale = width ** (-0.5)
         self.lower = self.back + 1
-        self.window_ranges = self.back + 2
+        self.half = self.cols // 2
+        self.window_ranges = self.back + 3
+
+    def is_middle(self, own):
+        return jnp.logical_or(own == self.back - 1, own == self.back)
 
     def ends(self, meta):
         return [meta[1 + i] for i in range(self.ndocs)]
@@ -73,31 +77,32 @@
 
 
 def fill_window(plan, own, refs, k_win, v_win):
-    rows = plan.rows
-    k_win[pl.ds(0, rows), :] = jnp.zeros((rows, plan.width), k_win.dtype)
-    v_win[pl.ds(0, rows), :] = jnp.zeros((rows, plan.width), v_win.dtype)
-    k_win[pl.ds(plan.back * rows, rows), :] = refs[0][pl.ds(0, rows), :]
-    v_win[pl.ds(plan.back * rows, rows), :] = refs[0][pl.ds(rows, rows), :]
-    for i in range(1, plan.back + 1):
-        place = plan.back - i if i < plan.back else jnp.where(own == plan.back - 1, plan.back + 1, 0)
+    rows, back = plan.rows, plan.back
+    for win in (k_win, v_win):
+        win[pl.ds(0, 2 * rows), :] = jnp.zeros((2 * rows, plan.width), win.dtype)
+    k_win[pl.ds((back + 1) * rows, rows), :] = refs[0][pl.ds(0, rows), :]
+    v_win[pl.ds((back + 1) * rows, rows), :] = refs[0][pl.ds(rows, rows), :]
+    for i in range(1, back + 1):
+        place = back + 1 - i if i < back else jnp.where(own == back - 1, back + 2, 1)
         to = pl.ds(pl.multiple_of(place * rows, rows), rows)
         k_win[to, :] = refs[2 * i - 1][...]
         v_win[to, :] = refs[2 * i][...]
 
 
-def attend_at(plan, meta, loader, slot, q, g, k_win, v_win):
-    start = (loader - meta[0]) * plan.rows + slot * plan.block
+def attend_at(plan, meta, loader, owner, q, g, k_win, v_win, skipped=0):
+    slot = plan.slot(meta, loader, owner)
+    start = (loader - meta[0] + 1) * plan.rows + slot * plan.block
     keys_here = pl.ds(pl.multiple_of(start, plan.block), plan.reach + plan.block)
     out = attend_block(
-        loader * plan.rows + slot * plan.block, plan.ends(meta), q, g, k_win[keys_here, :], v_win[keys_here, :],
-        plan.reach, plan.heads, plan.scale,
+        loader * plan.rows + slot * plan.block, skipped, plan.ends(meta), q, g, k_win[keys_here, :],
+        v_win[keys_here, :], plan.reach, plan.heads, plan.scale,
     )
     return keys_here, out
 
 
 def pack_kernel(plan, ends_ref, owners_ref, q_ref, g_ref, k_ref, v_ref, *refs):
     n = plan.n
-    blocks, (kv, meta, sems, kv_sems) = refs[:n], refs[n:]
+    blocks, (kv, meta, sems, kv_sems) = refs[: n + 1], refs[n + 1 :]
     own = lax.axis_index("ctx")
     copies = []
     for i, ref in enumerate((k_ref, v_ref)):
@@ -110,11 +115,12 @@
             meta[1 + plan.ndocs + loader * n + owners_ref[loader, slot]] = slot
 
     slots_of(own)
-    for apart in range(n - 1, -1, -1):
-        slot = plan.slot(meta, own, own ^ apart)
-        at = pl.ds(pl.multiple_of(slot * plan.cols, plan.cols), plan.cols)
-        copies.append(pltpu.make_async_copy(q_ref.at[at, :], blocks[apart].at[0], sems.at[apart, 0]))
-        copies.append(pltpu.make_async_copy(g_ref.at[at, :], blocks[apart].at[1], sems.at[apart, 1]))
+    for i in range(n, -1, -1):
+        apart, size = min(i, n - 1), blocks[i].shape[1]
+        at = plan.slot(meta, own, own ^ apart) * plan.cols + (i - apart) * plan.half
+        at = pl.ds(pl.multiple_of(at, plan.half), size)
+        copies.append(pltpu.make_async_copy(q_ref.at[at, :], blocks[i].at[0], sems.at[i, 0]))
+        copies.append(pltpu.make_async_copy(g_ref.at[at, :], blocks[i].at[1], sems.at[i, 1]))
         copies[-2].start()
         copies[-1].start()
     meta[0] = own
@@ -131,10 +137,9 @@
 def first_kernel(plan, apart, meta, qg, *refs):
     kv_refs, (pay_ref, grad_ref, k_win, v_win) = refs[:-4], refs[-4:]
     own = meta[0]
-    slot = plan.slot(meta, own, own ^ apart)
     fill_window(plan, own, kv_refs, k_win, v_win)
     _, (attended, query_grad, key_part, value_part) = attend_at(
-        plan, meta, own, slot, qg[0], qg[1], k_win, v_win
+        plan, meta, own, own ^ apart, qg[0], qg[1], k_win, v_win
     )
     pay_ref[0] = attended
     pay_ref[1] = query_grad
@@ -164,39 +169,43 @@
     def _():
         fill_window(plan, own, kv_refs, k_win, v_win)
         acc[...] = jnp.zeros_like(acc)
-        slot = plan.slot(meta, own, own ^ first)
-        start = pl.multiple_of(slot * plan.block, plan.block)
+        start = pl.multiple_of(plan.rows + plan.slot(meta, own, own ^ first) * plan.block, plan.block)
         acc[pl.ds(start, plan.reach + plan.block), :] = first_grad[...]
 
     for i, item in enumerate(items):
-        here = step == i
-        if item == n - 1:
-            here = jnp.logical_and(here, own != plan.back)
-
-        @pl.when(here)
+
+        @pl.when(step == i)
         def _():
-            slot = plan.slot(meta, own, own ^ item)
             keys_here, (attended, query_grad, *parts) = attend_at(
-                plan, meta, own, slot, qg_refs[i][0], qg_refs[i][1], k_win, v_win
+                plan, meta, own, own ^ item, qg_refs[i][0], qg_refs[i][1], k_win, v_win,
+                plan.block // 2 if item == n - 1 else 0,
             )
             add_parts(plan, acc, keys_here, *parts)
             put_rows(plan, pay_refs[i], attended, query_grad)
 
 
-def last_kernel(plan, meta, got_ref, acc_ref, *refs):
+def last_kernel(plan, meta, own_ref, got_ref, acc_ref, *refs):
     n, block, rows = plan.n, plan.block, plan.rows
-    kv_refs, (pay_ref, *grad_refs), (k_win, v_win, acc) = refs[:-8], refs[-8:-3], refs[-3:]
+    kv_refs, (pay_ref, *grad_refs), (k_win, v_win, acc, qg) = refs[:-9], refs[-9:-4], refs[-4:]
     own = meta[0]
+    middle = plan.is_middle(own)
+
+    @pl.when(middle)
+    def _():
+        qg[...] = got_ref[...]
+
+    @pl.when(jnp.logical_not(middle))
+    def _():
+        qg[...] = own_ref[...]
+
     acc[...] = acc_ref[...]
-
-    @pl.when(own == plan.back - 1)
-    def _():
-        fill_window(plan, own, kv_refs, k_win, v_win)
-        keys_here, (attended, query_grad, *parts) = attend_at(
-            plan, meta, own + 1, plan.slot(meta, own + 1, own), got_ref[0], got_ref[1], k_win, v_win
-        )
-        add_parts(plan, acc, keys_here, *parts)
-        put_rows(plan, pay_ref, attended, query_grad)
+    fill_window(plan, own, kv_refs, k_win, v_win)
+    other = own ^ (n - 1)
+    keys_here, (attended, query_grad, *parts) = attend_at(
+        plan, meta, jnp.where(middle, other, own), jnp.where(middle, own, other), qg[0], qg[1], k_win, v_win
+    )
+    add_parts(plan, acc, keys_here, *parts)
+    put_rows(plan, pay_ref, attended, query_grad)
 
     def put_part(key_range, entry, part):
         @pl.when(key_range < plan.lower)
@@ -208,7 +217,7 @@
             grad_refs[3][entry, key_range - plan.lower] = part.astype(jnp.bfloat16)
 
     def of_range(key_range, carry):
-        at = lax.rem(key_range - own + plan.back + n, n) * rows
+        at = (lax.rem(key_range - own + plan.back + n, n) + 1) * rows
         for apart in range(n):
             slot = plan.slot(meta, key_range, own ^ apart)
             part = acc[pl.ds(pl.multiple_of(at + slot * block, block), block), :]
@@ -240,15 +249,16 @@
 
 def pack(plan, doc_lengths, block_owner, *operands):
     n = plan.n
-    out_shape = [jax.ShapeDtypeStruct((2, plan.cols, plan.width), jnp.bfloat16)] * n
+    sizes = [plan.cols] * (n - 1) + [plan.half] * 2
+    out_shape = [jax.ShapeDtypeStruct((2, size, plan.width), jnp.bfloat16) for size in sizes]
     out_shape.append(jax.ShapeDtypeStruct((2 * plan.rows, plan.width), jnp.bfloat16))
     out_shape.append(jax.ShapeDtypeStruct((1 + plan.ndocs + n * n,), jnp.int32))
     operands = [pltpu.with_memory_space_constraint(x, pltpu.HBM) for x in operands]
     return kernel_call(
         functools.partial(pack_kernel, plan), "pack", (doc_lengths, block_owner, *operands),
         [pltpu.SMEM] * 2 + [pl.ANY] * 4, out_shape,
-        [pltpu.SemaphoreType.DMA((n, 2)), pltpu.SemaphoreType.DMA((2,))],
-        out_specs=[spec_of(pltpu.VMEM)] * (n + 1) + [spec_of(pltpu.SMEM)],
+        [pltpu.SemaphoreType.DMA((n + 1, 2)), pltpu.SemaphoreType.DMA((2,))],
+        out_specs=[spec_of(pltpu.VMEM)] * (n + 2) + [spec_of(pltpu.SMEM)],
     )
 
 
@@ -268,8 +278,8 @@
 
 def attend_next(plan, first, items, meta, qg_list, first_grad, kv_list):
     window = pltpu.VMEM((plan.window_ranges * plan.rows, plan.width), jnp.bfloat16)
-    out_shape = [jax.ShapeDtypeStruct((2, plan.cols, plan.width), jnp.bfloat16)] * len(items)
-    out_shape.append(jax.ShapeDtypeStruct((plan.n * plan.rows, 2 * plan.width), jnp.float32))
+    out_shape = [jax.ShapeDtypeStruct(qg.shape, jnp.bfloat16) for qg in qg_list]
+    out_shape.append(jax.ShapeDtypeStruct(((plan.n + 1) * plan.rows, 2 * plan.width), jnp.float32))
     operands = (meta, *qg_list, first_grad, *kv_list)
     return kernel_call(
         functools.partial(next_kernel, plan, first, items), "attend_next", operands,
@@ -278,19 +288,19 @@
     )
 
 
-def attend_last(plan, meta, got, sums, kv_list):
+def attend_last(plan, meta, qg, got, sums, kv_list):
     n = plan.n
     window = pltpu.VMEM((plan.window_ranges * plan.rows, plan.width), jnp.bfloat16)
     part = (plan.block, 2 * plan.width)
     keep = jax.ShapeDtypeStruct((n // 4, n, *part), jnp.float32)
     lower = jax.ShapeDtypeStruct((n // 2, plan.lower, *part), jnp.bfloat16)
     upper = jax.ShapeDtypeStruct((n // 2, n - plan.lower, *part), jnp.bfloat16)
-    out_shape = [jax.ShapeDtypeStruct((2, plan.cols, plan.width), jnp.bfloat16), keep, keep, lower, upper]
-    operands = (meta, got, sums, *kv_list)
+    out_shape = [jax.ShapeDtypeStruct(qg.shape, jnp.bfloat16), keep, keep, lower, upper]
+    operands = (meta, qg, got, sums, *kv_list)
     return kernel_call(
         functools.partial(last_kernel, plan), "attend_last", operands,
         [pltpu.SMEM] + [pltpu.VMEM] * (len(operands) - 1), out_shape,
-        [window, window, pltpu.VMEM(sums.shape, jnp.float32)],
+        [window, window, pltpu.VMEM(sums.shape, jnp.float32), pltpu.VMEM(qg.shape, jnp.bfloat16)],
         out_specs=[spec_of(pltpu.VMEM)] * len(out_shape), cost_estimate=plan.cost(1),
     )
 
@@ -303,17 +313,13 @@
         grads, (_, _, attended, query_grad, key_grad, value_grad, sums, sems, sum_sems) = refs[:-9], refs[-9:]
     else:
         grads, (attended, query_grad, send, kept, sems) = refs[:-5], refs[-5:]
+    middle = plan.is_middle(own)
     copies = []
-    for i, item in enumerate(items):
-        to = pl.ds(pl.multiple_of((own ^ (n - 1 if item == "got" else item)) * cols, cols), cols)
-        pair = [
-            pltpu.make_async_copy(pay_refs[i].at[0], attended.at[to, :], sems.at[i, 0]),
-            pltpu.make_async_copy(pay_refs[i].at[1], query_grad.at[to, :], sems.at[i, 1]),
-        ]
-        if item in ("got", n - 1):
-            copies += [(copy, (own == plan.back - 1) == (item == "got")) for copy in pair]
-        else:
-            copies += [(copy, None) for copy in pair]
+    for i, (x, skipped, on_middle) in enumerate(items):
+        here = None if on_middle is None else middle if on_middle else jnp.logical_not(middle)
+        to = pl.ds(pl.multiple_of((own ^ x) * cols + skipped, plan.half), pay_refs[i].shape[1])
+        copies.append((pltpu.make_async_copy(pay_refs[i].at[0], attended.at[to, :], sems.at[i, 0]), here))
+        copies.append((pltpu.make_async_copy(pay_refs[i].at[1], query_grad.at[to, :], sems.at[i, 1]), here))
 
     def each(act):
         for copy, here in copies:
@@ -387,16 +393,22 @@
     q, g = (x.reshape(rows * heads, width) for x in (query, output_gradient))
     *blocks, kv, meta = pack(plan, doc_lengths, block_owner, q, g, k, v)
     kv_list = [kv, *kv_list]
-    got = permuted(blocks[n - 1], [(plan.back, plan.back - 1)])
+    half = plan.half
+    pairs = [(plan.back - 1, plan.back), (plan.back, plan.back - 1)]
+    got = permuted(blocks[n - 1], pairs)
     first = n // 2
     first_pay, first_grad = attend_first(plan, first, meta, blocks[first], kv_list)
-    stay = {first: across(first_pay, first)}
+    first_pay = across(first_pay, first)
     items = tuple(x for x in range(n - 1, -1, -1) if x != first)
-    *pays, sums = attend_next(plan, first, items, meta, [blocks[x] for x in items], first_grad, kv_list)
-    stay["got"], *out = attend_last(plan, meta, got, sums, kv_list)
-    stay[0] = pays[-1]
-    late = {n - 1: permuted(pays[0], [(i, i ^ (n - 1)) for i in range(n) if i != plan.back])}
-    late.update({x: across(pay, x) for x, pay in zip(items[1:-1], pays[1:-1])})
+    qg_list = [blocks[n], *[blocks[x] for x in items[1:]]]
+    *pays, sums = attend_next(plan, first, items, meta, qg_list, first_grad, kv_list)
+    last_pay, *out = attend_last(plan, meta, blocks[n - 1], got, sums, kv_list)
+    stay = {(first, 0, None): first_pay, (0, 0, None): pays[-1], (n - 1, 0, True): last_pay}
+    late = {
+        (n - 1, 0, False): permuted(last_pay, [(i, i ^ (n - 1)) for i in range(n) if (i, i ^ (n - 1)) not in pairs]),
+        (n - 1, half, None): across(pays[0], n - 1),
+    }
+    late.update({(x, 0, None): across(pay, x) for x, pay in zip(items[1:-1], pays[1:-1])})
     keep, pass_on, lower, upper = out
     upper = permuted(upper, [(i, i ^ 1) for i in range(plan.back, n)])
     attended, query_grad, send, keep = place(plan, stay, (pass_on, keep, across(lower, 1), upper))

time: 50.5 us -> 52.6 us (1.042)
  starting transfers between devices: 24.2 us -> 29.3 us
  waiting for transfers between devices: 12.9 us -> 8.28 us
  Pallas kernels: 11.8 us -> 12.6 us
  local copies, waits for them, and re-layouts: 0.66 us -> 1.34 us
    ppermute x11 -> x12, starting transfers between devices: 24.2 us -> 29.3 us  [permuted(): return lax.ppermute(array, 'ctx', pairs)]
    ppermute x11 -> x12, waiting for transfers between devices: 12.9 us -> 8.28 us  [permuted(): return lax.ppermute(array, 'ctx', pairs)]
    pallas_call x6, Pallas kernels: 11.8 us -> 12.6 us  [kernel_call(): pl.pallas_call(body, out_shape=out_shape, in_specs=[spec_of(space) for sp...]
    unnamed x4, local copies, waits for them, and re-layouts: 0.66 us -> 1.34 us
  transfers between devices with their start and end apart: 11 -> 12, of which waited for: 4 -> 2; matrix products, arithmetic and copies ran while one was open for 0% -> 0% of each run, Pallas kernels for 22% -> 22%
where the time goes in v12:
time: 52.6 us; the launch traced here: 52.3 us
  starting transfers between devices  29.3 us (56%)
  Pallas kernels  12.6 us (24%)
  waiting for transfers between devices  8.28 us (16%)
  local copies, waits for them, and re-layouts  1.34 us (3%)
  between operations  0.78 us (1%)
    ppermute x12, starting transfers between devices, permuted(): return lax.ppermute(array, 'ctx', pairs)  29.3 us
    pallas_call x6, Pallas kernels, kernel_call(): pl.pallas_call(body, out_shape=out_shape, in_specs=[spec_of(space) for sp...  12.6 us
    ppermute x12, waiting for transfers between devices, permuted(): return lax.ppermute(array, 'ctx', pairs)  8.28 us
    unnamed x4, local copies, waits for them, and re-layouts  1.34 us
  transfers between devices with their start and end apart: 12, of which 2 were waited for; matrix products, arithmetic and copies ran while one was open for 0% of the time, Pallas kernels for 22%

profile of v12, /device:TPU:0, one launch (start us, length us, event | category | flops | bytes accessed | tf_op | source)
XLA Modules:
  0.0 52.3 jit_solution(529815068267587424)
XLA Ops:
  0.6 3.1 %collective-permute-start.1 = (bf16[256,128]{1,0:T(8,128)(2,1)}, bf16[256,128]{1,0:T(8,128)(2,1)S(1)}, u32[]{:S(2)}, u32[]{:S(2)}) collective-permute-start(bf16[256,128]{1,0:T(8,128)(2,1)} %bitcast.14), channel_id=1, source_target_pairs={{0,4},{4,8},{8,12},{12,0},{1,5},{5,9},{9,13},{13,1},{2,6},{6,10},{... | collective-permute-start | bytes 196616 | tf_op jit(solution)/shard_map/ppermute | solution.py:379
  3.7 1.6 %collective-permute-start.2 = (bf16[256,128]{1,0:T(8,128)(2,1)}, bf16[256,128]{1,0:T(8,128)(2,1)S(1)}, u32[]{:S(2)}, u32[]{:S(2)}) collective-permute-start(bf16[256,128]{1,0:T(8,128)(2,1)} %bitcast.17), channel_id=1, source_target_pairs={{0,4},{4,8},{8,12},{12,0},{1,5},{5,9},{9,13},{13,1},{2,6},{6,10},{... | collective-permute-start | bytes 196616 | tf_op jit(solution)/shard_map/ppermute | solution.py:379
  5.3 1.1 %collective-permute-start.3 = (bf16[256,128]{1,0:T(8,128)(2,1)}, bf16[256,128]{1,0:T(8,128)(2,1)S(1)}, u32[]{:S(2)}, u32[]{:S(2)}) collective-permute-start(bf16[256,128]{1,0:T(8,128)(2,1)} %bitcast.15), channel_id=1, source_target_pairs={{0,8},{4,12},{8,4},{12,0},{1,9},{5,13},{9,5},{13,1},{2,10},{6,14},... | collective-permute-start | bytes 196616 | tf_op jit(solution)/shard_map/ppermute | solution.py:379
  6.4 2.0 %collective-permute-start.4 = (bf16[256,128]{1,0:T(8,128)(2,1)}, bf16[256,128]{1,0:T(8,128)(2,1)S(1)}, u32[]{:S(2)}, u32[]{:S(2)}) collective-permute-start(bf16[256,128]{1,0:T(8,128)(2,1)} %bitcast.18), channel_id=1, source_target_pairs={{0,8},{4,12},{8,4},{12,0},{1,9},{5,13},{9,5},{13,1},{2,10},{6,14},... | collective-permute-start | bytes 196616 | tf_op jit(solution)/shard_map/ppermute | solution.py:379
  8.3 0.7 %copy-done = s32[4,4]{1,0:T(4,128)S(1)} copy-done((s32[4,4]{1,0:T(4,128)S(1)}, s32[4,4]{1,0:T(4,128)}, u32[]{:S(2)}) %copy-start) | copy-done | bytes 88
  9.0 0.7 %copy-done.1 = s32[8]{0:T(128)S(1)} copy-done((s32[8]{0:T(128)S(1)}, s32[8]{0:T(128)}, u32[]{:S(2)}) %copy-start.1) | copy-done | bytes 56
  9.7 2.6 %pack.1 = (bf16[2,512,128]{2,1,0:T(8,128)(2,1)S(1)}, bf16[2,512,128]{2,1,0:T(8,128)(2,1)S(1)}, bf16[2,512,128]{2,1,0:T(8,128)(2,1)S(1)}, bf16[2,256,128]{2,1,0:T...) custom-call(s32[8]{0:T(128)S(1)} %copy-done.1, ...), custom_call_target="tpu_custom_call" | custom-call | tf_op jit(solution)/shard_map/pack/pallas_call | solution.py:239
  12.3 0.7 %collective-permute-start = (bf16[2,256,128]{2,1,0:T(8,128)(2,1)S(1)}, bf16[2,256,128]{2,1,0:T(8,128)(2,1)S(1)}, u32[]{:S(2)}, u32[]{:S(2)}) collective-permute-start(bf16[2,256,128]{2,1,0:T(8,128)(2,1)S(1)} %get-tuple-element.31.own_ref), channel_id=1, source_target_pairs={{4,8},{8,4},{5,9},{9,5},{6,10},{10,6},{7,11},{11,7},{20,24},{24,20... | collective-permute-start | bytes 393224 | tf_op jit(solution)/shard_map/ppermute | solution.py:379
  13.0 0.0 collective-permute-done.1.refs_1_.refs_5_
  13.0 0.0 collective-permute-done.2.refs_2_.refs_6_
  13.0 0.0 collective-permute-done.3.refs_3_.refs_7_
  13.0 0.0 collective-permute-done.4.refs_4_.refs_8_
  13.0 2.0 %attend_first.1 = (bf16[2,512,128]{2,1,0:T(8,128)(2,1)S(1)}, f32[576,256]{1,0:T(8,128)S(1)}) custom-call(s32[25]{0:T(128)S(1)} %get-tuple-element.30.meta, bf16[2,512,128]{2,1,0:T(8,128)(2,1)S(1)} %get-tuple-element.35.qg, bf16[512,128]{1,0:T(8,128)(2,1)S(1)} %get-tuple-element.36.refs_0_.refs_4_, ...), custom_call_target="tpu_custom_call" | custom-call | flops 4227858432 | bytes 1048576 | tf_op jit(solution)/shard_map/attend_first/pallas_call | solution.py:239
  15.0 4.1 %collective-permute-start.8 = (bf16[2,512,128]{2,1,0:T(8,128)(2,1)S(1)}, bf16[2,512,128]{2,1,0:T(8,128)(2,1)S(1)}, u32[]{:S(2)}, u32[]{:S(2)}) collective-permute-start(bf16[2,512,128]{2,1,0:T(8,128)(2,1)S(1)} %get-tuple-element.42), channel_id=1, source_target_pairs={{0,8},{4,12},{8,0},{12,4},{1,9},{5,13},{9,1},{13,5},{2,10},{6,14},... | collective-permute-start | bytes 786440 | tf_op jit(solution)/shard_map/ppermute | solution.py:379
  19.1 4.4 %attend_next.1 = (bf16[2,256,128]{2,1,0:T(8,128)(2,1)S(1)}, bf16[2,512,128]{2,1,0:T(8,128)(2,1)S(1)}, bf16[2,512,128]{2,1,0:T(8,128)(2,1)S(1)}, f32[1280,256]{1,0:T(8,128)S(1)}) custom-call(s32[25]{0:T(128)S(1)} %get-tuple-element.30.meta, bf16[2,256,128]{2,1,0:T(8,128)(2,1)S(1)} %get-tuple-element.32.refs_0_, ...), custom_call_target="tpu_custom_call" | custom-call | flops 12683575296 | bytes 3145728 | tf_op jit(solution)/shard_map/attend_next/pallas_call | solution.py:239
  23.5 0.0 collective-permute-done.got_ref
  23.5 1.8 %attend_last.1 = (bf16[2,256,128]{2,1,0:T(8,128)(2,1)S(1)}, f32[1,4,64,256]{3,2,1,0:T(8,128)S(1)}, f32[1,4,64,256]{3,2,1,0:T(8,128)S(1)}, bf16[2,3,64,256]{3,2,1,0:T(8,128)(2,1)S(1)}, bf16[2,1,64,256]{3,2,1,0:T(8,128)(2,1)S(1)}) custom-call(s32[25]{0:T(128)S(1)} %get-tuple-element.30.meta, bf16[2,256,128]{2,1,0:T(8,128)(2,1)S(1)} %get-tuple-element.31.own_ref, ...), custom_call_target="tpu_custom_call" | custom-call | flops 4227858432 | bytes 1048576 | tf_op jit(solution)/shard_map/attend_last/pallas_call | solution.py:239
  25.4 4.0 %collective-permute-start.9 = (bf16[2,3,64,256]{3,2,1,0:T(8,128)(2,1)S(1)}, bf16[2,3,64,256]{3,2,1,0:T(8,128)(2,1)S(1)}, u32[]{:S(2)}, u32[]{:S(2)}) collective-permute-start(bf16[2,3,64,256]{3,2,1,0:T(8,128)(2,1)S(1)} %get-tuple-element.46), channel_id=1, source_target_pairs={{0,4},{4,0},{8,12},{12,8},{1,5},{5,1},{9,13},{13,9},{2,6},{6,2},{1... | collective-permute-start | bytes 589832 | tf_op jit(solution)/shard_map/ppermute | solution.py:379
  29.4 0.7 %collective-permute-start.10 = (bf16[2,1,64,256]{3,2,1,0:T(8,128)(2,1)S(1)}, bf16[2,1,64,256]{3,2,1,0:T(8,128)(2,1)S(1)}, u32[]{:S(2)}, u32[]{:S(2)}) collective-permute-start(bf16[2,1,64,256]{3,2,1,0:T(8,128)(2,1)S(1)} %get-tuple-element.47), channel_id=1, source_target_pairs={{8,12},{12,8},{9,13},{13,9},{10,14},{14,10},{11,15},{15,11},{24,28... | collective-permute-start | bytes 196616 | tf_op jit(solution)/shard_map/ppermute | solution.py:379
  30.1 0.1 collective-permute-start.7
  30.1 3.5 %collective-permute-start.6 = (bf16[2,256,128]{2,1,0:T(8,128)(2,1)S(1)}, bf16[2,256,128]{2,1,0:T(8,128)(2,1)S(1)}, u32[]{:S(2)}, u32[]{:S(2)}) collective-permute-start(bf16[2,256,128]{2,1,0:T(8,128)(2,1)S(1)} %get-tuple-element.40), channel_id=1, source_target_pairs={{0,12},{4,8},{8,4},{12,0},{1,13},{5,9},{9,5},{13,1},{2,14},{6,10},... | collective-permute-start | bytes 393224 | tf_op jit(solution)/shard_map/ppermute | solution.py:379
  33.7 0.0 collective-permute-done.10.refs_6_
  33.7 8.5 %collective-permute-start.5 = (bf16[2,256,128]{2,1,0:T(8,128)(2,1)S(1)}, bf16[2,256,128]{2,1,0:T(8,128)(2,1)S(1)}, u32[]{:S(2)}, u32[]{:S(2)}) collective-permute-start(bf16[2,256,128]{2,1,0:T(8,128)(2,1)S(1)} %get-tuple-element.39.refs_2_), channel_id=1, source_target_pairs={{0,12},{12,0},{1,13},{13,1},{2,14},{14,2},{3,15},{15,3},{16,28},{2... | collective-permute-start | bytes 393224 | tf_op jit(solution)/shard_map/ppermute | solution.py:379
  42.2 0.0 collective-permute-done.9.refs_5_
  42.2 0.0 collective-permute-done.8.refs_0_
  42.2 0.9 %place_first.1 = (bf16[2048,128]{1,0:T(8,128)(2,1)}, bf16[2048,128]{1,0:T(8,128)(2,1)}, bf16[1,4,64,256]{3,2,1,0:T(8,128)(2,1)S(1)}, f32[1,4,64,256]{3,2,1,0:T(8,128)S(1)}) custom-call(bf16[2,512,128]{2,1,0:T(8,128)(2,1)S(1)} %collective-permute-done.8.refs_0_, bf16[2,512,128]{2,1,0:T(8,128)(2,1)S(1)} %get-tuple-element.43.refs_1_, ...), custom_call_target="tpu_custom_call" | custom-call | flops 12683575296 | bytes 3145728 | tf_op jit(solution)/shard_map/place_first/pallas_call | solution.py:239
  43.1 0.1 collective-permute-start.11
  43.1 0.0 collective-permute-done.6.refs_1_
  43.2 3.4 %collective-permute-done.5.refs_0_ = bf16[2,256,128]{2,1,0:T(8,128)(2,1)S(1)} collective-permute-done((bf16[2,256,128]{2,1,0:T(8,128)(2,1)S(1)}, bf16[2,256,128]{2,1,0:T(8,128)(2,1)S(1)}, u32[]{:S(2)}, u32[]{:S(2)}) %collective-permute-start.5) | collective-permute-done | bytes 131104 | tf_op jit(solution)/shard_map/ppermute | solution.py:379
  46.6 0.0 collective-permute-done.7.refs_2_
  46.6 4.9 %collective-permute-done.11 = bf16[1,4,64,256]{3,2,1,0:T(8,128)(2,1)S(1)} collective-permute-done((bf16[1,4,64,256]{3,2,1,0:T(8,128)(2,1)S(1)}, bf16[1,4,64,256]{3,2,1,0:T(8,128)(2,1)S(1)}, u32[]{:S(2)}, u32[]{:S(2)}) %collective-permute-start.11) | collective-permute-done | bytes 131104 | tf_op jit(solution)/shard_map/ppermute | solution.py:379
  51.4 0.9 %place_last.1 = (bf16[2048,128]{1,0:T(8,128)(2,1)}, bf16[2048,128]{1,0:T(8,128)(2,1)}, bf16[256,128]{1,0:T(8,128)(2,1)}, bf16[256,128]{1,0:T(8,128)(2,1)}) custom-call(bf16[2,256,128]{2,1,0:T(8,128)(2,1)S(1)} %collective-permute-done.5.refs_0_, ...), custom_call_target="tpu_custom_call", output_to_operand_aliasing={{0}: (5, {}), {1}: (6, {})} | custom-call | flops 12683575296 | bytes 3145728 | tf_op jit(solution)/shard_map/place_last/pallas_call | solution.py:239
  (2 shorter events, 0.0 us)
Async XLA Ops:
  0.6 12.3 %collective-permute-start.1 = (bf16[256,128]{1,0:T(8,128)(2,1)}, bf16[256,128]{1,0:T(8,128)(2,1)S(1)}, u32[]{:S(2)}, u32[]{:S(2)}) collective-permute-start(bf16[256,128]{1,0:T(8,128)(2,1)} %bitcast.14), channel_id=1, source_target_pairs={{0,4},{4,8},{8,12},{12,0},{1,5},{5,9},{9,13},{13,1},{2,6},{6,10},{... | collective-permute-start | bytes 196616 | tf_op jit(solution)/shard_map/ppermute | solution.py:379
  3.7 9.3 %collective-permute-start.2 = (bf16[256,128]{1,0:T(8,128)(2,1)}, bf16[256,128]{1,0:T(8,128)(2,1)S(1)}, u32[]{:S(2)}, u32[]{:S(2)}) collective-permute-start(bf16[256,128]{1,0:T(8,128)(2,1)} %bitcast.17), channel_id=1, source_target_pairs={{0,4},{4,8},{8,12},{12,0},{1,5},{5,9},{9,13},{13,1},{2,6},{6,10},{... | collective-permute-start | bytes 196616 | tf_op jit(solution)/shard_map/ppermute | solution.py:379
  5.3 7.7 %collective-permute-start.3 = (bf16[256,128]{1,0:T(8,128)(2,1)}, bf16[256,128]{1,0:T(8,128)(2,1)S(1)}, u32[]{:S(2)}, u32[]{:S(2)}) collective-permute-start(bf16[256,128]{1,0:T(8,128)(2,1)} %bitcast.15), channel_id=1, source_target_pairs={{0,8},{4,12},{8,4},{12,0},{1,9},{5,13},{9,5},{13,1},{2,10},{6,14},... | collective-permute-start | bytes 196616 | tf_op jit(solution)/shard_map/ppermute | solution.py:379
  6.4 6.6 %collective-permute-start.4 = (bf16[256,128]{1,0:T(8,128)(2,1)}, bf16[256,128]{1,0:T(8,128)(2,1)S(1)}, u32[]{:S(2)}, u32[]{:S(2)}) collective-permute-start(bf16[256,128]{1,0:T(8,128)(2,1)} %bitcast.18), channel_id=1, source_target_pairs={{0,8},{4,12},{8,4},{12,0},{1,9},{5,13},{9,5},{13,1},{2,10},{6,14},... | collective-permute-start | bytes 196616 | tf_op jit(solution)/shard_map/ppermute | solution.py:379
  8.3 0.7 %copy-start = (s32[4,4]{1,0:T(4,128)S(1)}, s32[4,4]{1,0:T(4,128)}, u32[]{:S(2)}) copy-start(s32[4,4]{1,0:T(4,128)} %owners_ref.1) | copy-start | bytes 196
  9.0 0.7 %copy-start.1 = (s32[8]{0:T(128)S(1)}, s32[8]{0:T(128)}, u32[]{:S(2)}) copy-start(s32[8]{0:T(128)} %ends_ref.1) | copy-start | bytes 100
  12.3 11.3 %collective-permute-start = (bf16[2,256,128]{2,1,0:T(8,128)(2,1)S(1)}, bf16[2,256,128]{2,1,0:T(8,128)(2,1)S(1)}, u32[]{:S(2)}, u32[]{:S(2)}) collective-permute-start(bf16[2,256,128]{2,1,0:T(8,128)(2,1)S(1)} %get-tuple-element.31.own_ref), channel_id=1, source_target_pairs={{4,8},{8,4},{5,9},{9,5},{6,10},{10,6},{7,11},{11,7},{20,24},{24,20... | collective-permute-start | bytes 393224 | tf_op jit(solution)/shard_map/ppermute | solution.py:379
  15.0 27.2 %collective-permute-start.8 = (bf16[2,512,128]{2,1,0:T(8,128)(2,1)S(1)}, bf16[2,512,128]{2,1,0:T(8,128)(2,1)S(1)}, u32[]{:S(2)}, u32[]{:S(2)}) collective-permute-start(bf16[2,512,128]{2,1,0:T(8,128)(2,1)S(1)} %get-tuple-element.42), channel_id=1, source_target_pairs={{0,8},{4,12},{8,0},{12,4},{1,9},{5,13},{9,1},{13,5},{2,10},{6,14},... | collective-permute-start | bytes 786440 | tf_op jit(solution)/shard_map/ppermute | solution.py:379
  25.4 16.8 %collective-permute-start.9 = (bf16[2,3,64,256]{3,2,1,0:T(8,128)(2,1)S(1)}, bf16[2,3,64,256]{3,2,1,0:T(8,128)(2,1)S(1)}, u32[]{:S(2)}, u32[]{:S(2)}) collective-permute-start(bf16[2,3,64,256]{3,2,1,0:T(8,128)(2,1)S(1)} %get-tuple-element.46), channel_id=1, source_target_pairs={{0,4},{4,0},{8,12},{12,8},{1,5},{5,1},{9,13},{13,9},{2,6},{6,2},{1... | collective-permute-start | bytes 589832 | tf_op jit(solution)/shard_map/ppermute | solution.py:379
  29.4 4.3 %collective-permute-start.10 = (bf16[2,1,64,256]{3,2,1,0:T(8,128)(2,1)S(1)}, bf16[2,1,64,256]{3,2,1,0:T(8,128)(2,1)S(1)}, u32[]{:S(2)}, u32[]{:S(2)}) collective-permute-start(bf16[2,1,64,256]{3,2,1,0:T(8,128)(2,1)S(1)} %get-tuple-element.47), channel_id=1, source_target_pairs={{8,12},{12,8},{9,13},{13,9},{10,14},{14,10},{11,15},{15,11},{24,28... | collective-permute-start | bytes 196616 | tf_op jit(solution)/shard_map/ppermute | solution.py:379
  30.1 16.5 %collective-permute-start.7 = (bf16[2,512,128]{2,1,0:T(8,128)(2,1)S(1)}, bf16[2,512,128]{2,1,0:T(8,128)(2,1)S(1)}, u32[]{:S(2)}, u32[]{:S(2)}) collective-permute-start(bf16[2,512,128]{2,1,0:T(8,128)(2,1)S(1)} %get-tuple-element.41), channel_id=1, source_target_pairs={{0,4},{4,0},{8,12},{12,8},{1,5},{5,1},{9,13},{13,9},{2,6},{6,2},{1... | collective-permute-start | bytes 786440 | tf_op jit(solution)/shard_map/ppermute | solution.py:379
  30.1 13.0 %collective-permute-start.6 = (bf16[2,256,128]{2,1,0:T(8,128)(2,1)S(1)}, bf16[2,256,128]{2,1,0:T(8,128)(2,1)S(1)}, u32[]{:S(2)}, u32[]{:S(2)}) collective-permute-start(bf16[2,256,128]{2,1,0:T(8,128)(2,1)S(1)} %get-tuple-element.40), channel_id=1, source_target_pairs={{0,12},{4,8},{8,4},{12,0},{1,13},{5,9},{9,5},{13,1},{2,14},{6,10},... | collective-permute-start | bytes 393224 | tf_op jit(solution)/shard_map/ppermute | solution.py:379
  33.7 12.9 %collective-permute-start.5 = (bf16[2,256,128]{2,1,0:T(8,128)(2,1)S(1)}, bf16[2,256,128]{2,1,0:T(8,128)(2,1)S(1)}, u32[]{:S(2)}, u32[]{:S(2)}) collective-permute-start(bf16[2,256,128]{2,1,0:T(8,128)(2,1)S(1)} %get-tuple-element.39.refs_2_), channel_id=1, source_target_pairs={{0,12},{12,0},{1,13},{13,1},{2,14},{14,2},{3,15},{15,3},{16,28},{2... | collective-permute-start | bytes 393224 | tf_op jit(solution)/shard_map/ppermute | solution.py:379
  43.1 8.4 %collective-permute-start.11 = (bf16[1,4,64,256]{3,2,1,0:T(8,128)(2,1)S(1)}, bf16[1,4,64,256]{3,2,1,0:T(8,128)(2,1)S(1)}, u32[]{:S(2)}, u32[]{:S(2)}) collective-permute-start(bf16[1,4,64,256]{3,2,1,0:T(8,128)(2,1)S(1)} %get-tuple-element.49), channel_id=1, source_target_pairs={{0,8},{4,12},{8,0},{12,4},{1,9},{5,13},{9,1},{13,5},{2,10},{6,14},... | collective-permute-start | bytes 393224 | tf_op jit(solution)/shard_map/ppermute | solution.py:379

commit v13 on v9

--- a/solution.py
+++ b/solution.py
@@ -109,24 +109,27 @@
         copy.wait()
 
 
-def first_kernel(plan, apart, meta, qg, *refs):
-    kv_refs, (pay_ref, grad_ref, k_win, v_win) = refs[:-4], refs[-4:]
+def first_kernel(plan, entries, meta, *refs):
+    count = len(entries)
+    qg_refs, kv_refs = refs[:count], refs[count : -2 * count - 2]
+    pay_refs, grad_refs, (k_win, v_win) = refs[-2 * count - 2 : -count - 2], refs[-count - 2 : -2], refs[-2:]
     own = meta[0]
-    slot = plan.slot(meta, own, own ^ apart)
     fill_window(plan, kv_refs, k_win, v_win)
-    _, (attended, query_grad, key_part, value_part) = attend_at(
-        plan, meta, own, slot, qg[0], qg[1], k_win, v_win
-    )
-    pay_ref[0] = attended
-    pay_ref[1] = query_grad
-    grad_ref[:, : plan.width] = key_part
-    grad_ref[:, plan.width :] = value_part
-
-
-def last_kernel(plan, first, items, meta, *refs):
+    for apart, qg, pay_ref, grad_ref in zip(entries, qg_refs, pay_refs, grad_refs):
+        slot = plan.slot(meta, own, own ^ apart)
+        _, (attended, query_grad, key_part, value_part) = attend_at(
+            plan, meta, own, slot, qg[0], qg[1], k_win, v_win
+        )
+        pay_ref[0] = attended
+        pay_ref[1] = query_grad
+        grad_ref[:, : plan.width] = key_part
+        grad_ref[:, plan.width :] = value_part
+
+
+def last_kernel(plan, done, items, meta, *refs):
     n, width, rows, block = plan.n, plan.width, plan.rows, plan.block
     qg_refs, refs = refs[: len(items)], refs[len(items) :]
-    first_grad, refs = refs[0], refs[1:]
+    done_refs, refs = refs[: len(done)], refs[len(done) :]
     kv_refs, refs = refs[: -(len(items) + 7)], refs[-(len(items) + 7) :]
     pay_refs, grad_refs, (k_win, v_win, acc) = refs[: len(items)], refs[len(items) : -3], refs[-3:]
     step = pl.program_id(0)
@@ -136,9 +139,10 @@
     def _():
         fill_window(plan, kv_refs, k_win, v_win)
         acc[...] = jnp.zeros_like(acc)
-        slot = plan.slot(meta, own, own ^ first)
-        keys_here = pl.ds(pl.multiple_of(slot * block, block), plan.reach + block)
-        acc[keys_here, :] = first_grad[...]
+        for x, grad_ref in zip(done, done_refs):
+            slot = plan.slot(meta, own, own ^ x)
+            keys_here = pl.ds(pl.multiple_of(slot * block, block), plan.reach + block)
+            acc[keys_here, :] = acc[keys_here, :] + grad_ref[...]
 
     for i, item in enumerate(items):
 
@@ -207,30 +211,29 @@
     )
 
 
-def attend_first(plan, apart, meta, qg, kv_list):
+def attend_first(plan, entries, meta, qg_list, kv_list):
     window = pltpu.VMEM((plan.window_ranges * plan.rows, plan.width), jnp.bfloat16)
-    out_shape = [
-        jax.ShapeDtypeStruct((2, plan.cols, plan.width), jnp.bfloat16),
-        jax.ShapeDtypeStruct((plan.reach + plan.block, 2 * plan.width), jnp.float32),
-    ]
-    operands = (meta, qg, *kv_list)
+    rows = jax.ShapeDtypeStruct((2, plan.cols, plan.width), jnp.bfloat16)
+    grad = jax.ShapeDtypeStruct((plan.reach + plan.block, 2 * plan.width), jnp.float32)
+    out_shape = [rows] * len(entries) + [grad] * len(entries)
+    operands = (meta, *qg_list, *kv_list)
     return kernel_call(
-        functools.partial(first_kernel, plan, apart), "attend_first", operands,
+        functools.partial(first_kernel, plan, entries), "attend_first", operands,
         [pltpu.SMEM] + [pltpu.VMEM] * (len(operands) - 1), out_shape, [window, window],
-        out_specs=[spec_of(pltpu.VMEM)] * 2, cost_estimate=plan.cost(1),
-    )
-
-
-def attend_last(plan, first, items, meta, qg_list, first_grad, kv_list):
+        out_specs=[spec_of(pltpu.VMEM)] * len(out_shape), cost_estimate=plan.cost(len(entries)),
+    )
+
+
+def attend_last(plan, done, items, meta, qg_list, done_grads, kv_list):
     n = plan.n
     window = pltpu.VMEM((plan.window_ranges * plan.rows, plan.width), jnp.bfloat16)
     keep = jax.ShapeDtypeStruct((n // 4, n, plan.block, 2 * plan.width), jnp.float32)
     send = jax.ShapeDtypeStruct((n // 2, n // 2, plan.block, 2 * plan.width), jnp.bfloat16)
     out_shape = [jax.ShapeDtypeStruct((2, plan.cols, plan.width), jnp.bfloat16)] * len(items)
     out_shape += [keep, keep, send, send]
-    operands = (meta, *qg_list, first_grad, *kv_list)
+    operands = (meta, *qg_list, *done_grads, *kv_list)
     return kernel_call(
-        functools.partial(last_kernel, plan, first, items), "attend_last", operands,
+        functools.partial(last_kernel, plan, done, items), "attend_last", operands,
         [pltpu.SMEM] + [pltpu.VMEM] * (len(operands) - 1), out_shape,
         [window, window, pltpu.VMEM((n * plan.rows, 2 * plan.width), jnp.float32)],
         out_specs=[spec_of(pltpu.VMEM)] * len(out_shape), cost_estimate=plan.cost(len(items)), grid=(len(items),),
@@ -273,22 +276,24 @@
         copy.wait()
 
 
-def place(plan, payloads, grads, filled=()):
+def place(plan, payloads, grads, filled=(), final=False):
     items = tuple(payloads)
-    big = jax.ShapeDtypeStruct((plan.rows * plan.heads, plan.width), jnp.bfloat16)
-    small = jax.ShapeDtypeStruct((plan.rows, plan.width), jnp.bfloat16)
-    final = len(filled) > 0
-    at = len(items) + len(grads)
+    out_shape = [jax.ShapeDtypeStruct((plan.rows * plan.heads, plan.width), jnp.bfloat16)] * 2
+    out_specs = [spec_of(pl.ANY)] * 2
     scratch = [pltpu.SemaphoreType.DMA((len(items), 2))]
     if final:
+        out_shape += [jax.ShapeDtypeStruct((plan.rows, plan.width), jnp.bfloat16)] * 2
+        out_specs += [spec_of(pl.ANY)] * 2
         scratch = [pltpu.VMEM((2, plan.rows, plan.width), jnp.bfloat16), *scratch, pltpu.SemaphoreType.DMA((2,))]
+    else:
+        out_shape += [jax.ShapeDtypeStruct(grads[0].shape, kind) for kind in (jnp.bfloat16, jnp.float32)]
+        out_specs += [spec_of(pltpu.VMEM)] * 2
+    at = len(items) + len(grads)
     return kernel_call(
-        functools.partial(place_kernel, plan, items, final), "place_last" if final else "place_first",
+        functools.partial(place_kernel, plan, items, final), "place_" + "_".join(map(str, items)),
         (*payloads.values(), *grads, *filled),
         [pl.ANY] * len(items) + [pltpu.VMEM] * len(grads) + [pl.ANY] * len(filled),
-        [big, big] + ([small, small] if final else [jax.ShapeDtypeStruct(grads[0].shape, t) for t in (jnp.bfloat16, jnp.float32)]), scratch,
-        out_specs=[spec_of(pl.ANY)] * 2 + [spec_of(pl.ANY if final else pltpu.VMEM)] * 2,
-        input_output_aliases={at: 0, at + 1: 1} if final else {},
+        out_shape, scratch, out_specs=out_specs, input_output_aliases={at: 0, at + 1: 1} if filled else {},
         cost_estimate=plan.cost(len(items)),
     )
 
@@ -322,17 +327,17 @@
     q, g = (x.reshape(rows * heads, width) for x in (query, output_gradient))
     *blocks, kv = pack(plan, meta, q, g, k, v)
     kv_list = [kv, *kv_list]
-    first = n // 2
-    first_pay, first_grad = attend_first(plan, first, meta, blocks[first], kv_list)
-    stay = {first: across(first_pay, first)}
-    sent = [x for x in range(1, n) if x != first]
+    first = (n // 2, 1)
+    first_pay, near_pay, *first_grads = attend_first(plan, first, meta, [blocks[x] for x in first], kv_list)
+    stay = {x: across(pay, x) for x, pay in zip(first, (first_pay, near_pay))}
+    sent = [x for x in range(1, n) if x not in first]
     items = (*sent, 0)
-    out = attend_last(plan, first, items, meta, [blocks[x] for x in items], first_grad, kv_list)
+    out = attend_last(plan, first, items, meta, [blocks[x] for x in items], first_grads, kv_list)
     late = {x: across(pay, x) for x, pay in zip(sent, out)}
     stay[0] = out[len(sent)]
     keep, pass_on, lower, upper = out[len(items) :]
     upper = permuted(upper, [(i, i ^ 1) for i in range(n // 2, n)])
-    attended, query_grad, send, keep = place(plan, stay, (pass_on, keep, across(lower, 1), upper))
+    *filled, send, keep = place(plan, stay, (pass_on, keep, across(lower, 1), upper))
     terms = (keep, across(send, 2))
     bit = 4
     while bit < n:
@@ -340,7 +345,7 @@
         terms = (total[0::2], across(total[1::2].astype(jnp.bfloat16), bit))
         bit *= 2
     terms = [term.reshape(rows, 2 * width) for term in terms]
-    attended, query_grad, key_grad, value_grad = place(plan, late, terms, (attended, query_grad))
+    attended, query_grad, key_grad, value_grad = place(plan, late, terms, filled, final=True)
     return (
         attended.reshape(rows, heads, width),
         query_grad.reshape(rows, heads, width),

time: 49.6 us -> 51.6 us (1.040)
  starting transfers between devices: 19.3 us -> 24.3 us
  waiting for transfers between devices: 17.1 us -> 14.2 us
    ppermute x10, starting transfers between devices: 19.3 us -> 24.3 us  [permuted(): return lax.ppermute(array, 'ctx', pairs)]
    ppermute x10, waiting for transfers between devices: 17.1 us -> 14.2 us  [permuted(): return lax.ppermute(array, 'ctx', pairs)]
  transfers between devices with their start and end apart: 10 -> 10, of which waited for: 4 -> 3; matrix products, arithmetic and copies ran while one was open for 1% -> 1% of each run, Pallas kernels for 15% -> 13%
where the time goes in v13:
time: 51.6 us; the launch traced here: 51.4 us
  starting transfers between devices  24.3 us (47%)
  waiting for transfers between devices  14.2 us (28%)
  Pallas kernels  10.4 us (20%)
  local copies, waits for them, and re-layouts  1.43 us (3%)
  between operations  0.7 us (1%)
    ppermute x10, starting transfers between devices, permuted(): return lax.ppermute(array, 'ctx', pairs)  24.3 us
    ppermute x10, waiting for transfers between devices, permuted(): return lax.ppermute(array, 'ctx', pairs)  14.2 us
    pallas_call x5, Pallas kernels, kernel_call(): pl.pallas_call(body, out_shape=out_shape, in_specs=[spec_of(space) for sp...  10.4 us
    unnamed x4, local copies, waits for them, and re-layouts  1.35 us
  transfers between devices with their start and end apart: 10, of which 3 were waited for; matrix products, arithmetic and copies ran while one was open for 1% of the time, Pallas kernels for 13%

profile of v13, /device:TPU:0, one launch (start us, length us, event | category | flops | bytes accessed | tf_op | source)
XLA Modules:
  0.0 51.4 jit_solution(9335638237938094196)
XLA Ops:
  0.6 4.1 %collective-permute-start.2 = (bf16[256,128]{1,0:T(8,128)(2,1)}, bf16[256,128]{1,0:T(8,128)(2,1)S(1)}, u32[]{:S(2)}, u32[]{:S(2)}) collective-permute-start(bf16[256,128]{1,0:T(8,128)(2,1)} %bitcast.17), channel_id=1, source_target_pairs={{0,8},{4,12},{8,0},{12,4},{1,9},{5,13},{9,1},{13,5},{2,10},{6,14},... | collective-permute-start | bytes 196616 | tf_op jit(solution)/shard_map/ppermute | solution.py:308
  4.7 1.6 %collective-permute-start = (bf16[256,128]{1,0:T(8,128)(2,1)}, bf16[256,128]{1,0:T(8,128)(2,1)S(1)}, u32[]{:S(2)}, u32[]{:S(2)}) collective-permute-start(bf16[256,128]{1,0:T(8,128)(2,1)} %bitcast.18), channel_id=1, source_target_pairs={{0,4},{4,8},{8,12},{12,0},{1,5},{5,9},{9,13},{13,1},{2,6},{6,10},{... | collective-permute-start | bytes 196616 | tf_op jit(solution)/shard_map/ppermute | solution.py:308
  6.3 0.3 collective-permute-start.3
  6.6 2.5 %collective-permute-start.1 = (bf16[256,128]{1,0:T(8,128)(2,1)}, bf16[256,128]{1,0:T(8,128)(2,1)S(1)}, u32[]{:S(2)}, u32[]{:S(2)}) collective-permute-start(bf16[256,128]{1,0:T(8,128)(2,1)} %bitcast.21), channel_id=1, source_target_pairs={{0,4},{4,8},{8,12},{12,0},{1,5},{5,9},{9,13},{13,1},{2,6},{6,10},{... | collective-permute-start | bytes 196616 | tf_op jit(solution)/shard_map/ppermute | solution.py:308
  9.1 0.0 copy-start
  9.1 0.7 %copy-done = s32[4,4]{1,0:T(4,128)S(1)} copy-done((s32[4,4]{1,0:T(4,128)S(1)}, s32[4,4]{1,0:T(4,128)}, u32[]{:S(2)}) %copy-start) | copy-done | bytes 88
  9.8 0.1 select_reduce_fusion
  9.9 0.1 reshape.74
  10.0 0.7 %copy-done.1 = s32[8]{0:T(128)S(1)} copy-done((s32[8]{0:T(128)S(1)}, s32[8]{0:T(128)}, u32[]{:S(2)}) %copy-start.1) | copy-done | bytes 56
  10.7 0.2 reduce-window.9
  10.9 0.1 pad_add_fusion.meta
  11.0 1.9 %pack.1 = (bf16[2,512,128]{2,1,0:T(8,128)(2,1)S(1)}, bf16[2,512,128]{2,1,0:T(8,128)(2,1)S(1)}, bf16[2,512,128]{2,1,0:T(8,128)(2,1)S(1)}, bf16[2,512,128]{2,1,0:T(8,128)(2,1)S(1)}, bf16[512,128]{1,0:T(8,128)(2,1)S(1)}) custom-call(s32[25]{0:T(128)S(1)} %pad_add_fusion.meta, bf16[2048,128]{1,0:T(8,128)(2,1)} %bitcast.15, bf16[2048,128]{1,0:T(8,128)(2,1)} %bitcast.16, ...), custom_call_target="tpu_custom_call" | custom-call | tf_op jit(solution)/shard_map/pack/pallas_call | solution.py:192
  12.9 0.0 collective-permute-done.2.refs_5_.refs_7_
  12.9 0.0 collective-permute-done.refs_3_.refs_5_
  12.9 1.6 %collective-permute-done.3.refs_6_.refs_8_ = bf16[256,128]{1,0:T(8,128)(2,1)S(1)} collective-permute-done((bf16[256,128]{1,0:T(8,128)(2,1)}, bf16[256,128]{1,0:T(8,128)(2,1)S(1)}, u32[]{:S(2)}, u32[]{:S(2)}) %collective-permute-start.3) | collective-permute-done | bytes 65568 | tf_op jit(solution)/shard_map/ppermute | solution.py:308
  14.5 0.0 collective-permute-done.1.refs_4_.refs_6_
  14.5 3.2 %attend_first.1 = (bf16[2,512,128]{2,1,0:T(8,128)(2,1)S(1)}, bf16[2,512,128]{2,1,0:T(8,128)(2,1)S(1)}, f32[576,256]{1,0:T(8,128)S(1)}, f32[576,256]{1,0:T(8,128)S(1)}) custom-call(s32[25]{0:T(128)S(1)} %pad_add_fusion.meta, bf16[2,512,128]{2,1,0:T(8,128)(2,1)S(1)} %get-tuple-element.29.refs_0_, bf16[2,512,128]{2,1,0:T(8,128)(2,1)S(1)} %get-tuple-element.30.refs_1_, ...), custom_call_target="tpu_custom_call" | custom-call | flops 8455716864 | bytes 2097152 | tf_op jit(solution)/shard_map/attend_first/pallas_call | solution.py:192
  17.7 2.3 %collective-permute-start.5 = (bf16[2,512,128]{2,1,0:T(8,128)(2,1)S(1)}, bf16[2,512,128]{2,1,0:T(8,128)(2,1)S(1)}, u32[]{:S(2)}, u32[]{:S(2)}) collective-permute-start(bf16[2,512,128]{2,1,0:T(8,128)(2,1)S(1)} %get-tuple-element.35), channel_id=1, source_target_pairs={{0,8},{4,12},{8,0},{12,4},{1,9},{5,13},{9,1},{13,5},{2,10},{6,14},... | collective-permute-start | bytes 786440 | tf_op jit(solution)/shard_map/ppermute | solution.py:308
  19.9 0.5 collective-permute-start.6
  20.4 3.6 %attend_last.1 = (bf16[2,512,128]{2,1,0:T(8,128)(2,1)S(1)}, bf16[2,512,128]{2,1,0:T(8,128)(2,1)S(1)}, f32[1,4,64,256]{3,2,1,0:T(8,128)S(1)}, f32[1,4,64,256]{3,2...) custom-call(s32[25]{0:T(128)S(1)} %pad_add_fusion.meta, ...), custom_call_target="tpu_custom_call" | custom-call | flops 8455716864 | bytes 2097152 | tf_op jit(solution)/shard_map/attend_last/pallas_call | solution.py:192
  24.1 1.6 %collective-permute-start.7 = (bf16[2,2,64,256]{3,2,1,0:T(8,128)(2,1)S(1)}, bf16[2,2,64,256]{3,2,1,0:T(8,128)(2,1)S(1)}, u32[]{:S(2)}, u32[]{:S(2)}) collective-permute-start(bf16[2,2,64,256]{3,2,1,0:T(8,128)(2,1)S(1)} %get-tuple-element.40), channel_id=1, source_target_pairs={{0,4},{4,0},{8,12},{12,8},{1,5},{5,1},{9,13},{13,9},{2,6},{6,2},{1... | collective-permute-start | bytes 393224 | tf_op jit(solution)/shard_map/ppermute | solution.py:308
  25.6 0.7 %collective-permute-start.8 = (bf16[2,2,64,256]{3,2,1,0:T(8,128)(2,1)S(1)}, bf16[2,2,64,256]{3,2,1,0:T(8,128)(2,1)S(1)}, u32[]{:S(2)}, u32[]{:S(2)}) collective-permute-start(bf16[2,2,64,256]{3,2,1,0:T(8,128)(2,1)S(1)} %get-tuple-element.41), channel_id=1, source_target_pairs={{8,12},{12,8},{9,13},{13,9},{10,14},{14,10},{11,15},{15,11},{24,28... | collective-permute-start | bytes 393224 | tf_op jit(solution)/shard_map/ppermute | solution.py:308
  26.3 3.5 %collective-permute-start.4 = (bf16[2,512,128]{2,1,0:T(8,128)(2,1)S(1)}, bf16[2,512,128]{2,1,0:T(8,128)(2,1)S(1)}, u32[]{:S(2)}, u32[]{:S(2)}) collective-permute-start(bf16[2,512,128]{2,1,0:T(8,128)(2,1)S(1)} %get-tuple-element.34), channel_id=1, source_target_pairs={{0,12},{4,8},{8,4},{12,0},{1,13},{5,9},{9,5},{13,1},{2,14},{6,10},... | collective-permute-start | bytes 786440 | tf_op jit(solution)/shard_map/ppermute | solution.py:308
  29.8 6.1 %collective-permute-done.7.refs_5_ = bf16[2,2,64,256]{3,2,1,0:T(8,128)(2,1)S(1)} collective-permute-done((bf16[2,2,64,256]{3,2,1,0:T(8,128)(2,1)S(1)}, bf16[2,2,64,256]{3,2,1,0:T(8,128)(2,1)S(1)}, u32[]{:S(2)}, u32[]{:S(2)}) %collective-permute-start.7) | collective-permute-done | bytes 131104 | tf_op jit(solution)/shard_map/ppermute | solution.py:308
  35.9 0.0 collective-permute-done.8.refs_6_
  35.9 0.0 collective-permute-done.5.refs_0_
  35.9 0.0 collective-permute-done.6.refs_1_
  35.9 0.9 %place_2_1_0.1 = (bf16[2048,128]{1,0:T(8,128)(2,1)}, bf16[2048,128]{1,0:T(8,128)(2,1)}, bf16[1,4,64,256]{3,2,1,0:T(8,128)(2,1)S(1)}, f32[1,4,64,256]{3,2,1,0:T(8,128)S(1)}) custom-call(bf16[2,512,128]{2,1,0:T(8,128)(2,1)S(1)} %collective-permute-done.5.refs_0_, bf16[2,512,128]{2,1,0:T(8,128)(2,1)S(1)} %collective-permute-done.6.refs_1_, ...), custom_call_target="tpu_custom_call" | custom-call | flops 12683575296 | bytes 3145728 | tf_op jit(solution)/shard_map/place_2_1_0/pallas_call | solution.py:192
  36.9 7.3 %collective-permute-start.9 = (bf16[1,4,64,256]{3,2,1,0:T(8,128)(2,1)S(1)}, bf16[1,4,64,256]{3,2,1,0:T(8,128)(2,1)S(1)}, u32[]{:S(2)}, u32[]{:S(2)}) collective-permute-start(bf16[1,4,64,256]{3,2,1,0:T(8,128)(2,1)S(1)} %get-tuple-element.43), channel_id=1, source_target_pairs={{0,8},{4,12},{8,0},{12,4},{1,9},{5,13},{9,1},{13,5},{2,10},{6,14},... | collective-permute-start | bytes 393224 | tf_op jit(solution)/shard_map/ppermute | solution.py:308
  44.2 0.0 collective-permute-done.4.refs_0_
  44.2 6.5 %collective-permute-done.9 = bf16[1,4,64,256]{3,2,1,0:T(8,128)(2,1)S(1)} collective-permute-done((bf16[1,4,64,256]{3,2,1,0:T(8,128)(2,1)S(1)}, bf16[1,4,64,256]{3,2,1,0:T(8,128)(2,1)S(1)}, u32[]{:S(2)}, u32[]{:S(2)}) %collective-permute-start.9) | collective-permute-done | bytes 131104 | tf_op jit(solution)/shard_map/ppermute | solution.py:308
  50.6 0.8 %place_3.1 = (bf16[2048,128]{1,0:T(8,128)(2,1)}, bf16[2048,128]{1,0:T(8,128)(2,1)}, bf16[256,128]{1,0:T(8,128)(2,1)}, bf16[256,128]{1,0:T(8,128)(2,1)}) custom-call(bf16[2,512,128]{2,1,0:T(8,128)(2,1)S(1)} %collective-permute-done.4.refs_0_, f32[256,256]{1,0:T(8,128)S(1)} %bitcast.14, ...), custom_call_target="tpu_custom_call", output_to_operand_aliasing={{0}: (3, {}), {1}: (4, {})} | custom-call | flops 4227858432 | bytes 1048576 | tf_op jit(solution)/shard_map/place_3/pallas_call | solution.py:192
  (1 shorter events, 0.0 us)
Async XLA Ops:
  0.6 12.3 %collective-permute-start.2 = (bf16[256,128]{1,0:T(8,128)(2,1)}, bf16[256,128]{1,0:T(8,128)(2,1)S(1)}, u32[]{:S(2)}, u32[]{:S(2)}) collective-permute-start(bf16[256,128]{1,0:T(8,128)(2,1)} %bitcast.17), channel_id=1, source_target_pairs={{0,8},{4,12},{8,0},{12,4},{1,9},{5,13},{9,1},{13,5},{2,10},{6,14},... | collective-permute-start | bytes 196616 | tf_op jit(solution)/shard_map/ppermute | solution.py:308
  4.7 8.2 %collective-permute-start = (bf16[256,128]{1,0:T(8,128)(2,1)}, bf16[256,128]{1,0:T(8,128)(2,1)S(1)}, u32[]{:S(2)}, u32[]{:S(2)}) collective-permute-start(bf16[256,128]{1,0:T(8,128)(2,1)} %bitcast.18), channel_id=1, source_target_pairs={{0,4},{4,8},{8,12},{12,0},{1,5},{5,9},{9,13},{13,1},{2,6},{6,10},{... | collective-permute-start | bytes 196616 | tf_op jit(solution)/shard_map/ppermute | solution.py:308
  6.3 8.2 %collective-permute-start.3 = (bf16[256,128]{1,0:T(8,128)(2,1)}, bf16[256,128]{1,0:T(8,128)(2,1)S(1)}, u32[]{:S(2)}, u32[]{:S(2)}) collective-permute-start(bf16[256,128]{1,0:T(8,128)(2,1)} %bitcast.20), channel_id=1, source_target_pairs={{0,8},{4,12},{8,0},{12,4},{1,9},{5,13},{9,1},{13,5},{2,10},{6,14},... | collective-permute-start | bytes 196616 | tf_op jit(solution)/shard_map/ppermute | solution.py:308
  6.6 7.9 %collective-permute-start.1 = (bf16[256,128]{1,0:T(8,128)(2,1)}, bf16[256,128]{1,0:T(8,128)(2,1)S(1)}, u32[]{:S(2)}, u32[]{:S(2)}) collective-permute-start(bf16[256,128]{1,0:T(8,128)(2,1)} %bitcast.21), channel_id=1, source_target_pairs={{0,4},{4,8},{8,12},{12,0},{1,5},{5,9},{9,13},{13,1},{2,6},{6,10},{... | collective-permute-start | bytes 196616 | tf_op jit(solution)/shard_map/ppermute | solution.py:308
  9.1 0.7 %copy-start = (s32[4,4]{1,0:T(4,128)S(1)}, s32[4,4]{1,0:T(4,128)}, u32[]{:S(2)}) copy-start(s32[4,4]{1,0:T(4,128)} %param.11) | copy-start | bytes 196
  10.0 0.7 %copy-start.1 = (s32[8]{0:T(128)S(1)}, s32[8]{0:T(128)}, u32[]{:S(2)}) copy-start(s32[8]{0:T(128)} %param.10) | copy-start | bytes 100
  17.7 18.2 %collective-permute-start.5 = (bf16[2,512,128]{2,1,0:T(8,128)(2,1)S(1)}, bf16[2,512,128]{2,1,0:T(8,128)(2,1)S(1)}, u32[]{:S(2)}, u32[]{:S(2)}) collective-permute-start(bf16[2,512,128]{2,1,0:T(8,128)(2,1)S(1)} %get-tuple-element.35), channel_id=1, source_target_pairs={{0,8},{4,12},{8,0},{12,4},{1,9},{5,13},{9,1},{13,5},{2,10},{6,14},... | collective-permute-start | bytes 786440 | tf_op jit(solution)/shard_map/ppermute | solution.py:308
  19.9 16.0 %collective-permute-start.6 = (bf16[2,512,128]{2,1,0:T(8,128)(2,1)S(1)}, bf16[2,512,128]{2,1,0:T(8,128)(2,1)S(1)}, u32[]{:S(2)}, u32[]{:S(2)}) collective-permute-start(bf16[2,512,128]{2,1,0:T(8,128)(2,1)S(1)} %get-tuple-element.36), channel_id=1, source_target_pairs={{0,4},{4,0},{8,12},{12,8},{1,5},{5,1},{9,13},{13,9},{2,6},{6,2},{1... | collective-permute-start | bytes 786440 | tf_op jit(solution)/shard_map/ppermute | solution.py:308
  24.1 11.8 %collective-permute-start.7 = (bf16[2,2,64,256]{3,2,1,0:T(8,128)(2,1)S(1)}, bf16[2,2,64,256]{3,2,1,0:T(8,128)(2,1)S(1)}, u32[]{:S(2)}, u32[]{:S(2)}) collective-permute-start(bf16[2,2,64,256]{3,2,1,0:T(8,128)(2,1)S(1)} %get-tuple-element.40), channel_id=1, source_target_pairs={{0,4},{4,0},{8,12},{12,8},{1,5},{5,1},{9,13},{13,9},{2,6},{6,2},{1... | collective-permute-start | bytes 393224 | tf_op jit(solution)/shard_map/ppermute | solution.py:308
  25.6 10.3 %collective-permute-start.8 = (bf16[2,2,64,256]{3,2,1,0:T(8,128)(2,1)S(1)}, bf16[2,2,64,256]{3,2,1,0:T(8,128)(2,1)S(1)}, u32[]{:S(2)}, u32[]{:S(2)}) collective-permute-start(bf16[2,2,64,256]{3,2,1,0:T(8,128)(2,1)S(1)} %get-tuple-element.41), channel_id=1, source_target_pairs={{8,12},{12,8},{9,13},{13,9},{10,14},{14,10},{11,15},{15,11},{24,28... | collective-permute-start | bytes 393224 | tf_op jit(solution)/shard_map/ppermute | solution.py:308
  26.3 17.9 %collective-permute-start.4 = (bf16[2,512,128]{2,1,0:T(8,128)(2,1)S(1)}, bf16[2,512,128]{2,1,0:T(8,128)(2,1)S(1)}, u32[]{:S(2)}, u32[]{:S(2)}) collective-permute-start(bf16[2,512,128]{2,1,0:T(8,128)(2,1)S(1)} %get-tuple-element.34), channel_id=1, source_target_pairs={{0,12},{4,8},{8,4},{12,0},{1,13},{5,9},{9,5},{13,1},{2,14},{6,10},... | collective-permute-start | bytes 786440 | tf_op jit(solution)/shard_map/ppermute | solution.py:308
  36.9 13.8 %collective-permute-start.9 = (bf16[1,4,64,256]{3,2,1,0:T(8,128)(2,1)S(1)}, bf16[1,4,64,256]{3,2,1,0:T(8,128)(2,1)S(1)}, u32[]{:S(2)}, u32[]{:S(2)}) collective-permute-start(bf16[1,4,64,256]{3,2,1,0:T(8,128)(2,1)S(1)} %get-tuple-element.43), channel_id=1, source_target_pairs={{0,8},{4,12},{8,0},{12,4},{1,9},{5,13},{9,1},{13,5},{2,10},{6,14},... | collective-permute-start | bytes 393224 | tf_op jit(solution)/shard_map/ppermute | solution.py:308

commit v14 on v8

--- a/solution.py
+++ b/solution.py
@@ -56,6 +56,9 @@
         self.reach = self.back * rows
         self.scale = width ** (-0.5)
         self.window_ranges = self.back + 1
+
+    def pay_rows(self, x):
+        return 2 * self.cols + (2 * (self.n // 4) * self.n * self.block if x == 1 else 0)
 
     def ends(self, meta):
         return [meta[1 + i] for i in range(self.ndocs)]
@@ -117,8 +120,8 @@
     _, (attended, query_grad, key_part, value_part) = attend_at(
         plan, meta, own, slot, qg[0], qg[1], k_win, v_win
     )
-    pay_ref[0] = attended
-    pay_ref[1] = query_grad
+    pay_ref[pl.ds(0, plan.cols), :] = attended
+    pay_ref[pl.ds(plan.cols, plan.cols), :] = query_grad
     grad_ref[:, : plan.width] = key_part
     grad_ref[:, plan.width :] = value_part
 
@@ -151,18 +154,36 @@
             )
             acc[keys_here, :width] = acc[keys_here, :width] + key_part
             acc[keys_here, width:] = acc[keys_here, width:] + value_part
-            pay_refs[i][0] = attended
-            pay_refs[i][1] = query_grad
+            pay_refs[i][pl.ds(0, plan.cols), :] = attended
+            pay_refs[i][pl.ds(plan.cols, plan.cols), :] = query_grad
 
     @pl.when(step == len(items) - 1)
     def _():
+        near_ref = pay_refs[items.index(1)]
+
         def of_range(key_range, carry):
             at = lax.rem(key_range - own + plan.back + n, n) * rows
             for apart in range(n):
                 slot = plan.slot(meta, key_range, own ^ apart)
                 part = acc[pl.ds(pl.multiple_of(at + slot * block, block), block), :]
-                to = grad_refs[apart % 4]
-                to[apart // 4, key_range] = part.astype(to.dtype)
+                entry = apart // 4
+                if apart % 2 == 0:
+                    grad_refs[apart % 4 // 2][entry, key_range] = part
+                elif apart % 4 == 1:
+                    for half in range(2):
+                        to = 2 * plan.cols + ((half * (n // 4) + entry) * n + key_range) * block
+                        value = part[:, half * width : (half + 1) * width].astype(jnp.bfloat16)
+                        near_ref[pl.ds(pl.multiple_of(to, block), block), :] = value
+                else:
+
+                    @pl.when(key_range < n // 2)
+                    def _():
+                        grad_refs[2][entry, key_range] = part.astype(jnp.bfloat16)
+
+                    @pl.when(key_range >= n // 2)
+                    def _():
+                        grad_refs[3][entry, key_range - n // 2] = part.astype(jnp.bfloat16)
+
             return carry
 
         lax.fori_loop(0, n, of_range, 0)
@@ -198,7 +219,7 @@
 def attend_first(plan, apart, meta, qg, kv_list):
     window = pltpu.VMEM((plan.window_ranges * plan.rows, plan.width), jnp.bfloat16)
     out_shape = [
-        jax.ShapeDtypeStruct((2, plan.cols, plan.width), jnp.bfloat16),
+        jax.ShapeDtypeStruct((plan.pay_rows(apart), plan.width), jnp.bfloat16),
         jax.ShapeDtypeStruct((plan.reach + plan.block, 2 * plan.width), jnp.float32),
     ]
     operands = (meta, qg, *kv_list)
@@ -212,9 +233,10 @@
 def attend_last(plan, first, items, meta, qg_list, first_grad, kv_list):
     n = plan.n
     window = pltpu.VMEM((plan.window_ranges * plan.rows, plan.width), jnp.bfloat16)
-    grads = (n // 4, n, plan.block, 2 * plan.width)
-    out_shape = [jax.ShapeDtypeStruct((2, plan.cols, plan.width), jnp.bfloat16)] * len(items)
-    out_shape += [jax.ShapeDtypeStruct(grads, jnp.bfloat16 if apart % 2 else jnp.float32) for apart in range(4)]
+    keep = jax.ShapeDtypeStruct((n // 4, n, plan.block, 2 * plan.width), jnp.float32)
+    send = jax.ShapeDtypeStruct((n // 4, n // 2, plan.block, 2 * plan.width), jnp.bfloat16)
+    out_shape = [jax.ShapeDtypeStruct((plan.pay_rows(x), plan.width), jnp.bfloat16) for x in items]
+    out_shape += [keep, keep, send, send]
     operands = (meta, *qg_list, first_grad, *kv_list)
     return kernel_call(
         functools.partial(last_kernel, plan, first, items), "attend_last", operands,
@@ -225,47 +247,53 @@
 
 
 def place_kernel(plan, items, final, *refs):
-    n, cols, width = plan.n, plan.cols, plan.width
+    n, cols, width, rows = plan.n, plan.cols, plan.width, plan.rows
     own = lax.axis_index("ctx")
     pay_refs, refs = refs[: len(items)], refs[len(items) :]
     if final:
         grads, (_, _, attended, query_grad, key_grad, value_grad, sums, sems, sum_sems) = refs[:-9], refs[-9:]
     else:
-        grads, (attended, query_grad, send, sems) = refs[:-4], refs[-4:]
+        (pass_on, *arrived), (attended, query_grad, send, sems) = refs[:-4], refs[-4:]
     copies = []
     for i, item in enumerate(items):
         to = pl.ds(pl.multiple_of((own ^ item) * cols, cols), cols)
-        copies.append(pltpu.make_async_copy(pay_refs[i].at[0], attended.at[to, :], sems.at[i, 0]))
-        copies.append(pltpu.make_async_copy(pay_refs[i].at[1], query_grad.at[to, :], sems.at[i, 1]))
+        for part, ref in enumerate((attended, query_grad)):
+            source = pay_refs[i].at[pl.ds(part * cols, cols), :]
+            copies.append(pltpu.make_async_copy(source, ref.at[to, :], sems.at[i, part]))
     for copy in copies:
         copy.start()
-    total = sum(grad[...].astype(jnp.float32) for grad in grads).astype(jnp.bfloat16)
     if final:
-        sums[0] = total[:, :width]
-        sums[1] = total[:, width:]
         for i, ref in enumerate((key_grad, value_grad)):
+            total = sum(grad[:, i * width : (i + 1) * width].astype(jnp.float32) for grad in grads)
+            if n == 4:
+                total = total + pay_refs[items.index(1)][pl.ds(2 * cols + i * rows, rows), :].astype(jnp.float32)
+            sums[i] = total.astype(jnp.bfloat16)
             copies.append(pltpu.make_async_copy(sums.at[i], ref, sum_sems.at[i]))
             copies[-1].start()
     else:
-        send[...] = total
+        for half, ref in enumerate(arrived):
+            ranges = pl.ds(half * (n // 2), n // 2)
+            send[:, ranges] = (pass_on[:, ranges] + ref[...].astype(jnp.float32)).astype(jnp.bfloat16)
     for copy in copies:
         copy.wait()
 
 
 def place(plan, payloads, grads, filled=()):
     items = tuple(payloads)
-    big = jax.ShapeDtypeStruct((plan.rows * plan.heads, plan.width), jnp.bfloat16)
-    small = jax.ShapeDtypeStruct((plan.rows, plan.width), jnp.bfloat16)
     final = len(filled) > 0
-    at = len(items) + len(grads)
+    out_shape = [jax.ShapeDtypeStruct((plan.rows * plan.heads, plan.width), jnp.bfloat16)] * 2
     scratch = [pltpu.SemaphoreType.DMA((len(items), 2))]
     if final:
+        out_shape += [jax.ShapeDtypeStruct((plan.rows, plan.width), jnp.bfloat16)] * 2
         scratch = [pltpu.VMEM((2, plan.rows, plan.width), jnp.bfloat16), *scratch, pltpu.SemaphoreType.DMA((2,))]
+    else:
+        out_shape.append(jax.ShapeDtypeStruct(grads[0].shape, jnp.bfloat16))
+    at = len(items) + len(grads)
     return kernel_call(
         functools.partial(place_kernel, plan, items, final), "place_last" if final else "place_first",
         (*payloads.values(), *grads, *filled),
-        [pl.ANY] * len(items) + [pltpu.VMEM] * len(grads) + [pl.ANY] * len(filled),
-        [big, big] + ([small, small] if final else [jax.ShapeDtypeStruct(grads[0].shape, jnp.bfloat16)]), scratch,
+        [pltpu.VMEM if x == 1 else pl.ANY for x in items] + [pltpu.VMEM] * len(grads) + [pl.ANY] * len(filled),
+        out_shape, scratch,
         out_specs=[spec_of(pl.ANY)] * 2 + ([spec_of(pl.ANY)] * 2 if final else [spec_of(pltpu.VMEM)]),
         input_output_aliases={at: 0, at + 1: 1} if final else {},
         cost_estimate=plan.cost(len(items)),
@@ -309,16 +337,20 @@
     out = attend_last(plan, first, items, meta, [blocks[x] for x in items], first_grad, kv_list)
     late = {x: across(pay, x) for x, pay in zip(sent, out)}
     stay[0] = out[len(sent)]
-    keep, to_keep, pass_on, to_pass_on = out[len(items) :]
-    attended, query_grad, send = place(plan, stay, (pass_on, across(to_pass_on, 1)))
-    terms = (keep, across(to_keep, 1), across(send, 2))
+    keep, pass_on, lower, upper = out[len(items) :]
+    upper = permuted(upper, [(i, i ^ 1) for i in range(n // 2, n)])
+    *filled, send = place(plan, stay, (pass_on, across(lower, 1), upper))
+    terms = [keep, across(send, 2)]
     bit = 4
     while bit < n:
         total = sum(term.astype(jnp.float32) for term in terms)
-        terms = (total[0::2], across(total[1::2].astype(jnp.bfloat16), bit))
+        if bit == 4:
+            near = late[1][2 * plan.cols :].reshape(2, n // 4, n, plan.block, width)
+            total = total + jnp.concatenate([near[0], near[1]], axis=-1).astype(jnp.float32)
+        terms = [total[0::2], across(total[1::2].astype(jnp.bfloat16), bit)]
         bit *= 2
     terms = [term.reshape(rows, 2 * width) for term in terms]
-    attended, query_grad, key_grad, value_grad = place(plan, late, terms, (attended, query_grad))
+    attended, query_grad, key_grad, value_grad = place(plan, late, terms, filled)
     return (
         attended.reshape(rows, heads, width),
         query_grad.reshape(rows, heads, width),

time: 51.5 us -> 50.1 us (0.973)
  waiting for transfers between devices: 24.1 us -> 20.7 us
  starting transfers between devices: 14.2 us -> 16.2 us
    ppermute x10, waiting for transfers between devices: 24.1 us -> 20.7 us  [permuted(): return lax.ppermute(array, 'ctx', pairs)]
    ppermute x10, starting transfers between devices: 14.2 us -> 16.2 us  [permuted(): return lax.ppermute(array, 'ctx', pairs)]
where the time goes in v14:
time: 50.1 us; the launch traced here: 49.9 us
  waiting for transfers between devices  20.7 us (41%)
  starting transfers between devices  16.2 us (32%)
  Pallas kernels  10.5 us (21%)
  local copies, waits for them, and re-layouts  1.43 us (3%)
  between operations  0.71 us (1%)
    ppermute x10, waiting for transfers between devices, permuted(): return lax.ppermute(array, 'ctx', pairs)  20.7 us
    ppermute x10, starting transfers between devices, permuted(): return lax.ppermute(array, 'ctx', pairs)  16.2 us
    pallas_call x5, Pallas kernels, kernel_call(): pl.pallas_call(body, out_shape=out_shape, in_specs=[spec_of(space) for sp...  10.5 us
    unnamed x4, local copies, waits for them, and re-layouts  1.35 us
  transfers between devices with their start and end apart: 10, of which 4 were waited for; matrix products, arithmetic and copies ran while one was open for 1% of the time, Pallas kernels for 15%

profile of v14, /device:TPU:0, one launch (start us, length us, event | category | flops | bytes accessed | tf_op | source)
XLA Modules:
  0.0 49.9 jit_solution(4121140732672502116)
XLA Ops:
  0.6 4.1 %collective-permute-start.2 = (bf16[256,128]{1,0:T(8,128)(2,1)}, bf16[256,128]{1,0:T(8,128)(2,1)S(1)}, u32[]{:S(2)}, u32[]{:S(2)}) collective-permute-start(bf16[256,128]{1,0:T(8,128)(2,1)} %bitcast.17), channel_id=1, source_target_pairs={{0,8},{4,12},{8,0},{12,4},{1,9},{5,13},{9,1},{13,5},{2,10},{6,14},... | collective-permute-start | bytes 196616 | tf_op jit(solution)/shard_map/ppermute | solution.py:310
  4.7 1.6 %collective-permute-start = (bf16[256,128]{1,0:T(8,128)(2,1)}, bf16[256,128]{1,0:T(8,128)(2,1)S(1)}, u32[]{:S(2)}, u32[]{:S(2)}) collective-permute-start(bf16[256,128]{1,0:T(8,128)(2,1)} %bitcast.18), channel_id=1, source_target_pairs={{0,4},{4,8},{8,12},{12,0},{1,5},{5,9},{9,13},{13,1},{2,6},{6,10},{... | collective-permute-start | bytes 196616 | tf_op jit(solution)/shard_map/ppermute | solution.py:310
  6.3 0.3 collective-permute-start.3
  6.6 2.5 %collective-permute-start.1 = (bf16[256,128]{1,0:T(8,128)(2,1)}, bf16[256,128]{1,0:T(8,128)(2,1)S(1)}, u32[]{:S(2)}, u32[]{:S(2)}) collective-permute-start(bf16[256,128]{1,0:T(8,128)(2,1)} %bitcast.21), channel_id=1, source_target_pairs={{0,4},{4,8},{8,12},{12,0},{1,5},{5,9},{9,13},{13,1},{2,6},{6,10},{... | collective-permute-start | bytes 196616 | tf_op jit(solution)/shard_map/ppermute | solution.py:310
  9.1 0.0 copy-start
  9.1 0.7 %copy-done = s32[4,4]{1,0:T(4,128)S(1)} copy-done((s32[4,4]{1,0:T(4,128)S(1)}, s32[4,4]{1,0:T(4,128)}, u32[]{:S(2)}) %copy-start) | copy-done | bytes 88
  9.8 0.1 select_reduce_fusion
  9.9 0.1 reshape.74
  10.0 0.7 %copy-done.1 = s32[8]{0:T(128)S(1)} copy-done((s32[8]{0:T(128)S(1)}, s32[8]{0:T(128)}, u32[]{:S(2)}) %copy-start.1) | copy-done | bytes 56
  10.7 0.2 reduce-window.9
  10.9 0.1 pad_add_fusion.meta
  11.0 1.9 %pack.1 = (bf16[2,512,128]{2,1,0:T(8,128)(2,1)S(1)}, bf16[2,512,128]{2,1,0:T(8,128)(2,1)S(1)}, bf16[2,512,128]{2,1,0:T(8,128)(2,1)S(1)}, bf16[2,512,128]{2,1,0:T(8,128)(2,1)S(1)}, bf16[512,128]{1,0:T(8,128)(2,1)S(1)}) custom-call(s32[25]{0:T(128)S(1)} %pad_add_fusion.meta, bf16[2048,128]{1,0:T(8,128)(2,1)} %bitcast.15, bf16[2048,128]{1,0:T(8,128)(2,1)} %bitcast.16, ...), custom_call_target="tpu_custom_call" | custom-call | tf_op jit(solution)/shard_map/pack/pallas_call | solution.py:197
  12.9 0.0 collective-permute-done.2.refs_3_.refs_7_
  12.9 0.0 collective-permute-done.refs_1_.refs_5_
  12.9 1.6 %collective-permute-done.3.refs_4_.refs_8_ = bf16[256,128]{1,0:T(8,128)(2,1)S(1)} collective-permute-done((bf16[256,128]{1,0:T(8,128)(2,1)}, bf16[256,128]{1,0:T(8,128)(2,1)S(1)}, u32[]{:S(2)}, u32[]{:S(2)}) %collective-permute-start.3) | collective-permute-done | bytes 65568 | tf_op jit(solution)/shard_map/ppermute | solution.py:310
  14.5 0.0 collective-permute-done.1.refs_2_.refs_6_
  14.5 2.0 %attend_first.1 = (bf16[1024,128]{1,0:T(8,128)(2,1)S(1)}, f32[576,256]{1,0:T(8,128)S(1)}) custom-call(s32[25]{0:T(128)S(1)} %pad_add_fusion.meta, bf16[2,512,128]{2,1,0:T(8,128)(2,1)S(1)} %get-tuple-element.28.qg, bf16[512,128]{1,0:T(8,128)(2,1)S(1)} %get-tuple-element.29.refs_0_.refs_4_, bf16[256,128]{1,0:T(8,128)(2,1)S(1)} %collective-permute-done.refs_1_.refs_5_, ...), custom_call_target="tpu_custom_call" | custom-call | flops 4227858432 | bytes 1048576 | tf_op jit(solution)/shard_map/attend_first/pallas_call | solution.py:197
  16.5 2.3 %collective-permute-start.6 = (bf16[1024,128]{1,0:T(8,128)(2,1)S(1)}, bf16[1024,128]{1,0:T(8,128)(2,1)S(1)}, u32[]{:S(2)}, u32[]{:S(2)}) collective-permute-start(bf16[1024,128]{1,0:T(8,128)(2,1)S(1)} %get-tuple-element.34), channel_id=1, source_target_pairs={{0,8},{4,12},{8,0},{12,4},{1,9},{5,13},{9,1},{13,5},{2,10},{6,14},... | collective-permute-start | bytes 786440 | tf_op jit(solution)/shard_map/ppermute | solution.py:310
  18.7 4.8 %attend_last.1 = (bf16[1024,128]{1,0:T(8,128)(2,1)S(1)}, bf16[1536,128]{1,0:T(8,128)(2,1)S(1)}, bf16[1024,128]{1,0:T(8,128)(2,1)S(1)}, f32[1,4,64,256]{3,2,1,0:T...) custom-call(s32[25]{0:T(128)S(1)} %pad_add_fusion.meta, ...), custom_call_target="tpu_custom_call" | custom-call | flops 12683575296 | bytes 3145728 | tf_op jit(solution)/shard_map/attend_last/pallas_call | solution.py:197
  23.6 0.6 %collective-permute-start.7 = (bf16[1,2,64,256]{3,2,1,0:T(8,128)(2,1)S(1)}, bf16[1,2,64,256]{3,2,1,0:T(8,128)(2,1)S(1)}, u32[]{:S(2)}, u32[]{:S(2)}) collective-permute-start(bf16[1,2,64,256]{3,2,1,0:T(8,128)(2,1)S(1)} %get-tuple-element.37), channel_id=1, source_target_pairs={{0,4},{4,0},{8,12},{12,8},{1,5},{5,1},{9,13},{13,9},{2,6},{6,2},{1... | collective-permute-start | bytes 196616 | tf_op jit(solution)/shard_map/ppermute | solution.py:310
  24.2 0.7 %collective-permute-start.8 = (bf16[1,2,64,256]{3,2,1,0:T(8,128)(2,1)S(1)}, bf16[1,2,64,256]{3,2,1,0:T(8,128)(2,1)S(1)}, u32[]{:S(2)}, u32[]{:S(2)}) collective-permute-start(bf16[1,2,64,256]{3,2,1,0:T(8,128)(2,1)S(1)} %get-tuple-element.38), channel_id=1, source_target_pairs={{8,12},{12,8},{9,13},{13,9},{10,14},{14,10},{11,15},{15,11},{24,28... | collective-permute-start | bytes 196616 | tf_op jit(solution)/shard_map/ppermute | solution.py:310
  24.8 3.4 %collective-permute-start.4 = (bf16[1024,128]{1,0:T(8,128)(2,1)S(1)}, bf16[1024,128]{1,0:T(8,128)(2,1)S(1)}, u32[]{:S(2)}, u32[]{:S(2)}) collective-permute-start(bf16[1024,128]{1,0:T(8,128)(2,1)S(1)} %get-tuple-element.31), channel_id=1, source_target_pairs={{0,12},{4,8},{8,4},{12,0},{1,13},{5,9},{9,5},{13,1},{2,14},{6,10},... | collective-permute-start | bytes 786440 | tf_op jit(solution)/shard_map/ppermute | solution.py:310
  28.2 0.8 %collective-permute-start.5 = (bf16[1536,128]{1,0:T(8,128)(2,1)S(1)}, bf16[1536,128]{1,0:T(8,128)(2,1)S(1)}, u32[]{:S(2)}, u32[]{:S(2)}) collective-permute-start(bf16[1536,128]{1,0:T(8,128)(2,1)S(1)} %get-tuple-element.32), channel_id=1, source_target_pairs={{0,4},{4,0},{8,12},{12,8},{1,5},{5,1},{9,13},{13,9},{2,6},{6,2},{1... | collective-permute-start | bytes 1179656 | tf_op jit(solution)/shard_map/ppermute | solution.py:310
  29.0 8.9 %collective-permute-done.7.refs_3_ = bf16[1,2,64,256]{3,2,1,0:T(8,128)(2,1)S(1)} collective-permute-done((bf16[1,2,64,256]{3,2,1,0:T(8,128)(2,1)S(1)}, bf16[1,2,64,256]{3,2,1,0:T(8,128)(2,1)S(1)}, u32[]{:S(2)}, u32[]{:S(2)}) %collective-permute-start.7) | collective-permute-done | bytes 65568 | tf_op jit(solution)/shard_map/ppermute | solution.py:310
  37.9 0.0 collective-permute-done.8.refs_4_
  37.9 0.0 collective-permute-done.6.refs_0_
  37.9 0.8 %place_first.1 = (bf16[2048,128]{1,0:T(8,128)(2,1)}, bf16[2048,128]{1,0:T(8,128)(2,1)}, bf16[1,4,64,256]{3,2,1,0:T(8,128)(2,1)S(1)}) custom-call(bf16[1024,128]{1,0:T(8,128)(2,1)S(1)} %collective-permute-done.6.refs_0_, bf16[1024,128]{1,0:T(8,128)(2,1)S(1)} %get-tuple-element.35.refs_1_, f32[1,4,64,256]{3,2,1,0:T(8,128)S(1)} %get-tuple-element.36.refs_2_, ...), custom_call_target="tpu_custom_call" | custom-call | flops 8455716864 | bytes 2097152 | tf_op jit(solution)/shard_map/place_first/pallas_call | solution.py:197
  38.7 0.1 collective-permute-start.9
  38.8 0.0 collective-permute-done.4.refs_0_
  38.8 9.0 %collective-permute-done.9 = bf16[1,4,64,256]{3,2,1,0:T(8,128)(2,1)S(1)} collective-permute-done((bf16[1,4,64,256]{3,2,1,0:T(8,128)(2,1)S(1)}, bf16[1,4,64,256]{3,2,1,0:T(8,128)(2,1)S(1)}, u32[]{:S(2)}, u32[]{:S(2)}) %collective-permute-start.9) | collective-permute-done | bytes 131104 | tf_op jit(solution)/shard_map/ppermute | solution.py:310
  47.8 1.2 %collective-permute-done.5.refs_1_ = bf16[1536,128]{1,0:T(8,128)(2,1)S(1)} collective-permute-done((bf16[1536,128]{1,0:T(8,128)(2,1)S(1)}, bf16[1536,128]{1,0:T(8,128)(2,1)S(1)}, u32[]{:S(2)}, u32[]{:S(2)}) %collective-permute-start.5) | collective-permute-done | bytes 393248 | tf_op jit(solution)/shard_map/ppermute | solution.py:310
  49.0 0.9 %place_last.1 = (bf16[2048,128]{1,0:T(8,128)(2,1)}, bf16[2048,128]{1,0:T(8,128)(2,1)}, bf16[256,128]{1,0:T(8,128)(2,1)}, bf16[256,128]{1,0:T(8,128)(2,1)}) custom-call(bf16[1024,128]{1,0:T(8,128)(2,1)S(1)} %collective-permute-done.4.refs_0_, bf16[1536,128]{1,0:T(8,128)(2,1)S(1)} %collective-permute-done.5.refs_1_, ...), custom_call_target="tpu_custom_call", output_to_operand_aliasing={{0}: (4, {}), {1}: (5, {})} | custom-call | flops 8455716864 | bytes 2097152 | tf_op jit(solution)/shard_map/place_last/pallas_call | solution.py:197
  (1 shorter events, 0.0 us)
Async XLA Ops:
  0.6 12.3 %collective-permute-start.2 = (bf16[256,128]{1,0:T(8,128)(2,1)}, bf16[256,128]{1,0:T(8,128)(2,1)S(1)}, u32[]{:S(2)}, u32[]{:S(2)}) collective-permute-start(bf16[256,128]{1,0:T(8,128)(2,1)} %bitcast.17), channel_id=1, source_target_pairs={{0,8},{4,12},{8,0},{12,4},{1,9},{5,13},{9,1},{13,5},{2,10},{6,14},... | collective-permute-start | bytes 196616 | tf_op jit(solution)/shard_map/ppermute | solution.py:310
  4.7 8.2 %collective-permute-start = (bf16[256,128]{1,0:T(8,128)(2,1)}, bf16[256,128]{1,0:T(8,128)(2,1)S(1)}, u32[]{:S(2)}, u32[]{:S(2)}) collective-permute-start(bf16[256,128]{1,0:T(8,128)(2,1)} %bitcast.18), channel_id=1, source_target_pairs={{0,4},{4,8},{8,12},{12,0},{1,5},{5,9},{9,13},{13,1},{2,6},{6,10},{... | collective-permute-start | bytes 196616 | tf_op jit(solution)/shard_map/ppermute | solution.py:310
  6.3 8.2 %collective-permute-start.3 = (bf16[256,128]{1,0:T(8,128)(2,1)}, bf16[256,128]{1,0:T(8,128)(2,1)S(1)}, u32[]{:S(2)}, u32[]{:S(2)}) collective-permute-start(bf16[256,128]{1,0:T(8,128)(2,1)} %bitcast.20), channel_id=1, source_target_pairs={{0,8},{4,12},{8,0},{12,4},{1,9},{5,13},{9,1},{13,5},{2,10},{6,14},... | collective-permute-start | bytes 196616 | tf_op jit(solution)/shard_map/ppermute | solution.py:310
  6.6 7.9 %collective-permute-start.1 = (bf16[256,128]{1,0:T(8,128)(2,1)}, bf16[256,128]{1,0:T(8,128)(2,1)S(1)}, u32[]{:S(2)}, u32[]{:S(2)}) collective-permute-start(bf16[256,128]{1,0:T(8,128)(2,1)} %bitcast.21), channel_id=1, source_target_pairs={{0,4},{4,8},{8,12},{12,0},{1,5},{5,9},{9,13},{13,1},{2,6},{6,10},{... | collective-permute-start | bytes 196616 | tf_op jit(solution)/shard_map/ppermute | solution.py:310
  9.1 0.7 %copy-start = (s32[4,4]{1,0:T(4,128)S(1)}, s32[4,4]{1,0:T(4,128)}, u32[]{:S(2)}) copy-start(s32[4,4]{1,0:T(4,128)} %param.11) | copy-start | bytes 196
  10.0 0.7 %copy-start.1 = (s32[8]{0:T(128)S(1)}, s32[8]{0:T(128)}, u32[]{:S(2)}) copy-start(s32[8]{0:T(128)} %param.10) | copy-start | bytes 100
  16.5 21.4 %collective-permute-start.6 = (bf16[1024,128]{1,0:T(8,128)(2,1)S(1)}, bf16[1024,128]{1,0:T(8,128)(2,1)S(1)}, u32[]{:S(2)}, u32[]{:S(2)}) collective-permute-start(bf16[1024,128]{1,0:T(8,128)(2,1)S(1)} %get-tuple-element.34), channel_id=1, source_target_pairs={{0,8},{4,12},{8,0},{12,4},{1,9},{5,13},{9,1},{13,5},{2,10},{6,14},... | collective-permute-start | bytes 786440 | tf_op jit(solution)/shard_map/ppermute | solution.py:310
  23.6 14.3 %collective-permute-start.7 = (bf16[1,2,64,256]{3,2,1,0:T(8,128)(2,1)S(1)}, bf16[1,2,64,256]{3,2,1,0:T(8,128)(2,1)S(1)}, u32[]{:S(2)}, u32[]{:S(2)}) collective-permute-start(bf16[1,2,64,256]{3,2,1,0:T(8,128)(2,1)S(1)} %get-tuple-element.37), channel_id=1, source_target_pairs={{0,4},{4,0},{8,12},{12,8},{1,5},{5,1},{9,13},{13,9},{2,6},{6,2},{1... | collective-permute-start | bytes 196616 | tf_op jit(solution)/shard_map/ppermute | solution.py:310
  24.2 13.7 %collective-permute-start.8 = (bf16[1,2,64,256]{3,2,1,0:T(8,128)(2,1)S(1)}, bf16[1,2,64,256]{3,2,1,0:T(8,128)(2,1)S(1)}, u32[]{:S(2)}, u32[]{:S(2)}) collective-permute-start(bf16[1,2,64,256]{3,2,1,0:T(8,128)(2,1)S(1)} %get-tuple-element.38), channel_id=1, source_target_pairs={{8,12},{12,8},{9,13},{13,9},{10,14},{14,10},{11,15},{15,11},{24,28... | collective-permute-start | bytes 196616 | tf_op jit(solution)/shard_map/ppermute | solution.py:310
  24.8 14.0 %collective-permute-start.4 = (bf16[1024,128]{1,0:T(8,128)(2,1)S(1)}, bf16[1024,128]{1,0:T(8,128)(2,1)S(1)}, u32[]{:S(2)}, u32[]{:S(2)}) collective-permute-start(bf16[1024,128]{1,0:T(8,128)(2,1)S(1)} %get-tuple-element.31), channel_id=1, source_target_pairs={{0,12},{4,8},{8,4},{12,0},{1,13},{5,9},{9,5},{13,1},{2,14},{6,10},... | collective-permute-start | bytes 786440 | tf_op jit(solution)/shard_map/ppermute | solution.py:310
  28.2 20.8 %collective-permute-start.5 = (bf16[1536,128]{1,0:T(8,128)(2,1)S(1)}, bf16[1536,128]{1,0:T(8,128)(2,1)S(1)}, u32[]{:S(2)}, u32[]{:S(2)}) collective-permute-start(bf16[1536,128]{1,0:T(8,128)(2,1)S(1)} %get-tuple-element.32), channel_id=1, source_target_pairs={{0,4},{4,0},{8,12},{12,8},{1,5},{5,1},{9,13},{13,9},{2,6},{6,2},{1... | collective-permute-start | bytes 1179656 | tf_op jit(solution)/shard_map/ppermute | solution.py:310
  38.7 9.1 %collective-permute-start.9 = (bf16[1,4,64,256]{3,2,1,0:T(8,128)(2,1)S(1)}, bf16[1,4,64,256]{3,2,1,0:T(8,128)(2,1)S(1)}, u32[]{:S(2)}, u32[]{:S(2)}) collective-permute-start(bf16[1,4,64,256]{3,2,1,0:T(8,128)(2,1)S(1)} %get-tuple-element.39), channel_id=1, source_target_pairs={{0,8},{4,12},{8,0},{12,4},{1,9},{5,13},{9,1},{13,5},{2,10},{6,14},... | collective-permute-start | bytes 393224 | tf_op jit(solution)/shard_map/ppermute | solution.py:310

commit v15 on v11

--- a/solution.py
+++ b/solution.py
@@ -95,9 +95,22 @@
     return keys_here, out
 
 
+def early_kernel(plan, owners_ref, q_ref, g_ref, block, sems):
+    own = lax.axis_index("ctx")
+    owner, slot = own ^ (plan.n - 1), jnp.int32(0)
+    for i in range(1, plan.n):
+        slot = jnp.where(owners_ref[own, i] == owner, i, slot)
+    at = pl.ds(pl.multiple_of(slot * plan.cols, plan.cols), plan.cols)
+    copies = [pltpu.make_async_copy(ref.at[at, :], block.at[i], sems.at[i]) for i, ref in enumerate((q_ref, g_ref))]
+    for copy in copies:
+        copy.start()
+    for copy in copies:
+        copy.wait()
+
+
 def pack_kernel(plan, ends_ref, owners_ref, q_ref, g_ref, k_ref, v_ref, *refs):
     n = plan.n
-    blocks, (kv, meta, sems, kv_sems) = refs[:n], refs[n:]
+    blocks, (kv, meta, sems, kv_sems) = refs[: n - 1], refs[n - 1 :]
     own = lax.axis_index("ctx")
     copies = []
     for i, ref in enumerate((k_ref, v_ref)):
@@ -110,7 +123,7 @@
             meta[1 + plan.ndocs + loader * n + owners_ref[loader, slot]] = slot
 
     slots_of(own)
-    for apart in range(n - 1, -1, -1):
+    for apart in range(n - 2, -1, -1):
         slot = plan.slot(meta, own, own ^ apart)
         at = pl.ds(pl.multiple_of(slot * plan.cols, plan.cols), plan.cols)
         copies.append(pltpu.make_async_copy(q_ref.at[at, :], blocks[apart].at[0], sems.at[apart, 0]))
@@ -238,17 +251,28 @@
     )(*operands)
 
 
+def in_hbm(*operands):
+    return [pltpu.with_memory_space_constraint(x, pltpu.HBM) for x in operands]
+
+
+def pack_early(plan, block_owner, q, g):
+    return kernel_call(
+        functools.partial(early_kernel, plan), "pack_early", (block_owner, *in_hbm(q, g)),
+        [pltpu.SMEM] + [pl.ANY] * 2, jax.ShapeDtypeStruct((2, plan.cols, plan.width), jnp.bfloat16),
+        [pltpu.SemaphoreType.DMA((2,))], out_specs=spec_of(pltpu.VMEM),
+    )
+
+
 def pack(plan, doc_lengths, block_owner, *operands):
     n = plan.n
-    out_shape = [jax.ShapeDtypeStruct((2, plan.cols, plan.width), jnp.bfloat16)] * n
+    out_shape = [jax.ShapeDtypeStruct((2, plan.cols, plan.width), jnp.bfloat16)] * (n - 1)
     out_shape.append(jax.ShapeDtypeStruct((2 * plan.rows, plan.width), jnp.bfloat16))
     out_shape.append(jax.ShapeDtypeStruct((1 + plan.ndocs + n * n,), jnp.int32))
-    operands = [pltpu.with_memory_space_constraint(x, pltpu.HBM) for x in operands]
-    return kernel_call(
-        functools.partial(pack_kernel, plan), "pack", (doc_lengths, block_owner, *operands),
+    return kernel_call(
+        functools.partial(pack_kernel, plan), "pack", (doc_lengths, block_owner, *in_hbm(*operands)),
         [pltpu.SMEM] * 2 + [pl.ANY] * 4, out_shape,
         [pltpu.SemaphoreType.DMA((n, 2)), pltpu.SemaphoreType.DMA((2,))],
-        out_specs=[spec_of(pltpu.VMEM)] * (n + 1) + [spec_of(pltpu.SMEM)],
+        out_specs=[spec_of(pltpu.VMEM)] * n + [spec_of(pltpu.SMEM)],
     )
 
 
@@ -385,18 +409,20 @@
         kv_list += [permuted(k, pairs), permuted(v, pairs)]
 
     q, g = (x.reshape(rows * heads, width) for x in (query, output_gradient))
+    last_block = pack_early(plan, block_owner, q, g)
+    got = permuted(last_block, [(plan.back, plan.back - 1)])
     *blocks, kv, meta = pack(plan, doc_lengths, block_owner, q, g, k, v)
+    blocks.append(last_block)
     kv_list = [kv, *kv_list]
-    got = permuted(blocks[n - 1], [(plan.back, plan.back - 1)])
     first = n // 2
     first_pay, first_grad = attend_first(plan, first, meta, blocks[first], kv_list)
     stay = {first: across(first_pay, first)}
-    items = tuple(x for x in range(n - 1, -1, -1) if x != first)
+    items = (*[x for x in range(1, n) if x != first], 0)
     *pays, sums = attend_next(plan, first, items, meta, [blocks[x] for x in items], first_grad, kv_list)
     stay["got"], *out = attend_last(plan, meta, got, sums, kv_list)
     stay[0] = pays[-1]
-    late = {n - 1: permuted(pays[0], [(i, i ^ (n - 1)) for i in range(n) if i != plan.back])}
-    late.update({x: across(pay, x) for x, pay in zip(items[1:-1], pays[1:-1])})
+    late = {x: across(pay, x) for x, pay in zip(items[:-2], pays[:-2])}
+    late[n - 1] = permuted(pays[-2], [(i, i ^ (n - 1)) for i in range(n) if i != plan.back])
     keep, pass_on, lower, upper = out
     upper = permuted(upper, [(i, i ^ 1) for i in range(plan.back, n)])
     attended, query_grad, send, keep = place(plan, stay, (pass_on, keep, across(lower, 1), upper))

time: 50.5 us -> 51 us (level)
  Pallas kernels: 11.8 us -> 13.3 us
  waiting for transfers between devices: 12.9 us -> 11.7 us
  starting transfers between devices: 24.2 us -> 25 us
  local copies, waits for them, and re-layouts: 0.66 us -> 0.01 us
    pallas_call x6 -> x7, Pallas kernels: 11.8 us -> 13.3 us  [kernel_call(): pl.pallas_call(body, out_shape=out_shape, in_specs=[spec_of(space) for sp...]
    ppermute x11, waiting for transfers between devices: 12.9 us -> 11.7 us  [permuted(): return lax.ppermute(array, 'ctx', pairs)]
    ppermute x11, starting transfers between devices: 24.2 us -> 25 us  [permuted(): return lax.ppermute(array, 'ctx', pairs)]
    unnamed x4, local copies, waits for them, and re-layouts: 0.66 us -> 0.01 us
  transfers between devices with their start and end apart: 11 -> 11, of which waited for: 4 -> 3; matrix products, arithmetic and copies ran while one was open for 0% -> 0% of each run, Pallas kernels for 22% -> 24%
where the time goes in v15:
time: 51 us; the launch traced here: 50.8 us
  starting transfers between devices  25 us (49%)
  Pallas kernels  13.3 us (26%)
  waiting for transfers between devices  11.7 us (23%)
  between operations  0.77 us (2%)
    ppermute x11, starting transfers between devices, permuted(): return lax.ppermute(array, 'ctx', pairs)  25 us
    pallas_call x7, Pallas kernels, kernel_call(): pl.pallas_call(body, out_shape=out_shape, in_specs=[spec_of(space) for sp...  13.3 us
    ppermute x11, waiting for transfers between devices, permuted(): return lax.ppermute(array, 'ctx', pairs)  11.7 us
  transfers between devices with their start and end apart: 11, of which 3 were waited for; matrix products, arithmetic and copies ran while one was open for 0% of the time, Pallas kernels for 24%

profile of v15, /device:TPU:0, one launch (start us, length us, event | category | flops | bytes accessed | tf_op | source)
XLA Modules:
  0.0 50.8 jit_solution(18109945084220458687)
XLA Ops:
  0.6 3.1 %collective-permute-start = (bf16[256,128]{1,0:T(8,128)(2,1)}, bf16[256,128]{1,0:T(8,128)(2,1)S(1)}, u32[]{:S(2)}, u32[]{:S(2)}) collective-permute-start(bf16[256,128]{1,0:T(8,128)(2,1)} %bitcast.16), channel_id=1, source_target_pairs={{0,4},{4,8},{8,12},{12,0},{1,5},{5,9},{9,13},{13,1},{2,6},{6,10},{... | collective-permute-start | bytes 196616 | tf_op jit(solution)/shard_map/ppermute | solution.py:397
  3.7 0.0 copy-start
  3.7 1.6 %collective-permute-start.1 = (bf16[256,128]{1,0:T(8,128)(2,1)}, bf16[256,128]{1,0:T(8,128)(2,1)S(1)}, u32[]{:S(2)}, u32[]{:S(2)}) collective-permute-start(bf16[256,128]{1,0:T(8,128)(2,1)} %bitcast.19), channel_id=1, source_target_pairs={{0,4},{4,8},{8,12},{12,0},{1,5},{5,9},{9,13},{13,1},{2,6},{6,10},{... | collective-permute-start | bytes 196616 | tf_op jit(solution)/shard_map/ppermute | solution.py:397
  5.3 1.1 %collective-permute-start.2 = (bf16[256,128]{1,0:T(8,128)(2,1)}, bf16[256,128]{1,0:T(8,128)(2,1)S(1)}, u32[]{:S(2)}, u32[]{:S(2)}) collective-permute-start(bf16[256,128]{1,0:T(8,128)(2,1)} %bitcast.17), channel_id=1, source_target_pairs={{0,8},{4,12},{8,4},{12,0},{1,9},{5,13},{9,5},{13,1},{2,10},{6,14},... | collective-permute-start | bytes 196616 | tf_op jit(solution)/shard_map/ppermute | solution.py:397
  6.4 1.9 %collective-permute-start.3 = (bf16[256,128]{1,0:T(8,128)(2,1)}, bf16[256,128]{1,0:T(8,128)(2,1)S(1)}, u32[]{:S(2)}, u32[]{:S(2)}) collective-permute-start(bf16[256,128]{1,0:T(8,128)(2,1)} %bitcast.20), channel_id=1, source_target_pairs={{0,8},{4,12},{8,4},{12,0},{1,9},{5,13},{9,5},{13,1},{2,10},{6,14},... | collective-permute-start | bytes 196616 | tf_op jit(solution)/shard_map/ppermute | solution.py:397
  8.3 0.0 copy-done
  8.3 1.6 %pack_early.1.refs_1_ = bf16[2,512,128]{2,1,0:T(8,128)(2,1)S(1)} custom-call(s32[4,4]{1,0:T(4,128)S(1)} %copy-done, bf16[2048,128]{1,0:T(8,128)(2,1)} %bitcast.12, bf16[2048,128]{1,0:T(8,128)(2,1)} %bitcast.14), custom_call_target="tpu_custom_call" | custom-call | tf_op jit(solution)/shard_map/pack_early/pallas_call | solution.py:243
  9.9 0.7 %collective-permute-start.7 = (bf16[2,512,128]{2,1,0:T(8,128)(2,1)S(1)}, bf16[2,512,128]{2,1,0:T(8,128)(2,1)S(1)}, u32[]{:S(2)}, u32[]{:S(2)}) collective-permute-start(bf16[2,512,128]{2,1,0:T(8,128)(2,1)S(1)} %pack_early.1.refs_1_), channel_id=1, source_target_pairs={{8,4},{9,5},{10,6},{11,7},{24,20},{25,21},{26,22},{27,23}} | collective-permute-start | bytes 786440 | tf_op jit(solution)/shard_map/ppermute | solution.py:397
  10.6 0.0 copy-done.1
  10.6 2.5 %pack.1 = (bf16[2,512,128]{2,1,0:T(8,128)(2,1)S(1)}, bf16[2,512,128]{2,1,0:T(8,128)(2,1)S(1)}, bf16[2,512,128]{2,1,0:T(8,128)(2,1)S(1)}, bf16[512,128]{1,0:T(8,128)(2,1)S(1)}, s32[25]{0:T(128)S(1)}) custom-call(s32[8]{0:T(128)S(1)} %copy-done.1, s32[4,4]{1,0:T(4,128)S(1)} %copy-done, bf16[2048,128]{1,0:T(8,128)(2,1)} %bitcast.13, ...), custom_call_target="tpu_custom_call" | custom-call | tf_op jit(solution)/shard_map/pack/pallas_call | solution.py:243
  13.1 0.0 collective-permute-done.refs_1_.refs_5_
  13.1 0.0 collective-permute-done.1.refs_2_.refs_6_
  13.1 0.0 collective-permute-done.2.refs_3_.refs_7_
  13.1 0.0 collective-permute-done.3.refs_4_.refs_8_
  13.2 2.0 %attend_first.1 = (bf16[2,512,128]{2,1,0:T(8,128)(2,1)S(1)}, f32[576,256]{1,0:T(8,128)S(1)}) custom-call(s32[25]{0:T(128)S(1)} %get-tuple-element.28.meta, bf16[2,512,128]{2,1,0:T(8,128)(2,1)S(1)} %get-tuple-element.31.qg, bf16[512,128]{1,0:T(8,128)(2,1)S(1)} %get-tuple-element.32.refs_0_.refs_4_, bf16[256,128]{1,0:T(8,128)(2,1)S(1)} %collective-permute-done.refs_1_.refs_5_, ...), custom_call_target="tpu_custom_call" | custom-call | flops 4227858432 | bytes 1048576 | tf_op jit(solution)/shard_map/attend_first/pallas_call | solution.py:243
  15.1 4.1 %collective-permute-start.6 = (bf16[2,512,128]{2,1,0:T(8,128)(2,1)S(1)}, bf16[2,512,128]{2,1,0:T(8,128)(2,1)S(1)}, u32[]{:S(2)}, u32[]{:S(2)}) collective-permute-start(bf16[2,512,128]{2,1,0:T(8,128)(2,1)S(1)} %get-tuple-element.36), channel_id=1, source_target_pairs={{0,8},{4,12},{8,0},{12,4},{1,9},{5,13},{9,1},{13,5},{2,10},{6,14},... | collective-permute-start | bytes 786440 | tf_op jit(solution)/shard_map/ppermute | solution.py:397
  19.3 4.7 %attend_next.1 = (bf16[2,512,128]{2,1,0:T(8,128)(2,1)S(1)}, bf16[2,512,128]{2,1,0:T(8,128)(2,1)S(1)}, bf16[2,512,128]{2,1,0:T(8,128)(2,1)S(1)}, f32[1024,256]{1,0:T(8,128)S(1)}) custom-call(s32[25]{0:T(128)S(1)} %get-tuple-element.28.meta, bf16[2,512,128]{2,1,0:T(8,128)(2,1)S(1)} %get-tuple-element.29.refs_0_, bf16[2,512,128]{2,1,0:T(8,128)(2,1)S(1)} %pack_early.1.refs_1_, ...), custom_call_target="tpu_custom_call" | custom-call | flops 12683575296 | bytes 3145728 | tf_op jit(solution)/shard_map/attend_next/pallas_call | solution.py:243
  24.0 0.0 collective-permute-done.7.got_ref
  24.0 0.8 %attend_last.1 = (bf16[2,512,128]{2,1,0:T(8,128)(2,1)S(1)}, f32[1,4,64,256]{3,2,1,0:T(8,128)S(1)}, f32[1,4,64,256]{3,2,1,0:T(8,128)S(1)}, bf16[2,3,64,256]{3,2,1,0:T(8,128)(2,1)S(1)}, bf16[2,1,64,256]{3,2,1,0:T(8,128)(2,1)S(1)}) custom-call(s32[25]{0:T(128)S(1)} %get-tuple-element.28.meta, bf16[2,512,128]{2,1,0:T(8,128)(2,1)S(1)} %collective-permute-done.7.got_ref, ...), custom_call_target="tpu_custom_call" | custom-call | flops 4227858432 | bytes 1048576 | tf_op jit(solution)/shard_map/attend_last/pallas_call | solution.py:243
  24.8 5.4 %collective-permute-start.8 = (bf16[2,3,64,256]{3,2,1,0:T(8,128)(2,1)S(1)}, bf16[2,3,64,256]{3,2,1,0:T(8,128)(2,1)S(1)}, u32[]{:S(2)}, u32[]{:S(2)}) collective-permute-start(bf16[2,3,64,256]{3,2,1,0:T(8,128)(2,1)S(1)} %get-tuple-element.42), channel_id=1, source_target_pairs={{0,4},{4,0},{8,12},{12,8},{1,5},{5,1},{9,13},{13,9},{2,6},{6,2},{1... | collective-permute-start | bytes 589832 | tf_op jit(solution)/shard_map/ppermute | solution.py:397
  30.2 0.7 %collective-permute-start.9 = (bf16[2,1,64,256]{3,2,1,0:T(8,128)(2,1)S(1)}, bf16[2,1,64,256]{3,2,1,0:T(8,128)(2,1)S(1)}, u32[]{:S(2)}, u32[]{:S(2)}) collective-permute-start(bf16[2,1,64,256]{3,2,1,0:T(8,128)(2,1)S(1)} %get-tuple-element.43), channel_id=1, source_target_pairs={{8,12},{12,8},{9,13},{13,9},{10,14},{14,10},{11,15},{15,11},{24,28... | collective-permute-start | bytes 196616 | tf_op jit(solution)/shard_map/ppermute | solution.py:397
  30.9 0.1 collective-permute-start.4
  31.0 4.3 %collective-permute-start.5 = (bf16[2,512,128]{2,1,0:T(8,128)(2,1)S(1)}, bf16[2,512,128]{2,1,0:T(8,128)(2,1)S(1)}, u32[]{:S(2)}, u32[]{:S(2)}) collective-permute-start(bf16[2,512,128]{2,1,0:T(8,128)(2,1)S(1)} %get-tuple-element.35), channel_id=1, source_target_pairs={{0,12},{4,8},{12,0},{1,13},{5,9},{13,1},{2,14},{6,10},{14,2},{3,15... | collective-permute-start | bytes 786440 | tf_op jit(solution)/shard_map/ppermute | solution.py:397
  35.2 0.0 collective-permute-done.9.refs_6_
  35.2 0.0 collective-permute-done.6.refs_0_
  35.3 2.6 %collective-permute-done.8.refs_5_ = bf16[2,3,64,256]{3,2,1,0:T(8,128)(2,1)S(1)} collective-permute-done((bf16[2,3,64,256]{3,2,1,0:T(8,128)(2,1)S(1)}, bf16[2,3,64,256]{3,2,1,0:T(8,128)(2,1)S(1)}, u32[]{:S(2)}, u32[]{:S(2)}) %collective-permute-start.8) | collective-permute-done | bytes 196640 | tf_op jit(solution)/shard_map/ppermute | solution.py:397
  37.9 0.9 %place_first.1 = (bf16[2048,128]{1,0:T(8,128)(2,1)}, bf16[2048,128]{1,0:T(8,128)(2,1)}, bf16[1,4,64,256]{3,2,1,0:T(8,128)(2,1)S(1)}, f32[1,4,64,256]{3,2,1,0:T(8,128)S(1)}) custom-call(bf16[2,512,128]{2,1,0:T(8,128)(2,1)S(1)} %collective-permute-done.6.refs_0_, bf16[2,512,128]{2,1,0:T(8,128)(2,1)S(1)} %get-tuple-element.38.refs_1_, ...), custom_call_target="tpu_custom_call" | custom-call | flops 12683575296 | bytes 3145728 | tf_op jit(solution)/shard_map/place_first/pallas_call | solution.py:243
  38.7 2.1 %collective-permute-start.10 = (bf16[1,4,64,256]{3,2,1,0:T(8,128)(2,1)S(1)}, bf16[1,4,64,256]{3,2,1,0:T(8,128)(2,1)S(1)}, u32[]{:S(2)}, u32[]{:S(2)}) collective-permute-start(bf16[1,4,64,256]{3,2,1,0:T(8,128)(2,1)S(1)} %get-tuple-element.45), channel_id=1, source_target_pairs={{0,8},{4,12},{8,0},{12,4},{1,9},{5,13},{9,1},{13,5},{2,10},{6,14},... | collective-permute-start | bytes 393224 | tf_op jit(solution)/shard_map/ppermute | solution.py:397
  40.8 6.4 %collective-permute-done.4.refs_0_ = bf16[2,512,128]{2,1,0:T(8,128)(2,1)S(1)} collective-permute-done((bf16[2,512,128]{2,1,0:T(8,128)(2,1)S(1)}, bf16[2,512,128]{2,1,0:T(8,128)(2,1)S(1)}, u32[]{:S(2)}, u32[]{:S(2)}) %collective-permute-start.4) | collective-permute-done | bytes 262176 | tf_op jit(solution)/shard_map/ppermute | solution.py:397
  47.2 0.0 collective-permute-done.5.refs_1_
  47.2 2.7 %collective-permute-done.10 = bf16[1,4,64,256]{3,2,1,0:T(8,128)(2,1)S(1)} collective-permute-done((bf16[1,4,64,256]{3,2,1,0:T(8,128)(2,1)S(1)}, bf16[1,4,64,256]{3,2,1,0:T(8,128)(2,1)S(1)}, u32[]{:S(2)}, u32[]{:S(2)}) %collective-permute-start.10) | collective-permute-done | bytes 131104 | tf_op jit(solution)/shard_map/ppermute | solution.py:397
  49.9 0.9 %place_last.1 = (bf16[2048,128]{1,0:T(8,128)(2,1)}, bf16[2048,128]{1,0:T(8,128)(2,1)}, bf16[256,128]{1,0:T(8,128)(2,1)}, bf16[256,128]{1,0:T(8,128)(2,1)}) custom-call(bf16[2,512,128]{2,1,0:T(8,128)(2,1)S(1)} %collective-permute-done.4.refs_0_, ...), custom_call_target="tpu_custom_call", output_to_operand_aliasing={{0}: (4, {}), {1}: (5, {})} | custom-call | flops 8455716864 | bytes 2097152 | tf_op jit(solution)/shard_map/place_last/pallas_call | solution.py:243
  (1 shorter events, 0.0 us)
Async XLA Ops:
  0.6 12.5 %collective-permute-start = (bf16[256,128]{1,0:T(8,128)(2,1)}, bf16[256,128]{1,0:T(8,128)(2,1)S(1)}, u32[]{:S(2)}, u32[]{:S(2)}) collective-permute-start(bf16[256,128]{1,0:T(8,128)(2,1)} %bitcast.16), channel_id=1, source_target_pairs={{0,4},{4,8},{8,12},{12,0},{1,5},{5,9},{9,13},{13,1},{2,6},{6,10},{... | collective-permute-start | bytes 196616 | tf_op jit(solution)/shard_map/ppermute | solution.py:397
  3.7 4.6 %copy-start = (s32[4,4]{1,0:T(4,128)S(1)}, s32[4,4]{1,0:T(4,128)}, u32[]{:S(2)}) copy-start(s32[4,4]{1,0:T(4,128)} %owners_ref.3) | copy-start | bytes 196
  3.7 9.4 %collective-permute-start.1 = (bf16[256,128]{1,0:T(8,128)(2,1)}, bf16[256,128]{1,0:T(8,128)(2,1)S(1)}, u32[]{:S(2)}, u32[]{:S(2)}) collective-permute-start(bf16[256,128]{1,0:T(8,128)(2,1)} %bitcast.19), channel_id=1, source_target_pairs={{0,4},{4,8},{8,12},{12,0},{1,5},{5,9},{9,13},{13,1},{2,6},{6,10},{... | collective-permute-start | bytes 196616 | tf_op jit(solution)/shard_map/ppermute | solution.py:397
  5.3 7.8 %collective-permute-start.2 = (bf16[256,128]{1,0:T(8,128)(2,1)}, bf16[256,128]{1,0:T(8,128)(2,1)S(1)}, u32[]{:S(2)}, u32[]{:S(2)}) collective-permute-start(bf16[256,128]{1,0:T(8,128)(2,1)} %bitcast.17), channel_id=1, source_target_pairs={{0,8},{4,12},{8,4},{12,0},{1,9},{5,13},{9,5},{13,1},{2,10},{6,14},... | collective-permute-start | bytes 196616 | tf_op jit(solution)/shard_map/ppermute | solution.py:397
  6.4 6.8 %collective-permute-start.3 = (bf16[256,128]{1,0:T(8,128)(2,1)}, bf16[256,128]{1,0:T(8,128)(2,1)S(1)}, u32[]{:S(2)}, u32[]{:S(2)}) collective-permute-start(bf16[256,128]{1,0:T(8,128)(2,1)} %bitcast.20), channel_id=1, source_target_pairs={{0,8},{4,12},{8,4},{12,0},{1,9},{5,13},{9,5},{13,1},{2,10},{6,14},... | collective-permute-start | bytes 196616 | tf_op jit(solution)/shard_map/ppermute | solution.py:397
  8.3 2.3 %copy-start.1 = (s32[8]{0:T(128)S(1)}, s32[8]{0:T(128)}, u32[]{:S(2)}) copy-start(s32[8]{0:T(128)} %ends_ref.1) | copy-start | bytes 100
  9.9 14.1 %collective-permute-start.7 = (bf16[2,512,128]{2,1,0:T(8,128)(2,1)S(1)}, bf16[2,512,128]{2,1,0:T(8,128)(2,1)S(1)}, u32[]{:S(2)}, u32[]{:S(2)}) collective-permute-start(bf16[2,512,128]{2,1,0:T(8,128)(2,1)S(1)} %pack_early.1.refs_1_), channel_id=1, source_target_pairs={{8,4},{9,5},{10,6},{11,7},{24,20},{25,21},{26,22},{27,23}} | collective-permute-start | bytes 786440 | tf_op jit(solution)/shard_map/ppermute | solution.py:397
  15.1 20.1 %collective-permute-start.6 = (bf16[2,512,128]{2,1,0:T(8,128)(2,1)S(1)}, bf16[2,512,128]{2,1,0:T(8,128)(2,1)S(1)}, u32[]{:S(2)}, u32[]{:S(2)}) collective-permute-start(bf16[2,512,128]{2,1,0:T(8,128)(2,1)S(1)} %get-tuple-element.36), channel_id=1, source_target_pairs={{0,8},{4,12},{8,0},{12,4},{1,9},{5,13},{9,1},{13,5},{2,10},{6,14},... | collective-permute-start | bytes 786440 | tf_op jit(solution)/shard_map/ppermute | solution.py:397
  24.8 13.1 %collective-permute-start.8 = (bf16[2,3,64,256]{3,2,1,0:T(8,128)(2,1)S(1)}, bf16[2,3,64,256]{3,2,1,0:T(8,128)(2,1)S(1)}, u32[]{:S(2)}, u32[]{:S(2)}) collective-permute-start(bf16[2,3,64,256]{3,2,1,0:T(8,128)(2,1)S(1)} %get-tuple-element.42), channel_id=1, source_target_pairs={{0,4},{4,0},{8,12},{12,8},{1,5},{5,1},{9,13},{13,9},{2,6},{6,2},{1... | collective-permute-start | bytes 589832 | tf_op jit(solution)/shard_map/ppermute | solution.py:397
  30.2 5.0 %collective-permute-start.9 = (bf16[2,1,64,256]{3,2,1,0:T(8,128)(2,1)S(1)}, bf16[2,1,64,256]{3,2,1,0:T(8,128)(2,1)S(1)}, u32[]{:S(2)}, u32[]{:S(2)}) collective-permute-start(bf16[2,1,64,256]{3,2,1,0:T(8,128)(2,1)S(1)} %get-tuple-element.43), channel_id=1, source_target_pairs={{8,12},{12,8},{9,13},{13,9},{10,14},{14,10},{11,15},{15,11},{24,28... | collective-permute-start | bytes 196616 | tf_op jit(solution)/shard_map/ppermute | solution.py:397
  30.9 16.3 %collective-permute-start.4 = (bf16[2,512,128]{2,1,0:T(8,128)(2,1)S(1)}, bf16[2,512,128]{2,1,0:T(8,128)(2,1)S(1)}, u32[]{:S(2)}, u32[]{:S(2)}) collective-permute-start(bf16[2,512,128]{2,1,0:T(8,128)(2,1)S(1)} %get-tuple-element.34), channel_id=1, source_target_pairs={{0,4},{4,0},{8,12},{12,8},{1,5},{5,1},{9,13},{13,9},{2,6},{6,2},{1... | collective-permute-start | bytes 786440 | tf_op jit(solution)/shard_map/ppermute | solution.py:397
  31.0 16.2 %collective-permute-start.5 = (bf16[2,512,128]{2,1,0:T(8,128)(2,1)S(1)}, bf16[2,512,128]{2,1,0:T(8,128)(2,1)S(1)}, u32[]{:S(2)}, u32[]{:S(2)}) collective-permute-start(bf16[2,512,128]{2,1,0:T(8,128)(2,1)S(1)} %get-tuple-element.35), channel_id=1, source_target_pairs={{0,12},{4,8},{12,0},{1,13},{5,9},{13,1},{2,14},{6,10},{14,2},{3,15... | collective-permute-start | bytes 786440 | tf_op jit(solution)/shard_map/ppermute | solution.py:397
  38.7 11.1 %collective-permute-start.10 = (bf16[1,4,64,256]{3,2,1,0:T(8,128)(2,1)S(1)}, bf16[1,4,64,256]{3,2,1,0:T(8,128)(2,1)S(1)}, u32[]{:S(2)}, u32[]{:S(2)}) collective-permute-start(bf16[1,4,64,256]{3,2,1,0:T(8,128)(2,1)S(1)} %get-tuple-element.45), channel_id=1, source_target_pairs={{0,8},{4,12},{8,0},{12,4},{1,9},{5,13},{9,1},{13,5},{2,10},{6,14},... | collective-permute-start | bytes 393224 | tf_op jit(solution)/shard_map/ppermute | solution.py:397

commit v16 on v13

--- a/solution.py
+++ b/solution.py
@@ -130,7 +130,7 @@
     n, width, rows, block = plan.n, plan.width, plan.rows, plan.block
     qg_refs, refs = refs[: len(items)], refs[len(items) :]
     done_refs, refs = refs[: len(done)], refs[len(done) :]
-    kv_refs, refs = refs[: -(len(items) + 7)], refs[-(len(items) + 7) :]
+    kv_refs, refs = refs[: -(len(items) + 8)], refs[-(len(items) + 8) :]
     pay_refs, grad_refs, (k_win, v_win, acc) = refs[: len(items)], refs[len(items) : -3], refs[-3:]
     step = pl.program_id(0)
     own = meta[0]
@@ -160,25 +160,24 @@
 
     @pl.when(step == len(items) - 1)
     def _():
-        def put_part(key_range, entry, part):
-            @pl.when(key_range < n // 2)
-            def _():
-                grad_refs[2][entry, key_range] = part.astype(jnp.bfloat16)
-
-            @pl.when(key_range >= n // 2)
-            def _():
-                grad_refs[3][entry, key_range - n // 2] = part.astype(jnp.bfloat16)
-
         def of_range(key_range, carry):
             at = lax.rem(key_range - own + plan.back + n, n) * rows
             for apart in range(n):
                 slot = plan.slot(meta, key_range, own ^ apart)
                 part = acc[pl.ds(pl.multiple_of(at + slot * block, block), block), :]
-                if apart % 2 == 0:
-                    to = grad_refs[apart % 4 // 2]
-                    to[apart // 4, key_range] = part
+                entry = apart // 4
+                if apart % 4 == 3:
+
+                    @pl.when(key_range < n // 2)
+                    def _():
+                        grad_refs[2][entry, key_range] = part.astype(jnp.bfloat16)
+
+                    @pl.when(key_range >= n // 2)
+                    def _():
+                        grad_refs[3][entry, key_range - n // 2] = part.astype(jnp.bfloat16)
                 else:
-                    put_part(key_range, apart // 2, part)
+                    to = grad_refs[(0, 4, 1)[apart % 4]]
+                    to[entry, key_range] = part.astype(to.dtype)
             return carry
 
         lax.fori_loop(0, n, of_range, 0)
@@ -228,9 +227,10 @@
     n = plan.n
     window = pltpu.VMEM((plan.window_ranges * plan.rows, plan.width), jnp.bfloat16)
     keep = jax.ShapeDtypeStruct((n // 4, n, plan.block, 2 * plan.width), jnp.float32)
-    send = jax.ShapeDtypeStruct((n // 2, n // 2, plan.block, 2 * plan.width), jnp.bfloat16)
+    send = jax.ShapeDtypeStruct((n // 4, n // 2, plan.block, 2 * plan.width), jnp.bfloat16)
+    near = jax.ShapeDtypeStruct(keep.shape, jnp.bfloat16)
     out_shape = [jax.ShapeDtypeStruct((2, plan.cols, plan.width), jnp.bfloat16)] * len(items)
-    out_shape += [keep, keep, send, send]
+    out_shape += [keep, keep, send, send, near]
     operands = (meta, *qg_list, *done_grads, *kv_list)
     return kernel_call(
         functools.partial(last_kernel, plan, done, items), "attend_last", operands,
@@ -247,7 +247,7 @@
     if final:
         grads, (_, _, attended, query_grad, key_grad, value_grad, sums, sems, sum_sems) = refs[:-9], refs[-9:]
     else:
-        grads, (attended, query_grad, send, kept, sems) = refs[:-5], refs[-5:]
+        (pass_on, to_near, *arrived), (attended, query_grad, send, near, sems) = refs[:-5], refs[-5:]
     copies = []
     for i, item in enumerate(items):
         to = pl.ds(pl.multiple_of((own ^ item) * cols, cols), cols)
@@ -263,15 +263,10 @@
             copies.append(pltpu.make_async_copy(sums.at[i], ref, sum_sems.at[i]))
             copies[-1].start()
     else:
-        pass_on, keep, *arrived = grads
-        for entry in range(n // 2):
-            for half, ref in enumerate(arrived):
-                ranges = pl.ds(half * (n // 2), n // 2)
-                total = (keep, pass_on)[entry % 2][entry // 2, ranges] + ref[entry].astype(jnp.float32)
-                if entry % 2:
-                    send[entry // 2, ranges] = total.astype(jnp.bfloat16)
-                else:
-                    kept[entry // 2, ranges] = total
+        near[...] = to_near[...]
+        for half, ref in enumerate(arrived):
+            ranges = pl.ds(half * (n // 2), n // 2)
+            send[:, ranges] = (pass_on[:, ranges] + ref[...].astype(jnp.float32)).astype(jnp.bfloat16)
     for copy in copies:
         copy.wait()
 
@@ -286,7 +281,7 @@
         out_specs += [spec_of(pl.ANY)] * 2
         scratch = [pltpu.VMEM((2, plan.rows, plan.width), jnp.bfloat16), *scratch, pltpu.SemaphoreType.DMA((2,))]
     else:
-        out_shape += [jax.ShapeDtypeStruct(grads[0].shape, kind) for kind in (jnp.bfloat16, jnp.float32)]
+        out_shape += [jax.ShapeDtypeStruct(grads[0].shape, jnp.bfloat16)] * 2
         out_specs += [spec_of(pltpu.VMEM)] * 2
     at = len(items) + len(grads)
     return kernel_call(
@@ -335,10 +330,10 @@
     out = attend_last(plan, first, items, meta, [blocks[x] for x in items], first_grads, kv_list)
     late = {x: across(pay, x) for x, pay in zip(sent, out)}
     stay[0] = out[len(sent)]
-    keep, pass_on, lower, upper = out[len(items) :]
+    keep, pass_on, lower, upper, to_near = out[len(items) :]
     upper = permuted(upper, [(i, i ^ 1) for i in range(n // 2, n)])
-    *filled, send, keep = place(plan, stay, (pass_on, keep, across(lower, 1), upper))
-    terms = (keep, across(send, 2))
+    *filled, send, to_near = place(plan, stay, (pass_on, to_near, across(lower, 1), upper))
+    terms = (keep, across(send, 2), across(to_near, 1))
     bit = 4
     while bit < n:
         total = sum(term.astype(jnp.float32) for term in terms)

time: 51.6 us -> 49.8 us (0.965)
  starting transfers between devices: 24.3 us -> 20 us
  waiting for transfers between devices: 14.2 us -> 16.7 us
    ppermute x10 -> x11, starting transfers between devices: 24.3 us -> 20 us  [permuted(): return lax.ppermute(array, 'ctx', pairs)]
    ppermute x10 -> x11, waiting for transfers between devices: 14.2 us -> 16.7 us  [permuted(): return lax.ppermute(array, 'ctx', pairs)]
  transfers between devices with their start and end apart: 10 -> 11, of which waited for: 3 -> 4; matrix products, arithmetic and copies ran while one was open for 1% -> 1% of each run, Pallas kernels for 13% -> 13%
where the time goes in v16:
time: 49.8 us; the launch traced here: 49.6 us
  starting transfers between devices  20 us (40%)
  waiting for transfers between devices  16.7 us (34%)
  Pallas kernels  10.4 us (21%)
  local copies, waits for them, and re-layouts  1.43 us (3%)
  between operations  0.7 us (1%)
    ppermute x11, starting transfers between devices, permuted(): return lax.ppermute(array, 'ctx', pairs)  20 us
    ppermute x11, waiting for transfers between devices, permuted(): return lax.ppermute(array, 'ctx', pairs)  16.7 us
    pallas_call x5, Pallas kernels, kernel_call(): pl.pallas_call(body, out_shape=out_shape, in_specs=[spec_of(space) for sp...  10.4 us
    unnamed x4, local copies, waits for them, and re-layouts  1.35 us
  transfers between devices with their start and end apart: 11, of which 4 were waited for; matrix products, arithmetic and copies ran while one was open for 1% of the time, Pallas kernels for 13%

profile of v16, /device:TPU:0, one launch (start us, length us, event | category | flops | bytes accessed | tf_op | source)
XLA Modules:
  0.0 49.6 jit_solution(9293004613469718604)
XLA Ops:
  0.6 4.1 %collective-permute-start.2 = (bf16[256,128]{1,0:T(8,128)(2,1)}, bf16[256,128]{1,0:T(8,128)(2,1)S(1)}, u32[]{:S(2)}, u32[]{:S(2)}) collective-permute-start(bf16[256,128]{1,0:T(8,128)(2,1)} %bitcast.19), channel_id=1, source_target_pairs={{0,8},{4,12},{8,0},{12,4},{1,9},{5,13},{9,1},{13,5},{2,10},{6,14},... | collective-permute-start | bytes 196616 | tf_op jit(solution)/shard_map/ppermute | solution.py:303
  4.7 1.6 %collective-permute-start = (bf16[256,128]{1,0:T(8,128)(2,1)}, bf16[256,128]{1,0:T(8,128)(2,1)S(1)}, u32[]{:S(2)}, u32[]{:S(2)}) collective-permute-start(bf16[256,128]{1,0:T(8,128)(2,1)} %bitcast.20), channel_id=1, source_target_pairs={{0,4},{4,8},{8,12},{12,0},{1,5},{5,9},{9,13},{13,1},{2,6},{6,10},{... | collective-permute-start | bytes 196616 | tf_op jit(solution)/shard_map/ppermute | solution.py:303
  6.3 0.3 collective-permute-start.3
  6.6 2.5 %collective-permute-start.1 = (bf16[256,128]{1,0:T(8,128)(2,1)}, bf16[256,128]{1,0:T(8,128)(2,1)S(1)}, u32[]{:S(2)}, u32[]{:S(2)}) collective-permute-start(bf16[256,128]{1,0:T(8,128)(2,1)} %bitcast.23), channel_id=1, source_target_pairs={{0,4},{4,8},{8,12},{12,0},{1,5},{5,9},{9,13},{13,1},{2,6},{6,10},{... | collective-permute-start | bytes 196616 | tf_op jit(solution)/shard_map/ppermute | solution.py:303
  9.1 0.7 %copy-done = s32[4,4]{1,0:T(4,128)S(1)} copy-done((s32[4,4]{1,0:T(4,128)S(1)}, s32[4,4]{1,0:T(4,128)}, u32[]{:S(2)}) %copy-start) | copy-done | bytes 88
  9.8 0.1 select_reduce_fusion
  9.9 0.1 reshape.77
  10.0 0.7 %copy-done.1 = s32[8]{0:T(128)S(1)} copy-done((s32[8]{0:T(128)S(1)}, s32[8]{0:T(128)}, u32[]{:S(2)}) %copy-start.1) | copy-done | bytes 56
  10.7 0.2 reduce-window.9
  10.9 0.1 pad_add_fusion.meta
  11.0 1.9 %pack.1 = (bf16[2,512,128]{2,1,0:T(8,128)(2,1)S(1)}, bf16[2,512,128]{2,1,0:T(8,128)(2,1)S(1)}, bf16[2,512,128]{2,1,0:T(8,128)(2,1)S(1)}, bf16[2,512,128]{2,1,0:T(8,128)(2,1)S(1)}, bf16[512,128]{1,0:T(8,128)(2,1)S(1)}) custom-call(s32[25]{0:T(128)S(1)} %pad_add_fusion.meta, bf16[2048,128]{1,0:T(8,128)(2,1)} %bitcast.17, bf16[2048,128]{1,0:T(8,128)(2,1)} %bitcast.18, ...), custom_call_target="tpu_custom_call" | custom-call | tf_op jit(solution)/shard_map/pack/pallas_call | solution.py:191
  12.9 0.0 collective-permute-done.2.refs_5_.refs_7_
  12.9 0.0 collective-permute-done.refs_3_.refs_5_
  12.9 1.6 %collective-permute-done.3.refs_6_.refs_8_ = bf16[256,128]{1,0:T(8,128)(2,1)S(1)} collective-permute-done((bf16[256,128]{1,0:T(8,128)(2,1)}, bf16[256,128]{1,0:T(8,128)(2,1)S(1)}, u32[]{:S(2)}, u32[]{:S(2)}) %collective-permute-start.3) | collective-permute-done | bytes 65568 | tf_op jit(solution)/shard_map/ppermute | solution.py:303
  14.5 0.0 collective-permute-done.1.refs_4_.refs_6_
  14.5 3.2 %attend_first.1 = (bf16[2,512,128]{2,1,0:T(8,128)(2,1)S(1)}, bf16[2,512,128]{2,1,0:T(8,128)(2,1)S(1)}, f32[576,256]{1,0:T(8,128)S(1)}, f32[576,256]{1,0:T(8,128)S(1)}) custom-call(s32[25]{0:T(128)S(1)} %pad_add_fusion.meta, bf16[2,512,128]{2,1,0:T(8,128)(2,1)S(1)} %get-tuple-element.30.refs_0_, bf16[2,512,128]{2,1,0:T(8,128)(2,1)S(1)} %get-tuple-element.31.refs_1_, ...), custom_call_target="tpu_custom_call" | custom-call | flops 8455716864 | bytes 2097152 | tf_op jit(solution)/shard_map/attend_first/pallas_call | solution.py:191
  17.7 2.3 %collective-permute-start.5 = (bf16[2,512,128]{2,1,0:T(8,128)(2,1)S(1)}, bf16[2,512,128]{2,1,0:T(8,128)(2,1)S(1)}, u32[]{:S(2)}, u32[]{:S(2)}) collective-permute-start(bf16[2,512,128]{2,1,0:T(8,128)(2,1)S(1)} %get-tuple-element.37), channel_id=1, source_target_pairs={{0,8},{4,12},{8,0},{12,4},{1,9},{5,13},{9,1},{13,5},{2,10},{6,14},... | collective-permute-start | bytes 786440 | tf_op jit(solution)/shard_map/ppermute | solution.py:303
  19.9 0.5 %collective-permute-start.6 = (bf16[2,512,128]{2,1,0:T(8,128)(2,1)S(1)}, bf16[2,512,128]{2,1,0:T(8,128)(2,1)S(1)}, u32[]{:S(2)}, u32[]{:S(2)}) collective-permute-start(bf16[2,512,128]{2,1,0:T(8,128)(2,1)S(1)} %get-tuple-element.38), channel_id=1, source_target_pairs={{0,4},{4,0},{8,12},{12,8},{1,5},{5,1},{9,13},{13,9},{2,6},{6,2},{1... | collective-permute-start | bytes 786440 | tf_op jit(solution)/shard_map/ppermute | solution.py:303
  20.4 3.6 %attend_last.1 = (bf16[2,512,128]{2,1,0:T(8,128)(2,1)S(1)}, bf16[2,512,128]{2,1,0:T(8,128)(2,1)S(1)}, f32[1,4,64,256]{3,2,1,0:T(8,128)S(1)}, f32[1,4,64,256]{3,2...) custom-call(s32[25]{0:T(128)S(1)} %pad_add_fusion.meta, ...), custom_call_target="tpu_custom_call" | custom-call | flops 8455716864 | bytes 2097152 | tf_op jit(solution)/shard_map/attend_last/pallas_call | solution.py:191
  24.0 1.6 %collective-permute-start.7 = (bf16[1,2,64,256]{3,2,1,0:T(8,128)(2,1)S(1)}, bf16[1,2,64,256]{3,2,1,0:T(8,128)(2,1)S(1)}, u32[]{:S(2)}, u32[]{:S(2)}) collective-permute-start(bf16[1,2,64,256]{3,2,1,0:T(8,128)(2,1)S(1)} %get-tuple-element.42), channel_id=1, source_target_pairs={{0,4},{4,0},{8,12},{12,8},{1,5},{5,1},{9,13},{13,9},{2,6},{6,2},{1... | collective-permute-start | bytes 196616 | tf_op jit(solution)/shard_map/ppermute | solution.py:303
  25.6 0.7 %collective-permute-start.8 = (bf16[1,2,64,256]{3,2,1,0:T(8,128)(2,1)S(1)}, bf16[1,2,64,256]{3,2,1,0:T(8,128)(2,1)S(1)}, u32[]{:S(2)}, u32[]{:S(2)}) collective-permute-start(bf16[1,2,64,256]{3,2,1,0:T(8,128)(2,1)S(1)} %get-tuple-element.43), channel_id=1, source_target_pairs={{8,12},{12,8},{9,13},{13,9},{10,14},{14,10},{11,15},{15,11},{24,28... | collective-permute-start | bytes 196616 | tf_op jit(solution)/shard_map/ppermute | solution.py:303
  26.2 3.5 %collective-permute-start.4 = (bf16[2,512,128]{2,1,0:T(8,128)(2,1)S(1)}, bf16[2,512,128]{2,1,0:T(8,128)(2,1)S(1)}, u32[]{:S(2)}, u32[]{:S(2)}) collective-permute-start(bf16[2,512,128]{2,1,0:T(8,128)(2,1)S(1)} %get-tuple-element.35), channel_id=1, source_target_pairs={{0,12},{4,8},{8,4},{12,0},{1,13},{5,9},{9,5},{13,1},{2,14},{6,10},... | collective-permute-start | bytes 786440 | tf_op jit(solution)/shard_map/ppermute | solution.py:303
  29.8 5.8 %collective-permute-done.7.refs_5_ = bf16[1,2,64,256]{3,2,1,0:T(8,128)(2,1)S(1)} collective-permute-done((bf16[1,2,64,256]{3,2,1,0:T(8,128)(2,1)S(1)}, bf16[1,2,64,256]{3,2,1,0:T(8,128)(2,1)S(1)}, u32[]{:S(2)}, u32[]{:S(2)}) %collective-permute-start.7) | collective-permute-done | bytes 65568 | tf_op jit(solution)/shard_map/ppermute | solution.py:303
  35.5 0.0 collective-permute-done.8.refs_6_
  35.5 0.0 collective-permute-done.5.refs_0_
  35.5 0.0 collective-permute-done.6.refs_1_
  35.5 0.9 %place_2_1_0.1 = (bf16[2048,128]{1,0:T(8,128)(2,1)}, bf16[2048,128]{1,0:T(8,128)(2,1)}, bf16[1,4,64,256]{3,2,1,0:T(8,128)(2,1)S(1)}, bf16[1,4,64,256]{3,2,1,0:T(8,128)(2,1)S(1)}) custom-call(bf16[2,512,128]{2,1,0:T(8,128)(2,1)S(1)} %collective-permute-done.5.refs_0_, bf16[2,512,128]{2,1,0:T(8,128)(2,1)S(1)} %collective-permute-done.6.refs_1_, ...), custom_call_target="tpu_custom_call" | custom-call | flops 12683575296 | bytes 3145728 | tf_op jit(solution)/shard_map/place_2_1_0/pallas_call | solution.py:191
  36.5 1.2 %collective-permute-start.9 = (bf16[1,4,64,256]{3,2,1,0:T(8,128)(2,1)S(1)}, bf16[1,4,64,256]{3,2,1,0:T(8,128)(2,1)S(1)}, u32[]{:S(2)}, u32[]{:S(2)}) collective-permute-start(bf16[1,4,64,256]{3,2,1,0:T(8,128)(2,1)S(1)} %get-tuple-element.44), channel_id=1, source_target_pairs={{0,8},{4,12},{8,0},{12,4},{1,9},{5,13},{9,1},{13,5},{2,10},{6,14},... | collective-permute-start | bytes 393224 | tf_op jit(solution)/shard_map/ppermute | solution.py:303
  37.7 1.7 %collective-permute-start.10 = (bf16[1,4,64,256]{3,2,1,0:T(8,128)(2,1)S(1)}, bf16[1,4,64,256]{3,2,1,0:T(8,128)(2,1)S(1)}, u32[]{:S(2)}, u32[]{:S(2)}) collective-permute-start(bf16[1,4,64,256]{3,2,1,0:T(8,128)(2,1)S(1)} %get-tuple-element.45), channel_id=1, source_target_pairs={{0,4},{4,0},{8,12},{12,8},{1,5},{5,1},{9,13},{13,9},{2,6},{6,2},{1... | collective-permute-start | bytes 393224 | tf_op jit(solution)/shard_map/ppermute | solution.py:303
  39.5 1.8 %collective-permute-done.4.refs_0_ = bf16[2,512,128]{2,1,0:T(8,128)(2,1)S(1)} collective-permute-done((bf16[2,512,128]{2,1,0:T(8,128)(2,1)S(1)}, bf16[2,512,128]{2,1,0:T(8,128)(2,1)S(1)}, u32[]{:S(2)}, u32[]{:S(2)}) %collective-permute-start.4) | collective-permute-done | bytes 262176 | tf_op jit(solution)/shard_map/ppermute | solution.py:303
  41.2 7.6 %collective-permute-done.9 = bf16[1,4,64,256]{3,2,1,0:T(8,128)(2,1)S(1)} collective-permute-done((bf16[1,4,64,256]{3,2,1,0:T(8,128)(2,1)S(1)}, bf16[1,4,64,256]{3,2,1,0:T(8,128)(2,1)S(1)}, u32[]{:S(2)}, u32[]{:S(2)}) %collective-permute-start.9) | collective-permute-done | bytes 131104 | tf_op jit(solution)/shard_map/ppermute | solution.py:303
  48.8 0.8 %place_3.1 = (bf16[2048,128]{1,0:T(8,128)(2,1)}, bf16[2048,128]{1,0:T(8,128)(2,1)}, bf16[256,128]{1,0:T(8,128)(2,1)}, bf16[256,128]{1,0:T(8,128)(2,1)}) custom-call(bf16[2,512,128]{2,1,0:T(8,128)(2,1)S(1)} %collective-permute-done.4.refs_0_, f32[256,256]{1,0:T(8,128)S(1)} %bitcast.16, ...), custom_call_target="tpu_custom_call", output_to_operand_aliasing={{0}: (4, {}), {1}: (5, {})} | custom-call | flops 4227858432 | bytes 1048576 | tf_op jit(solution)/shard_map/place_3/pallas_call | solution.py:191
  (3 shorter events, 0.0 us)
Async XLA Ops:
  0.6 12.3 %collective-permute-start.2 = (bf16[256,128]{1,0:T(8,128)(2,1)}, bf16[256,128]{1,0:T(8,128)(2,1)S(1)}, u32[]{:S(2)}, u32[]{:S(2)}) collective-permute-start(bf16[256,128]{1,0:T(8,128)(2,1)} %bitcast.19), channel_id=1, source_target_pairs={{0,8},{4,12},{8,0},{12,4},{1,9},{5,13},{9,1},{13,5},{2,10},{6,14},... | collective-permute-start | bytes 196616 | tf_op jit(solution)/shard_map/ppermute | solution.py:303
  4.7 8.2 %collective-permute-start = (bf16[256,128]{1,0:T(8,128)(2,1)}, bf16[256,128]{1,0:T(8,128)(2,1)S(1)}, u32[]{:S(2)}, u32[]{:S(2)}) collective-permute-start(bf16[256,128]{1,0:T(8,128)(2,1)} %bitcast.20), channel_id=1, source_target_pairs={{0,4},{4,8},{8,12},{12,0},{1,5},{5,9},{9,13},{13,1},{2,6},{6,10},{... | collective-permute-start | bytes 196616 | tf_op jit(solution)/shard_map/ppermute | solution.py:303
  6.3 8.2 %collective-permute-start.3 = (bf16[256,128]{1,0:T(8,128)(2,1)}, bf16[256,128]{1,0:T(8,128)(2,1)S(1)}, u32[]{:S(2)}, u32[]{:S(2)}) collective-permute-start(bf16[256,128]{1,0:T(8,128)(2,1)} %bitcast.22), channel_id=1, source_target_pairs={{0,8},{4,12},{8,0},{12,4},{1,9},{5,13},{9,1},{13,5},{2,10},{6,14},... | collective-permute-start | bytes 196616 | tf_op jit(solution)/shard_map/ppermute | solution.py:303
  6.6 7.9 %collective-permute-start.1 = (bf16[256,128]{1,0:T(8,128)(2,1)}, bf16[256,128]{1,0:T(8,128)(2,1)S(1)}, u32[]{:S(2)}, u32[]{:S(2)}) collective-permute-start(bf16[256,128]{1,0:T(8,128)(2,1)} %bitcast.23), channel_id=1, source_target_pairs={{0,4},{4,8},{8,12},{12,0},{1,5},{5,9},{9,13},{13,1},{2,6},{6,10},{... | collective-permute-start | bytes 196616 | tf_op jit(solution)/shard_map/ppermute | solution.py:303
  9.1 0.7 %copy-start = (s32[4,4]{1,0:T(4,128)S(1)}, s32[4,4]{1,0:T(4,128)}, u32[]{:S(2)}) copy-start(s32[4,4]{1,0:T(4,128)} %param.11) | copy-start | bytes 196
  10.0 0.7 %copy-start.1 = (s32[8]{0:T(128)S(1)}, s32[8]{0:T(128)}, u32[]{:S(2)}) copy-start(s32[8]{0:T(128)} %param.10) | copy-start | bytes 100
  17.7 17.9 %collective-permute-start.5 = (bf16[2,512,128]{2,1,0:T(8,128)(2,1)S(1)}, bf16[2,512,128]{2,1,0:T(8,128)(2,1)S(1)}, u32[]{:S(2)}, u32[]{:S(2)}) collective-permute-start(bf16[2,512,128]{2,1,0:T(8,128)(2,1)S(1)} %get-tuple-element.37), channel_id=1, source_target_pairs={{0,8},{4,12},{8,0},{12,4},{1,9},{5,13},{9,1},{13,5},{2,10},{6,14},... | collective-permute-start | bytes 786440 | tf_op jit(solution)/shard_map/ppermute | solution.py:303
  19.9 15.6 %collective-permute-start.6 = (bf16[2,512,128]{2,1,0:T(8,128)(2,1)S(1)}, bf16[2,512,128]{2,1,0:T(8,128)(2,1)S(1)}, u32[]{:S(2)}, u32[]{:S(2)}) collective-permute-start(bf16[2,512,128]{2,1,0:T(8,128)(2,1)S(1)} %get-tuple-element.38), channel_id=1, source_target_pairs={{0,4},{4,0},{8,12},{12,8},{1,5},{5,1},{9,13},{13,9},{2,6},{6,2},{1... | collective-permute-start | bytes 786440 | tf_op jit(solution)/shard_map/ppermute | solution.py:303
  24.0 11.5 %collective-permute-start.7 = (bf16[1,2,64,256]{3,2,1,0:T(8,128)(2,1)S(1)}, bf16[1,2,64,256]{3,2,1,0:T(8,128)(2,1)S(1)}, u32[]{:S(2)}, u32[]{:S(2)}) collective-permute-start(bf16[1,2,64,256]{3,2,1,0:T(8,128)(2,1)S(1)} %get-tuple-element.42), channel_id=1, source_target_pairs={{0,4},{4,0},{8,12},{12,8},{1,5},{5,1},{9,13},{13,9},{2,6},{6,2},{1... | collective-permute-start | bytes 196616 | tf_op jit(solution)/shard_map/ppermute | solution.py:303
  25.6 9.9 %collective-permute-start.8 = (bf16[1,2,64,256]{3,2,1,0:T(8,128)(2,1)S(1)}, bf16[1,2,64,256]{3,2,1,0:T(8,128)(2,1)S(1)}, u32[]{:S(2)}, u32[]{:S(2)}) collective-permute-start(bf16[1,2,64,256]{3,2,1,0:T(8,128)(2,1)S(1)} %get-tuple-element.43), channel_id=1, source_target_pairs={{8,12},{12,8},{9,13},{13,9},{10,14},{14,10},{11,15},{15,11},{24,28... | collective-permute-start | bytes 196616 | tf_op jit(solution)/shard_map/ppermute | solution.py:303
  26.2 15.0 %collective-permute-start.4 = (bf16[2,512,128]{2,1,0:T(8,128)(2,1)S(1)}, bf16[2,512,128]{2,1,0:T(8,128)(2,1)S(1)}, u32[]{:S(2)}, u32[]{:S(2)}) collective-permute-start(bf16[2,512,128]{2,1,0:T(8,128)(2,1)S(1)} %get-tuple-element.35), channel_id=1, source_target_pairs={{0,12},{4,8},{8,4},{12,0},{1,13},{5,9},{9,5},{13,1},{2,14},{6,10},... | collective-permute-start | bytes 786440 | tf_op jit(solution)/shard_map/ppermute | solution.py:303
  36.5 12.4 %collective-permute-start.9 = (bf16[1,4,64,256]{3,2,1,0:T(8,128)(2,1)S(1)}, bf16[1,4,64,256]{3,2,1,0:T(8,128)(2,1)S(1)}, u32[]{:S(2)}, u32[]{:S(2)}) collective-permute-start(bf16[1,4,64,256]{3,2,1,0:T(8,128)(2,1)S(1)} %get-tuple-element.44), channel_id=1, source_target_pairs={{0,8},{4,12},{8,0},{12,4},{1,9},{5,13},{9,1},{13,5},{2,10},{6,14},... | collective-permute-start | bytes 393224 | tf_op jit(solution)/shard_map/ppermute | solution.py:303
  37.7 11.1 %collective-permute-start.10 = (bf16[1,4,64,256]{3,2,1,0:T(8,128)(2,1)S(1)}, bf16[1,4,64,256]{3,2,1,0:T(8,128)(2,1)S(1)}, u32[]{:S(2)}, u32[]{:S(2)}) collective-permute-start(bf16[1,4,64,256]{3,2,1,0:T(8,128)(2,1)S(1)} %get-tuple-element.45), channel_id=1, source_target_pairs={{0,4},{4,0},{8,12},{12,8},{1,5},{5,1},{9,13},{13,9},{2,6},{6,2},{1... | collective-permute-start | bytes 393224 | tf_op jit(solution)/shard_map/ppermute | solution.py:303

commit v17 on v16

--- a/solution.py
+++ b/solution.py
@@ -217,7 +217,7 @@
     out_shape = [rows] * len(entries) + [grad] * len(entries)
     operands = (meta, *qg_list, *kv_list)
     return kernel_call(
-        functools.partial(first_kernel, plan, entries), "attend_first", operands,
+        functools.partial(first_kernel, plan, entries), f"attend_{entries[0]}", operands,
         [pltpu.SMEM] + [pltpu.VMEM] * (len(operands) - 1), out_shape, [window, window],
         out_specs=[spec_of(pltpu.VMEM)] * len(out_shape), cost_estimate=plan.cost(len(entries)),
     )
@@ -240,14 +240,16 @@
     )
 
 
-def place_kernel(plan, items, final, *refs):
+def place_kernel(plan, items, ngrads, final, *refs):
     n, cols, width = plan.n, plan.cols, plan.width
     own = lax.axis_index("ctx")
     pay_refs, refs = refs[: len(items)], refs[len(items) :]
     if final:
         grads, (_, _, attended, query_grad, key_grad, value_grad, sums, sems, sum_sems) = refs[:-9], refs[-9:]
+    elif ngrads:
+        (pass_on, to_near, *arrived), (_, _, attended, query_grad, send, near, sems) = refs[:-7], refs[-7:]
     else:
-        (pass_on, to_near, *arrived), (attended, query_grad, send, near, sems) = refs[:-5], refs[-5:]
+        attended, query_grad, sems = refs
     copies = []
     for i, item in enumerate(items):
         to = pl.ds(pl.multiple_of((own ^ item) * cols, cols), cols)
@@ -262,7 +264,7 @@
         for i, ref in enumerate((key_grad, value_grad)):
             copies.append(pltpu.make_async_copy(sums.at[i], ref, sum_sems.at[i]))
             copies[-1].start()
-    else:
+    elif ngrads:
         near[...] = to_near[...]
         for half, ref in enumerate(arrived):
             ranges = pl.ds(half * (n // 2), n // 2)
@@ -280,12 +282,12 @@
         out_shape += [jax.ShapeDtypeStruct((plan.rows, plan.width), jnp.bfloat16)] * 2
         out_specs += [spec_of(pl.ANY)] * 2
         scratch = [pltpu.VMEM((2, plan.rows, plan.width), jnp.bfloat16), *scratch, pltpu.SemaphoreType.DMA((2,))]
-    else:
+    elif grads:
         out_shape += [jax.ShapeDtypeStruct(grads[0].shape, jnp.bfloat16)] * 2
         out_specs += [spec_of(pltpu.VMEM)] * 2
     at = len(items) + len(grads)
     return kernel_call(
-        functools.partial(place_kernel, plan, items, final), "place_" + "_".join(map(str, items)),
+        functools.partial(place_kernel, plan, items, len(grads), final), "place_" + "_".join(map(str, items)),
         (*payloads.values(), *grads, *filled),
         [pl.ANY] * len(items) + [pltpu.VMEM] * len(grads) + [pl.ANY] * len(filled),
         out_shape, scratch, out_specs=out_specs, input_output_aliases={at: 0, at + 1: 1} if filled else {},
@@ -323,16 +325,20 @@
     *blocks, kv = pack(plan, meta, q, g, k, v)
     kv_list = [kv, *kv_list]
     first = (n // 2, 1)
-    first_pay, near_pay, *first_grads = attend_first(plan, first, meta, [blocks[x] for x in first], kv_list)
-    stay = {x: across(pay, x) for x, pay in zip(first, (first_pay, near_pay))}
+    pays, grads = {}, []
+    for x in first:
+        pay, grad = attend_first(plan, (x,), meta, [blocks[x]], kv_list)
+        pays[x] = across(pay, x)
+        grads.append(grad)
     sent = [x for x in range(1, n) if x not in first]
     items = (*sent, 0)
-    out = attend_last(plan, first, items, meta, [blocks[x] for x in items], first_grads, kv_list)
+    out = attend_last(plan, first, items, meta, [blocks[x] for x in items], grads, kv_list)
     late = {x: across(pay, x) for x, pay in zip(sent, out)}
-    stay[0] = out[len(sent)]
+    stay = {0: out[len(sent)]}
     keep, pass_on, lower, upper, to_near = out[len(items) :]
     upper = permuted(upper, [(i, i ^ 1) for i in range(n // 2, n)])
-    *filled, send, to_near = place(plan, stay, (pass_on, to_near, across(lower, 1), upper))
+    filled = place(plan, pays, ())
+    *filled, send, to_near = place(plan, stay, (pass_on, to_near, across(lower, 1), upper), filled)
     terms = (keep, across(send, 2), across(to_near, 1))
     bit = 4
     while bit < n:

time: 49.8 us -> 49.4 us (level)
  starting transfers between devices: 20 us -> 18.5 us
  Pallas kernels: 10.4 us -> 11.7 us
    ppermute x11, starting transfers between devices: 20 us -> 18.5 us  [permuted(): return lax.ppermute(array, 'ctx', pairs)]
    pallas_call x5 -> x7, Pallas kernels: 10.4 us -> 11.7 us  [kernel_call(): pl.pallas_call(body, out_shape=out_shape, in_specs=[spec_of(space) for sp...]
  transfers between devices with their start and end apart: 11 -> 11, of which waited for: 4 -> 4; matrix products, arithmetic and copies ran while one was open for 1% -> 1% of each run, Pallas kernels for 13% -> 18%
where the time goes in v17:
time: 49.4 us; the launch traced here: 49.2 us
  starting transfers between devices  18.5 us (37%)
  waiting for transfers between devices  16.3 us (33%)
  Pallas kernels  11.7 us (24%)
  local copies, waits for them, and re-layouts  1.43 us (3%)
  between operations  0.74 us (1%)
    ppermute x11, starting transfers between devices, permuted(): return lax.ppermute(array, 'ctx', pairs)  18.5 us
    ppermute x11, waiting for transfers between devices, permuted(): return lax.ppermute(array, 'ctx', pairs)  16.3 us
    pallas_call x7, Pallas kernels, kernel_call(): pl.pallas_call(body, out_shape=out_shape, in_specs=[spec_of(space) for sp...  11.7 us
    unnamed x4, local copies, waits for them, and re-layouts  1.35 us
  transfers between devices with their start and end apart: 11, of which 4 were waited for; matrix products, arithmetic and copies ran while one was open for 1% of the time, Pallas kernels for 18%

profile of v17, /device:TPU:0, one launch (start us, length us, event | category | flops | bytes accessed | tf_op | source)
XLA Modules:
  0.0 49.2 jit_solution(4180332725422648517)
XLA Ops:
  0.6 4.1 %collective-permute-start.2 = (bf16[256,128]{1,0:T(8,128)(2,1)}, bf16[256,128]{1,0:T(8,128)(2,1)S(1)}, u32[]{:S(2)}, u32[]{:S(2)}) collective-permute-start(bf16[256,128]{1,0:T(8,128)(2,1)} %bitcast.19), channel_id=1, source_target_pairs={{0,8},{4,12},{8,0},{12,4},{1,9},{5,13},{9,1},{13,5},{2,10},{6,14},... | collective-permute-start | bytes 196616 | tf_op jit(solution)/shard_map/ppermute | solution.py:305
  4.7 1.6 %collective-permute-start = (bf16[256,128]{1,0:T(8,128)(2,1)}, bf16[256,128]{1,0:T(8,128)(2,1)S(1)}, u32[]{:S(2)}, u32[]{:S(2)}) collective-permute-start(bf16[256,128]{1,0:T(8,128)(2,1)} %bitcast.20), channel_id=1, source_target_pairs={{0,4},{4,8},{8,12},{12,0},{1,5},{5,9},{9,13},{13,1},{2,6},{6,10},{... | collective-permute-start | bytes 196616 | tf_op jit(solution)/shard_map/ppermute | solution.py:305
  6.3 0.3 collective-permute-start.3
  6.6 2.5 %collective-permute-start.1 = (bf16[256,128]{1,0:T(8,128)(2,1)}, bf16[256,128]{1,0:T(8,128)(2,1)S(1)}, u32[]{:S(2)}, u32[]{:S(2)}) collective-permute-start(bf16[256,128]{1,0:T(8,128)(2,1)} %bitcast.23), channel_id=1, source_target_pairs={{0,4},{4,8},{8,12},{12,0},{1,5},{5,9},{9,13},{13,1},{2,6},{6,10},{... | collective-permute-start | bytes 196616 | tf_op jit(solution)/shard_map/ppermute | solution.py:305
  9.1 0.7 %copy-done = s32[4,4]{1,0:T(4,128)S(1)} copy-done((s32[4,4]{1,0:T(4,128)S(1)}, s32[4,4]{1,0:T(4,128)}, u32[]{:S(2)}) %copy-start) | copy-done | bytes 88
  9.8 0.1 select_reduce_fusion
  9.9 0.1 reshape.77
  10.0 0.7 %copy-done.1 = s32[8]{0:T(128)S(1)} copy-done((s32[8]{0:T(128)S(1)}, s32[8]{0:T(128)}, u32[]{:S(2)}) %copy-start.1) | copy-done | bytes 56
  10.7 0.2 reduce-window.9
  10.9 0.1 pad_add_fusion.meta
  11.0 1.9 %pack.1 = (bf16[2,512,128]{2,1,0:T(8,128)(2,1)S(1)}, bf16[2,512,128]{2,1,0:T(8,128)(2,1)S(1)}, bf16[2,512,128]{2,1,0:T(8,128)(2,1)S(1)}, bf16[2,512,128]{2,1,0:T(8,128)(2,1)S(1)}, bf16[512,128]{1,0:T(8,128)(2,1)S(1)}) custom-call(s32[25]{0:T(128)S(1)} %pad_add_fusion.meta, bf16[2048,128]{1,0:T(8,128)(2,1)} %bitcast.17, bf16[2048,128]{1,0:T(8,128)(2,1)} %bitcast.18, ...), custom_call_target="tpu_custom_call" | custom-call | tf_op jit(solution)/shard_map/pack/pallas_call | solution.py:191
  12.9 0.0 collective-permute-done.2.refs_4_.refs_7_
  12.9 1.6 %collective-permute-done.3.refs_5_.refs_8_ = bf16[256,128]{1,0:T(8,128)(2,1)S(1)} collective-permute-done((bf16[256,128]{1,0:T(8,128)(2,1)}, bf16[256,128]{1,0:T(8,128)(2,1)S(1)}, u32[]{:S(2)}, u32[]{:S(2)}) %collective-permute-start.3) | collective-permute-done | bytes 65568 | tf_op jit(solution)/shard_map/ppermute | solution.py:305
  14.5 0.0 collective-permute-done.1.refs_3_.refs_6_
  14.5 2.0 %attend_2.1 = (bf16[2,512,128]{2,1,0:T(8,128)(2,1)S(1)}, f32[576,256]{1,0:T(8,128)S(1)}) custom-call(s32[25]{0:T(128)S(1)} %pad_add_fusion.meta, bf16[2,512,128]{2,1,0:T(8,128)(2,1)S(1)} %get-tuple-element.32.refs_0_, bf16[512,128]{1,0:T(8,128)(2,1)S(1)} %get-tuple-element.33.refs_1_.refs_4_, bf16[256,128]{1,0:T(8,128)(2,1)S(1)} %collective-permute-done.refs_2_.refs_5_, ...), custom_call_target="tpu_custom_call" | custom-call | flops 4227858432 | bytes 1048576 | tf_op jit(solution)/shard_map/attend_2/pallas_call | solution.py:191
  16.5 2.3 %collective-permute-start.7 = (bf16[2,512,128]{2,1,0:T(8,128)(2,1)S(1)}, bf16[2,512,128]{2,1,0:T(8,128)(2,1)S(1)}, u32[]{:S(2)}, u32[]{:S(2)}) collective-permute-start(bf16[2,512,128]{2,1,0:T(8,128)(2,1)S(1)} %get-tuple-element.44), channel_id=1, source_target_pairs={{0,8},{4,12},{8,0},{12,4},{1,9},{5,13},{9,1},{13,5},{2,10},{6,14},... | collective-permute-start | bytes 786440 | tf_op jit(solution)/shard_map/ppermute | solution.py:305
  18.7 2.0 %attend_1.1 = (bf16[2,512,128]{2,1,0:T(8,128)(2,1)S(1)}, f32[576,256]{1,0:T(8,128)S(1)}) custom-call(s32[25]{0:T(128)S(1)} %pad_add_fusion.meta, bf16[2,512,128]{2,1,0:T(8,128)(2,1)S(1)} %get-tuple-element.35.refs_0_, bf16[512,128]{1,0:T(8,128)(2,1)S(1)} %get-tuple-element.33.refs_1_.refs_4_, bf16[256,128]{1,0:T(8,128)(2,1)S(1)} %collective-permute-done.refs_2_.refs_5_, ...), custom_call_target="tpu_custom_call" | custom-call | flops 4227858432 | bytes 1048576 | tf_op jit(solution)/shard_map/attend_1/pallas_call | solution.py:191
  20.7 0.6 %collective-permute-start.8 = (bf16[2,512,128]{2,1,0:T(8,128)(2,1)S(1)}, bf16[2,512,128]{2,1,0:T(8,128)(2,1)S(1)}, u32[]{:S(2)}, u32[]{:S(2)}) collective-permute-start(bf16[2,512,128]{2,1,0:T(8,128)(2,1)S(1)} %get-tuple-element.45), channel_id=1, source_target_pairs={{0,4},{4,0},{8,12},{12,8},{1,5},{5,1},{9,13},{13,9},{2,6},{6,2},{1... | collective-permute-start | bytes 786440 | tf_op jit(solution)/shard_map/ppermute | solution.py:305
  21.3 3.6 %attend_last.1 = (bf16[2,512,128]{2,1,0:T(8,128)(2,1)S(1)}, bf16[2,512,128]{2,1,0:T(8,128)(2,1)S(1)}, f32[1,4,64,256]{3,2,1,0:T(8,128)S(1)}, f32[1,4,64,256]{3,2...) custom-call(s32[25]{0:T(128)S(1)} %pad_add_fusion.meta, ...), custom_call_target="tpu_custom_call" | custom-call | flops 8455716864 | bytes 2097152 | tf_op jit(solution)/shard_map/attend_last/pallas_call | solution.py:191
  24.8 1.6 %collective-permute-start.5 = (bf16[1,2,64,256]{3,2,1,0:T(8,128)(2,1)S(1)}, bf16[1,2,64,256]{3,2,1,0:T(8,128)(2,1)S(1)}, u32[]{:S(2)}, u32[]{:S(2)}) collective-permute-start(bf16[1,2,64,256]{3,2,1,0:T(8,128)(2,1)S(1)} %get-tuple-element.42), channel_id=1, source_target_pairs={{0,4},{4,0},{8,12},{12,8},{1,5},{5,1},{9,13},{13,9},{2,6},{6,2},{1... | collective-permute-start | bytes 196616 | tf_op jit(solution)/shard_map/ppermute | solution.py:305
  26.4 0.7 %collective-permute-start.6 = (bf16[1,2,64,256]{3,2,1,0:T(8,128)(2,1)S(1)}, bf16[1,2,64,256]{3,2,1,0:T(8,128)(2,1)S(1)}, u32[]{:S(2)}, u32[]{:S(2)}) collective-permute-start(bf16[1,2,64,256]{3,2,1,0:T(8,128)(2,1)S(1)} %get-tuple-element.43), channel_id=1, source_target_pairs={{8,12},{12,8},{9,13},{13,9},{10,14},{14,10},{11,15},{15,11},{24,28... | collective-permute-start | bytes 196616 | tf_op jit(solution)/shard_map/ppermute | solution.py:305
  27.1 3.5 %collective-permute-start.4 = (bf16[2,512,128]{2,1,0:T(8,128)(2,1)S(1)}, bf16[2,512,128]{2,1,0:T(8,128)(2,1)S(1)}, u32[]{:S(2)}, u32[]{:S(2)}) collective-permute-start(bf16[2,512,128]{2,1,0:T(8,128)(2,1)S(1)} %get-tuple-element.37), channel_id=1, source_target_pairs={{0,12},{4,8},{8,4},{12,0},{1,13},{5,9},{9,5},{13,1},{2,14},{6,10},... | collective-permute-start | bytes 786440 | tf_op jit(solution)/shard_map/ppermute | solution.py:305
  30.6 0.3 collective-permute-done.7.refs_0_
  30.9 9.2 %collective-permute-done.8.refs_1_ = bf16[2,512,128]{2,1,0:T(8,128)(2,1)S(1)} collective-permute-done((bf16[2,512,128]{2,1,0:T(8,128)(2,1)S(1)}, bf16[2,512,128]{2,1,0:T(8,128)(2,1)S(1)}, u32[]{:S(2)}, u32[]{:S(2)}) %collective-permute-start.8) | collective-permute-done | bytes 262176 | tf_op jit(solution)/shard_map/ppermute | solution.py:305
  40.1 0.8 %place_2_1.1 = (bf16[2048,128]{1,0:T(8,128)(2,1)}, bf16[2048,128]{1,0:T(8,128)(2,1)}) custom-call(bf16[2,512,128]{2,1,0:T(8,128)(2,1)S(1)} %collective-permute-done.7.refs_0_, bf16[2,512,128]{2,1,0:T(8,128)(2,1)S(1)} %collective-permute-done.8.refs_1_), custom_call_target="tpu_custom_call" | custom-call | flops 8455716864 | bytes 2097152 | tf_op jit(solution)/shard_map/place_2_1/pallas_call | solution.py:191
  40.9 0.0 collective-permute-done.5.refs_3_
  40.9 0.0 collective-permute-done.6.refs_4_
  41.0 0.7 %place_0.1 = (bf16[2048,128]{1,0:T(8,128)(2,1)}, bf16[2048,128]{1,0:T(8,128)(2,1)}, bf16[1,4,64,256]{3,2,1,0:T(8,128)(2,1)S(1)}, bf16[1,4,64,256]{3,2,1,0:T(8,128)(2,1)S(1)}) custom-call(bf16[2,512,128]{2,1,0:T(8,128)(2,1)S(1)} %get-tuple-element.39.refs_0_, ...), custom_call_target="tpu_custom_call", output_to_operand_aliasing={{0}: (5, {}), {1}: (6, {})} | custom-call | flops 4227858432 | bytes 1048576 | tf_op jit(solution)/shard_map/place_0/pallas_call | solution.py:191
  41.7 0.1 collective-permute-start.9
  41.8 1.4 %collective-permute-start.10 = (bf16[1,4,64,256]{3,2,1,0:T(8,128)(2,1)S(1)}, bf16[1,4,64,256]{3,2,1,0:T(8,128)(2,1)S(1)}, u32[]{:S(2)}, u32[]{:S(2)}) collective-permute-start(bf16[1,4,64,256]{3,2,1,0:T(8,128)(2,1)S(1)} %get-tuple-element.49), channel_id=1, source_target_pairs={{0,4},{4,0},{8,12},{12,8},{1,5},{5,1},{9,13},{13,9},{2,6},{6,2},{1... | collective-permute-start | bytes 393224 | tf_op jit(solution)/shard_map/ppermute | solution.py:305
  43.2 5.2 %collective-permute-done.9 = bf16[1,4,64,256]{3,2,1,0:T(8,128)(2,1)S(1)} collective-permute-done((bf16[1,4,64,256]{3,2,1,0:T(8,128)(2,1)S(1)}, bf16[1,4,64,256]{3,2,1,0:T(8,128)(2,1)S(1)}, u32[]{:S(2)}, u32[]{:S(2)}) %collective-permute-start.9) | collective-permute-done | bytes 131104 | tf_op jit(solution)/shard_map/ppermute | solution.py:305
  48.4 0.8 %place_3.1 = (bf16[2048,128]{1,0:T(8,128)(2,1)}, bf16[2048,128]{1,0:T(8,128)(2,1)}, bf16[256,128]{1,0:T(8,128)(2,1)}, bf16[256,128]{1,0:T(8,128)(2,1)}) custom-call(bf16[2,512,128]{2,1,0:T(8,128)(2,1)S(1)} %collective-permute-done.4.refs_0_, f32[256,256]{1,0:T(8,128)S(1)} %bitcast.16, ...), custom_call_target="tpu_custom_call", output_to_operand_aliasing={{0}: (4, {}), {1}: (5, {})} | custom-call | flops 4227858432 | bytes 1048576 | tf_op jit(solution)/shard_map/place_3/pallas_call | solution.py:191
  (5 shorter events, 0.0 us)
Async XLA Ops:
  0.6 12.3 %collective-permute-start.2 = (bf16[256,128]{1,0:T(8,128)(2,1)}, bf16[256,128]{1,0:T(8,128)(2,1)S(1)}, u32[]{:S(2)}, u32[]{:S(2)}) collective-permute-start(bf16[256,128]{1,0:T(8,128)(2,1)} %bitcast.19), channel_id=1, source_target_pairs={{0,8},{4,12},{8,0},{12,4},{1,9},{5,13},{9,1},{13,5},{2,10},{6,14},... | collective-permute-start | bytes 196616 | tf_op jit(solution)/shard_map/ppermute | solution.py:305
  4.7 8.2 %collective-permute-start = (bf16[256,128]{1,0:T(8,128)(2,1)}, bf16[256,128]{1,0:T(8,128)(2,1)S(1)}, u32[]{:S(2)}, u32[]{:S(2)}) collective-permute-start(bf16[256,128]{1,0:T(8,128)(2,1)} %bitcast.20), channel_id=1, source_target_pairs={{0,4},{4,8},{8,12},{12,0},{1,5},{5,9},{9,13},{13,1},{2,6},{6,10},{... | collective-permute-start | bytes 196616 | tf_op jit(solution)/shard_map/ppermute | solution.py:305
  6.3 8.2 %collective-permute-start.3 = (bf16[256,128]{1,0:T(8,128)(2,1)}, bf16[256,128]{1,0:T(8,128)(2,1)S(1)}, u32[]{:S(2)}, u32[]{:S(2)}) collective-permute-start(bf16[256,128]{1,0:T(8,128)(2,1)} %bitcast.22), channel_id=1, source_target_pairs={{0,8},{4,12},{8,0},{12,4},{1,9},{5,13},{9,1},{13,5},{2,10},{6,14},... | collective-permute-start | bytes 196616 | tf_op jit(solution)/shard_map/ppermute | solution.py:305
  6.6 7.9 %collective-permute-start.1 = (bf16[256,128]{1,0:T(8,128)(2,1)}, bf16[256,128]{1,0:T(8,128)(2,1)S(1)}, u32[]{:S(2)}, u32[]{:S(2)}) collective-permute-start(bf16[256,128]{1,0:T(8,128)(2,1)} %bitcast.23), channel_id=1, source_target_pairs={{0,4},{4,8},{8,12},{12,0},{1,5},{5,9},{9,13},{13,1},{2,6},{6,10},{... | collective-permute-start | bytes 196616 | tf_op jit(solution)/shard_map/ppermute | solution.py:305
  9.1 0.7 %copy-start = (s32[4,4]{1,0:T(4,128)S(1)}, s32[4,4]{1,0:T(4,128)}, u32[]{:S(2)}) copy-start(s32[4,4]{1,0:T(4,128)} %param.11) | copy-start | bytes 196
  10.0 0.7 %copy-start.1 = (s32[8]{0:T(128)S(1)}, s32[8]{0:T(128)}, u32[]{:S(2)}) copy-start(s32[8]{0:T(128)} %param.10) | copy-start | bytes 100
  16.5 14.4 %collective-permute-start.7 = (bf16[2,512,128]{2,1,0:T(8,128)(2,1)S(1)}, bf16[2,512,128]{2,1,0:T(8,128)(2,1)S(1)}, u32[]{:S(2)}, u32[]{:S(2)}) collective-permute-start(bf16[2,512,128]{2,1,0:T(8,128)(2,1)S(1)} %get-tuple-element.44), channel_id=1, source_target_pairs={{0,8},{4,12},{8,0},{12,4},{1,9},{5,13},{9,1},{13,5},{2,10},{6,14},... | collective-permute-start | bytes 786440 | tf_op jit(solution)/shard_map/ppermute | solution.py:305
  20.7 19.4 %collective-permute-start.8 = (bf16[2,512,128]{2,1,0:T(8,128)(2,1)S(1)}, bf16[2,512,128]{2,1,0:T(8,128)(2,1)S(1)}, u32[]{:S(2)}, u32[]{:S(2)}) collective-permute-start(bf16[2,512,128]{2,1,0:T(8,128)(2,1)S(1)} %get-tuple-element.45), channel_id=1, source_target_pairs={{0,4},{4,0},{8,12},{12,8},{1,5},{5,1},{9,13},{13,9},{2,6},{6,2},{1... | collective-permute-start | bytes 786440 | tf_op jit(solution)/shard_map/ppermute | solution.py:305
  24.8 16.1 %collective-permute-start.5 = (bf16[1,2,64,256]{3,2,1,0:T(8,128)(2,1)S(1)}, bf16[1,2,64,256]{3,2,1,0:T(8,128)(2,1)S(1)}, u32[]{:S(2)}, u32[]{:S(2)}) collective-permute-start(bf16[1,2,64,256]{3,2,1,0:T(8,128)(2,1)S(1)} %get-tuple-element.42), channel_id=1, source_target_pairs={{0,4},{4,0},{8,12},{12,8},{1,5},{5,1},{9,13},{13,9},{2,6},{6,2},{1... | collective-permute-start | bytes 196616 | tf_op jit(solution)/shard_map/ppermute | solution.py:305
  26.4 14.5 %collective-permute-start.6 = (bf16[1,2,64,256]{3,2,1,0:T(8,128)(2,1)S(1)}, bf16[1,2,64,256]{3,2,1,0:T(8,128)(2,1)S(1)}, u32[]{:S(2)}, u32[]{:S(2)}) collective-permute-start(bf16[1,2,64,256]{3,2,1,0:T(8,128)(2,1)S(1)} %get-tuple-element.43), channel_id=1, source_target_pairs={{8,12},{12,8},{9,13},{13,9},{10,14},{14,10},{11,15},{15,11},{24,28... | collective-permute-start | bytes 196616 | tf_op jit(solution)/shard_map/ppermute | solution.py:305
  27.1 16.1 %collective-permute-start.4 = (bf16[2,512,128]{2,1,0:T(8,128)(2,1)S(1)}, bf16[2,512,128]{2,1,0:T(8,128)(2,1)S(1)}, u32[]{:S(2)}, u32[]{:S(2)}) collective-permute-start(bf16[2,512,128]{2,1,0:T(8,128)(2,1)S(1)} %get-tuple-element.37), channel_id=1, source_target_pairs={{0,12},{4,8},{8,4},{12,0},{1,13},{5,9},{9,5},{13,1},{2,14},{6,10},... | collective-permute-start | bytes 786440 | tf_op jit(solution)/shard_map/ppermute | solution.py:305
  41.7 6.7 %collective-permute-start.9 = (bf16[1,4,64,256]{3,2,1,0:T(8,128)(2,1)S(1)}, bf16[1,4,64,256]{3,2,1,0:T(8,128)(2,1)S(1)}, u32[]{:S(2)}, u32[]{:S(2)}) collective-permute-start(bf16[1,4,64,256]{3,2,1,0:T(8,128)(2,1)S(1)} %get-tuple-element.48), channel_id=1, source_target_pairs={{0,8},{4,12},{8,0},{12,4},{1,9},{5,13},{9,1},{13,5},{2,10},{6,14},... | collective-permute-start | bytes 393224 | tf_op jit(solution)/shard_map/ppermute | solution.py:305
  41.8 6.6 %collective-permute-start.10 = (bf16[1,4,64,256]{3,2,1,0:T(8,128)(2,1)S(1)}, bf16[1,4,64,256]{3,2,1,0:T(8,128)(2,1)S(1)}, u32[]{:S(2)}, u32[]{:S(2)}) collective-permute-start(bf16[1,4,64,256]{3,2,1,0:T(8,128)(2,1)S(1)} %get-tuple-element.49), channel_id=1, source_target_pairs={{0,4},{4,0},{8,12},{12,8},{1,5},{5,1},{9,13},{13,9},{2,6},{6,2},{1... | collective-permute-start | bytes 393224 | tf_op jit(solution)/shard_map/ppermute | solution.py:305

commit v18 on v17

--- a/solution.py
+++ b/solution.py
@@ -236,18 +236,32 @@
         functools.partial(last_kernel, plan, done, items), "attend_last", operands,
         [pltpu.SMEM] + [pltpu.VMEM] * (len(operands) - 1), out_shape,
         [window, window, pltpu.VMEM((n * plan.rows, 2 * plan.width), jnp.float32)],
-        out_specs=[spec_of(pltpu.VMEM)] * len(out_shape), cost_estimate=plan.cost(len(items)), grid=(len(items),),
-    )
-
-
-def place_kernel(plan, items, ngrads, final, *refs):
+        out_specs=[spec_of(pltpu.VMEM)] * len(out_shape), cost_estimate=plan.cost(4 * len(items)), grid=(len(items),),
+    )
+
+
+def fold_kernel(plan, pass_on, to_near, lower, upper, send, near):
+    near[...] = to_near[...]
+    for half, ref in enumerate((lower, upper)):
+        ranges = pl.ds(half * (plan.n // 2), plan.n // 2)
+        send[:, ranges] = (pass_on[:, ranges] + ref[...].astype(jnp.float32)).astype(jnp.bfloat16)
+
+
+def fold(plan, *operands):
+    out_shape = [jax.ShapeDtypeStruct(operands[1].shape, jnp.bfloat16)] * 2
+    return kernel_call(
+        functools.partial(fold_kernel, plan), "fold", operands, [pltpu.VMEM] * 4, out_shape, [],
+        out_specs=[spec_of(pltpu.VMEM)] * 2,
+        cost_estimate=pl.CostEstimate(flops=0, bytes_accessed=1024, transcendentals=0),
+    )
+
+
+def place_kernel(plan, items, final, *refs):
     n, cols, width = plan.n, plan.cols, plan.width
     own = lax.axis_index("ctx")
     pay_refs, refs = refs[: len(items)], refs[len(items) :]
     if final:
         grads, (_, _, attended, query_grad, key_grad, value_grad, sums, sems, sum_sems) = refs[:-9], refs[-9:]
-    elif ngrads:
-        (pass_on, to_near, *arrived), (_, _, attended, query_grad, send, near, sems) = refs[:-7], refs[-7:]
     else:
         attended, query_grad, sems = refs
     copies = []
@@ -264,11 +278,6 @@
         for i, ref in enumerate((key_grad, value_grad)):
             copies.append(pltpu.make_async_copy(sums.at[i], ref, sum_sems.at[i]))
             copies[-1].start()
-    elif ngrads:
-        near[...] = to_near[...]
-        for half, ref in enumerate(arrived):
-            ranges = pl.ds(half * (n // 2), n // 2)
-            send[:, ranges] = (pass_on[:, ranges] + ref[...].astype(jnp.float32)).astype(jnp.bfloat16)
     for copy in copies:
         copy.wait()
 
@@ -282,16 +291,13 @@
         out_shape += [jax.ShapeDtypeStruct((plan.rows, plan.width), jnp.bfloat16)] * 2
         out_specs += [spec_of(pl.ANY)] * 2
         scratch = [pltpu.VMEM((2, plan.rows, plan.width), jnp.bfloat16), *scratch, pltpu.SemaphoreType.DMA((2,))]
-    elif grads:
-        out_shape += [jax.ShapeDtypeStruct(grads[0].shape, jnp.bfloat16)] * 2
-        out_specs += [spec_of(pltpu.VMEM)] * 2
     at = len(items) + len(grads)
     return kernel_call(
-        functools.partial(place_kernel, plan, items, len(grads), final), "place_" + "_".join(map(str, items)),
+        functools.partial(place_kernel, plan, items, final), "place_" + "_".join(map(str, items)),
         (*payloads.values(), *grads, *filled),
         [pl.ANY] * len(items) + [pltpu.VMEM] * len(grads) + [pl.ANY] * len(filled),
         out_shape, scratch, out_specs=out_specs, input_output_aliases={at: 0, at + 1: 1} if filled else {},
-        cost_estimate=plan.cost(len(items)),
+        cost_estimate=plan.cost(4 * len(items)),
     )
 
 
@@ -334,11 +340,11 @@
     items = (*sent, 0)
     out = attend_last(plan, first, items, meta, [blocks[x] for x in items], grads, kv_list)
     late = {x: across(pay, x) for x, pay in zip(sent, out)}
-    stay = {0: out[len(sent)]}
+    pays[0] = out[len(sent)]
     keep, pass_on, lower, upper, to_near = out[len(items) :]
     upper = permuted(upper, [(i, i ^ 1) for i in range(n // 2, n)])
+    send, to_near = fold(plan, pass_on, to_near, across(lower, 1), upper)
     filled = place(plan, pays, ())
-    *filled, send, to_near = place(plan, stay, (pass_on, to_near, across(lower, 1), upper), filled)
     terms = (keep, across(send, 2), across(to_near, 1))
     bit = 4
     while bit < n:

time: 49.4 us -> 48.7 us (0.986)
  Pallas kernels: 11.7 us -> 11.2 us
    pallas_call x7, Pallas kernels: 11.7 us -> 11.2 us  [kernel_call(): pl.pallas_call(body, out_shape=out_shape, in_specs=[spec_of(space) for sp...]
  transfers between devices with their start and end apart: 11 -> 11, of which waited for: 4 -> 3; matrix products, arithmetic and copies ran while one was open for 1% -> 1% of each run, Pallas kernels for 18% -> 17%
where the time goes in v18:
time: 48.7 us; the launch traced here: 48.5 us
  starting transfers between devices  18.6 us (38%)
  waiting for transfers between devices  16.2 us (33%)
  Pallas kernels  11.2 us (23%)
  local copies, waits for them, and re-layouts  1.43 us (3%)
  between operations  0.72 us (1%)
    ppermute x11, starting transfers between devices, permuted(): return lax.ppermute(array, 'ctx', pairs)  18.6 us
    ppermute x11, waiting for transfers between devices, permuted(): return lax.ppermute(array, 'ctx', pairs)  16.2 us
    pallas_call x7, Pallas kernels, kernel_call(): pl.pallas_call(body, out_shape=out_shape, in_specs=[spec_of(space) for sp...  11.2 us
    unnamed x4, local copies, waits for them, and re-layouts  1.35 us
  transfers between devices with their start and end apart: 11, of which 3 were waited for; matrix products, arithmetic and copies ran while one was open for 1% of the time, Pallas kernels for 17%

profile of v18, /device:TPU:0, one launch (start us, length us, event | category | flops | bytes accessed | tf_op | source)
XLA Modules:
  0.0 48.5 jit_solution(785750957052067845)
XLA Ops:
  0.6 4.1 %collective-permute-start.2 = (bf16[256,128]{1,0:T(8,128)(2,1)}, bf16[256,128]{1,0:T(8,128)(2,1)S(1)}, u32[]{:S(2)}, u32[]{:S(2)}) collective-permute-start(bf16[256,128]{1,0:T(8,128)(2,1)} %bitcast.19), channel_id=1, source_target_pairs={{0,8},{4,12},{8,0},{12,4},{1,9},{5,13},{9,1},{13,5},{2,10},{6,14},... | collective-permute-start | bytes 196616 | tf_op jit(solution)/shard_map/ppermute | solution.py:311
  4.7 1.6 %collective-permute-start = (bf16[256,128]{1,0:T(8,128)(2,1)}, bf16[256,128]{1,0:T(8,128)(2,1)S(1)}, u32[]{:S(2)}, u32[]{:S(2)}) collective-permute-start(bf16[256,128]{1,0:T(8,128)(2,1)} %bitcast.20), channel_id=1, source_target_pairs={{0,4},{4,8},{8,12},{12,0},{1,5},{5,9},{9,13},{13,1},{2,6},{6,10},{... | collective-permute-start | bytes 196616 | tf_op jit(solution)/shard_map/ppermute | solution.py:311
  6.3 0.3 collective-permute-start.3
  6.6 2.5 %collective-permute-start.1 = (bf16[256,128]{1,0:T(8,128)(2,1)}, bf16[256,128]{1,0:T(8,128)(2,1)S(1)}, u32[]{:S(2)}, u32[]{:S(2)}) collective-permute-start(bf16[256,128]{1,0:T(8,128)(2,1)} %bitcast.23), channel_id=1, source_target_pairs={{0,4},{4,8},{8,12},{12,0},{1,5},{5,9},{9,13},{13,1},{2,6},{6,10},{... | collective-permute-start | bytes 196616 | tf_op jit(solution)/shard_map/ppermute | solution.py:311
  9.1 0.7 %copy-done = s32[4,4]{1,0:T(4,128)S(1)} copy-done((s32[4,4]{1,0:T(4,128)S(1)}, s32[4,4]{1,0:T(4,128)}, u32[]{:S(2)}) %copy-start) | copy-done | bytes 88
  9.8 0.1 select_reduce_fusion
  9.9 0.1 reshape.77
  10.0 0.7 %copy-done.1 = s32[8]{0:T(128)S(1)} copy-done((s32[8]{0:T(128)S(1)}, s32[8]{0:T(128)}, u32[]{:S(2)}) %copy-start.1) | copy-done | bytes 56
  10.7 0.2 reduce-window.9
  10.9 0.1 pad_add_fusion.meta
  11.0 1.9 %pack.1 = (bf16[2,512,128]{2,1,0:T(8,128)(2,1)S(1)}, bf16[2,512,128]{2,1,0:T(8,128)(2,1)S(1)}, bf16[2,512,128]{2,1,0:T(8,128)(2,1)S(1)}, bf16[2,512,128]{2,1,0:T(8,128)(2,1)S(1)}, bf16[512,128]{1,0:T(8,128)(2,1)S(1)}) custom-call(s32[25]{0:T(128)S(1)} %pad_add_fusion.meta, bf16[2048,128]{1,0:T(8,128)(2,1)} %bitcast.17, bf16[2048,128]{1,0:T(8,128)(2,1)} %bitcast.18, ...), custom_call_target="tpu_custom_call" | custom-call | tf_op jit(solution)/shard_map/pack/pallas_call | solution.py:191
  12.9 0.0 collective-permute-done.2.refs_4_.refs_7_
  12.9 0.0 collective-permute-done.refs_2_.refs_5_
  12.9 1.6 %collective-permute-done.3.refs_5_.refs_8_ = bf16[256,128]{1,0:T(8,128)(2,1)S(1)} collective-permute-done((bf16[256,128]{1,0:T(8,128)(2,1)}, bf16[256,128]{1,0:T(8,128)(2,1)S(1)}, u32[]{:S(2)}, u32[]{:S(2)}) %collective-permute-start.3) | collective-permute-done | bytes 65568 | tf_op jit(solution)/shard_map/ppermute | solution.py:311
  14.5 0.0 collective-permute-done.1.refs_3_.refs_6_
  14.5 2.0 %attend_2.1 = (bf16[2,512,128]{2,1,0:T(8,128)(2,1)S(1)}, f32[576,256]{1,0:T(8,128)S(1)}) custom-call(s32[25]{0:T(128)S(1)} %pad_add_fusion.meta, bf16[2,512,128]{2,1,0:T(8,128)(2,1)S(1)} %get-tuple-element.30.refs_0_, bf16[512,128]{1,0:T(8,128)(2,1)S(1)} %get-tuple-element.31.refs_1_.refs_4_, bf16[256,128]{1,0:T(8,128)(2,1)S(1)} %collective-permute-done.refs_2_.refs_5_, ...), custom_call_target="tpu_custom_call" | custom-call | flops 4227858432 | bytes 1048576 | tf_op jit(solution)/shard_map/attend_2/pallas_call | solution.py:191
  16.5 2.3 %collective-permute-start.9 = (bf16[2,512,128]{2,1,0:T(8,128)(2,1)S(1)}, bf16[2,512,128]{2,1,0:T(8,128)(2,1)S(1)}, u32[]{:S(2)}, u32[]{:S(2)}) collective-permute-start(bf16[2,512,128]{2,1,0:T(8,128)(2,1)S(1)} %get-tuple-element.43), channel_id=1, source_target_pairs={{0,8},{4,12},{8,0},{12,4},{1,9},{5,13},{9,1},{13,5},{2,10},{6,14},... | collective-permute-start | bytes 786440 | tf_op jit(solution)/shard_map/ppermute | solution.py:311
  18.7 2.0 %attend_1.1 = (bf16[2,512,128]{2,1,0:T(8,128)(2,1)S(1)}, f32[576,256]{1,0:T(8,128)S(1)}) custom-call(s32[25]{0:T(128)S(1)} %pad_add_fusion.meta, bf16[2,512,128]{2,1,0:T(8,128)(2,1)S(1)} %get-tuple-element.33.refs_0_, bf16[512,128]{1,0:T(8,128)(2,1)S(1)} %get-tuple-element.31.refs_1_.refs_4_, bf16[256,128]{1,0:T(8,128)(2,1)S(1)} %collective-permute-done.refs_2_.refs_5_, ...), custom_call_target="tpu_custom_call" | custom-call | flops 4227858432 | bytes 1048576 | tf_op jit(solution)/shard_map/attend_1/pallas_call | solution.py:191
  20.7 0.6 %collective-permute-start.10 = (bf16[2,512,128]{2,1,0:T(8,128)(2,1)S(1)}, bf16[2,512,128]{2,1,0:T(8,128)(2,1)S(1)}, u32[]{:S(2)}, u32[]{:S(2)}) collective-permute-start(bf16[2,512,128]{2,1,0:T(8,128)(2,1)S(1)} %get-tuple-element.44), channel_id=1, source_target_pairs={{0,4},{4,0},{8,12},{12,8},{1,5},{5,1},{9,13},{13,9},{2,6},{6,2},{1... | collective-permute-start | bytes 786440 | tf_op jit(solution)/shard_map/ppermute | solution.py:311
  21.3 3.6 %attend_last.1 = (bf16[2,512,128]{2,1,0:T(8,128)(2,1)S(1)}, bf16[2,512,128]{2,1,0:T(8,128)(2,1)S(1)}, f32[1,4,64,256]{3,2,1,0:T(8,128)S(1)}, f32[1,4,64,256]{3,2...) custom-call(s32[25]{0:T(128)S(1)} %pad_add_fusion.meta, ...), custom_call_target="tpu_custom_call" | custom-call | flops 33822867456 | bytes 8388608 | tf_op jit(solution)/shard_map/attend_last/pallas_call | solution.py:191
  24.8 1.6 %collective-permute-start.5 = (bf16[1,2,64,256]{3,2,1,0:T(8,128)(2,1)S(1)}, bf16[1,2,64,256]{3,2,1,0:T(8,128)(2,1)S(1)}, u32[]{:S(2)}, u32[]{:S(2)}) collective-permute-start(bf16[1,2,64,256]{3,2,1,0:T(8,128)(2,1)S(1)} %get-tuple-element.39), channel_id=1, source_target_pairs={{0,4},{4,0},{8,12},{12,8},{1,5},{5,1},{9,13},{13,9},{2,6},{6,2},{1... | collective-permute-start | bytes 196616 | tf_op jit(solution)/shard_map/ppermute | solution.py:311
  26.4 0.7 %collective-permute-start.6 = (bf16[1,2,64,256]{3,2,1,0:T(8,128)(2,1)S(1)}, bf16[1,2,64,256]{3,2,1,0:T(8,128)(2,1)S(1)}, u32[]{:S(2)}, u32[]{:S(2)}) collective-permute-start(bf16[1,2,64,256]{3,2,1,0:T(8,128)(2,1)S(1)} %get-tuple-element.40), channel_id=1, source_target_pairs={{8,12},{12,8},{9,13},{13,9},{10,14},{14,10},{11,15},{15,11},{24,28... | collective-permute-start | bytes 196616 | tf_op jit(solution)/shard_map/ppermute | solution.py:311
  27.1 3.5 %collective-permute-start.4 = (bf16[2,512,128]{2,1,0:T(8,128)(2,1)S(1)}, bf16[2,512,128]{2,1,0:T(8,128)(2,1)S(1)}, u32[]{:S(2)}, u32[]{:S(2)}) collective-permute-start(bf16[2,512,128]{2,1,0:T(8,128)(2,1)S(1)} %get-tuple-element.35), channel_id=1, source_target_pairs={{0,12},{4,8},{8,4},{12,0},{1,13},{5,9},{9,5},{13,1},{2,14},{6,10},... | collective-permute-start | bytes 786440 | tf_op jit(solution)/shard_map/ppermute | solution.py:311
  30.6 10.3 %collective-permute-done.5.lower = bf16[1,2,64,256]{3,2,1,0:T(8,128)(2,1)S(1)} collective-permute-done((bf16[1,2,64,256]{3,2,1,0:T(8,128)(2,1)S(1)}, bf16[1,2,64,256]{3,2,1,0:T(8,128)(2,1)S(1)}, u32[]{:S(2)}, u32[]{:S(2)}) %collective-permute-start.5) | collective-permute-done | bytes 65568 | tf_op jit(solution)/shard_map/ppermute | solution.py:311
  40.9 0.0 collective-permute-done.6.upper
  40.9 0.1 collective-permute-start.7
  41.0 1.4 %collective-permute-start.8 = (bf16[1,4,64,256]{3,2,1,0:T(8,128)(2,1)S(1)}, bf16[1,4,64,256]{3,2,1,0:T(8,128)(2,1)S(1)}, u32[]{:S(2)}, u32[]{:S(2)}) collective-permute-start(bf16[1,4,64,256]{3,2,1,0:T(8,128)(2,1)S(1)} %get-tuple-element.42), channel_id=1, source_target_pairs={{0,4},{4,0},{8,12},{12,8},{1,5},{5,1},{9,13},{13,9},{2,6},{6,2},{1... | collective-permute-start | bytes 393224 | tf_op jit(solution)/shard_map/ppermute | solution.py:311
  42.5 0.0 collective-permute-done.9.refs_0_
  42.5 0.0 collective-permute-done.10.refs_1_
  42.5 0.9 %place_2_1_0.1 = (bf16[2048,128]{1,0:T(8,128)(2,1)}, bf16[2048,128]{1,0:T(8,128)(2,1)}) custom-call(bf16[2,512,128]{2,1,0:T(8,128)(2,1)S(1)} %collective-permute-done.9.refs_0_, bf16[2,512,128]{2,1,0:T(8,128)(2,1)S(1)} %collective-permute-done.10.refs_1_, bf16[2,512,128]{2,1,0:T(8,128)(2,1)S(1)} %get-tuple-element.45.refs_2_), custom_call_target="tpu_custom_call" | custom-call | flops 50734301184 | bytes 12582912 | tf_op jit(solution)/shard_map/place_2_1_0/pallas_call | solution.py:191
  43.4 4.3 %collective-permute-done.7 = bf16[1,4,64,256]{3,2,1,0:T(8,128)(2,1)S(1)} collective-permute-done((bf16[1,4,64,256]{3,2,1,0:T(8,128)(2,1)S(1)}, bf16[1,4,64,256]{3,2,1,0:T(8,128)(2,1)S(1)}, u32[]{:S(2)}, u32[]{:S(2)}) %collective-permute-start.7) | collective-permute-done | bytes 131104 | tf_op jit(solution)/shard_map/ppermute | solution.py:311
  47.7 0.8 %place_3.1 = (bf16[2048,128]{1,0:T(8,128)(2,1)}, bf16[2048,128]{1,0:T(8,128)(2,1)}, bf16[256,128]{1,0:T(8,128)(2,1)}, bf16[256,128]{1,0:T(8,128)(2,1)}) custom-call(bf16[2,512,128]{2,1,0:T(8,128)(2,1)S(1)} %collective-permute-done.4.refs_0_, f32[256,256]{1,0:T(8,128)S(1)} %bitcast.16, ...), custom_call_target="tpu_custom_call", output_to_operand_aliasing={{0}: (4, {}), {1}: (5, {})} | custom-call | flops 16911433728 | bytes 4194304 | tf_op jit(solution)/shard_map/place_3/pallas_call | solution.py:191
  (5 shorter events, 0.0 us)
Async XLA Ops:
  0.6 12.3 %collective-permute-start.2 = (bf16[256,128]{1,0:T(8,128)(2,1)}, bf16[256,128]{1,0:T(8,128)(2,1)S(1)}, u32[]{:S(2)}, u32[]{:S(2)}) collective-permute-start(bf16[256,128]{1,0:T(8,128)(2,1)} %bitcast.19), channel_id=1, source_target_pairs={{0,8},{4,12},{8,0},{12,4},{1,9},{5,13},{9,1},{13,5},{2,10},{6,14},... | collective-permute-start | bytes 196616 | tf_op jit(solution)/shard_map/ppermute | solution.py:311
  4.7 8.2 %collective-permute-start = (bf16[256,128]{1,0:T(8,128)(2,1)}, bf16[256,128]{1,0:T(8,128)(2,1)S(1)}, u32[]{:S(2)}, u32[]{:S(2)}) collective-permute-start(bf16[256,128]{1,0:T(8,128)(2,1)} %bitcast.20), channel_id=1, source_target_pairs={{0,4},{4,8},{8,12},{12,0},{1,5},{5,9},{9,13},{13,1},{2,6},{6,10},{... | collective-permute-start | bytes 196616 | tf_op jit(solution)/shard_map/ppermute | solution.py:311
  6.3 8.2 %collective-permute-start.3 = (bf16[256,128]{1,0:T(8,128)(2,1)}, bf16[256,128]{1,0:T(8,128)(2,1)S(1)}, u32[]{:S(2)}, u32[]{:S(2)}) collective-permute-start(bf16[256,128]{1,0:T(8,128)(2,1)} %bitcast.22), channel_id=1, source_target_pairs={{0,8},{4,12},{8,0},{12,4},{1,9},{5,13},{9,1},{13,5},{2,10},{6,14},... | collective-permute-start | bytes 196616 | tf_op jit(solution)/shard_map/ppermute | solution.py:311
  6.6 7.9 %collective-permute-start.1 = (bf16[256,128]{1,0:T(8,128)(2,1)}, bf16[256,128]{1,0:T(8,128)(2,1)S(1)}, u32[]{:S(2)}, u32[]{:S(2)}) collective-permute-start(bf16[256,128]{1,0:T(8,128)(2,1)} %bitcast.23), channel_id=1, source_target_pairs={{0,4},{4,8},{8,12},{12,0},{1,5},{5,9},{9,13},{13,1},{2,6},{6,10},{... | collective-permute-start | bytes 196616 | tf_op jit(solution)/shard_map/ppermute | solution.py:311
  9.1 0.7 %copy-start = (s32[4,4]{1,0:T(4,128)S(1)}, s32[4,4]{1,0:T(4,128)}, u32[]{:S(2)}) copy-start(s32[4,4]{1,0:T(4,128)} %param.11) | copy-start | bytes 196
  10.0 0.7 %copy-start.1 = (s32[8]{0:T(128)S(1)}, s32[8]{0:T(128)}, u32[]{:S(2)}) copy-start(s32[8]{0:T(128)} %param.10) | copy-start | bytes 100
  16.5 26.0 %collective-permute-start.9 = (bf16[2,512,128]{2,1,0:T(8,128)(2,1)S(1)}, bf16[2,512,128]{2,1,0:T(8,128)(2,1)S(1)}, u32[]{:S(2)}, u32[]{:S(2)}) collective-permute-start(bf16[2,512,128]{2,1,0:T(8,128)(2,1)S(1)} %get-tuple-element.43), channel_id=1, source_target_pairs={{0,8},{4,12},{8,0},{12,4},{1,9},{5,13},{9,1},{13,5},{2,10},{6,14},... | collective-permute-start | bytes 786440 | tf_op jit(solution)/shard_map/ppermute | solution.py:311
  20.7 21.8 %collective-permute-start.10 = (bf16[2,512,128]{2,1,0:T(8,128)(2,1)S(1)}, bf16[2,512,128]{2,1,0:T(8,128)(2,1)S(1)}, u32[]{:S(2)}, u32[]{:S(2)}) collective-permute-start(bf16[2,512,128]{2,1,0:T(8,128)(2,1)S(1)} %get-tuple-element.44), channel_id=1, source_target_pairs={{0,4},{4,0},{8,12},{12,8},{1,5},{5,1},{9,13},{13,9},{2,6},{6,2},{1... | collective-permute-start | bytes 786440 | tf_op jit(solution)/shard_map/ppermute | solution.py:311
  24.8 16.1 %collective-permute-start.5 = (bf16[1,2,64,256]{3,2,1,0:T(8,128)(2,1)S(1)}, bf16[1,2,64,256]{3,2,1,0:T(8,128)(2,1)S(1)}, u32[]{:S(2)}, u32[]{:S(2)}) collective-permute-start(bf16[1,2,64,256]{3,2,1,0:T(8,128)(2,1)S(1)} %get-tuple-element.39), channel_id=1, source_target_pairs={{0,4},{4,0},{8,12},{12,8},{1,5},{5,1},{9,13},{13,9},{2,6},{6,2},{1... | collective-permute-start | bytes 196616 | tf_op jit(solution)/shard_map/ppermute | solution.py:311
  26.4 14.5 %collective-permute-start.6 = (bf16[1,2,64,256]{3,2,1,0:T(8,128)(2,1)S(1)}, bf16[1,2,64,256]{3,2,1,0:T(8,128)(2,1)S(1)}, u32[]{:S(2)}, u32[]{:S(2)}) collective-permute-start(bf16[1,2,64,256]{3,2,1,0:T(8,128)(2,1)S(1)} %get-tuple-element.40), channel_id=1, source_target_pairs={{8,12},{12,8},{9,13},{13,9},{10,14},{14,10},{11,15},{15,11},{24,28... | collective-permute-start | bytes 196616 | tf_op jit(solution)/shard_map/ppermute | solution.py:311
  27.1 20.6 %collective-permute-start.4 = (bf16[2,512,128]{2,1,0:T(8,128)(2,1)S(1)}, bf16[2,512,128]{2,1,0:T(8,128)(2,1)S(1)}, u32[]{:S(2)}, u32[]{:S(2)}) collective-permute-start(bf16[2,512,128]{2,1,0:T(8,128)(2,1)S(1)} %get-tuple-element.35), channel_id=1, source_target_pairs={{0,12},{4,8},{8,4},{12,0},{1,13},{5,9},{9,5},{13,1},{2,14},{6,10},... | collective-permute-start | bytes 786440 | tf_op jit(solution)/shard_map/ppermute | solution.py:311
  40.9 6.7 %collective-permute-start.7 = (bf16[1,4,64,256]{3,2,1,0:T(8,128)(2,1)S(1)}, bf16[1,4,64,256]{3,2,1,0:T(8,128)(2,1)S(1)}, u32[]{:S(2)}, u32[]{:S(2)}) collective-permute-start(bf16[1,4,64,256]{3,2,1,0:T(8,128)(2,1)S(1)} %get-tuple-element.41), channel_id=1, source_target_pairs={{0,8},{4,12},{8,0},{12,4},{1,9},{5,13},{9,1},{13,5},{2,10},{6,14},... | collective-permute-start | bytes 393224 | tf_op jit(solution)/shard_map/ppermute | solution.py:311
  41.0 6.7 %collective-permute-start.8 = (bf16[1,4,64,256]{3,2,1,0:T(8,128)(2,1)S(1)}, bf16[1,4,64,256]{3,2,1,0:T(8,128)(2,1)S(1)}, u32[]{:S(2)}, u32[]{:S(2)}) collective-permute-start(bf16[1,4,64,256]{3,2,1,0:T(8,128)(2,1)S(1)} %get-tuple-element.42), channel_id=1, source_target_pairs={{0,4},{4,0},{8,12},{12,8},{1,5},{5,1},{9,13},{13,9},{2,6},{6,2},{1... | collective-permute-start | bytes 393224 | tf_op jit(solution)/shard_map/ppermute | solution.py:311

commit v19 on v18

--- a/solution.py
+++ b/solution.py
@@ -330,7 +330,7 @@
     q, g = (x.reshape(rows * heads, width) for x in (query, output_gradient))
     *blocks, kv = pack(plan, meta, q, g, k, v)
     kv_list = [kv, *kv_list]
-    first = (n // 2, 1)
+    first = (n // 2,)
     pays, grads = {}, []
     for x in first:
         pay, grad = attend_first(plan, (x,), meta, [blocks[x]], kv_list)

time: 48.7 us -> 50.1 us (1.029)
  waiting for transfers between devices: 16.2 us -> 17.3 us
  starting transfers between devices: 18.6 us -> 19.5 us
  Pallas kernels: 11.2 us -> 10.5 us
    ppermute x11, waiting for transfers between devices: 16.2 us -> 17.3 us  [permuted(): return lax.ppermute(array, 'ctx', pairs)]
    ppermute x11, starting transfers between devices: 18.6 us -> 19.5 us  [permuted(): return lax.ppermute(array, 'ctx', pairs)]
    pallas_call x7 -> x6, Pallas kernels: 11.2 us -> 10.5 us  [kernel_call(): pl.pallas_call(body, out_shape=out_shape, in_specs=[spec_of(space) for sp...]
  transfers between devices with their start and end apart: 11 -> 11, of which waited for: 3 -> 4; matrix products, arithmetic and copies ran while one was open for 1% -> 1% of each run, Pallas kernels for 17% -> 15%
where the time goes in v19:
time: 50.1 us; the launch traced here: 49.9 us
  starting transfers between devices  19.5 us (39%)
  waiting for transfers between devices  17.3 us (35%)
  Pallas kernels  10.5 us (21%)
  local copies, waits for them, and re-layouts  1.43 us (3%)
  between operations  0.71 us (1%)
    ppermute x11, starting transfers between devices, permuted(): return lax.ppermute(array, 'ctx', pairs)  19.5 us
    ppermute x11, waiting for transfers between devices, permuted(): return lax.ppermute(array, 'ctx', pairs)  17.3 us
    pallas_call x6, Pallas kernels, kernel_call(): pl.pallas_call(body, out_shape=out_shape, in_specs=[spec_of(space) for sp...  10.5 us
    unnamed x4, local copies, waits for them, and re-layouts  1.35 us
  transfers between devices with their start and end apart: 11, of which 4 were waited for; matrix products, arithmetic and copies ran while one was open for 1% of the time, Pallas kernels for 15%

profile of v19, /device:TPU:0, one launch (start us, length us, event | category | flops | bytes accessed | tf_op | source)
XLA Modules:
  0.0 49.9 jit_solution(6362016565418626410)
XLA Ops:
  0.6 4.1 %collective-permute-start.2 = (bf16[256,128]{1,0:T(8,128)(2,1)}, bf16[256,128]{1,0:T(8,128)(2,1)S(1)}, u32[]{:S(2)}, u32[]{:S(2)}) collective-permute-start(bf16[256,128]{1,0:T(8,128)(2,1)} %bitcast.19), channel_id=1, source_target_pairs={{0,8},{4,12},{8,0},{12,4},{1,9},{5,13},{9,1},{13,5},{2,10},{6,14},... | collective-permute-start | bytes 196616 | tf_op jit(solution)/shard_map/ppermute | solution.py:311
  4.7 1.6 %collective-permute-start = (bf16[256,128]{1,0:T(8,128)(2,1)}, bf16[256,128]{1,0:T(8,128)(2,1)S(1)}, u32[]{:S(2)}, u32[]{:S(2)}) collective-permute-start(bf16[256,128]{1,0:T(8,128)(2,1)} %bitcast.20), channel_id=1, source_target_pairs={{0,4},{4,8},{8,12},{12,0},{1,5},{5,9},{9,13},{13,1},{2,6},{6,10},{... | collective-permute-start | bytes 196616 | tf_op jit(solution)/shard_map/ppermute | solution.py:311
  6.3 0.3 collective-permute-start.3
  6.6 2.5 %collective-permute-start.1 = (bf16[256,128]{1,0:T(8,128)(2,1)}, bf16[256,128]{1,0:T(8,128)(2,1)S(1)}, u32[]{:S(2)}, u32[]{:S(2)}) collective-permute-start(bf16[256,128]{1,0:T(8,128)(2,1)} %bitcast.23), channel_id=1, source_target_pairs={{0,4},{4,8},{8,12},{12,0},{1,5},{5,9},{9,13},{13,1},{2,6},{6,10},{... | collective-permute-start | bytes 196616 | tf_op jit(solution)/shard_map/ppermute | solution.py:311
  9.1 0.7 %copy-done = s32[4,4]{1,0:T(4,128)S(1)} copy-done((s32[4,4]{1,0:T(4,128)S(1)}, s32[4,4]{1,0:T(4,128)}, u32[]{:S(2)}) %copy-start) | copy-done | bytes 88
  9.8 0.1 select_reduce_fusion
  9.9 0.1 reshape.77
  10.0 0.7 %copy-done.1 = s32[8]{0:T(128)S(1)} copy-done((s32[8]{0:T(128)S(1)}, s32[8]{0:T(128)}, u32[]{:S(2)}) %copy-start.1) | copy-done | bytes 56
  10.7 0.2 reduce-window.9
  10.9 0.1 pad_add_fusion.meta
  11.0 1.9 %pack.1 = (bf16[2,512,128]{2,1,0:T(8,128)(2,1)S(1)}, bf16[2,512,128]{2,1,0:T(8,128)(2,1)S(1)}, bf16[2,512,128]{2,1,0:T(8,128)(2,1)S(1)}, bf16[2,512,128]{2,1,0:T(8,128)(2,1)S(1)}, bf16[512,128]{1,0:T(8,128)(2,1)S(1)}) custom-call(s32[25]{0:T(128)S(1)} %pad_add_fusion.meta, bf16[2048,128]{1,0:T(8,128)(2,1)} %bitcast.17, bf16[2048,128]{1,0:T(8,128)(2,1)} %bitcast.18, ...), custom_call_target="tpu_custom_call" | custom-call | tf_op jit(solution)/shard_map/pack/pallas_call | solution.py:191
  12.9 0.0 collective-permute-done.2.refs_4_.refs_7_
  12.9 0.0 collective-permute-done.refs_2_.refs_5_
  12.9 1.6 %collective-permute-done.3.refs_5_.refs_8_ = bf16[256,128]{1,0:T(8,128)(2,1)S(1)} collective-permute-done((bf16[256,128]{1,0:T(8,128)(2,1)}, bf16[256,128]{1,0:T(8,128)(2,1)S(1)}, u32[]{:S(2)}, u32[]{:S(2)}) %collective-permute-start.3) | collective-permute-done | bytes 65568 | tf_op jit(solution)/shard_map/ppermute | solution.py:311
  14.5 0.0 collective-permute-done.1.refs_3_.refs_6_
  14.5 2.0 %attend_2.1 = (bf16[2,512,128]{2,1,0:T(8,128)(2,1)S(1)}, f32[576,256]{1,0:T(8,128)S(1)}) custom-call(s32[25]{0:T(128)S(1)} %pad_add_fusion.meta, bf16[2,512,128]{2,1,0:T(8,128)(2,1)S(1)} %get-tuple-element.30.refs_0_, bf16[512,128]{1,0:T(8,128)(2,1)S(1)} %get-tuple-element.31.refs_1_.refs_4_, bf16[256,128]{1,0:T(8,128)(2,1)S(1)} %collective-permute-done.refs_2_.refs_5_, ...), custom_call_target="tpu_custom_call" | custom-call | flops 4227858432 | bytes 1048576 | tf_op jit(solution)/shard_map/attend_2/pallas_call | solution.py:191
  16.5 2.3 %collective-permute-start.10 = (bf16[2,512,128]{2,1,0:T(8,128)(2,1)S(1)}, bf16[2,512,128]{2,1,0:T(8,128)(2,1)S(1)}, u32[]{:S(2)}, u32[]{:S(2)}) collective-permute-start(bf16[2,512,128]{2,1,0:T(8,128)(2,1)S(1)} %get-tuple-element.42), channel_id=1, source_target_pairs={{0,8},{4,12},{8,0},{12,4},{1,9},{5,13},{9,1},{13,5},{2,10},{6,14},... | collective-permute-start | bytes 786440 | tf_op jit(solution)/shard_map/ppermute | solution.py:311
  18.7 4.9 %attend_last.1 = (bf16[2,512,128]{2,1,0:T(8,128)(2,1)S(1)}, bf16[2,512,128]{2,1,0:T(8,128)(2,1)S(1)}, bf16[2,512,128]{2,1,0:T(8,128)(2,1)S(1)}, f32[1,4,64,256]{...) custom-call(s32[25]{0:T(128)S(1)} %pad_add_fusion.meta, ...), custom_call_target="tpu_custom_call" | custom-call | flops 50734301184 | bytes 12582912 | tf_op jit(solution)/shard_map/attend_last/pallas_call | solution.py:191
  23.6 0.6 %collective-permute-start.6 = (bf16[1,2,64,256]{3,2,1,0:T(8,128)(2,1)S(1)}, bf16[1,2,64,256]{3,2,1,0:T(8,128)(2,1)S(1)}, u32[]{:S(2)}, u32[]{:S(2)}) collective-permute-start(bf16[1,2,64,256]{3,2,1,0:T(8,128)(2,1)S(1)} %get-tuple-element.38), channel_id=1, source_target_pairs={{0,4},{4,0},{8,12},{12,8},{1,5},{5,1},{9,13},{13,9},{2,6},{6,2},{1... | collective-permute-start | bytes 196616 | tf_op jit(solution)/shard_map/ppermute | solution.py:311
  24.2 0.7 %collective-permute-start.7 = (bf16[1,2,64,256]{3,2,1,0:T(8,128)(2,1)S(1)}, bf16[1,2,64,256]{3,2,1,0:T(8,128)(2,1)S(1)}, u32[]{:S(2)}, u32[]{:S(2)}) collective-permute-start(bf16[1,2,64,256]{3,2,1,0:T(8,128)(2,1)S(1)} %get-tuple-element.39), channel_id=1, source_target_pairs={{8,12},{12,8},{9,13},{13,9},{10,14},{14,10},{11,15},{15,11},{24,28... | collective-permute-start | bytes 196616 | tf_op jit(solution)/shard_map/ppermute | solution.py:311
  24.8 1.6 %collective-permute-start.4 = (bf16[2,512,128]{2,1,0:T(8,128)(2,1)S(1)}, bf16[2,512,128]{2,1,0:T(8,128)(2,1)S(1)}, u32[]{:S(2)}, u32[]{:S(2)}) collective-permute-start(bf16[2,512,128]{2,1,0:T(8,128)(2,1)S(1)} %get-tuple-element.33), channel_id=1, source_target_pairs={{0,4},{4,0},{8,12},{12,8},{1,5},{5,1},{9,13},{13,9},{2,6},{6,2},{1... | collective-permute-start | bytes 786440 | tf_op jit(solution)/shard_map/ppermute | solution.py:311
  26.4 3.4 %collective-permute-start.5 = (bf16[2,512,128]{2,1,0:T(8,128)(2,1)S(1)}, bf16[2,512,128]{2,1,0:T(8,128)(2,1)S(1)}, u32[]{:S(2)}, u32[]{:S(2)}) collective-permute-start(bf16[2,512,128]{2,1,0:T(8,128)(2,1)S(1)} %get-tuple-element.34), channel_id=1, source_target_pairs={{0,12},{4,8},{8,4},{12,0},{1,13},{5,9},{9,5},{13,1},{2,14},{6,10},... | collective-permute-start | bytes 786440 | tf_op jit(solution)/shard_map/ppermute | solution.py:311
  29.9 2.4 %collective-permute-done.6.lower = bf16[1,2,64,256]{3,2,1,0:T(8,128)(2,1)S(1)} collective-permute-done((bf16[1,2,64,256]{3,2,1,0:T(8,128)(2,1)S(1)}, bf16[1,2,64,256]{3,2,1,0:T(8,128)(2,1)S(1)}, u32[]{:S(2)}, u32[]{:S(2)}) %collective-permute-start.6) | collective-permute-done | bytes 65568 | tf_op jit(solution)/shard_map/ppermute | solution.py:311
  32.2 0.0 collective-permute-done.7.upper
  32.3 0.1 collective-permute-start.8
  32.4 2.4 %collective-permute-start.9 = (bf16[1,4,64,256]{3,2,1,0:T(8,128)(2,1)S(1)}, bf16[1,4,64,256]{3,2,1,0:T(8,128)(2,1)S(1)}, u32[]{:S(2)}, u32[]{:S(2)}) collective-permute-start(bf16[1,4,64,256]{3,2,1,0:T(8,128)(2,1)S(1)} %get-tuple-element.41), channel_id=1, source_target_pairs={{0,4},{4,0},{8,12},{12,8},{1,5},{5,1},{9,13},{13,9},{2,6},{6,2},{1... | collective-permute-start | bytes 393224 | tf_op jit(solution)/shard_map/ppermute | solution.py:311
  34.8 0.0 collective-permute-done.10.refs_0_
  34.8 0.8 %place_2_0.1 = (bf16[2048,128]{1,0:T(8,128)(2,1)}, bf16[2048,128]{1,0:T(8,128)(2,1)}) custom-call(bf16[2,512,128]{2,1,0:T(8,128)(2,1)S(1)} %collective-permute-done.10.refs_0_, bf16[2,512,128]{2,1,0:T(8,128)(2,1)S(1)} %get-tuple-element.43.refs_1_), custom_call_target="tpu_custom_call" | custom-call | flops 33822867456 | bytes 8388608 | tf_op jit(solution)/shard_map/place_2_0/pallas_call | solution.py:191
  35.6 12.1 %collective-permute-done.8 = bf16[1,4,64,256]{3,2,1,0:T(8,128)(2,1)S(1)} collective-permute-done((bf16[1,4,64,256]{3,2,1,0:T(8,128)(2,1)S(1)}, bf16[1,4,64,256]{3,2,1,0:T(8,128)(2,1)S(1)}, u32[]{:S(2)}, u32[]{:S(2)}) %collective-permute-start.8) | collective-permute-done | bytes 131104 | tf_op jit(solution)/shard_map/ppermute | solution.py:311
  47.7 1.3 %collective-permute-done.9 = bf16[1,4,64,256]{3,2,1,0:T(8,128)(2,1)S(1)} collective-permute-done((bf16[1,4,64,256]{3,2,1,0:T(8,128)(2,1)S(1)}, bf16[1,4,64,256]{3,2,1,0:T(8,128)(2,1)S(1)}, u32[]{:S(2)}, u32[]{:S(2)}) %collective-permute-start.9) | collective-permute-done | bytes 131104 | tf_op jit(solution)/shard_map/ppermute | solution.py:311
  49.0 0.0 collective-permute-done.4.refs_0_
  49.0 0.9 %place_1_3.1 = (bf16[2048,128]{1,0:T(8,128)(2,1)}, bf16[2048,128]{1,0:T(8,128)(2,1)}, bf16[256,128]{1,0:T(8,128)(2,1)}, bf16[256,128]{1,0:T(8,128)(2,1)}) custom-call(bf16[2,512,128]{2,1,0:T(8,128)(2,1)S(1)} %collective-permute-done.4.refs_0_, bf16[2,512,128]{2,1,0:T(8,128)(2,1)S(1)} %collective-permute-done.5.refs_1_, ...), custom_call_target="tpu_custom_call", output_to_operand_aliasing={{0}: (5, {}), {1}: (6, {})} | custom-call | flops 33822867456 | bytes 8388608 | tf_op jit(solution)/shard_map/place_1_3/pallas_call | solution.py:191
  (4 shorter events, 0.0 us)
Async XLA Ops:
  0.6 12.3 %collective-permute-start.2 = (bf16[256,128]{1,0:T(8,128)(2,1)}, bf16[256,128]{1,0:T(8,128)(2,1)S(1)}, u32[]{:S(2)}, u32[]{:S(2)}) collective-permute-start(bf16[256,128]{1,0:T(8,128)(2,1)} %bitcast.19), channel_id=1, source_target_pairs={{0,8},{4,12},{8,0},{12,4},{1,9},{5,13},{9,1},{13,5},{2,10},{6,14},... | collective-permute-start | bytes 196616 | tf_op jit(solution)/shard_map/ppermute | solution.py:311
  4.7 8.2 %collective-permute-start = (bf16[256,128]{1,0:T(8,128)(2,1)}, bf16[256,128]{1,0:T(8,128)(2,1)S(1)}, u32[]{:S(2)}, u32[]{:S(2)}) collective-permute-start(bf16[256,128]{1,0:T(8,128)(2,1)} %bitcast.20), channel_id=1, source_target_pairs={{0,4},{4,8},{8,12},{12,0},{1,5},{5,9},{9,13},{13,1},{2,6},{6,10},{... | collective-permute-start | bytes 196616 | tf_op jit(solution)/shard_map/ppermute | solution.py:311
  6.3 8.2 %collective-permute-start.3 = (bf16[256,128]{1,0:T(8,128)(2,1)}, bf16[256,128]{1,0:T(8,128)(2,1)S(1)}, u32[]{:S(2)}, u32[]{:S(2)}) collective-permute-start(bf16[256,128]{1,0:T(8,128)(2,1)} %bitcast.22), channel_id=1, source_target_pairs={{0,8},{4,12},{8,0},{12,4},{1,9},{5,13},{9,1},{13,5},{2,10},{6,14},... | collective-permute-start | bytes 196616 | tf_op jit(solution)/shard_map/ppermute | solution.py:311
  6.6 7.9 %collective-permute-start.1 = (bf16[256,128]{1,0:T(8,128)(2,1)}, bf16[256,128]{1,0:T(8,128)(2,1)S(1)}, u32[]{:S(2)}, u32[]{:S(2)}) collective-permute-start(bf16[256,128]{1,0:T(8,128)(2,1)} %bitcast.23), channel_id=1, source_target_pairs={{0,4},{4,8},{8,12},{12,0},{1,5},{5,9},{9,13},{13,1},{2,6},{6,10},{... | collective-permute-start | bytes 196616 | tf_op jit(solution)/shard_map/ppermute | solution.py:311
  9.1 0.7 %copy-start = (s32[4,4]{1,0:T(4,128)S(1)}, s32[4,4]{1,0:T(4,128)}, u32[]{:S(2)}) copy-start(s32[4,4]{1,0:T(4,128)} %param.11) | copy-start | bytes 196
  10.0 0.7 %copy-start.1 = (s32[8]{0:T(128)S(1)}, s32[8]{0:T(128)}, u32[]{:S(2)}) copy-start(s32[8]{0:T(128)} %param.10) | copy-start | bytes 100
  16.5 18.3 %collective-permute-start.10 = (bf16[2,512,128]{2,1,0:T(8,128)(2,1)S(1)}, bf16[2,512,128]{2,1,0:T(8,128)(2,1)S(1)}, u32[]{:S(2)}, u32[]{:S(2)}) collective-permute-start(bf16[2,512,128]{2,1,0:T(8,128)(2,1)S(1)} %get-tuple-element.42), channel_id=1, source_target_pairs={{0,8},{4,12},{8,0},{12,4},{1,9},{5,13},{9,1},{13,5},{2,10},{6,14},... | collective-permute-start | bytes 786440 | tf_op jit(solution)/shard_map/ppermute | solution.py:311
  23.6 8.6 %collective-permute-start.6 = (bf16[1,2,64,256]{3,2,1,0:T(8,128)(2,1)S(1)}, bf16[1,2,64,256]{3,2,1,0:T(8,128)(2,1)S(1)}, u32[]{:S(2)}, u32[]{:S(2)}) collective-permute-start(bf16[1,2,64,256]{3,2,1,0:T(8,128)(2,1)S(1)} %get-tuple-element.38), channel_id=1, source_target_pairs={{0,4},{4,0},{8,12},{12,8},{1,5},{5,1},{9,13},{13,9},{2,6},{6,2},{1... | collective-permute-start | bytes 196616 | tf_op jit(solution)/shard_map/ppermute | solution.py:311
  24.2 8.1 %collective-permute-start.7 = (bf16[1,2,64,256]{3,2,1,0:T(8,128)(2,1)S(1)}, bf16[1,2,64,256]{3,2,1,0:T(8,128)(2,1)S(1)}, u32[]{:S(2)}, u32[]{:S(2)}) collective-permute-start(bf16[1,2,64,256]{3,2,1,0:T(8,128)(2,1)S(1)} %get-tuple-element.39), channel_id=1, source_target_pairs={{8,12},{12,8},{9,13},{13,9},{10,14},{14,10},{11,15},{15,11},{24,28... | collective-permute-start | bytes 196616 | tf_op jit(solution)/shard_map/ppermute | solution.py:311
  24.8 24.2 %collective-permute-start.4 = (bf16[2,512,128]{2,1,0:T(8,128)(2,1)S(1)}, bf16[2,512,128]{2,1,0:T(8,128)(2,1)S(1)}, u32[]{:S(2)}, u32[]{:S(2)}) collective-permute-start(bf16[2,512,128]{2,1,0:T(8,128)(2,1)S(1)} %get-tuple-element.33), channel_id=1, source_target_pairs={{0,4},{4,0},{8,12},{12,8},{1,5},{5,1},{9,13},{13,9},{2,6},{6,2},{1... | collective-permute-start | bytes 786440 | tf_op jit(solution)/shard_map/ppermute | solution.py:311
  26.4 22.6 %collective-permute-start.5 = (bf16[2,512,128]{2,1,0:T(8,128)(2,1)S(1)}, bf16[2,512,128]{2,1,0:T(8,128)(2,1)S(1)}, u32[]{:S(2)}, u32[]{:S(2)}) collective-permute-start(bf16[2,512,128]{2,1,0:T(8,128)(2,1)S(1)} %get-tuple-element.34), channel_id=1, source_target_pairs={{0,12},{4,8},{8,4},{12,0},{1,13},{5,9},{9,5},{13,1},{2,14},{6,10},... | collective-permute-start | bytes 786440 | tf_op jit(solution)/shard_map/ppermute | solution.py:311
  32.3 15.5 %collective-permute-start.8 = (bf16[1,4,64,256]{3,2,1,0:T(8,128)(2,1)S(1)}, bf16[1,4,64,256]{3,2,1,0:T(8,128)(2,1)S(1)}, u32[]{:S(2)}, u32[]{:S(2)}) collective-permute-start(bf16[1,4,64,256]{3,2,1,0:T(8,128)(2,1)S(1)} %get-tuple-element.40), channel_id=1, source_target_pairs={{0,8},{4,12},{8,0},{12,4},{1,9},{5,13},{9,1},{13,5},{2,10},{6,14},... | collective-permute-start | bytes 393224 | tf_op jit(solution)/shard_map/ppermute | solution.py:311
  32.4 16.6 %collective-permute-start.9 = (bf16[1,4,64,256]{3,2,1,0:T(8,128)(2,1)S(1)}, bf16[1,4,64,256]{3,2,1,0:T(8,128)(2,1)S(1)}, u32[]{:S(2)}, u32[]{:S(2)}) collective-permute-start(bf16[1,4,64,256]{3,2,1,0:T(8,128)(2,1)S(1)} %get-tuple-element.41), channel_id=1, source_target_pairs={{0,4},{4,0},{8,12},{12,8},{1,5},{5,1},{9,13},{13,9},{2,6},{6,2},{1... | collective-permute-start | bytes 393224 | tf_op jit(solution)/shard_map/ppermute | solution.py:311
